TPU v7x, 32 devices: a whole 2x2x4 slice. The times are simulated.
32 devices in a mesh: section: 8 (over z, y), blk: 4 (over x, core).
Axes of the slice: x: 2, y: 2, z: 4, core: 2. Of those that a mesh axis runs over, the one named last changes fastest.
Arguments:
- pending_groups: bfloat16 [512, 16384], P('section', 'blk'), may hold values from -6 to 6
- coefficient_tiles: bfloat16 [8, 128, 8, 128, 128], P('section', 'blk'), may hold values from -0.25 to 0.25
- source_block_indices: int32 [8, 128, 8], P('section', 'blk'), may hold values from 0 to 127, as said below
- additive_offsets: float32 [8, 16384], P('section', 'blk'), may hold values from -1.75 to 1.75
Outputs:
- emitted: bfloat16 [8, 512, 16384], P(None, 'section', 'blk')
Inputs may be any that keep to these rules, and one draw needn't show every extreme that they name: `source_block_indices`: within a block-row the 8 block columns are distinct. A block-row held by index d of blk (block-rows d*32 to (d+1)*32 - 1) uses only block columns d*32 - 4 to (d+1)*32 + 3, taken modulo 128; in every layer the first block-row of each index uses column d*32 - 4 and the last uses (d+1)*32 + 3.
All inputs are finite; a program needn't handle non-finite values.
Results may differ from a plain program's by a relative error of at most 0.013.
Values may be sent and summed in bfloat16 or wider, within the bound.
No kernel may reach another device: no remote copies, remote signals or barrier semaphores. Data moves between devices by JAX's collectives and lax.ppermute only.
A program may use at most 64 MiB of HBM per device.

v0:
```python
import jax
import jax.numpy as jnp
from jax import lax
from jax.sharding import PartitionSpec as P

BLK = 128
HALO = 4
TICKS = 8


def padded_2(block, sides, width):
    for axis, dim in sides:
        count = lax.axis_size(axis)
        forward = [(i, i + 1) for i in range(count - 1)]
        forward.append((count - 1, 0))
        backward = [(target, source) for source, target in forward]
        low = lax.ppermute(
            lax.slice_in_dim(block, block.shape[dim] - width, None, axis=dim), axis, forward
        )
        high = lax.ppermute(lax.slice_in_dim(block, 0, width, axis=dim), axis, backward)
        block = jnp.concatenate([low, block, high], axis=dim)
    return block


def passed_along(block, axis, distance):
    devices = range(lax.axis_size(axis))
    route = [(i - distance, i) for i in devices if i - distance in devices]
    return lax.ppermute(block, axis, route)


def fringe(values):
    return padded_2(values, (("blk", 1),), HALO * BLK)


def passed_state(values):
    return passed_along(values, "section", 1)


def apply_layer(padded, layer_weights, local_cols, layer_bias):
    row_count = padded.shape[0]
    blocks = padded.reshape(row_count, padded.shape[1] // BLK, BLK)
    picked = jnp.take(blocks, local_cols, axis=1)
    summed = jnp.einsum("mikc,ikcd->mid", picked, layer_weights, preferred_element_type=jnp.float32)
    summed = summed.reshape(row_count, -1) + layer_bias
    return jnp.maximum(summed, 0.0)


def shards(pending_groups, coefficient_tiles, source_block_indices, additive_offsets):
    block_rows = coefficient_tiles.shape[1]
    segment_index = lax.axis_index("section")
    device_index = lax.axis_index("blk")
    local_cols = jnp.mod(
        source_block_indices[0] - device_index * block_rows + HALO,
        block_rows * lax.axis_size("blk"),
    )
    layer_weights = coefficient_tiles[0]
    layer_bias = additive_offsets[0][None, :]
    sample_groups = [pending_groups]
    emitted_ticks = []
    for tick_index in range(TICKS):
        batch_slice = sample_groups[0]
        padded = fringe(batch_slice)
        produced = apply_layer(padded, layer_weights, local_cols, layer_bias)
        produced = jnp.where(segment_index >= tick_index, produced, 0.0).astype(jnp.bfloat16)
        output_list = [produced]
        emitted_ticks.append(output_list[0])
        if tick_index + 1 < TICKS:
            sample_groups = [passed_state(result) for result in output_list]
    return jnp.stack(emitted_ticks)


def solution(mesh):
    in_specs = (
        P("section", "blk"),
        P("section", "blk", None, None, None),
        P("section", "blk", None),
        P("section", "blk"),
    )
    out_specs = P(None, "section", "blk")
    return jax.shard_map(shards, mesh=mesh, in_specs=in_specs, out_specs=out_specs, check_vma=False)
```

profile of v0, /device:TPU:1, one launch (start us, length us, event | category | flops | bytes accessed | tf_op | source)
XLA Modules:
  0.0 248.0 jit_solution(7289386867652475626)
XLA Ops:
  0.9 2.7 %collective-permute-start = (bf16[64,512]{1,0:T(8,128)(2,1)S(1)}, bf16[64,512]{1,0:T(8,128)(2,1)S(1)}, u32[]{:S(2)}, u32[]{:S(2)}) collective-permute-start(bf16[64,512]{1,0:T(8,128)(2,1)S(1)} %get-tuple-element.22), channel_id=1, source_target_pairs={{0,1},{1,2},{2,3},{3,0},{4,5},{5,6},{6,7},{7,4},{8,9},{9,10},{10,1... | collective-permute-start | bytes 196616 | tf_op jit(solution)/shard_map/ppermute | solution.py:17
  5.4 1.9 collective-permute-done.1
  7.2 1.2 copy_bitcast_fusion.7
  8.5 3.1 %gather_fusion = bf16[256,64,128]{2,1,0:T(8,128)(2,1)} fusion(bf16[64,40,128]{2,0,1:T(8,128)(2,1)S(1)} %copy_bitcast_fusion.7, s32[1024]{0:T(1024)S(1)} %pad_clamp_fusion), kind=kCustom, calls=%fused_computation.clone | custom fusion | bytes 8389632 | tf_op jit(solution)/shard_map/jit(_take)/gather | solution.py:42
  11.6 6.5 %fusion.14 = f32[32,64,128,1]{2,1,3,0:T(8,128)S(1)} fusion(bf16[1,32,8,128,128]{4,3,2,1,0:T(8,128)(2,1)} %param.7, bf16[32,8,64,128]{3,2,1,0:T(8,128)(2,1)} %bitcast.210, pred[32,8]{1,0:T(8,128)(4,1)S(1)} %copy.45), kind=kOutput, calls=%fused_computation.22 | convolution fusion | flops 538968064 | bytes 13631744 | tf_op jit(solution)/shard_map/mikc,ikcd->mid/dot_general | solution.py:43
  18.2 3.2 %collective-permute-start.2 = (bf16[64,4096]{1,0:T(8,128)(2,1)S(1)}, bf16[64,4096]{1,0:T(8,128)(2,1)S(1)}, u32[]{:S(2)}, u32[]{:S(2)}) collective-permute-start(bf16[64,4096]{1,0:T(8,128)(2,1)S(1)} %fusion.73), channel_id=1, source_target_pairs={{0,4},{4,8},{8,12},{12,16},{16,20},{20,24},{24,28},{1,5},{5,9},{9,... | collective-permute-start | bytes 1572872 | tf_op jit(solution)/shard_map/ppermute | solution.py:28
  21.4 11.1 %collective-permute-done.2 = bf16[64,4096]{1,0:T(8,128)(2,1)S(1)} collective-permute-done((bf16[64,4096]{1,0:T(8,128)(2,1)S(1)}, bf16[64,4096]{1,0:T(8,128)(2,1)S(1)}, u32[]{:S(2)}, u32[]{:S(2)}) %collective-permute-start.2) | collective-permute-done | bytes 524320 | tf_op jit(solution)/shard_map/ppermute | solution.py:28
  32.5 1.2 collective-permute-start.3
  33.7 1.3 collective-permute-done.3
  35.0 2.4 collective-permute-done.4
  37.6 3.1 %gather_fusion.1 = bf16[256,64,128]{2,1,0:T(8,128)(2,1)} fusion(bf16[64,40,128]{2,0,1:T(8,128)(2,1)S(1)} %copy_bitcast_fusion.6, s32[1024]{0:T(1024)S(1)} %pad_clamp_fusion), kind=kCustom, calls=%fused_computation.1.clone | custom fusion | bytes 8389632 | tf_op jit(solution)/shard_map/jit(_take)/gather | solution.py:42
  40.7 6.5 %fusion.12 = f32[32,64,128,1]{2,1,3,0:T(8,128)S(1)} fusion(bf16[1,32,8,128,128]{4,3,2,1,0:T(8,128)(2,1)} %param.7, bf16[32,8,64,128]{3,2,1,0:T(8,128)(2,1)} %bitcast.211, pred[32,8]{1,0:T(8,128)(4,1)S(1)} %copy.45), kind=kOutput, calls=%fused_computation.20 | convolution fusion | flops 538968064 | bytes 13631744 | tf_op jit(solution)/shard_map/mikc,ikcd->mid/dot_general | solution.py:43
  47.4 4.1 %collective-permute-start.5 = (bf16[64,4096]{1,0:T(8,128)(2,1)S(1)}, bf16[64,4096]{1,0:T(8,128)(2,1)S(1)}, u32[]{:S(2)}, u32[]{:S(2)}) collective-permute-start(bf16[64,4096]{1,0:T(8,128)(2,1)S(1)} %fusion.70), channel_id=1, source_target_pairs={{0,4},{4,8},{8,12},{12,16},{16,20},{20,24},{24,28},{1,5},{5,9},{9,... | collective-permute-start | bytes 1572872 | tf_op jit(solution)/shard_map/ppermute | solution.py:28
  51.5 10.8 %collective-permute-done.5 = bf16[64,4096]{1,0:T(8,128)(2,1)S(1)} collective-permute-done((bf16[64,4096]{1,0:T(8,128)(2,1)S(1)}, bf16[64,4096]{1,0:T(8,128)(2,1)S(1)}, u32[]{:S(2)}, u32[]{:S(2)}) %collective-permute-start.5) | collective-permute-done | bytes 524320 | tf_op jit(solution)/shard_map/ppermute | solution.py:28
  63.1 1.3 collective-permute-start.6
  64.5 1.7 collective-permute-done.6
  66.2 2.0 collective-permute-done.7
  68.2 1.2 copy_bitcast_fusion.5
  69.4 3.1 %gather_fusion.2 = bf16[256,64,128]{2,1,0:T(8,128)(2,1)} fusion(bf16[64,40,128]{2,0,1:T(8,128)(2,1)S(1)} %copy_bitcast_fusion.5, s32[1024]{0:T(1024)S(1)} %pad_clamp_fusion), kind=kCustom, calls=%fused_computation.2.clone | custom fusion | bytes 8389632 | tf_op jit(solution)/shard_map/jit(_take)/gather | solution.py:42
  72.5 6.5 %fusion.10 = f32[32,64,128,1]{2,1,3,0:T(8,128)S(1)} fusion(bf16[1,32,8,128,128]{4,3,2,1,0:T(8,128)(2,1)} %param.7, bf16[32,8,64,128]{3,2,1,0:T(8,128)(2,1)} %bitcast.212, pred[32,8]{1,0:T(8,128)(4,1)S(1)} %copy.45), kind=kOutput, calls=%fused_computation.18 | convolution fusion | flops 538968064 | bytes 13631744 | tf_op jit(solution)/shard_map/mikc,ikcd->mid/dot_general | solution.py:43
  79.0 1.0 copy-done
  80.1 4.1 %collective-permute-start.8 = (bf16[64,4096]{1,0:T(8,128)(2,1)S(1)}, bf16[64,4096]{1,0:T(8,128)(2,1)S(1)}, u32[]{:S(2)}, u32[]{:S(2)}) collective-permute-start(bf16[64,4096]{1,0:T(8,128)(2,1)S(1)} %fusion.67), channel_id=1, source_target_pairs={{0,4},{4,8},{8,12},{12,16},{16,20},{20,24},{24,28},{1,5},{5,9},{9,... | collective-permute-start | bytes 1572872 | tf_op jit(solution)/shard_map/ppermute | solution.py:28
  84.3 10.8 %collective-permute-done.8 = bf16[64,4096]{1,0:T(8,128)(2,1)S(1)} collective-permute-done((bf16[64,4096]{1,0:T(8,128)(2,1)S(1)}, bf16[64,4096]{1,0:T(8,128)(2,1)S(1)}, u32[]{:S(2)}, u32[]{:S(2)}) %collective-permute-start.8) | collective-permute-done | bytes 524320 | tf_op jit(solution)/shard_map/ppermute | solution.py:28
  95.9 1.5 collective-permute-start.9
  97.4 1.9 collective-permute-done.9
  99.3 1.8 collective-permute-done.10
  101.1 1.2 copy_bitcast_fusion.4
  102.3 3.1 %gather_fusion.3 = bf16[256,64,128]{2,1,0:T(8,128)(2,1)} fusion(bf16[64,40,128]{2,0,1:T(8,128)(2,1)S(1)} %copy_bitcast_fusion.4, s32[1024]{0:T(1024)S(1)} %pad_clamp_fusion), kind=kCustom, calls=%fused_computation.3.clone | custom fusion | bytes 8389632 | tf_op jit(solution)/shard_map/jit(_take)/gather | solution.py:42
  105.4 6.5 %fusion.8 = f32[32,64,128,1]{2,1,3,0:T(8,128)S(1)} fusion(bf16[1,32,8,128,128]{4,3,2,1,0:T(8,128)(2,1)} %param.7, bf16[32,8,64,128]{3,2,1,0:T(8,128)(2,1)} %bitcast.213, pred[32,8]{1,0:T(8,128)(4,1)S(1)} %copy.45), kind=kOutput, calls=%fused_computation.16 | convolution fusion | flops 538968064 | bytes 13631744 | tf_op jit(solution)/shard_map/mikc,ikcd->mid/dot_general | solution.py:43
  111.9 1.0 copy-done.2
  113.9 5.7 %collective-permute-start.11 = (bf16[64,4096]{1,0:T(8,128)(2,1)}, bf16[64,4096]{1,0:T(8,128)(2,1)}, u32[]{:S(2)}, u32[]{:S(2)}) collective-permute-start(bf16[64,4096]{1,0:T(8,128)(2,1)} %fusion.64), channel_id=1, source_target_pairs={{0,4},{4,8},{8,12},{12,16},{16,20},{20,24},{24,28},{1,5},{5,9},{9,... | collective-permute-start | bytes 1572872 | tf_op jit(solution)/shard_map/ppermute | solution.py:28
  119.6 1.6 copy.48
  121.1 1.4 reshape.416
  122.6 7.3 %collective-permute-done.11 = bf16[64,4096]{1,0:T(8,128)(2,1)} collective-permute-done((bf16[64,4096]{1,0:T(8,128)(2,1)}, bf16[64,4096]{1,0:T(8,128)(2,1)}, u32[]{:S(2)}, u32[]{:S(2)}) %collective-permute-start.11) | collective-permute-done | bytes 524320 | tf_op jit(solution)/shard_map/ppermute | solution.py:28
  130.8 1.7 collective-permute-start.12
  134.2 1.9 collective-permute-done.13
  136.1 1.2 copy_bitcast_fusion.3
  137.3 3.1 %gather_fusion.4 = bf16[256,64,128]{2,1,0:T(8,128)(2,1)} fusion(bf16[64,40,128]{2,0,1:T(8,128)(2,1)S(1)} %copy_bitcast_fusion.3, s32[1024]{0:T(1024)S(1)} %pad_clamp_fusion), kind=kCustom, calls=%fused_computation.4.clone | custom fusion | bytes 8389632 | tf_op jit(solution)/shard_map/jit(_take)/gather | solution.py:42
  140.4 6.6 %fusion.6 = f32[32,64,128,1]{2,1,3,0:T(8,128)S(1)} fusion(bf16[1,32,8,128,128]{4,3,2,1,0:T(8,128)(2,1)} %param.7, bf16[32,8,64,128]{3,2,1,0:T(8,128)(2,1)} %bitcast.214, pred[32,8]{1,0:T(8,128)(4,1)S(1)} %copy.45), kind=kOutput, calls=%fused_computation.14 | convolution fusion | flops 538968064 | bytes 13631744 | tf_op jit(solution)/shard_map/mikc,ikcd->mid/dot_general | solution.py:43
  147.0 0.9 fusion.61
  147.9 5.9 %collective-permute-start.14 = (bf16[64,4096]{1,0:T(8,128)(2,1)}, bf16[64,4096]{1,0:T(8,128)(2,1)}, u32[]{:S(2)}, u32[]{:S(2)}) collective-permute-start(bf16[64,4096]{1,0:T(8,128)(2,1)} %fusion.61), channel_id=1, source_target_pairs={{0,4},{4,8},{8,12},{12,16},{16,20},{20,24},{24,28},{1,5},{5,9},{9,... | collective-permute-start | bytes 1572872 | tf_op jit(solution)/shard_map/ppermute | solution.py:28
  154.8 1.6 copy.58
  156.4 1.4 reshape.422
  157.8 6.0 %collective-permute-done.14 = bf16[64,4096]{1,0:T(8,128)(2,1)} collective-permute-done((bf16[64,4096]{1,0:T(8,128)(2,1)}, bf16[64,4096]{1,0:T(8,128)(2,1)}, u32[]{:S(2)}, u32[]{:S(2)}) %collective-permute-start.14) | collective-permute-done | bytes 524320 | tf_op jit(solution)/shard_map/ppermute | solution.py:28
  164.7 1.7 collective-permute-start.15
  167.2 1.6 copy.63
  168.8 1.4 reshape.425
  170.3 1.2 copy_bitcast_fusion.2
  171.5 3.1 %gather_fusion.5 = bf16[256,64,128]{2,1,0:T(8,128)(2,1)} fusion(bf16[64,40,128]{2,0,1:T(8,128)(2,1)S(1)} %copy_bitcast_fusion.2, s32[1024]{0:T(1024)S(1)} %pad_clamp_fusion), kind=kCustom, calls=%fused_computation.5.clone | custom fusion | bytes 8389632 | tf_op jit(solution)/shard_map/jit(_take)/gather | solution.py:42
  174.6 6.5 %fusion.4 = f32[32,64,128,1]{2,1,3,0:T(8,128)S(1)} fusion(bf16[1,32,8,128,128]{4,3,2,1,0:T(8,128)(2,1)} %param.7, bf16[32,8,64,128]{3,2,1,0:T(8,128)(2,1)} %bitcast.215, pred[32,8]{1,0:T(8,128)(4,1)S(1)} %copy.45), kind=kOutput, calls=%fused_computation.12 | convolution fusion | flops 538968064 | bytes 13631744 | tf_op jit(solution)/shard_map/mikc,ikcd->mid/dot_general | solution.py:43
  182.0 5.8 %collective-permute-start.17 = (bf16[64,4096]{1,0:T(8,128)(2,1)}, bf16[64,4096]{1,0:T(8,128)(2,1)}, u32[]{:S(2)}, u32[]{:S(2)}) collective-permute-start(bf16[64,4096]{1,0:T(8,128)(2,1)} %fusion.58), channel_id=1, source_target_pairs={{0,4},{4,8},{8,12},{12,16},{16,20},{20,24},{24,28},{1,5},{5,9},{9,... | collective-permute-start | bytes 1572872 | tf_op jit(solution)/shard_map/ppermute | solution.py:28
  189.5 9.1 %collective-permute-done.17 = bf16[64,4096]{1,0:T(8,128)(2,1)} collective-permute-done((bf16[64,4096]{1,0:T(8,128)(2,1)}, bf16[64,4096]{1,0:T(8,128)(2,1)}, u32[]{:S(2)}, u32[]{:S(2)}) %collective-permute-start.17) | collective-permute-done | bytes 524320 | tf_op jit(solution)/shard_map/ppermute | solution.py:28
  202.2 1.9 collective-permute-done.19
  204.1 1.2 copy_bitcast_fusion.1
  205.4 3.1 %gather_fusion.6 = bf16[256,64,128]{2,1,0:T(8,128)(2,1)} fusion(bf16[64,40,128]{2,0,1:T(8,128)(2,1)S(1)} %copy_bitcast_fusion.1, s32[1024]{0:T(1024)S(1)} %pad_clamp_fusion), kind=kCustom, calls=%fused_computation.6.clone | custom fusion | bytes 8389632 | tf_op jit(solution)/shard_map/jit(_take)/gather | solution.py:42
  208.4 6.5 %fusion.2 = f32[32,64,128,1]{2,1,3,0:T(8,128)S(1)} fusion(bf16[1,32,8,128,128]{4,3,2,1,0:T(8,128)(2,1)} %param.7, bf16[32,8,64,128]{3,2,1,0:T(8,128)(2,1)} %bitcast.216, pred[32,8]{1,0:T(8,128)(4,1)S(1)} %copy.45), kind=kOutput, calls=%fused_computation.10 | convolution fusion | flops 538968064 | bytes 13631744 | tf_op jit(solution)/shard_map/mikc,ikcd->mid/dot_general | solution.py:43
  215.1 5.1 %collective-permute-start.20 = (bf16[64,4096]{1,0:T(8,128)(2,1)S(1)}, bf16[64,4096]{1,0:T(8,128)(2,1)S(1)}, u32[]{:S(2)}, u32[]{:S(2)}) collective-permute-start(bf16[64,4096]{1,0:T(8,128)(2,1)S(1)} %fusion.55), channel_id=1, source_target_pairs={{0,4},{4,8},{8,12},{12,16},{16,20},{20,24},{24,28},{1,5},{5,9},{9,... | collective-permute-start | bytes 1572872 | tf_op jit(solution)/shard_map/ppermute | solution.py:28
  220.1 0.9 fusion.79
  221.9 9.7 %collective-permute-done.20 = bf16[64,4096]{1,0:T(8,128)(2,1)S(1)} collective-permute-done((bf16[64,4096]{1,0:T(8,128)(2,1)S(1)}, bf16[64,4096]{1,0:T(8,128)(2,1)S(1)}, u32[]{:S(2)}, u32[]{:S(2)}) %collective-permute-start.20) | collective-permute-done | bytes 524320 | tf_op jit(solution)/shard_map/ppermute | solution.py:28
  231.5 1.2 collective-permute-start.21
  234.1 2.4 collective-permute-done.22
  236.6 3.1 %gather_fusion.7 = bf16[256,64,128]{2,1,0:T(8,128)(2,1)} fusion(bf16[64,40,128]{2,0,1:T(8,128)(2,1)S(1)} %copy_bitcast_fusion, s32[1024]{0:T(1024)S(1)} %pad_clamp_fusion), kind=kCustom, calls=%fused_computation.7.clone | custom fusion | bytes 8389632 | tf_op jit(solution)/shard_map/jit(_take)/gather | solution.py:42
  239.7 6.5 %fusion.48 = f32[64,32,128]{2,0,1:T(8,128)S(1)} fusion(bf16[1,32,8,128,128]{4,3,2,1,0:T(8,128)(2,1)} %param.7, bf16[32,8,64,128]{3,2,1,0:T(8,128)(2,1)} %bitcast.209, pred[32,8]{1,0:T(8,128)(4,1)S(1)} %copy.45), kind=kOutput, calls=%fused_computation.56 | convolution fusion | flops 538968064 | bytes 13631744 | tf_op jit(solution)/shard_map/mikc,ikcd->mid/dot_general | solution.py:43
  247.0 0.9 fusion.81
  (64 shorter events, 20.5 us)
Async XLA Ops:
  0.9 4.5 %collective-permute-start = (bf16[64,512]{1,0:T(8,128)(2,1)S(1)}, bf16[64,512]{1,0:T(8,128)(2,1)S(1)}, u32[]{:S(2)}, u32[]{:S(2)}) collective-permute-start(bf16[64,512]{1,0:T(8,128)(2,1)S(1)} %get-tuple-element.22), channel_id=1, source_target_pairs={{0,1},{1,2},{2,3},{3,0},{4,5},{5,6},{6,7},{7,4},{8,9},{9,10},{10,1... | collective-permute-start | bytes 196616 | tf_op jit(solution)/shard_map/ppermute | solution.py:17
  3.5 3.7 %collective-permute-start.1 = (bf16[64,512]{1,0:T(8,128)(2,1)S(1)}, bf16[64,512]{1,0:T(8,128)(2,1)S(1)}, u32[]{:S(2)}, u32[]{:S(2)}) collective-permute-start(bf16[64,512]{1,0:T(8,128)(2,1)S(1)} %get-tuple-element.23), channel_id=1, source_target_pairs={{1,0},{2,1},{3,2},{0,3},{5,4},{6,5},{7,6},{4,7},{9,8},{10,9},{11,1... | collective-permute-start | bytes 196616 | tf_op jit(solution)/shard_map/ppermute | solution.py:20
  11.6 6.5 %copy-start.4 = (f32[1,4096]{1,0:T(1,128)S(1)}, f32[1,4096]{1,0:T(1,128)}, u32[]{:S(2)}) copy-start(f32[1,4096]{1,0:T(1,128)} %param.9) | copy-start | bytes 49156
  18.2 14.3 %collective-permute-start.2 = (bf16[64,4096]{1,0:T(8,128)(2,1)S(1)}, bf16[64,4096]{1,0:T(8,128)(2,1)S(1)}, u32[]{:S(2)}, u32[]{:S(2)}) collective-permute-start(bf16[64,4096]{1,0:T(8,128)(2,1)S(1)} %fusion.73), channel_id=1, source_target_pairs={{0,4},{4,8},{8,12},{12,16},{16,20},{20,24},{24,28},{1,5},{5,9},{9,... | collective-permute-start | bytes 1572872 | tf_op jit(solution)/shard_map/ppermute | solution.py:28
  32.5 2.5 %collective-permute-start.3 = (bf16[64,512]{1,0:T(8,128)(2,1)S(1)}, bf16[64,512]{1,0:T(8,128)(2,1)S(1)}, u32[]{:S(2)}, u32[]{:S(2)}) collective-permute-start(bf16[64,512]{1,0:T(8,128)(2,1)S(1)} %get-tuple-element.20), channel_id=1, source_target_pairs={{0,1},{1,2},{2,3},{3,0},{4,5},{5,6},{6,7},{7,4},{8,9},{9,10},{10,1... | collective-permute-start | bytes 196616 | tf_op jit(solution)/shard_map/ppermute | solution.py:17
  33.7 3.7 %collective-permute-start.4 = (bf16[64,512]{1,0:T(8,128)(2,1)S(1)}, bf16[64,512]{1,0:T(8,128)(2,1)S(1)}, u32[]{:S(2)}, u32[]{:S(2)}) collective-permute-start(bf16[64,512]{1,0:T(8,128)(2,1)S(1)} %get-tuple-element.21), channel_id=1, source_target_pairs={{1,0},{2,1},{3,2},{0,3},{5,4},{6,5},{7,6},{4,7},{9,8},{10,9},{11,1... | collective-permute-start | bytes 196616 | tf_op jit(solution)/shard_map/ppermute | solution.py:20
  47.4 15.0 %collective-permute-start.5 = (bf16[64,4096]{1,0:T(8,128)(2,1)S(1)}, bf16[64,4096]{1,0:T(8,128)(2,1)S(1)}, u32[]{:S(2)}, u32[]{:S(2)}) collective-permute-start(bf16[64,4096]{1,0:T(8,128)(2,1)S(1)} %fusion.70), channel_id=1, source_target_pairs={{0,4},{4,8},{8,12},{12,16},{16,20},{20,24},{24,28},{1,5},{5,9},{9,... | collective-permute-start | bytes 1572872 | tf_op jit(solution)/shard_map/ppermute | solution.py:28
  62.3 0.8 copy-start.5
  63.1 3.1 %collective-permute-start.6 = (bf16[64,512]{1,0:T(8,128)(2,1)S(1)}, bf16[64,512]{1,0:T(8,128)(2,1)S(1)}, u32[]{:S(2)}, u32[]{:S(2)}) collective-permute-start(bf16[64,512]{1,0:T(8,128)(2,1)S(1)} %get-tuple-element.18), channel_id=1, source_target_pairs={{0,1},{1,2},{2,3},{3,0},{4,5},{5,6},{6,7},{7,4},{8,9},{9,10},{10,1... | collective-permute-start | bytes 196616 | tf_op jit(solution)/shard_map/ppermute | solution.py:17
  64.5 3.7 %collective-permute-start.7 = (bf16[64,512]{1,0:T(8,128)(2,1)S(1)}, bf16[64,512]{1,0:T(8,128)(2,1)S(1)}, u32[]{:S(2)}, u32[]{:S(2)}) collective-permute-start(bf16[64,512]{1,0:T(8,128)(2,1)S(1)} %get-tuple-element.19), channel_id=1, source_target_pairs={{1,0},{2,1},{3,2},{0,3},{5,4},{6,5},{7,6},{4,7},{9,8},{10,9},{11,1... | collective-permute-start | bytes 196616 | tf_op jit(solution)/shard_map/ppermute | solution.py:20
  79.0 1.0 copy-start
  80.1 14.9 %collective-permute-start.8 = (bf16[64,4096]{1,0:T(8,128)(2,1)S(1)}, bf16[64,4096]{1,0:T(8,128)(2,1)S(1)}, u32[]{:S(2)}, u32[]{:S(2)}) collective-permute-start(bf16[64,4096]{1,0:T(8,128)(2,1)S(1)} %fusion.67), channel_id=1, source_target_pairs={{0,4},{4,8},{8,12},{12,16},{16,20},{20,24},{24,28},{1,5},{5,9},{9,... | collective-permute-start | bytes 1572872 | tf_op jit(solution)/shard_map/ppermute | solution.py:28
  95.1 0.8 copy-start.6
  95.9 3.4 %collective-permute-start.9 = (bf16[64,512]{1,0:T(8,128)(2,1)S(1)}, bf16[64,512]{1,0:T(8,128)(2,1)S(1)}, u32[]{:S(2)}, u32[]{:S(2)}) collective-permute-start(bf16[64,512]{1,0:T(8,128)(2,1)S(1)} %get-tuple-element.16), channel_id=1, source_target_pairs={{0,1},{1,2},{2,3},{3,0},{4,5},{5,6},{6,7},{7,4},{8,9},{9,10},{10,1... | collective-permute-start | bytes 196616 | tf_op jit(solution)/shard_map/ppermute | solution.py:17
  97.4 3.7 %collective-permute-start.10 = (bf16[64,512]{1,0:T(8,128)(2,1)S(1)}, bf16[64,512]{1,0:T(8,128)(2,1)S(1)}, u32[]{:S(2)}, u32[]{:S(2)}) collective-permute-start(bf16[64,512]{1,0:T(8,128)(2,1)S(1)} %get-tuple-element.17), channel_id=1, source_target_pairs={{1,0},{2,1},{3,2},{0,3},{5,4},{6,5},{7,6},{4,7},{9,8},{10,9},{11,1... | collective-permute-start | bytes 196616 | tf_op jit(solution)/shard_map/ppermute | solution.py:20
  111.9 1.0 copy-start.2
  113.9 16.0 %collective-permute-start.11 = (bf16[64,4096]{1,0:T(8,128)(2,1)}, bf16[64,4096]{1,0:T(8,128)(2,1)}, u32[]{:S(2)}, u32[]{:S(2)}) collective-permute-start(bf16[64,4096]{1,0:T(8,128)(2,1)} %fusion.64), channel_id=1, source_target_pairs={{0,4},{4,8},{8,12},{12,16},{16,20},{20,24},{24,28},{1,5},{5,9},{9,... | collective-permute-start | bytes 1572872 | tf_op jit(solution)/shard_map/ppermute | solution.py:28
  130.8 3.4 %collective-permute-start.12 = (bf16[64,512]{1,0:T(8,128)(2,1)S(1)}, bf16[64,512]{1,0:T(8,128)(2,1)S(1)}, u32[]{:S(2)}, u32[]{:S(2)}) collective-permute-start(bf16[64,512]{1,0:T(8,128)(2,1)S(1)} %get-tuple-element.14), channel_id=1, source_target_pairs={{0,1},{1,2},{2,3},{3,0},{4,5},{5,6},{6,7},{7,4},{8,9},{9,10},{10,1... | collective-permute-start | bytes 196616 | tf_op jit(solution)/shard_map/ppermute | solution.py:17
  132.4 3.7 %collective-permute-start.13 = (bf16[64,512]{1,0:T(8,128)(2,1)S(1)}, bf16[64,512]{1,0:T(8,128)(2,1)S(1)}, u32[]{:S(2)}, u32[]{:S(2)}) collective-permute-start(bf16[64,512]{1,0:T(8,128)(2,1)S(1)} %get-tuple-element.15), channel_id=1, source_target_pairs={{1,0},{2,1},{3,2},{0,3},{5,4},{6,5},{7,6},{4,7},{9,8},{10,9},{11,1... | collective-permute-start | bytes 196616 | tf_op jit(solution)/shard_map/ppermute | solution.py:20
  140.4 14.4 %copy-start.1 = (f32[32,64,128,1]{2,1,3,0:T(8,128)S(1)}, f32[32,64,128,1]{2,1,3,0:T(8,128)}, u32[]{:S(2)}) copy-start(f32[32,64,128,1]{2,1,3,0:T(8,128)} %copy-done) | copy-start | bytes 3145732
  147.9 19.3 %copy-start.3 = (f32[32,64,128,1]{2,1,3,0:T(8,128)S(1)}, f32[32,64,128,1]{2,1,3,0:T(8,128)}, u32[]{:S(2)}) copy-start(f32[32,64,128,1]{2,1,3,0:T(8,128)} %copy-done.2) | copy-start | bytes 3145732
  147.9 15.8 %collective-permute-start.14 = (bf16[64,4096]{1,0:T(8,128)(2,1)}, bf16[64,4096]{1,0:T(8,128)(2,1)}, u32[]{:S(2)}, u32[]{:S(2)}) collective-permute-start(bf16[64,4096]{1,0:T(8,128)(2,1)} %fusion.61), channel_id=1, source_target_pairs={{0,4},{4,8},{8,12},{12,16},{16,20},{20,24},{24,28},{1,5},{5,9},{9,... | collective-permute-start | bytes 1572872 | tf_op jit(solution)/shard_map/ppermute | solution.py:28
  164.7 5.6 %collective-permute-start.15 = (bf16[64,512]{1,0:T(8,128)(2,1)S(1)}, bf16[64,512]{1,0:T(8,128)(2,1)S(1)}, u32[]{:S(2)}, u32[]{:S(2)}) collective-permute-start(bf16[64,512]{1,0:T(8,128)(2,1)S(1)} %get-tuple-element.12), channel_id=1, source_target_pairs={{0,1},{1,2},{2,3},{3,0},{4,5},{5,6},{6,7},{7,4},{8,9},{9,10},{10,1... | collective-permute-start | bytes 196616 | tf_op jit(solution)/shard_map/ppermute | solution.py:17
  166.3 3.9 %collective-permute-start.16 = (bf16[64,512]{1,0:T(8,128)(2,1)S(1)}, bf16[64,512]{1,0:T(8,128)(2,1)S(1)}, u32[]{:S(2)}, u32[]{:S(2)}) collective-permute-start(bf16[64,512]{1,0:T(8,128)(2,1)S(1)} %get-tuple-element.13), channel_id=1, source_target_pairs={{1,0},{2,1},{3,2},{0,3},{5,4},{6,5},{7,6},{4,7},{9,8},{10,9},{11,1... | collective-permute-start | bytes 196616 | tf_op jit(solution)/shard_map/ppermute | solution.py:20
  182.0 16.7 %collective-permute-start.17 = (bf16[64,4096]{1,0:T(8,128)(2,1)}, bf16[64,4096]{1,0:T(8,128)(2,1)}, u32[]{:S(2)}, u32[]{:S(2)}) collective-permute-start(bf16[64,4096]{1,0:T(8,128)(2,1)} %fusion.58), channel_id=1, source_target_pairs={{0,4},{4,8},{8,12},{12,16},{16,20},{20,24},{24,28},{1,5},{5,9},{9,... | collective-permute-start | bytes 1572872 | tf_op jit(solution)/shard_map/ppermute | solution.py:28
  199.5 2.6 %collective-permute-start.18 = (bf16[64,512]{1,0:T(8,128)(2,1)S(1)}, bf16[64,512]{1,0:T(8,128)(2,1)S(1)}, u32[]{:S(2)}, u32[]{:S(2)}) collective-permute-start(bf16[64,512]{1,0:T(8,128)(2,1)S(1)} %get-tuple-element.10), channel_id=1, source_target_pairs={{0,1},{1,2},{2,3},{3,0},{4,5},{5,6},{6,7},{7,4},{8,9},{9,10},{10,1... | collective-permute-start | bytes 196616 | tf_op jit(solution)/shard_map/ppermute | solution.py:17
  200.4 3.7 %collective-permute-start.19 = (bf16[64,512]{1,0:T(8,128)(2,1)S(1)}, bf16[64,512]{1,0:T(8,128)(2,1)S(1)}, u32[]{:S(2)}, u32[]{:S(2)}) collective-permute-start(bf16[64,512]{1,0:T(8,128)(2,1)S(1)} %get-tuple-element.11), channel_id=1, source_target_pairs={{1,0},{2,1},{3,2},{0,3},{5,4},{6,5},{7,6},{4,7},{9,8},{10,9},{11,1... | collective-permute-start | bytes 196616 | tf_op jit(solution)/shard_map/ppermute | solution.py:20
  215.1 16.4 %collective-permute-start.20 = (bf16[64,4096]{1,0:T(8,128)(2,1)S(1)}, bf16[64,4096]{1,0:T(8,128)(2,1)S(1)}, u32[]{:S(2)}, u32[]{:S(2)}) collective-permute-start(bf16[64,4096]{1,0:T(8,128)(2,1)S(1)} %fusion.55), channel_id=1, source_target_pairs={{0,4},{4,8},{8,12},{12,16},{16,20},{20,24},{24,28},{1,5},{5,9},{9,... | collective-permute-start | bytes 1572872 | tf_op jit(solution)/shard_map/ppermute | solution.py:28
  231.5 2.5 %collective-permute-start.21 = (bf16[64,512]{1,0:T(8,128)(2,1)S(1)}, bf16[64,512]{1,0:T(8,128)(2,1)S(1)}, u32[]{:S(2)}, u32[]{:S(2)}) collective-permute-start(bf16[64,512]{1,0:T(8,128)(2,1)S(1)} %get-tuple-element.8), channel_id=1, source_target_pairs={{0,1},{1,2},{2,3},{3,0},{4,5},{5,6},{6,7},{7,4},{8,9},{9,10},{10,1... | collective-permute-start | bytes 196616 | tf_op jit(solution)/shard_map/ppermute | solution.py:17
  232.8 3.7 %collective-permute-start.22 = (bf16[64,512]{1,0:T(8,128)(2,1)S(1)}, bf16[64,512]{1,0:T(8,128)(2,1)S(1)}, u32[]{:S(2)}, u32[]{:S(2)}) collective-permute-start(bf16[64,512]{1,0:T(8,128)(2,1)S(1)} %get-tuple-element.9), channel_id=1, source_target_pairs={{1,0},{2,1},{3,2},{0,3},{5,4},{6,5},{7,6},{4,7},{9,8},{10,9},{11,1... | collective-permute-start | bytes 196616 | tf_op jit(solution)/shard_map/ppermute | solution.py:20
where the time goes:
time: 252 us; the launch traced here: 248 us
  waiting for transfers between devices  85.2 us (34%)
  matrix products  52.2 us (21%)
  starting transfers between devices  46.1 us (18%)
  local copies, waits for them, and re-layouts  45.1 us (18%)
  other arithmetic  18.9 us (7%)
    ppermute x7, waiting for transfers between devices, passed_along(): return lax.ppermute(block, axis, route)  64.7 us
    dot_general x8, matrix products, apply_layer(): jnp.einsum('mikc,ikcd->mid', picked, layer_weights, preferred_element_typ...  52.2 us
    ppermute x7, starting transfers between devices, passed_along(): return lax.ppermute(block, axis, route)  33.9 us
    gather x8, local copies, waits for them, and re-layouts, apply_layer(): picked = jnp.take(blocks, local_cols, axis=1)  24.7 us
    ppermute x8, waiting for transfers between devices, padded_2(): lax.ppermute(lax.slice_in_dim(block, 0, width, axis=dim), axis, backward)  14.2 us
    ppermute x8, starting transfers between devices, padded_2(): lax.ppermute(lax.slice_in_dim(block, block.shape[dim] - width, None, axis...  12.2 us
    transpose x8, local copies, waits for them, and re-layouts, apply_layer(): jnp.einsum('mikc,ikcd->mid', picked, layer_weights, preferred_element_typ...  7.79 us
    reshape x8, other arithmetic, apply_layer(): blocks = padded.reshape(row_count, padded.shape[1] // BLK, BLK)  7.64 us
  transfers between devices with their start and end apart: 23, of which 19 were waited for; matrix products, arithmetic and copies ran while one was open for 8% of the time, Pallas kernels for 0%

commit v1 on v0

v1 whole, which is shorter than its diff:
```python
import functools

import jax
import jax.numpy as jnp
from jax import lax
from jax.experimental import pallas as pl
from jax.experimental.pallas import tpu as pltpu
from jax.sharding import PartitionSpec as P

BLK = 128
HALO = 4
TICKS = 8
CHUNKS = 2


def layer_kernel(tick, src_row, dst_row, rows, brs, nzb, meta, main, low, high, w, bias, emitted_in, emitted, out, left, right, xbuf, sem):
    del emitted_in
    edge = HALO * BLK
    width = brs * BLK
    live = meta[brs * nzb] >= tick

    @pl.when(live)
    def _():
        src = pl.ds(src_row, rows)
        xbuf[:, 0:edge] = low[src, :]
        xbuf[:, edge : edge + width] = main[src, :]
        xbuf[:, edge + width : edge + width + edge] = high[src, :]
        for i in range(brs):
            picked = jnp.concatenate(
                [
                    xbuf[:, pl.ds(pl.multiple_of(meta[i * nzb + k] * BLK, BLK), BLK)]
                    for k in range(nzb)
                ],
                axis=1,
            )
            cols = pl.ds(i * BLK, BLK)
            summed = jnp.dot(picked, w[i], preferred_element_type=jnp.float32) + bias[:, cols]
            made = jnp.maximum(summed, 0.0).astype(jnp.bfloat16)
            out[:, cols] = made
            if i < HALO:
                left[:, cols] = made
            if i >= brs - HALO:
                right[:, pl.ds((i - brs + HALO) * BLK, BLK)] = made

    @pl.when(jnp.logical_not(live))
    def _():
        out[...] = jnp.zeros_like(out)
        left[...] = jnp.zeros_like(left)
        right[...] = jnp.zeros_like(right)

    copy = pltpu.make_async_copy(out, emitted.at[tick, pl.ds(dst_row, rows), :], sem)
    copy.start()
    copy.wait()


def apply_layer(tick, src_row, dst_row, rows, meta, main, low, high, w, bias, emitted, out_aval):
    brs = w.shape[0]
    nzb = w.shape[1] // BLK
    width = brs * BLK
    edge = HALO * BLK
    vmem = pl.BlockSpec(memory_space=pltpu.VMEM)
    anywhere = pl.BlockSpec(memory_space=pl.ANY)
    body = functools.partial(layer_kernel, tick, src_row, dst_row, rows, brs, nzb)
    operands = [
        pltpu.with_memory_space_constraint(meta, pltpu.SMEM),
        main,
        low,
        high,
        pltpu.with_memory_space_constraint(w, pltpu.VMEM),
        bias,
    ]
    specs = [pl.BlockSpec(memory_space=pltpu.SMEM), vmem, vmem, vmem, vmem, vmem]
    aliases = {}
    if emitted is not None:
        operands.append(emitted)
        specs.append(anywhere)
        aliases = {6: 0}
    else:
        inner = body
        body = lambda *refs: inner(*refs[:6], None, *refs[6:])
    return pl.pallas_call(
        body,
        out_shape=(
            out_aval,
            jax.ShapeDtypeStruct((rows, width), jnp.bfloat16),
            jax.ShapeDtypeStruct((rows, edge), jnp.bfloat16),
            jax.ShapeDtypeStruct((rows, edge), jnp.bfloat16),
        ),
        in_specs=specs,
        out_specs=(anywhere, vmem, vmem, vmem),
        scratch_shapes=[
            pltpu.VMEM((rows, width + 2 * edge), jnp.bfloat16),
            pltpu.SemaphoreType.DMA,
        ],
        input_output_aliases=aliases,
        compiler_params=pltpu.CompilerParams(vmem_limit_bytes=8 * 1024 * 1024),
        cost_estimate=pl.CostEstimate(
            flops=2 * rows * brs * nzb * BLK * BLK, bytes_accessed=w.size * 2, transcendentals=0
        ),
        name=f"layer_t{tick}_r{dst_row}",
    )(*operands)


def shards(sections, blks, pending_groups, coefficient_tiles, source_block_indices, additive_offsets):
    block_rows, nzb = coefficient_tiles.shape[1:3]
    height, width = pending_groups.shape
    rows = height // CHUNKS
    edge = HALO * BLK
    section = lax.axis_index("section")
    me = lax.axis_index("blk")
    local_cols = jnp.mod(source_block_indices[0] - me * block_rows + HALO, block_rows * blks)
    meta = jnp.concatenate([local_cols.reshape(-1), section.astype(jnp.int32)[None]])
    w = coefficient_tiles.reshape(block_rows, nzb * BLK, BLK)
    emitted_aval = jax.ShapeDtypeStruct((TICKS, height, width), jnp.bfloat16)

    def ring(shift):
        return [(i, (i + shift) % blks) for i in range(blks)]

    def onward(first, shift):
        return [
            (s * blks + i, (s + 1) * blks + (i + shift) % blks)
            for s in range(first, sections - 1)
            for i in range(blks)
        ]

    low = lax.ppermute(pending_groups[:, width - edge :], "blk", ring(1))
    high = lax.ppermute(pending_groups[:, :edge], "blk", ring(-1))
    parts = [(pending_groups, low, high, c * rows) for c in range(CHUNKS)]
    emitted = None
    for tick in range(TICKS):
        for c in range(CHUNKS):
            main, low, high, src_row = parts[c]
            emitted, out, left, right = apply_layer(
                tick, src_row, c * rows, rows, meta, main, low, high, w, additive_offsets, emitted, emitted_aval
            )
            if tick + 1 < TICKS:
                axes = ("section", "blk")
                parts[c] = (
                    lax.ppermute(out, axes, onward(tick, 0)),
                    lax.ppermute(right, axes, onward(tick, 1)),
                    lax.ppermute(left, axes, onward(tick, -1)),
                    0,
                )
    return emitted


def solution(mesh):
    in_specs = (
        P("section", "blk"),
        P("section", "blk", None, None, None),
        P("section", "blk", None),
        P("section", "blk"),
    )
    out_specs = P(None, "section", "blk")
    body = functools.partial(shards, mesh.shape["section"], mesh.shape["blk"])
    return jax.shard_map(body, mesh=mesh, in_specs=in_specs, out_specs=out_specs, check_vma=False)
```

time: 252 us -> 208 us (0.83)
  the two profiles are of different devices: /device:TPU:1 before, /device:TPU:29 now
where the time goes in v1:
time: 208 us; the launch traced here: 207 us
  starting transfers between devices  97.4 us (47%)
  waiting for transfers between devices  55.6 us (27%)
  Pallas kernels  46.1 us (22%)
  local copies, waits for them, and re-layouts  6.2 us (3%)
    ppermute x14, waiting for transfers between devices, shards(): lax.ppermute(right, axes, onward(tick, 1))  50.2 us
    pallas_call x16, Pallas kernels, apply_layer(): pl.pallas_call(body, out_shape=(out_aval, jax.ShapeDtypeStruct((rows, wid...  46.1 us
    ppermute x14, starting transfers between devices, shards(): lax.ppermute(out, axes, onward(tick, 0))  29.2 us
    ppermute x14, starting transfers between devices, shards(): lax.ppermute(right, axes, onward(tick, 1))  28.2 us
    ppermute x14, starting transfers between devices, shards(): lax.ppermute(left, axes, onward(tick, -1))  28.2 us
    ppermute x1, starting transfers between devices, shards(): high = lax.ppermute(pending_groups[:, :edge], 'blk', ring(-1))  6.12 us
    ppermute x1, starting transfers between devices, shards(): low = lax.ppermute(pending_groups[:, width - edge:], 'blk', ring(1))  5.73 us
    unnamed x12, local copies, waits for them, and re-layouts  5.15 us
  transfers between devices with their start and end apart: 44, of which 13 were waited for; matrix products, arithmetic and copies ran while one was open for 0% of the time, Pallas kernels for 19%

profile of v1, /device:TPU:29, one launch (start us, length us, event | category | flops | bytes accessed | tf_op | source)
XLA Modules:
  0.0 206.9 jit_solution(18195811915669891447)
XLA Ops:
  0.9 6.1 %collective-permute-start.1 = (bf16[64,512]{1,0:T(8,128)(2,1)S(1)}, bf16[64,512]{1,0:T(8,128)(2,1)S(1)}, u32[]{:S(2)}, u32[]{:S(2)}) collective-permute-start(bf16[64,512]{1,0:T(8,128)(2,1)S(1)} %get-tuple-element.121), channel_id=1, source_target_pairs={{0,3},{1,0},{2,1},{3,2},{4,7},{5,4},{6,5},{7,6},{8,11},{9,8},{10,9... | collective-permute-start | bytes 196616 | tf_op jit(solution)/shard_map/ppermute | solution.py:127
  7.0 5.7 %collective-permute-start = (bf16[64,512]{1,0:T(8,128)(2,1)S(1)}, bf16[64,512]{1,0:T(8,128)(2,1)S(1)}, u32[]{:S(2)}, u32[]{:S(2)}) collective-permute-start(bf16[64,512]{1,0:T(8,128)(2,1)S(1)} %get-tuple-element.122), channel_id=1, source_target_pairs={{0,1},{1,2},{2,3},{3,0},{4,5},{5,6},{6,7},{7,4},{8,9},{9,10},{10,1... | collective-permute-start | bytes 196616 | tf_op jit(solution)/shard_map/ppermute | solution.py:126
  14.1 3.4 %copy-done = bf16[1,32,8,128,128]{4,3,2,1,0:T(8,128)(2,1)S(1)} copy-done((bf16[1,32,8,128,128]{4,3,2,1,0:T(8,128)(2,1)S(1)}, bf16[1,32,8,128,128]{4,3,2,1,0:T(8,128)(2,1)}, u32[]{:S(2)}) %copy-start) | copy-done | bytes 8388632
  19.2 2.8 %layer_t0_r0.1 = (bf16[8,64,4096]{2,1,0:T(8,128)(2,1)}, bf16[32,4096]{1,0:T(8,128)(2,1)S(1)}, bf16[32,512]{1,0:T(8,128)(2,1)S(1)}, bf16[32,512]{1,0:T(8,128)(2,1)S(1)}) custom-call(s32[257]{0:T(512)S(1)} %pad_add_fusion.refs_0_.meta, bf16[64,4096]{1,0:T(8,128)(2,1)S(1)} %copy-done.3, bf16[64,512]{1,0:T(8,128)(2,1)S(1)} %collective-permute-done.refs_2_.low, ...), custom_call_target="tpu_custom_call" | custom-call | flops 268435456 | bytes 8388608 | tf_op jit(solution)/shard_map/layer_t0_r0/pallas_call | solution.py:81
  22.0 7.3 %collective-permute-start.5 = (bf16[32,4096]{1,0:T(8,128)(2,1)S(1)}, bf16[32,4096]{1,0:T(8,128)(2,1)S(1)}, u32[]{:S(2)}, u32[]{:S(2)}) collective-permute-start(bf16[32,4096]{1,0:T(8,128)(2,1)S(1)} %get-tuple-element.67), channel_id=1, source_target_pairs={{0,4},{1,5},{2,6},{3,7},{4,8},{5,9},{6,10},{7,11},{8,12},{9,13},{1... | collective-permute-start | bytes 786440 | tf_op jit(solution)/shard_map/ppermute | solution.py:139
  29.3 2.8 %layer_t0_r32.1 = (bf16[8,64,4096]{2,1,0:T(8,128)(2,1)}, bf16[32,4096]{1,0:T(8,128)(2,1)S(1)}, bf16[32,512]{1,0:T(8,128)(2,1)S(1)}, bf16[32,512]{1,0:T(8,128)(2,1)S(1)}) custom-call(s32[257]{0:T(512)S(1)} %pad_add_fusion.refs_0_.meta, bf16[64,4096]{1,0:T(8,128)(2,1)S(1)} %copy-done.3, ...), custom_call_target="tpu_custom_call", output_to_operand_aliasing={{0}: (6, {})} | custom-call | flops 268435456 | bytes 8388608 | tf_op jit(solution)/shard_map/layer_t0_r32/pallas_call | solution.py:81
  32.0 6.4 %collective-permute-start.2 = (bf16[32,4096]{1,0:T(8,128)(2,1)S(1)}, bf16[32,4096]{1,0:T(8,128)(2,1)S(1)}, u32[]{:S(2)}, u32[]{:S(2)}) collective-permute-start(bf16[32,4096]{1,0:T(8,128)(2,1)S(1)} %get-tuple-element.64), channel_id=1, source_target_pairs={{0,4},{1,5},{2,6},{3,7},{4,8},{5,9},{6,10},{7,11},{8,12},{9,13},{1... | collective-permute-start | bytes 786440 | tf_op jit(solution)/shard_map/ppermute | solution.py:139
  38.4 6.4 %collective-permute-start.6 = (bf16[32,512]{1,0:T(8,128)(2,1)S(1)}, bf16[32,512]{1,0:T(8,128)(2,1)S(1)}, u32[]{:S(2)}, u32[]{:S(2)}) collective-permute-start(bf16[32,512]{1,0:T(8,128)(2,1)S(1)} %get-tuple-element.68), channel_id=1, source_target_pairs={{0,5},{1,6},{2,7},{3,4},{4,9},{5,10},{6,11},{7,8},{8,13},{9,14},{1... | collective-permute-start | bytes 98312 | tf_op jit(solution)/shard_map/ppermute | solution.py:140
  44.8 6.4 %collective-permute-start.7 = (bf16[32,512]{1,0:T(8,128)(2,1)S(1)}, bf16[32,512]{1,0:T(8,128)(2,1)S(1)}, u32[]{:S(2)}, u32[]{:S(2)}) collective-permute-start(bf16[32,512]{1,0:T(8,128)(2,1)S(1)} %get-tuple-element.69), channel_id=1, source_target_pairs={{0,7},{1,4},{2,5},{3,6},{4,11},{5,8},{6,9},{7,10},{8,15},{9,12},{1... | collective-permute-start | bytes 98312 | tf_op jit(solution)/shard_map/ppermute | solution.py:141
  51.1 6.4 %collective-permute-start.3 = (bf16[32,512]{1,0:T(8,128)(2,1)S(1)}, bf16[32,512]{1,0:T(8,128)(2,1)S(1)}, u32[]{:S(2)}, u32[]{:S(2)}) collective-permute-start(bf16[32,512]{1,0:T(8,128)(2,1)S(1)} %get-tuple-element.65), channel_id=1, source_target_pairs={{0,5},{1,6},{2,7},{3,4},{4,9},{5,10},{6,11},{7,8},{8,13},{9,14},{1... | collective-permute-start | bytes 98312 | tf_op jit(solution)/shard_map/ppermute | solution.py:140
  57.5 6.4 %collective-permute-start.4 = (bf16[32,512]{1,0:T(8,128)(2,1)S(1)}, bf16[32,512]{1,0:T(8,128)(2,1)S(1)}, u32[]{:S(2)}, u32[]{:S(2)}) collective-permute-start(bf16[32,512]{1,0:T(8,128)(2,1)S(1)} %get-tuple-element.66), channel_id=1, source_target_pairs={{0,7},{1,4},{2,5},{3,6},{4,11},{5,8},{6,9},{7,10},{8,15},{9,12},{1... | collective-permute-start | bytes 98312 | tf_op jit(solution)/shard_map/ppermute | solution.py:141
  63.9 2.8 %layer_t1_r0.1 = (bf16[8,64,4096]{2,1,0:T(8,128)(2,1)}, bf16[32,4096]{1,0:T(8,128)(2,1)S(1)}, bf16[32,512]{1,0:T(8,128)(2,1)S(1)}, bf16[32,512]{1,0:T(8,128)(2,1)S(1)}) custom-call(s32[257]{0:T(512)S(1)} %pad_add_fusion.refs_0_.meta, bf16[32,4096]{1,0:T(8,128)(2,1)S(1)} %collective-permute-done.5.main, ...), custom_call_target="tpu_custom_call", output_to_operand_aliasing={{0}: (6, {})} | custom-call | flops 268435456 | bytes 8388608 | tf_op jit(solution)/shard_map/layer_t1_r0/pallas_call | solution.py:81
  66.7 1.3 collective-permute-start.11
  68.0 2.8 %layer_t1_r32.1 = (bf16[8,64,4096]{2,1,0:T(8,128)(2,1)}, bf16[32,4096]{1,0:T(8,128)(2,1)S(1)}, bf16[32,512]{1,0:T(8,128)(2,1)S(1)}, bf16[32,512]{1,0:T(8,128)(2,1)S(1)}) custom-call(s32[257]{0:T(512)S(1)} %pad_add_fusion.refs_0_.meta, bf16[32,4096]{1,0:T(8,128)(2,1)S(1)} %collective-permute-done.2.main, ...), custom_call_target="tpu_custom_call", output_to_operand_aliasing={{0}: (6, {})} | custom-call | flops 268435456 | bytes 8388608 | tf_op jit(solution)/shard_map/layer_t1_r32/pallas_call | solution.py:81
  70.8 1.3 collective-permute-start.8
  72.1 1.3 collective-permute-start.12
  73.4 1.3 collective-permute-start.13
  74.7 1.3 collective-permute-start.9
  76.0 8.0 %collective-permute-done.12.low = bf16[32,512]{1,0:T(8,128)(2,1)S(1)} collective-permute-done((bf16[32,512]{1,0:T(8,128)(2,1)S(1)}, bf16[32,512]{1,0:T(8,128)(2,1)S(1)}, u32[]{:S(2)}, u32[]{:S(2)}) %collective-permute-start.12) | collective-permute-done | bytes 32800 | tf_op jit(solution)/shard_map/ppermute | solution.py:140
  84.0 1.3 collective-permute-start.10
  85.3 2.8 %layer_t2_r0.1 = (bf16[8,64,4096]{2,1,0:T(8,128)(2,1)}, bf16[32,4096]{1,0:T(8,128)(2,1)S(1)}, bf16[32,512]{1,0:T(8,128)(2,1)S(1)}, bf16[32,512]{1,0:T(8,128)(2,1)S(1)}) custom-call(s32[257]{0:T(512)S(1)} %pad_add_fusion.refs_0_.meta, bf16[32,4096]{1,0:T(8,128)(2,1)S(1)} %collective-permute-done.11.main, ...), custom_call_target="tpu_custom_call", output_to_operand_aliasing={{0}: (6, {})} | custom-call | flops 268435456 | bytes 8388608 | tf_op jit(solution)/shard_map/layer_t2_r0/pallas_call | solution.py:81
  88.1 1.3 collective-permute-start.17
  90.1 2.8 %layer_t2_r32.1 = (bf16[8,64,4096]{2,1,0:T(8,128)(2,1)}, bf16[32,4096]{1,0:T(8,128)(2,1)S(1)}, bf16[32,512]{1,0:T(8,128)(2,1)S(1)}, bf16[32,512]{1,0:T(8,128)(2,1)S(1)}) custom-call(s32[257]{0:T(512)S(1)} %pad_add_fusion.refs_0_.meta, bf16[32,4096]{1,0:T(8,128)(2,1)S(1)} %collective-permute-done.8.main, ...), custom_call_target="tpu_custom_call", output_to_operand_aliasing={{0}: (6, {})} | custom-call | flops 268435456 | bytes 8388608 | tf_op jit(solution)/shard_map/layer_t2_r32/pallas_call | solution.py:81
  92.9 1.3 collective-permute-start.14
  94.2 1.3 collective-permute-start.18
  95.5 1.3 collective-permute-start.19
  96.8 1.3 collective-permute-start.15
  98.1 7.9 %collective-permute-done.18.low = bf16[32,512]{1,0:T(8,128)(2,1)S(1)} collective-permute-done((bf16[32,512]{1,0:T(8,128)(2,1)S(1)}, bf16[32,512]{1,0:T(8,128)(2,1)S(1)}, u32[]{:S(2)}, u32[]{:S(2)}) %collective-permute-start.18) | collective-permute-done | bytes 32800 | tf_op jit(solution)/shard_map/ppermute | solution.py:140
  107.3 2.8 %layer_t3_r0.1 = (bf16[8,64,4096]{2,1,0:T(8,128)(2,1)}, bf16[32,4096]{1,0:T(8,128)(2,1)S(1)}, bf16[32,512]{1,0:T(8,128)(2,1)S(1)}, bf16[32,512]{1,0:T(8,128)(2,1)S(1)}) custom-call(s32[257]{0:T(512)S(1)} %pad_add_fusion.refs_0_.meta, bf16[32,4096]{1,0:T(8,128)(2,1)S(1)} %collective-permute-done.17.main, ...), custom_call_target="tpu_custom_call", output_to_operand_aliasing={{0}: (6, {})} | custom-call | flops 268435456 | bytes 8388608 | tf_op jit(solution)/shard_map/layer_t3_r0/pallas_call | solution.py:81
  110.1 1.3 collective-permute-start.23
  112.1 2.9 %layer_t3_r32.1 = (bf16[8,64,4096]{2,1,0:T(8,128)(2,1)}, bf16[32,4096]{1,0:T(8,128)(2,1)S(1)}, bf16[32,512]{1,0:T(8,128)(2,1)S(1)}, bf16[32,512]{1,0:T(8,128)(2,1)S(1)}) custom-call(s32[257]{0:T(512)S(1)} %pad_add_fusion.refs_0_.meta, bf16[32,4096]{1,0:T(8,128)(2,1)S(1)} %collective-permute-done.14.main, ...), custom_call_target="tpu_custom_call", output_to_operand_aliasing={{0}: (6, {})} | custom-call | flops 268435456 | bytes 8388608 | tf_op jit(solution)/shard_map/layer_t3_r32/pallas_call | solution.py:81
  115.1 1.3 collective-permute-start.20
  116.4 1.3 collective-permute-start.24
  117.7 1.3 collective-permute-start.25
  119.0 1.3 collective-permute-start.21
  120.3 8.7 %collective-permute-done.24.low = bf16[32,512]{1,0:T(8,128)(2,1)S(1)} collective-permute-done((bf16[32,512]{1,0:T(8,128)(2,1)S(1)}, bf16[32,512]{1,0:T(8,128)(2,1)S(1)}, u32[]{:S(2)}, u32[]{:S(2)}) %collective-permute-start.24) | collective-permute-done | bytes 32800 | tf_op jit(solution)/shard_map/ppermute | solution.py:140
  128.9 1.3 collective-permute-start.22
  130.2 2.8 %layer_t4_r0.1 = (bf16[8,64,4096]{2,1,0:T(8,128)(2,1)}, bf16[32,4096]{1,0:T(8,128)(2,1)S(1)}, bf16[32,512]{1,0:T(8,128)(2,1)S(1)}, bf16[32,512]{1,0:T(8,128)(2,1)S(1)}) custom-call(s32[257]{0:T(512)S(1)} %pad_add_fusion.refs_0_.meta, bf16[32,4096]{1,0:T(8,128)(2,1)S(1)} %collective-permute-done.23.main, ...), custom_call_target="tpu_custom_call", output_to_operand_aliasing={{0}: (6, {})} | custom-call | flops 268435456 | bytes 8388608 | tf_op jit(solution)/shard_map/layer_t4_r0/pallas_call | solution.py:81
  133.0 1.3 collective-permute-start.29
  135.1 2.8 %layer_t4_r32.1 = (bf16[8,64,4096]{2,1,0:T(8,128)(2,1)}, bf16[32,4096]{1,0:T(8,128)(2,1)S(1)}, bf16[32,512]{1,0:T(8,128)(2,1)S(1)}, bf16[32,512]{1,0:T(8,128)(2,1)S(1)}) custom-call(s32[257]{0:T(512)S(1)} %pad_add_fusion.refs_0_.meta, bf16[32,4096]{1,0:T(8,128)(2,1)S(1)} %collective-permute-done.20.main, ...), custom_call_target="tpu_custom_call", output_to_operand_aliasing={{0}: (6, {})} | custom-call | flops 268435456 | bytes 8388608 | tf_op jit(solution)/shard_map/layer_t4_r32/pallas_call | solution.py:81
  137.8 1.3 collective-permute-start.26
  139.1 1.3 collective-permute-start.30
  140.4 1.3 collective-permute-start.31
  141.7 1.3 collective-permute-start.27
  143.0 8.8 %collective-permute-done.30.low = bf16[32,512]{1,0:T(8,128)(2,1)S(1)} collective-permute-done((bf16[32,512]{1,0:T(8,128)(2,1)S(1)}, bf16[32,512]{1,0:T(8,128)(2,1)S(1)}, u32[]{:S(2)}, u32[]{:S(2)}) %collective-permute-start.30) | collective-permute-done | bytes 32800 | tf_op jit(solution)/shard_map/ppermute | solution.py:140
  153.2 2.8 %layer_t5_r0.1 = (bf16[8,64,4096]{2,1,0:T(8,128)(2,1)}, bf16[32,4096]{1,0:T(8,128)(2,1)S(1)}, bf16[32,512]{1,0:T(8,128)(2,1)S(1)}, bf16[32,512]{1,0:T(8,128)(2,1)S(1)}) custom-call(s32[257]{0:T(512)S(1)} %pad_add_fusion.refs_0_.meta, bf16[32,4096]{1,0:T(8,128)(2,1)S(1)} %collective-permute-done.29.main, ...), custom_call_target="tpu_custom_call", output_to_operand_aliasing={{0}: (6, {})} | custom-call | flops 268435456 | bytes 8388608 | tf_op jit(solution)/shard_map/layer_t5_r0/pallas_call | solution.py:81
  155.9 1.3 collective-permute-start.35
  158.2 2.8 %layer_t5_r32.1 = (bf16[8,64,4096]{2,1,0:T(8,128)(2,1)}, bf16[32,4096]{1,0:T(8,128)(2,1)S(1)}, bf16[32,512]{1,0:T(8,128)(2,1)S(1)}, bf16[32,512]{1,0:T(8,128)(2,1)S(1)}) custom-call(s32[257]{0:T(512)S(1)} %pad_add_fusion.refs_0_.meta, bf16[32,4096]{1,0:T(8,128)(2,1)S(1)} %collective-permute-done.26.main, ...), custom_call_target="tpu_custom_call", output_to_operand_aliasing={{0}: (6, {})} | custom-call | flops 268435456 | bytes 8388608 | tf_op jit(solution)/shard_map/layer_t5_r32/pallas_call | solution.py:81
  161.0 1.3 collective-permute-start.32
  162.3 1.3 collective-permute-start.36
  163.6 1.3 collective-permute-start.37
  164.9 1.3 collective-permute-start.33
  166.2 9.0 %collective-permute-done.36.low = bf16[32,512]{1,0:T(8,128)(2,1)S(1)} collective-permute-done((bf16[32,512]{1,0:T(8,128)(2,1)S(1)}, bf16[32,512]{1,0:T(8,128)(2,1)S(1)}, u32[]{:S(2)}, u32[]{:S(2)}) %collective-permute-start.36) | collective-permute-done | bytes 32800 | tf_op jit(solution)/shard_map/ppermute | solution.py:140
  176.5 2.8 %layer_t6_r0.1 = (bf16[8,64,4096]{2,1,0:T(8,128)(2,1)}, bf16[32,4096]{1,0:T(8,128)(2,1)S(1)}, bf16[32,512]{1,0:T(8,128)(2,1)S(1)}, bf16[32,512]{1,0:T(8,128)(2,1)S(1)}) custom-call(s32[257]{0:T(512)S(1)} %pad_add_fusion.refs_0_.meta, bf16[32,4096]{1,0:T(8,128)(2,1)S(1)} %collective-permute-done.35.main, ...), custom_call_target="tpu_custom_call", output_to_operand_aliasing={{0}: (6, {})} | custom-call | flops 268435456 | bytes 8388608 | tf_op jit(solution)/shard_map/layer_t6_r0/pallas_call | solution.py:81
  179.3 1.3 collective-permute-start.41
  181.3 2.8 %layer_t6_r32.1 = (bf16[8,64,4096]{2,1,0:T(8,128)(2,1)}, bf16[32,4096]{1,0:T(8,128)(2,1)S(1)}, bf16[32,512]{1,0:T(8,128)(2,1)S(1)}, bf16[32,512]{1,0:T(8,128)(2,1)S(1)}) custom-call(s32[257]{0:T(512)S(1)} %pad_add_fusion.refs_0_.meta, bf16[32,4096]{1,0:T(8,128)(2,1)S(1)} %collective-permute-done.32.main, ...), custom_call_target="tpu_custom_call", output_to_operand_aliasing={{0}: (6, {})} | custom-call | flops 268435456 | bytes 8388608 | tf_op jit(solution)/shard_map/layer_t6_r32/pallas_call | solution.py:81
  184.1 1.3 collective-permute-start.38
  185.4 1.3 collective-permute-start.42
  186.7 1.3 collective-permute-start.43
  188.0 1.3 collective-permute-start.39
  189.3 7.8 %collective-permute-done.42.low = bf16[32,512]{1,0:T(8,128)(2,1)S(1)} collective-permute-done((bf16[32,512]{1,0:T(8,128)(2,1)S(1)}, bf16[32,512]{1,0:T(8,128)(2,1)S(1)}, u32[]{:S(2)}, u32[]{:S(2)}) %collective-permute-start.42) | collective-permute-done | bytes 32800 | tf_op jit(solution)/shard_map/ppermute | solution.py:140
  197.1 1.3 collective-permute-start.40
  198.4 3.7 %layer_t7_r0.1 = (bf16[8,64,4096]{2,1,0:T(8,128)(2,1)}, bf16[32,4096]{1,0:T(8,128)(2,1)}, bf16[32,512]{1,0:T(8,128)(2,1)}, bf16[32,512]{1,0:T(8,128)(2,1)}) custom-call(s32[257]{0:T(512)S(1)} %pad_add_fusion.refs_0_.meta, bf16[32,4096]{1,0:T(8,128)(2,1)S(1)} %collective-permute-done.41.main, ...), custom_call_target="tpu_custom_call", output_to_operand_aliasing={{0}: (6, {})} | custom-call | flops 268435456 | bytes 8388608 | tf_op jit(solution)/shard_map/layer_t7_r0/pallas_call | solution.py:81
  203.2 3.5 %layer_t7_r32.1 = (bf16[8,64,4096]{2,1,0:T(8,128)(2,1)}, bf16[32,4096]{1,0:T(8,128)(2,1)}, bf16[32,512]{1,0:T(8,128)(2,1)}, bf16[32,512]{1,0:T(8,128)(2,1)}) custom-call(s32[257]{0:T(512)S(1)} %pad_add_fusion.refs_0_.meta, bf16[32,4096]{1,0:T(8,128)(2,1)S(1)} %collective-permute-done.38.main, ...), custom_call_target="tpu_custom_call", output_to_operand_aliasing={{0}: (6, {})} | custom-call | flops 268435456 | bytes 8388608 | tf_op jit(solution)/shard_map/layer_t7_r32/pallas_call | solution.py:81
  (59 shorter events, 12.8 us)
Async XLA Ops:
  0.9 12.7 %collective-permute-start.1 = (bf16[64,512]{1,0:T(8,128)(2,1)S(1)}, bf16[64,512]{1,0:T(8,128)(2,1)S(1)}, u32[]{:S(2)}, u32[]{:S(2)}) collective-permute-start(bf16[64,512]{1,0:T(8,128)(2,1)S(1)} %get-tuple-element.121), channel_id=1, source_target_pairs={{0,3},{1,0},{2,1},{3,2},{4,7},{5,4},{6,5},{7,6},{8,11},{9,8},{10,9... | collective-permute-start | bytes 196616 | tf_op jit(solution)/shard_map/ppermute | solution.py:127
  7.0 7.1 %collective-permute-start = (bf16[64,512]{1,0:T(8,128)(2,1)S(1)}, bf16[64,512]{1,0:T(8,128)(2,1)S(1)}, u32[]{:S(2)}, u32[]{:S(2)}) collective-permute-start(bf16[64,512]{1,0:T(8,128)(2,1)S(1)} %get-tuple-element.122), channel_id=1, source_target_pairs={{0,1},{1,2},{2,3},{3,0},{4,5},{5,6},{6,7},{7,4},{8,9},{9,10},{10,1... | collective-permute-start | bytes 196616 | tf_op jit(solution)/shard_map/ppermute | solution.py:126
  14.1 3.4 %copy-start = (bf16[1,32,8,128,128]{4,3,2,1,0:T(8,128)(2,1)S(1)}, bf16[1,32,8,128,128]{4,3,2,1,0:T(8,128)(2,1)}, u32[]{:S(2)}) copy-start(bf16[1,32,8,128,128]{4,3,2,1,0:T(8,128)(2,1)} %param.5) | copy-start | bytes 25165828
  17.4 0.7 copy-start.1
  18.2 1.0 copy-start.3
  19.2 44.7 %slice-start = ((s8[8388608]{0:T(1024)(128)(4,1)}), s8[4194304]{0:T(1024)(128)(4,1)S(1)}, s32[]{:S(2)}) async-start(s8[8388608]{0:T(1024)(128)(4,1)} %bitcast.4), calls=%async_computation | async-start | bytes 8388608
  22.0 41.9 %collective-permute-start.5 = (bf16[32,4096]{1,0:T(8,128)(2,1)S(1)}, bf16[32,4096]{1,0:T(8,128)(2,1)S(1)}, u32[]{:S(2)}, u32[]{:S(2)}) collective-permute-start(bf16[32,4096]{1,0:T(8,128)(2,1)S(1)} %get-tuple-element.67), channel_id=1, source_target_pairs={{0,4},{1,5},{2,6},{3,7},{4,8},{5,9},{6,10},{7,11},{8,12},{9,13},{1... | collective-permute-start | bytes 786440 | tf_op jit(solution)/shard_map/ppermute | solution.py:139
  29.3 34.6 %slice-start.1 = ((s8[8388608]{0:T(1024)(128)(4,1)}), s8[4194304]{0:T(1024)(128)(4,1)S(1)}, s32[]{:S(2)}) async-start(s8[8388608]{0:T(1024)(128)(4,1)} %bitcast.4), calls=%async_computation.1 | async-start | bytes 8388608
  29.3 34.6 %copy-start.2 = (f32[1,4096]{1,0:T(1,128)S(1)}, f32[1,4096]{1,0:T(1,128)}, u32[]{:S(2)}) copy-start(f32[1,4096]{1,0:T(1,128)} %bias.29) | copy-start | bytes 49156
  32.0 35.9 %collective-permute-start.2 = (bf16[32,4096]{1,0:T(8,128)(2,1)S(1)}, bf16[32,4096]{1,0:T(8,128)(2,1)S(1)}, u32[]{:S(2)}, u32[]{:S(2)}) collective-permute-start(bf16[32,4096]{1,0:T(8,128)(2,1)S(1)} %get-tuple-element.64), channel_id=1, source_target_pairs={{0,4},{1,5},{2,6},{3,7},{4,8},{5,9},{6,10},{7,11},{8,12},{9,13},{1... | collective-permute-start | bytes 786440 | tf_op jit(solution)/shard_map/ppermute | solution.py:139
  38.4 19.1 %collective-permute-start.6 = (bf16[32,512]{1,0:T(8,128)(2,1)S(1)}, bf16[32,512]{1,0:T(8,128)(2,1)S(1)}, u32[]{:S(2)}, u32[]{:S(2)}) collective-permute-start(bf16[32,512]{1,0:T(8,128)(2,1)S(1)} %get-tuple-element.68), channel_id=1, source_target_pairs={{0,5},{1,6},{2,7},{3,4},{4,9},{5,10},{6,11},{7,8},{8,13},{9,14},{1... | collective-permute-start | bytes 98312 | tf_op jit(solution)/shard_map/ppermute | solution.py:140
  44.8 19.1 %collective-permute-start.7 = (bf16[32,512]{1,0:T(8,128)(2,1)S(1)}, bf16[32,512]{1,0:T(8,128)(2,1)S(1)}, u32[]{:S(2)}, u32[]{:S(2)}) collective-permute-start(bf16[32,512]{1,0:T(8,128)(2,1)S(1)} %get-tuple-element.69), channel_id=1, source_target_pairs={{0,7},{1,4},{2,5},{3,6},{4,11},{5,8},{6,9},{7,10},{8,15},{9,12},{1... | collective-permute-start | bytes 98312 | tf_op jit(solution)/shard_map/ppermute | solution.py:141
  51.1 16.8 %collective-permute-start.3 = (bf16[32,512]{1,0:T(8,128)(2,1)S(1)}, bf16[32,512]{1,0:T(8,128)(2,1)S(1)}, u32[]{:S(2)}, u32[]{:S(2)}) collective-permute-start(bf16[32,512]{1,0:T(8,128)(2,1)S(1)} %get-tuple-element.65), channel_id=1, source_target_pairs={{0,5},{1,6},{2,7},{3,4},{4,9},{5,10},{6,11},{7,8},{8,13},{9,14},{1... | collective-permute-start | bytes 98312 | tf_op jit(solution)/shard_map/ppermute | solution.py:140
  57.5 10.5 %collective-permute-start.4 = (bf16[32,512]{1,0:T(8,128)(2,1)S(1)}, bf16[32,512]{1,0:T(8,128)(2,1)S(1)}, u32[]{:S(2)}, u32[]{:S(2)}) collective-permute-start(bf16[32,512]{1,0:T(8,128)(2,1)S(1)} %get-tuple-element.66), channel_id=1, source_target_pairs={{0,7},{1,4},{2,5},{3,6},{4,11},{5,8},{6,9},{7,10},{8,15},{9,12},{1... | collective-permute-start | bytes 98312 | tf_op jit(solution)/shard_map/ppermute | solution.py:141
  66.7 18.6 %collective-permute-start.11 = (bf16[32,4096]{1,0:T(8,128)(2,1)S(1)}, bf16[32,4096]{1,0:T(8,128)(2,1)S(1)}, u32[]{:S(2)}, u32[]{:S(2)}) collective-permute-start(bf16[32,4096]{1,0:T(8,128)(2,1)S(1)} %get-tuple-element.75), channel_id=1, source_target_pairs={{4,8},{5,9},{6,10},{7,11},{8,12},{9,13},{10,14},{11,15},{12,16},{1... | collective-permute-start | bytes 786440 | tf_op jit(solution)/shard_map/ppermute | solution.py:139
  70.8 19.3 %collective-permute-start.8 = (bf16[32,4096]{1,0:T(8,128)(2,1)S(1)}, bf16[32,4096]{1,0:T(8,128)(2,1)S(1)}, u32[]{:S(2)}, u32[]{:S(2)}) collective-permute-start(bf16[32,4096]{1,0:T(8,128)(2,1)S(1)} %get-tuple-element.72), channel_id=1, source_target_pairs={{4,8},{5,9},{6,10},{7,11},{8,12},{9,13},{10,14},{11,15},{12,16},{1... | collective-permute-start | bytes 786440 | tf_op jit(solution)/shard_map/ppermute | solution.py:139
  72.1 11.9 %collective-permute-start.12 = (bf16[32,512]{1,0:T(8,128)(2,1)S(1)}, bf16[32,512]{1,0:T(8,128)(2,1)S(1)}, u32[]{:S(2)}, u32[]{:S(2)}) collective-permute-start(bf16[32,512]{1,0:T(8,128)(2,1)S(1)} %get-tuple-element.76), channel_id=1, source_target_pairs={{4,9},{5,10},{6,11},{7,8},{8,13},{9,14},{10,15},{11,12},{12,17},{1... | collective-permute-start | bytes 98312 | tf_op jit(solution)/shard_map/ppermute | solution.py:140
  73.4 11.9 %collective-permute-start.13 = (bf16[32,512]{1,0:T(8,128)(2,1)S(1)}, bf16[32,512]{1,0:T(8,128)(2,1)S(1)}, u32[]{:S(2)}, u32[]{:S(2)}) collective-permute-start(bf16[32,512]{1,0:T(8,128)(2,1)S(1)} %get-tuple-element.77), channel_id=1, source_target_pairs={{4,11},{5,8},{6,9},{7,10},{8,15},{9,12},{10,13},{11,14},{12,19},{1... | collective-permute-start | bytes 98312 | tf_op jit(solution)/shard_map/ppermute | solution.py:141
  74.7 14.7 %collective-permute-start.9 = (bf16[32,512]{1,0:T(8,128)(2,1)S(1)}, bf16[32,512]{1,0:T(8,128)(2,1)S(1)}, u32[]{:S(2)}, u32[]{:S(2)}) collective-permute-start(bf16[32,512]{1,0:T(8,128)(2,1)S(1)} %get-tuple-element.73), channel_id=1, source_target_pairs={{4,9},{5,10},{6,11},{7,8},{8,13},{9,14},{10,15},{11,12},{12,17},{1... | collective-permute-start | bytes 98312 | tf_op jit(solution)/shard_map/ppermute | solution.py:140
  84.0 6.1 %collective-permute-start.10 = (bf16[32,512]{1,0:T(8,128)(2,1)S(1)}, bf16[32,512]{1,0:T(8,128)(2,1)S(1)}, u32[]{:S(2)}, u32[]{:S(2)}) collective-permute-start(bf16[32,512]{1,0:T(8,128)(2,1)S(1)} %get-tuple-element.74), channel_id=1, source_target_pairs={{4,11},{5,8},{6,9},{7,10},{8,15},{9,12},{10,13},{11,14},{12,19},{1... | collective-permute-start | bytes 98312 | tf_op jit(solution)/shard_map/ppermute | solution.py:141
  88.1 19.2 %collective-permute-start.17 = (bf16[32,4096]{1,0:T(8,128)(2,1)S(1)}, bf16[32,4096]{1,0:T(8,128)(2,1)S(1)}, u32[]{:S(2)}, u32[]{:S(2)}) collective-permute-start(bf16[32,4096]{1,0:T(8,128)(2,1)S(1)} %get-tuple-element.83), channel_id=1, source_target_pairs={{8,12},{9,13},{10,14},{11,15},{12,16},{13,17},{14,18},{15,19},{16,... | collective-permute-start | bytes 786440 | tf_op jit(solution)/shard_map/ppermute | solution.py:139
  92.9 19.3 %collective-permute-start.14 = (bf16[32,4096]{1,0:T(8,128)(2,1)S(1)}, bf16[32,4096]{1,0:T(8,128)(2,1)S(1)}, u32[]{:S(2)}, u32[]{:S(2)}) collective-permute-start(bf16[32,4096]{1,0:T(8,128)(2,1)S(1)} %get-tuple-element.80), channel_id=1, source_target_pairs={{8,12},{9,13},{10,14},{11,15},{12,16},{13,17},{14,18},{15,19},{16,... | collective-permute-start | bytes 786440 | tf_op jit(solution)/shard_map/ppermute | solution.py:139
  94.2 11.8 %collective-permute-start.18 = (bf16[32,512]{1,0:T(8,128)(2,1)S(1)}, bf16[32,512]{1,0:T(8,128)(2,1)S(1)}, u32[]{:S(2)}, u32[]{:S(2)}) collective-permute-start(bf16[32,512]{1,0:T(8,128)(2,1)S(1)} %get-tuple-element.84), channel_id=1, source_target_pairs={{8,13},{9,14},{10,15},{11,12},{12,17},{13,18},{14,19},{15,16},{16,... | collective-permute-start | bytes 98312 | tf_op jit(solution)/shard_map/ppermute | solution.py:140
  95.5 11.8 %collective-permute-start.19 = (bf16[32,512]{1,0:T(8,128)(2,1)S(1)}, bf16[32,512]{1,0:T(8,128)(2,1)S(1)}, u32[]{:S(2)}, u32[]{:S(2)}) collective-permute-start(bf16[32,512]{1,0:T(8,128)(2,1)S(1)} %get-tuple-element.85), channel_id=1, source_target_pairs={{8,15},{9,12},{10,13},{11,14},{12,19},{13,16},{14,17},{15,18},{16,... | collective-permute-start | bytes 98312 | tf_op jit(solution)/shard_map/ppermute | solution.py:141
  96.8 14.6 %collective-permute-start.15 = (bf16[32,512]{1,0:T(8,128)(2,1)S(1)}, bf16[32,512]{1,0:T(8,128)(2,1)S(1)}, u32[]{:S(2)}, u32[]{:S(2)}) collective-permute-start(bf16[32,512]{1,0:T(8,128)(2,1)S(1)} %get-tuple-element.81), channel_id=1, source_target_pairs={{8,13},{9,14},{10,15},{11,12},{12,17},{13,18},{14,19},{15,16},{16,... | collective-permute-start | bytes 98312 | tf_op jit(solution)/shard_map/ppermute | solution.py:140
  106.0 6.1 %collective-permute-start.16 = (bf16[32,512]{1,0:T(8,128)(2,1)S(1)}, bf16[32,512]{1,0:T(8,128)(2,1)S(1)}, u32[]{:S(2)}, u32[]{:S(2)}) collective-permute-start(bf16[32,512]{1,0:T(8,128)(2,1)S(1)} %get-tuple-element.82), channel_id=1, source_target_pairs={{8,15},{9,12},{10,13},{11,14},{12,19},{13,16},{14,17},{15,18},{16,... | collective-permute-start | bytes 98312 | tf_op jit(solution)/shard_map/ppermute | solution.py:141
  110.1 20.1 %collective-permute-start.23 = (bf16[32,4096]{1,0:T(8,128)(2,1)S(1)}, bf16[32,4096]{1,0:T(8,128)(2,1)S(1)}, u32[]{:S(2)}, u32[]{:S(2)}) collective-permute-start(bf16[32,4096]{1,0:T(8,128)(2,1)S(1)} %get-tuple-element.91), channel_id=1, source_target_pairs={{12,16},{13,17},{14,18},{15,19},{16,20},{17,21},{18,22},{19,23},{2... | collective-permute-start | bytes 786440 | tf_op jit(solution)/shard_map/ppermute | solution.py:139
  115.1 20.0 %collective-permute-start.20 = (bf16[32,4096]{1,0:T(8,128)(2,1)S(1)}, bf16[32,4096]{1,0:T(8,128)(2,1)S(1)}, u32[]{:S(2)}, u32[]{:S(2)}) collective-permute-start(bf16[32,4096]{1,0:T(8,128)(2,1)S(1)} %get-tuple-element.88), channel_id=1, source_target_pairs={{12,16},{13,17},{14,18},{15,19},{16,20},{17,21},{18,22},{19,23},{2... | collective-permute-start | bytes 786440 | tf_op jit(solution)/shard_map/ppermute | solution.py:139
  116.4 12.6 %collective-permute-start.24 = (bf16[32,512]{1,0:T(8,128)(2,1)S(1)}, bf16[32,512]{1,0:T(8,128)(2,1)S(1)}, u32[]{:S(2)}, u32[]{:S(2)}) collective-permute-start(bf16[32,512]{1,0:T(8,128)(2,1)S(1)} %get-tuple-element.92), channel_id=1, source_target_pairs={{12,17},{13,18},{14,19},{15,16},{16,21},{17,22},{18,23},{19,20},{2... | collective-permute-start | bytes 98312 | tf_op jit(solution)/shard_map/ppermute | solution.py:140
  117.7 12.6 %collective-permute-start.25 = (bf16[32,512]{1,0:T(8,128)(2,1)S(1)}, bf16[32,512]{1,0:T(8,128)(2,1)S(1)}, u32[]{:S(2)}, u32[]{:S(2)}) collective-permute-start(bf16[32,512]{1,0:T(8,128)(2,1)S(1)} %get-tuple-element.93), channel_id=1, source_target_pairs={{12,19},{13,16},{14,17},{15,18},{16,23},{17,20},{18,21},{19,22},{2... | collective-permute-start | bytes 98312 | tf_op jit(solution)/shard_map/ppermute | solution.py:141
  119.0 15.4 %collective-permute-start.21 = (bf16[32,512]{1,0:T(8,128)(2,1)S(1)}, bf16[32,512]{1,0:T(8,128)(2,1)S(1)}, u32[]{:S(2)}, u32[]{:S(2)}) collective-permute-start(bf16[32,512]{1,0:T(8,128)(2,1)S(1)} %get-tuple-element.89), channel_id=1, source_target_pairs={{12,17},{13,18},{14,19},{15,16},{16,21},{17,22},{18,23},{19,20},{2... | collective-permute-start | bytes 98312 | tf_op jit(solution)/shard_map/ppermute | solution.py:140
  128.9 6.1 %collective-permute-start.22 = (bf16[32,512]{1,0:T(8,128)(2,1)S(1)}, bf16[32,512]{1,0:T(8,128)(2,1)S(1)}, u32[]{:S(2)}, u32[]{:S(2)}) collective-permute-start(bf16[32,512]{1,0:T(8,128)(2,1)S(1)} %get-tuple-element.90), channel_id=1, source_target_pairs={{12,19},{13,16},{14,17},{15,18},{16,23},{17,20},{18,21},{19,22},{2... | collective-permute-start | bytes 98312 | tf_op jit(solution)/shard_map/ppermute | solution.py:141
  133.0 20.1 %collective-permute-start.29 = (bf16[32,4096]{1,0:T(8,128)(2,1)S(1)}, bf16[32,4096]{1,0:T(8,128)(2,1)S(1)}, u32[]{:S(2)}, u32[]{:S(2)}) collective-permute-start(bf16[32,4096]{1,0:T(8,128)(2,1)S(1)} %get-tuple-element.99), channel_id=1, source_target_pairs={{16,20},{17,21},{18,22},{19,23},{20,24},{21,25},{22,26},{23,27},{2... | collective-permute-start | bytes 786440 | tf_op jit(solution)/shard_map/ppermute | solution.py:139
  137.8 20.4 %collective-permute-start.26 = (bf16[32,4096]{1,0:T(8,128)(2,1)S(1)}, bf16[32,4096]{1,0:T(8,128)(2,1)S(1)}, u32[]{:S(2)}, u32[]{:S(2)}) collective-permute-start(bf16[32,4096]{1,0:T(8,128)(2,1)S(1)} %get-tuple-element.96), channel_id=1, source_target_pairs={{16,20},{17,21},{18,22},{19,23},{20,24},{21,25},{22,26},{23,27},{2... | collective-permute-start | bytes 786440 | tf_op jit(solution)/shard_map/ppermute | solution.py:139
  139.1 12.7 %collective-permute-start.30 = (bf16[32,512]{1,0:T(8,128)(2,1)S(1)}, bf16[32,512]{1,0:T(8,128)(2,1)S(1)}, u32[]{:S(2)}, u32[]{:S(2)}) collective-permute-start(bf16[32,512]{1,0:T(8,128)(2,1)S(1)} %get-tuple-element.100), channel_id=1, source_target_pairs={{16,21},{17,22},{18,23},{19,20},{20,25},{21,26},{22,27},{23,24},{2... | collective-permute-start | bytes 98312 | tf_op jit(solution)/shard_map/ppermute | solution.py:140
  140.4 12.7 %collective-permute-start.31 = (bf16[32,512]{1,0:T(8,128)(2,1)S(1)}, bf16[32,512]{1,0:T(8,128)(2,1)S(1)}, u32[]{:S(2)}, u32[]{:S(2)}) collective-permute-start(bf16[32,512]{1,0:T(8,128)(2,1)S(1)} %get-tuple-element.101), channel_id=1, source_target_pairs={{16,23},{17,20},{18,21},{19,22},{20,27},{21,24},{22,25},{23,26},{2... | collective-permute-start | bytes 98312 | tf_op jit(solution)/shard_map/ppermute | solution.py:141
  141.7 15.5 %collective-permute-start.27 = (bf16[32,512]{1,0:T(8,128)(2,1)S(1)}, bf16[32,512]{1,0:T(8,128)(2,1)S(1)}, u32[]{:S(2)}, u32[]{:S(2)}) collective-permute-start(bf16[32,512]{1,0:T(8,128)(2,1)S(1)} %get-tuple-element.97), channel_id=1, source_target_pairs={{16,21},{17,22},{18,23},{19,20},{20,25},{21,26},{22,27},{23,24},{2... | collective-permute-start | bytes 98312 | tf_op jit(solution)/shard_map/ppermute | solution.py:140
  151.9 6.4 %collective-permute-start.28 = (bf16[32,512]{1,0:T(8,128)(2,1)S(1)}, bf16[32,512]{1,0:T(8,128)(2,1)S(1)}, u32[]{:S(2)}, u32[]{:S(2)}) collective-permute-start(bf16[32,512]{1,0:T(8,128)(2,1)S(1)} %get-tuple-element.98), channel_id=1, source_target_pairs={{16,23},{17,20},{18,21},{19,22},{20,27},{21,24},{22,25},{23,26},{2... | collective-permute-start | bytes 98312 | tf_op jit(solution)/shard_map/ppermute | solution.py:141
  155.9 20.5 %collective-permute-start.35 = (bf16[32,4096]{1,0:T(8,128)(2,1)S(1)}, bf16[32,4096]{1,0:T(8,128)(2,1)S(1)}, u32[]{:S(2)}, u32[]{:S(2)}) collective-permute-start(bf16[32,4096]{1,0:T(8,128)(2,1)S(1)} %get-tuple-element.107), channel_id=1, source_target_pairs={{20,24},{21,25},{22,26},{23,27},{24,28},{25,29},{26,30},{27,31}} | collective-permute-start | bytes 786440 | tf_op jit(solution)/shard_map/ppermute | solution.py:139
  161.0 20.3 %collective-permute-start.32 = (bf16[32,4096]{1,0:T(8,128)(2,1)S(1)}, bf16[32,4096]{1,0:T(8,128)(2,1)S(1)}, u32[]{:S(2)}, u32[]{:S(2)}) collective-permute-start(bf16[32,4096]{1,0:T(8,128)(2,1)S(1)} %get-tuple-element.104), channel_id=1, source_target_pairs={{20,24},{21,25},{22,26},{23,27},{24,28},{25,29},{26,30},{27,31}} | collective-permute-start | bytes 786440 | tf_op jit(solution)/shard_map/ppermute | solution.py:139
  162.3 12.9 %collective-permute-start.36 = (bf16[32,512]{1,0:T(8,128)(2,1)S(1)}, bf16[32,512]{1,0:T(8,128)(2,1)S(1)}, u32[]{:S(2)}, u32[]{:S(2)}) collective-permute-start(bf16[32,512]{1,0:T(8,128)(2,1)S(1)} %get-tuple-element.108), channel_id=1, source_target_pairs={{20,25},{21,26},{22,27},{23,24},{24,29},{25,30},{26,31},{27,28}} | collective-permute-start | bytes 98312 | tf_op jit(solution)/shard_map/ppermute | solution.py:140
  163.6 12.9 %collective-permute-start.37 = (bf16[32,512]{1,0:T(8,128)(2,1)S(1)}, bf16[32,512]{1,0:T(8,128)(2,1)S(1)}, u32[]{:S(2)}, u32[]{:S(2)}) collective-permute-start(bf16[32,512]{1,0:T(8,128)(2,1)S(1)} %get-tuple-element.109), channel_id=1, source_target_pairs={{20,27},{21,24},{22,25},{23,26},{24,31},{25,28},{26,29},{27,30}} | collective-permute-start | bytes 98312 | tf_op jit(solution)/shard_map/ppermute | solution.py:141
  164.9 15.7 %collective-permute-start.33 = (bf16[32,512]{1,0:T(8,128)(2,1)S(1)}, bf16[32,512]{1,0:T(8,128)(2,1)S(1)}, u32[]{:S(2)}, u32[]{:S(2)}) collective-permute-start(bf16[32,512]{1,0:T(8,128)(2,1)S(1)} %get-tuple-element.105), channel_id=1, source_target_pairs={{20,25},{21,26},{22,27},{23,24},{24,29},{25,30},{26,31},{27,28}} | collective-permute-start | bytes 98312 | tf_op jit(solution)/shard_map/ppermute | solution.py:140
  175.2 6.1 %collective-permute-start.34 = (bf16[32,512]{1,0:T(8,128)(2,1)S(1)}, bf16[32,512]{1,0:T(8,128)(2,1)S(1)}, u32[]{:S(2)}, u32[]{:S(2)}) collective-permute-start(bf16[32,512]{1,0:T(8,128)(2,1)S(1)} %get-tuple-element.106), channel_id=1, source_target_pairs={{20,27},{21,24},{22,25},{23,26},{24,31},{25,28},{26,29},{27,30}} | collective-permute-start | bytes 98312 | tf_op jit(solution)/shard_map/ppermute | solution.py:141
  179.3 19.1 %collective-permute-start.41 = (bf16[32,4096]{1,0:T(8,128)(2,1)S(1)}, bf16[32,4096]{1,0:T(8,128)(2,1)S(1)}, u32[]{:S(2)}, u32[]{:S(2)}) collective-permute-start(bf16[32,4096]{1,0:T(8,128)(2,1)S(1)} %get-tuple-element.115), channel_id=1, source_target_pairs={{24,28},{25,29},{26,30},{27,31}} | collective-permute-start | bytes 786440 | tf_op jit(solution)/shard_map/ppermute | solution.py:139
  184.1 19.1 %collective-permute-start.38 = (bf16[32,4096]{1,0:T(8,128)(2,1)S(1)}, bf16[32,4096]{1,0:T(8,128)(2,1)S(1)}, u32[]{:S(2)}, u32[]{:S(2)}) collective-permute-start(bf16[32,4096]{1,0:T(8,128)(2,1)S(1)} %get-tuple-element.112), channel_id=1, source_target_pairs={{24,28},{25,29},{26,30},{27,31}} | collective-permute-start | bytes 786440 | tf_op jit(solution)/shard_map/ppermute | solution.py:139
  185.4 11.7 %collective-permute-start.42 = (bf16[32,512]{1,0:T(8,128)(2,1)S(1)}, bf16[32,512]{1,0:T(8,128)(2,1)S(1)}, u32[]{:S(2)}, u32[]{:S(2)}) collective-permute-start(bf16[32,512]{1,0:T(8,128)(2,1)S(1)} %get-tuple-element.116), channel_id=1, source_target_pairs={{24,29},{25,30},{26,31},{27,28}} | collective-permute-start | bytes 98312 | tf_op jit(solution)/shard_map/ppermute | solution.py:140
  186.7 11.7 %collective-permute-start.43 = (bf16[32,512]{1,0:T(8,128)(2,1)S(1)}, bf16[32,512]{1,0:T(8,128)(2,1)S(1)}, u32[]{:S(2)}, u32[]{:S(2)}) collective-permute-start(bf16[32,512]{1,0:T(8,128)(2,1)S(1)} %get-tuple-element.117), channel_id=1, source_target_pairs={{24,31},{25,28},{26,29},{27,30}} | collective-permute-start | bytes 98312 | tf_op jit(solution)/shard_map/ppermute | solution.py:141
  188.0 14.1 %collective-permute-start.39 = (bf16[32,512]{1,0:T(8,128)(2,1)S(1)}, bf16[32,512]{1,0:T(8,128)(2,1)S(1)}, u32[]{:S(2)}, u32[]{:S(2)}) collective-permute-start(bf16[32,512]{1,0:T(8,128)(2,1)S(1)} %get-tuple-element.113), channel_id=1, source_target_pairs={{24,29},{25,30},{26,31},{27,28}} | collective-permute-start | bytes 98312 | tf_op jit(solution)/shard_map/ppermute | solution.py:140
  197.1 6.1 %collective-permute-start.40 = (bf16[32,512]{1,0:T(8,128)(2,1)S(1)}, bf16[32,512]{1,0:T(8,128)(2,1)S(1)}, u32[]{:S(2)}, u32[]{:S(2)}) collective-permute-start(bf16[32,512]{1,0:T(8,128)(2,1)S(1)} %get-tuple-element.114), channel_id=1, source_target_pairs={{24,31},{25,28},{26,29},{27,30}} | collective-permute-start | bytes 98312 | tf_op jit(solution)/shard_map/ppermute | solution.py:141

commit v2 on v1

v2 whole, which is shorter than its diff:
```python
import functools

import jax
import jax.numpy as jnp
from jax import lax
from jax.experimental import pallas as pl
from jax.experimental.pallas import tpu as pltpu
from jax.sharding import PartitionSpec as P

BLK = 128
HALO = 4
TICKS = 8
CHUNKS = 2
VMEM = pl.BlockSpec(memory_space=pltpu.VMEM)
SMEM = pl.BlockSpec(memory_space=pltpu.SMEM)
ANY = pl.BlockSpec(memory_space=pl.ANY)


def load_kernel(state, w, bias, state_out, w_out, bias_out, sems):
    copies = [
        pltpu.make_async_copy(src, dst, sems.at[i])
        for i, (src, dst) in enumerate(((state, state_out), (bias, bias_out), (w, w_out)))
    ]
    for copy in copies:
        copy.start()
    for copy in copies:
        copy.wait()


def load(*arrays):
    return pl.pallas_call(
        load_kernel,
        out_shape=tuple(pltpu.VMEM(a.shape, a.dtype) for a in arrays),
        in_specs=[ANY] * 3,
        out_specs=(VMEM,) * 3,
        scratch_shapes=[pltpu.SemaphoreType.DMA((3,))],
        compiler_params=pltpu.CompilerParams(vmem_limit_bytes=16 * 1024 * 1024),
        cost_estimate=pl.CostEstimate(flops=0, bytes_accessed=arrays[1].size * 2, transcendentals=0),
        name="load",
    )(*(pltpu.with_memory_space_constraint(a, pltpu.HBM) for a in arrays))


def layer_kernel(tick, src_row, rows, brs, nzb, own_slot, prev_slot, aliased, *refs):
    refs = list(refs)
    meta, main, low, high, w, bias = refs[:6]
    del refs[:6]
    prev = refs.pop(0) if prev_slot is not None else None
    if aliased:
        refs.pop(0)
    emitted = refs.pop(0) if prev_slot is not None or own_slot is not None else None
    out, xbuf, sems = refs
    edge = HALO * BLK
    width = brs * BLK

    def write(src, slot, sem):
        slot_tick, row = slot
        return pltpu.make_async_copy(src, emitted.at[slot_tick, pl.ds(row, rows), :], sem)

    if prev is not None:
        write(prev, prev_slot, sems.at[0]).start()
    live = meta[brs * nzb] >= tick

    @pl.when(live)
    def _():
        src = pl.ds(src_row, rows)
        xbuf[:, 0:edge] = low[src, :]
        xbuf[:, edge : edge + width] = main[src, :]
        xbuf[:, edge + width : edge + width + edge] = high[src, :]
        for i in range(brs):
            picked = jnp.concatenate(
                [
                    xbuf[:, pl.ds(pl.multiple_of(meta[i * nzb + k] * BLK, BLK), BLK)]
                    for k in range(nzb)
                ],
                axis=1,
            )
            cols = pl.ds(i * BLK, BLK)
            summed = jnp.dot(picked, w[i], preferred_element_type=jnp.float32) + bias[:, cols]
            out[:, cols] = jnp.maximum(summed, 0.0).astype(jnp.bfloat16)

    @pl.when(jnp.logical_not(live))
    def _():
        out[...] = jnp.zeros_like(out)

    if own_slot is not None:
        write(out, own_slot, sems.at[1]).start()
    if prev is not None:
        write(prev, prev_slot, sems.at[0]).wait()
    if own_slot is not None:
        write(out, own_slot, sems.at[1]).wait()


def apply_layer(tick, src_row, row, rows, last, operands, prev, prev_slot, emitted, emitted_aval):
    meta, main, low, high, w, bias = operands
    brs, depth = w.shape[:2]
    nzb = depth // BLK
    width = brs * BLK
    edge = HALO * BLK
    args = [
        pltpu.with_memory_space_constraint(meta, pltpu.SMEM),
        *(pltpu.with_memory_space_constraint(a, pltpu.VMEM) for a in (main, low, high, w, bias)),
    ]
    specs = [SMEM] + [VMEM] * 5
    out_shape = []
    out_specs = []
    scratch = [
        pltpu.VMEM((rows, width + 2 * edge), jnp.bfloat16),
        pltpu.SemaphoreType.DMA((2,)),
    ]
    aliases = {}
    if prev is not None:
        args.append(pltpu.with_memory_space_constraint(prev, pltpu.VMEM))
        specs.append(VMEM)
    if emitted is not None:
        aliases = {len(args): 0}
        args.append(emitted)
        specs.append(ANY)
    if prev is not None or last:
        out_shape.append(emitted_aval)
        out_specs.append(ANY)
    if last:
        scratch.insert(0, pltpu.VMEM((rows, width), jnp.bfloat16))
    else:
        out_shape.append(pltpu.VMEM((rows, width), jnp.bfloat16))
        out_specs.append(VMEM)
    body = functools.partial(
        layer_kernel, tick, src_row, rows, brs, nzb, (tick, row) if last else None, prev_slot, emitted is not None
    )
    return pl.pallas_call(
        body,
        out_shape=tuple(out_shape),
        in_specs=specs,
        out_specs=tuple(out_specs),
        scratch_shapes=scratch,
        input_output_aliases=aliases,
        compiler_params=pltpu.CompilerParams(vmem_limit_bytes=8 * 1024 * 1024),
        cost_estimate=pl.CostEstimate(
            flops=2 * rows * brs * nzb * BLK * BLK, bytes_accessed=w.size * 2, transcendentals=0
        ),
        name=f"layer_t{tick}_r{row}",
    )(*args)


def edges_kernel(main, after, left, right):
    del after
    edge = HALO * BLK
    left[...] = main[:, 0:edge]
    right[...] = main[:, main.shape[1] - edge :]


def edges(main, after):
    aval = pltpu.VMEM((main.shape[0], HALO * BLK), main.dtype)
    return pl.pallas_call(
        edges_kernel,
        out_shape=(aval, aval),
        in_specs=[VMEM, ANY],
        out_specs=(VMEM, VMEM),
        name="edges",
    )(pltpu.with_memory_space_constraint(main, pltpu.VMEM), after)


def shards(sections, blks, pending_groups, coefficient_tiles, source_block_indices, additive_offsets):
    block_rows, nzb = coefficient_tiles.shape[1:3]
    height, width = pending_groups.shape
    rows = height // CHUNKS
    edge = HALO * BLK
    section = lax.axis_index("section")
    me = lax.axis_index("blk")
    emitted_aval = jax.ShapeDtypeStruct((TICKS, height, width), jnp.bfloat16)

    def cycle(axis, count, shift, values):
        return lax.ppermute(values, axis, [(i, (i + shift) % count) for i in range(count)])

    def halos(left, right):
        return cycle("blk", blks, 1, right), cycle("blk", blks, -1, left)

    low, high = halos(pending_groups[:, :edge], pending_groups[:, width - edge :])
    state, w, bias = load(
        pending_groups, coefficient_tiles.reshape(block_rows, nzb * BLK, BLK), additive_offsets
    )
    local_cols = jnp.mod(source_block_indices[0] - me * block_rows + HALO, block_rows * blks)
    meta = jnp.concatenate([local_cols.reshape(-1), section.astype(jnp.int32)[None]])
    parts = [state] * CHUNKS
    emitted = prev = prev_slot = None
    for tick in range(TICKS):
        last = tick + 1 == TICKS
        for c in range(CHUNKS):
            src_row = c * rows
            if tick > 0:
                low, high = halos(*edges(parts[c], made))
                src_row = 0
            outs = list(
                apply_layer(
                    tick, src_row, c * rows, rows, last, (meta, parts[c], low, high, w, bias), prev, prev_slot, emitted, emitted_aval
                )
            )
            if prev is not None or last:
                emitted = outs.pop(0)
            prev = prev_slot = None
            made = emitted if last else outs[0]
            if not last:
                prev, prev_slot = outs[0], (tick, c * rows)
                parts[c] = cycle("section", sections, 1, prev)
    return emitted


def solution(mesh):
    in_specs = (
        P("section", "blk"),
        P("section", "blk", None, None, None),
        P("section", "blk", None),
        P("section", "blk"),
    )
    out_specs = P(None, "section", "blk")
    body = functools.partial(shards, mesh.shape["section"], mesh.shape["blk"])
    return jax.shard_map(body, mesh=mesh, in_specs=in_specs, out_specs=out_specs, check_vma=False)
```

time: 208 us -> 175 us (0.84)
  the two profiles are of different devices: /device:TPU:29 before, /device:TPU:1 now
where the time goes in v2:
time: 175 us; the launch traced here: 173 us
  local copies, waits for them, and re-layouts  61.6 us (35%)
  waiting for transfers between devices  50.4 us (29%)
  starting transfers between devices  33.8 us (19%)
  Pallas kernels  25.8 us (15%)
    unnamed x82, local copies, waits for them, and re-layouts  60.5 us
    ppermute x44, waiting for transfers between devices, cycle(): lax.ppermute(values, axis, [(i, (i + shift) % count) for i in range(count)])  50.4 us
    ppermute x44, starting transfers between devices, cycle(): lax.ppermute(values, axis, [(i, (i + shift) % count) for i in range(count)])  33.8 us
    pallas_call x16, Pallas kernels, apply_layer(): pl.pallas_call(body, out_shape=tuple(out_shape), in_specs=specs, out_spec...  22.1 us
    pallas_call x1, Pallas kernels, load(): pl.pallas_call(load_kernel, out_shape=tuple((pltpu.VMEM(a.shape, a.dtype)...  3.61 us
  transfers between devices with their start and end apart: 44, of which 29 were waited for; matrix products, arithmetic and copies ran while one was open for 1% of the time, Pallas kernels for 13%

profile of v2, /device:TPU:1, one launch (start us, length us, event | category | flops | bytes accessed | tf_op | source)
XLA Modules:
  0.0 172.9 jit_solution(15006063858040627570)
XLA Ops:
  0.9 2.7 %collective-permute-start = (bf16[64,512]{1,0:T(8,128)(2,1)S(1)}, bf16[64,512]{1,0:T(8,128)(2,1)S(1)}, u32[]{:S(2)}, u32[]{:S(2)}) collective-permute-start(bf16[64,512]{1,0:T(8,128)(2,1)S(1)} %get-tuple-element.120), channel_id=1, source_target_pairs={{0,1},{1,2},{2,3},{3,0},{4,5},{5,6},{6,7},{7,4},{8,9},{9,10},{10,1... | collective-permute-start | bytes 196616 | tf_op jit(solution)/shard_map/ppermute | solution.py:172
  4.4 3.6 %load.1 = (bf16[64,4096]{1,0:T(8,128)(2,1)S(1)}, bf16[32,1024,128]{2,1,0:T(8,128)(2,1)S(1)}, f32[1,4096]{1,0:T(1,128)S(1)}) custom-call(bf16[64,4096]{1,0:T(8,128)(2,1)} %state.1, bf16[32,1024,128]{2,1,0:T(8,128)(2,1)} %bitcast.2, f32[1,4096]{1,0:T(1,128)} %bias.1), custom_call_target="tpu_custom_call" | custom-call | bytes 8388608 | tf_op jit(solution)/shard_map/load/pallas_call | solution.py:31
  8.1 2.1 %layer_t0_r0.1.refs_6_ = bf16[32,4096]{1,0:T(8,128)(2,1)S(1)} custom-call(s32[257]{0:T(512)S(1)} %pad_add_fusion.refs_0_, bf16[64,4096]{1,0:T(8,128)(2,1)S(1)} %get-tuple-element.62.refs_1_, bf16[64,512]{1,0:T(8,128)(2,1)S(1)} %collective-permute-done.refs_2_, bf16[64,512]{1,0:T(8,128)(2,1)S(1)} %collective-permute-done.1.refs_3_, ...), custom_call_target="tpu_custom_call" | custom-call | flops 268435456 | bytes 8388608 | tf_op jit(solution)/shard_map/layer_t0_r0/pallas_call | solution.py:129
  10.2 1.3 collective-permute-start.3
  11.4 2.1 %layer_t0_r32.1 = (bf16[8,64,4096]{2,1,0:T(8,128)(2,1)}, bf16[32,4096]{1,0:T(8,128)(2,1)S(1)}) custom-call(s32[257]{0:T(512)S(1)} %pad_add_fusion.refs_0_, bf16[64,4096]{1,0:T(8,128)(2,1)S(1)} %get-tuple-element.62.refs_1_, bf16[64,512]{1,0:T(8,128)(2,1)S(1)} %collective-permute-done.refs_2_, bf16[64,512]{1,0:T(8,128)(2,1)S(1)} %collective-permute-done.1.refs_3_, ...), custom_call_target="tpu_custom_call" | custom-call | flops 268435456 | bytes 8388608 | tf_op jit(solution)/shard_map/layer_t0_r32/pallas_call | solution.py:129
  13.5 1.3 collective-permute-start.2
  14.8 5.7 %collective-permute-done.3.main.refs_1_ = bf16[32,4096]{1,0:T(8,128)(2,1)S(1)} collective-permute-done((bf16[32,4096]{1,0:T(8,128)(2,1)S(1)}, bf16[32,4096]{1,0:T(8,128)(2,1)S(1)}, u32[]{:S(2)}, u32[]{:S(2)}) %collective-permute-start.3) | collective-permute-done | bytes 262176 | tf_op jit(solution)/shard_map/ppermute | solution.py:172
  20.6 3.4 %collective-permute-start.4 = (bf16[32,512]{1,0:T(8,128)(2,1)S(1)}, bf16[32,512]{1,0:T(8,128)(2,1)S(1)}, u32[]{:S(2)}, u32[]{:S(2)}) collective-permute-start(bf16[32,512]{1,0:T(8,128)(2,1)S(1)} %get-tuple-element.66), channel_id=1, source_target_pairs={{0,1},{1,2},{2,3},{3,0},{4,5},{5,6},{6,7},{7,4},{8,9},{9,10},{10,1... | collective-permute-start | bytes 98312 | tf_op jit(solution)/shard_map/ppermute | solution.py:172
  24.0 1.0 collective-permute-done.4.refs_2_
  25.0 2.3 %collective-permute-done.5.refs_3_ = bf16[32,512]{1,0:T(8,128)(2,1)S(1)} collective-permute-done((bf16[32,512]{1,0:T(8,128)(2,1)S(1)}, bf16[32,512]{1,0:T(8,128)(2,1)S(1)}, u32[]{:S(2)}, u32[]{:S(2)}) %collective-permute-start.5) | collective-permute-done | bytes 32800 | tf_op jit(solution)/shard_map/ppermute | solution.py:172
  27.3 3.4 %copy-done.1 = bf16[32,1024,128]{2,1,0:T(8,128)(2,1)S(1)} copy-done((bf16[32,1024,128]{2,1,0:T(8,128)(2,1)S(1)}, bf16[32,1024,128]{2,1,0:T(8,128)(2,1)}, u32[]{:S(2)}) %copy-start.1) | copy-done | bytes 8388632
  31.6 1.3 layer_t1_r0.1
  34.8 2.2 %collective-permute-done.7.refs_3_ = bf16[32,512]{1,0:T(8,128)(2,1)S(1)} collective-permute-done((bf16[32,512]{1,0:T(8,128)(2,1)S(1)}, bf16[32,512]{1,0:T(8,128)(2,1)S(1)}, u32[]{:S(2)}, u32[]{:S(2)}) %collective-permute-start.7) | collective-permute-done | bytes 32800 | tf_op jit(solution)/shard_map/ppermute | solution.py:172
  37.0 3.4 %copy-done.2 = bf16[32,1024,128]{2,1,0:T(8,128)(2,1)S(1)} copy-done((bf16[32,1024,128]{2,1,0:T(8,128)(2,1)S(1)}, bf16[32,1024,128]{2,1,0:T(8,128)(2,1)}, u32[]{:S(2)}) %copy-start.2) | copy-done | bytes 8388632
  40.4 0.9 copy-done.18
  41.4 1.3 layer_t1_r32.1
  42.6 2.2 %collective-permute-start.8 = (bf16[32,4096]{1,0:T(8,128)(2,1)S(1)}, bf16[32,4096]{1,0:T(8,128)(2,1)S(1)}, u32[]{:S(2)}, u32[]{:S(2)}) collective-permute-start(bf16[32,4096]{1,0:T(8,128)(2,1)S(1)} %get-tuple-element.73.after.refs_6_), channel_id=1, source_target_pairs={{0,4},{4,8},{8,12},{12,16},{16,20},{20,24},{24,28},{28,0},{1,5},{5... | collective-permute-start | bytes 786440 | tf_op jit(solution)/shard_map/ppermute | solution.py:172
  46.1 2.5 %collective-permute-done.11.refs_3_ = bf16[32,512]{1,0:T(8,128)(2,1)S(1)} collective-permute-done((bf16[32,512]{1,0:T(8,128)(2,1)S(1)}, bf16[32,512]{1,0:T(8,128)(2,1)S(1)}, u32[]{:S(2)}, u32[]{:S(2)}) %collective-permute-start.11) | collective-permute-done | bytes 32800 | tf_op jit(solution)/shard_map/ppermute | solution.py:172
  48.6 3.4 %copy-done.3 = bf16[32,1024,128]{2,1,0:T(8,128)(2,1)S(1)} copy-done((bf16[32,1024,128]{2,1,0:T(8,128)(2,1)S(1)}, bf16[32,1024,128]{2,1,0:T(8,128)(2,1)}, u32[]{:S(2)}) %copy-start.3) | copy-done | bytes 8388632
  52.0 0.9 copy-done.20
  53.0 1.3 layer_t2_r0.1
  56.2 2.2 %collective-permute-done.13.refs_3_ = bf16[32,512]{1,0:T(8,128)(2,1)S(1)} collective-permute-done((bf16[32,512]{1,0:T(8,128)(2,1)S(1)}, bf16[32,512]{1,0:T(8,128)(2,1)S(1)}, u32[]{:S(2)}, u32[]{:S(2)}) %collective-permute-start.13) | collective-permute-done | bytes 32800 | tf_op jit(solution)/shard_map/ppermute | solution.py:172
  58.4 3.4 %copy-done.4 = bf16[32,1024,128]{2,1,0:T(8,128)(2,1)S(1)} copy-done((bf16[32,1024,128]{2,1,0:T(8,128)(2,1)S(1)}, bf16[32,1024,128]{2,1,0:T(8,128)(2,1)}, u32[]{:S(2)}) %copy-start.4) | copy-done | bytes 8388632
  62.7 1.3 layer_t2_r32.1
  64.0 2.9 %collective-permute-start.14 = (bf16[32,4096]{1,0:T(8,128)(2,1)S(1)}, bf16[32,4096]{1,0:T(8,128)(2,1)S(1)}, u32[]{:S(2)}, u32[]{:S(2)}) collective-permute-start(bf16[32,4096]{1,0:T(8,128)(2,1)S(1)} %get-tuple-element.81.after.refs_6_), channel_id=1, source_target_pairs={{0,4},{4,8},{8,12},{12,16},{16,20},{20,24},{24,28},{28,0},{1,5},{5... | collective-permute-start | bytes 786440 | tf_op jit(solution)/shard_map/ppermute | solution.py:172
  68.2 2.6 %collective-permute-done.17.refs_3_ = bf16[32,512]{1,0:T(8,128)(2,1)S(1)} collective-permute-done((bf16[32,512]{1,0:T(8,128)(2,1)S(1)}, bf16[32,512]{1,0:T(8,128)(2,1)S(1)}, u32[]{:S(2)}, u32[]{:S(2)}) %collective-permute-start.17) | collective-permute-done | bytes 32800 | tf_op jit(solution)/shard_map/ppermute | solution.py:172
  70.8 3.4 %copy-done.5 = bf16[32,1024,128]{2,1,0:T(8,128)(2,1)S(1)} copy-done((bf16[32,1024,128]{2,1,0:T(8,128)(2,1)S(1)}, bf16[32,1024,128]{2,1,0:T(8,128)(2,1)}, u32[]{:S(2)}) %copy-start.5) | copy-done | bytes 8388632
  74.2 0.9 copy-done.24
  75.1 1.3 layer_t3_r0.1
  76.4 1.5 collective-permute-start.21
  79.4 2.5 %collective-permute-done.19.refs_3_ = bf16[32,512]{1,0:T(8,128)(2,1)S(1)} collective-permute-done((bf16[32,512]{1,0:T(8,128)(2,1)S(1)}, bf16[32,512]{1,0:T(8,128)(2,1)S(1)}, u32[]{:S(2)}, u32[]{:S(2)}) %collective-permute-start.19) | collective-permute-done | bytes 32800 | tf_op jit(solution)/shard_map/ppermute | solution.py:172
  81.8 3.4 %copy-done.6 = bf16[32,1024,128]{2,1,0:T(8,128)(2,1)S(1)} copy-done((bf16[32,1024,128]{2,1,0:T(8,128)(2,1)S(1)}, bf16[32,1024,128]{2,1,0:T(8,128)(2,1)}, u32[]{:S(2)}) %copy-start.6) | copy-done | bytes 8388632
  86.2 1.3 layer_t3_r32.1
  87.5 1.9 %collective-permute-start.20 = (bf16[32,4096]{1,0:T(8,128)(2,1)S(1)}, bf16[32,4096]{1,0:T(8,128)(2,1)S(1)}, u32[]{:S(2)}, u32[]{:S(2)}) collective-permute-start(bf16[32,4096]{1,0:T(8,128)(2,1)S(1)} %get-tuple-element.89.after.refs_6_), channel_id=1, source_target_pairs={{0,4},{4,8},{8,12},{12,16},{16,20},{20,24},{24,28},{28,0},{1,5},{5... | collective-permute-start | bytes 786440 | tf_op jit(solution)/shard_map/ppermute | solution.py:172
  90.7 2.5 %collective-permute-done.23.refs_3_ = bf16[32,512]{1,0:T(8,128)(2,1)S(1)} collective-permute-done((bf16[32,512]{1,0:T(8,128)(2,1)S(1)}, bf16[32,512]{1,0:T(8,128)(2,1)S(1)}, u32[]{:S(2)}, u32[]{:S(2)}) %collective-permute-start.23) | collective-permute-done | bytes 32800 | tf_op jit(solution)/shard_map/ppermute | solution.py:172
  93.2 3.4 %copy-done.7 = bf16[32,1024,128]{2,1,0:T(8,128)(2,1)S(1)} copy-done((bf16[32,1024,128]{2,1,0:T(8,128)(2,1)S(1)}, bf16[32,1024,128]{2,1,0:T(8,128)(2,1)}, u32[]{:S(2)}) %copy-start.7) | copy-done | bytes 8388632
  97.5 1.3 layer_t4_r0.1
  98.8 1.4 collective-permute-start.27
  101.5 2.5 %collective-permute-done.25.refs_3_ = bf16[32,512]{1,0:T(8,128)(2,1)S(1)} collective-permute-done((bf16[32,512]{1,0:T(8,128)(2,1)S(1)}, bf16[32,512]{1,0:T(8,128)(2,1)S(1)}, u32[]{:S(2)}, u32[]{:S(2)}) %collective-permute-start.25) | collective-permute-done | bytes 32800 | tf_op jit(solution)/shard_map/ppermute | solution.py:172
  104.0 3.4 %copy-done.8 = bf16[32,1024,128]{2,1,0:T(8,128)(2,1)S(1)} copy-done((bf16[32,1024,128]{2,1,0:T(8,128)(2,1)S(1)}, bf16[32,1024,128]{2,1,0:T(8,128)(2,1)}, u32[]{:S(2)}) %copy-start.8) | copy-done | bytes 8388632
  108.3 1.3 layer_t4_r32.1
  109.6 2.4 %collective-permute-start.26 = (bf16[32,4096]{1,0:T(8,128)(2,1)S(1)}, bf16[32,4096]{1,0:T(8,128)(2,1)S(1)}, u32[]{:S(2)}, u32[]{:S(2)}) collective-permute-start(bf16[32,4096]{1,0:T(8,128)(2,1)S(1)} %get-tuple-element.97.after.refs_6_), channel_id=1, source_target_pairs={{0,4},{4,8},{8,12},{12,16},{16,20},{20,24},{24,28},{28,0},{1,5},{5... | collective-permute-start | bytes 786440 | tf_op jit(solution)/shard_map/ppermute | solution.py:172
  113.3 2.5 %collective-permute-done.29.refs_3_ = bf16[32,512]{1,0:T(8,128)(2,1)S(1)} collective-permute-done((bf16[32,512]{1,0:T(8,128)(2,1)S(1)}, bf16[32,512]{1,0:T(8,128)(2,1)S(1)}, u32[]{:S(2)}, u32[]{:S(2)}) %collective-permute-start.29) | collective-permute-done | bytes 32800 | tf_op jit(solution)/shard_map/ppermute | solution.py:172
  115.8 3.4 %copy-done.9 = bf16[32,1024,128]{2,1,0:T(8,128)(2,1)S(1)} copy-done((bf16[32,1024,128]{2,1,0:T(8,128)(2,1)S(1)}, bf16[32,1024,128]{2,1,0:T(8,128)(2,1)}, u32[]{:S(2)}) %copy-start.9) | copy-done | bytes 8388632
  120.1 1.3 layer_t5_r0.1
  123.3 2.5 %collective-permute-done.31.refs_3_ = bf16[32,512]{1,0:T(8,128)(2,1)S(1)} collective-permute-done((bf16[32,512]{1,0:T(8,128)(2,1)S(1)}, bf16[32,512]{1,0:T(8,128)(2,1)S(1)}, u32[]{:S(2)}, u32[]{:S(2)}) %collective-permute-start.31) | collective-permute-done | bytes 32800 | tf_op jit(solution)/shard_map/ppermute | solution.py:172
  125.8 3.4 %copy-done.10 = bf16[32,1024,128]{2,1,0:T(8,128)(2,1)S(1)} copy-done((bf16[32,1024,128]{2,1,0:T(8,128)(2,1)S(1)}, bf16[32,1024,128]{2,1,0:T(8,128)(2,1)}, u32[]{:S(2)}) %copy-start.10) | copy-done | bytes 8388632
  130.1 1.3 layer_t5_r32.1
  131.4 1.4 collective-permute-start.32
  134.1 2.5 %collective-permute-done.35.refs_3_ = bf16[32,512]{1,0:T(8,128)(2,1)S(1)} collective-permute-done((bf16[32,512]{1,0:T(8,128)(2,1)S(1)}, bf16[32,512]{1,0:T(8,128)(2,1)S(1)}, u32[]{:S(2)}, u32[]{:S(2)}) %collective-permute-start.35) | collective-permute-done | bytes 32800 | tf_op jit(solution)/shard_map/ppermute | solution.py:172
  136.6 3.4 %copy-done.11 = bf16[32,1024,128]{2,1,0:T(8,128)(2,1)S(1)} copy-done((bf16[32,1024,128]{2,1,0:T(8,128)(2,1)S(1)}, bf16[32,1024,128]{2,1,0:T(8,128)(2,1)}, u32[]{:S(2)}) %copy-start.11) | copy-done | bytes 8388632
  141.0 1.3 layer_t6_r0.1
  142.3 1.4 collective-permute-start.39
  145.0 2.5 %collective-permute-done.37.refs_3_ = bf16[32,512]{1,0:T(8,128)(2,1)S(1)} collective-permute-done((bf16[32,512]{1,0:T(8,128)(2,1)S(1)}, bf16[32,512]{1,0:T(8,128)(2,1)S(1)}, u32[]{:S(2)}, u32[]{:S(2)}) %collective-permute-start.37) | collective-permute-done | bytes 32800 | tf_op jit(solution)/shard_map/ppermute | solution.py:172
  147.4 3.4 %copy-done.12 = bf16[32,1024,128]{2,1,0:T(8,128)(2,1)S(1)} copy-done((bf16[32,1024,128]{2,1,0:T(8,128)(2,1)S(1)}, bf16[32,1024,128]{2,1,0:T(8,128)(2,1)}, u32[]{:S(2)}) %copy-start.12) | copy-done | bytes 8388632
  151.8 1.3 layer_t6_r32.1
  155.0 2.7 %collective-permute-done.41.refs_3_ = bf16[32,512]{1,0:T(8,128)(2,1)S(1)} collective-permute-done((bf16[32,512]{1,0:T(8,128)(2,1)S(1)}, bf16[32,512]{1,0:T(8,128)(2,1)S(1)}, u32[]{:S(2)}, u32[]{:S(2)}) %collective-permute-start.41) | collective-permute-done | bytes 32800 | tf_op jit(solution)/shard_map/ppermute | solution.py:172
  157.7 3.4 %copy-done.13 = bf16[32,1024,128]{2,1,0:T(8,128)(2,1)S(1)} copy-done((bf16[32,1024,128]{2,1,0:T(8,128)(2,1)S(1)}, bf16[32,1024,128]{2,1,0:T(8,128)(2,1)}, u32[]{:S(2)}) %copy-start.13) | copy-done | bytes 8388632
  162.0 1.4 layer_t7_r0.1.after.refs_6_
  163.4 1.3 collective-permute-start.42
  164.7 1.0 collective-permute-done.42.refs_2_
  165.7 2.3 %collective-permute-done.43.refs_3_ = bf16[32,512]{1,0:T(8,128)(2,1)S(1)} collective-permute-done((bf16[32,512]{1,0:T(8,128)(2,1)S(1)}, bf16[32,512]{1,0:T(8,128)(2,1)S(1)}, u32[]{:S(2)}, u32[]{:S(2)}) %collective-permute-start.43) | collective-permute-done | bytes 32800 | tf_op jit(solution)/shard_map/ppermute | solution.py:172
  168.0 3.4 %copy-done.14 = bf16[32,1024,128]{2,1,0:T(8,128)(2,1)S(1)} copy-done((bf16[32,1024,128]{2,1,0:T(8,128)(2,1)S(1)}, bf16[32,1024,128]{2,1,0:T(8,128)(2,1)}, u32[]{:S(2)}) %copy-start.14) | copy-done | bytes 8388632
  171.4 1.3 layer_t7_r32.1
  (143 shorter events, 29.2 us)
Async XLA Ops:
  0.9 7.2 %collective-permute-start = (bf16[64,512]{1,0:T(8,128)(2,1)S(1)}, bf16[64,512]{1,0:T(8,128)(2,1)S(1)}, u32[]{:S(2)}, u32[]{:S(2)}) collective-permute-start(bf16[64,512]{1,0:T(8,128)(2,1)S(1)} %get-tuple-element.120), channel_id=1, source_target_pairs={{0,1},{1,2},{2,3},{3,0},{4,5},{5,6},{6,7},{7,4},{8,9},{9,10},{10,1... | collective-permute-start | bytes 196616 | tf_op jit(solution)/shard_map/ppermute | solution.py:172
  3.5 4.5 %collective-permute-start.1 = (bf16[64,512]{1,0:T(8,128)(2,1)S(1)}, bf16[64,512]{1,0:T(8,128)(2,1)S(1)}, u32[]{:S(2)}, u32[]{:S(2)}) collective-permute-start(bf16[64,512]{1,0:T(8,128)(2,1)S(1)} %get-tuple-element.119), channel_id=1, source_target_pairs={{0,3},{1,0},{2,1},{3,2},{4,7},{5,4},{6,5},{7,6},{8,11},{9,8},{10,9... | collective-permute-start | bytes 196616 | tf_op jit(solution)/shard_map/ppermute | solution.py:172
  8.0 3.4 %copy-start = (bf16[32,1024,128]{2,1,0:T(8,128)(2,1)}, bf16[32,1024,128]{2,1,0:T(8,128)(2,1)S(1)}, u32[]{:S(2)}) copy-start(bf16[32,1024,128]{2,1,0:T(8,128)(2,1)S(1)} %get-tuple-element.63.refs_4_) | copy-start | bytes 25165828
  10.2 10.4 %collective-permute-start.3 = (bf16[32,4096]{1,0:T(8,128)(2,1)S(1)}, bf16[32,4096]{1,0:T(8,128)(2,1)S(1)}, u32[]{:S(2)}, u32[]{:S(2)}) collective-permute-start(bf16[32,4096]{1,0:T(8,128)(2,1)S(1)} %layer_t0_r0.1.refs_6_), channel_id=1, source_target_pairs={{0,4},{4,8},{8,12},{12,16},{16,20},{20,24},{24,28},{28,0},{1,5},{5... | collective-permute-start | bytes 786440 | tf_op jit(solution)/shard_map/ppermute | solution.py:172
  13.5 7.0 %copy-start.39 = (bf16[32,4096]{1,0:T(8,128)(2,1)}, bf16[32,4096]{1,0:T(8,128)(2,1)S(1)}, u32[]{:S(2)}) copy-start(bf16[32,4096]{1,0:T(8,128)(2,1)S(1)} %get-tuple-element.65.after.refs_6_) | copy-start | bytes 786436
  13.5 19.5 %collective-permute-start.2 = (bf16[32,4096]{1,0:T(8,128)(2,1)S(1)}, bf16[32,4096]{1,0:T(8,128)(2,1)S(1)}, u32[]{:S(2)}, u32[]{:S(2)}) collective-permute-start(bf16[32,4096]{1,0:T(8,128)(2,1)S(1)} %get-tuple-element.65.after.refs_6_), channel_id=1, source_target_pairs={{0,4},{4,8},{8,12},{12,16},{16,20},{20,24},{24,28},{28,0},{1,5},{5... | collective-permute-start | bytes 786440 | tf_op jit(solution)/shard_map/ppermute | solution.py:172
  20.6 4.4 %collective-permute-start.4 = (bf16[32,512]{1,0:T(8,128)(2,1)S(1)}, bf16[32,512]{1,0:T(8,128)(2,1)S(1)}, u32[]{:S(2)}, u32[]{:S(2)}) collective-permute-start(bf16[32,512]{1,0:T(8,128)(2,1)S(1)} %get-tuple-element.66), channel_id=1, source_target_pairs={{0,1},{1,2},{2,3},{3,0},{4,5},{5,6},{6,7},{7,4},{8,9},{9,10},{10,1... | collective-permute-start | bytes 98312 | tf_op jit(solution)/shard_map/ppermute | solution.py:172
  24.0 3.3 %collective-permute-start.5 = (bf16[32,512]{1,0:T(8,128)(2,1)S(1)}, bf16[32,512]{1,0:T(8,128)(2,1)S(1)}, u32[]{:S(2)}, u32[]{:S(2)}) collective-permute-start(bf16[32,512]{1,0:T(8,128)(2,1)S(1)} %get-tuple-element.67), channel_id=1, source_target_pairs={{0,3},{1,0},{2,1},{3,2},{4,7},{5,4},{6,5},{7,6},{8,11},{9,8},{10,9... | collective-permute-start | bytes 98312 | tf_op jit(solution)/shard_map/ppermute | solution.py:172
  27.3 3.4 %copy-start.1 = (bf16[32,1024,128]{2,1,0:T(8,128)(2,1)S(1)}, bf16[32,1024,128]{2,1,0:T(8,128)(2,1)}, u32[]{:S(2)}) copy-start(bf16[32,1024,128]{2,1,0:T(8,128)(2,1)} %copy-done) | copy-start | bytes 25165828
  32.9 12.0 %collective-permute-start.9 = (bf16[32,4096]{1,0:T(8,128)(2,1)S(1)}, bf16[32,4096]{1,0:T(8,128)(2,1)S(1)}, u32[]{:S(2)}, u32[]{:S(2)}) collective-permute-start(bf16[32,4096]{1,0:T(8,128)(2,1)S(1)} %get-tuple-element.69.after.refs_6_), channel_id=1, source_target_pairs={{0,4},{4,8},{8,12},{12,16},{16,20},{20,24},{24,28},{28,0},{1,5},{5... | collective-permute-start | bytes 786440 | tf_op jit(solution)/shard_map/ppermute | solution.py:172
  33.6 1.2 collective-permute-start.6
  33.6 3.4 %collective-permute-start.7 = (bf16[32,512]{1,0:T(8,128)(2,1)S(1)}, bf16[32,512]{1,0:T(8,128)(2,1)S(1)}, u32[]{:S(2)}, u32[]{:S(2)}) collective-permute-start(bf16[32,512]{1,0:T(8,128)(2,1)S(1)} %get-tuple-element.71), channel_id=1, source_target_pairs={{0,3},{1,0},{2,1},{3,2},{4,7},{5,4},{6,5},{7,6},{8,11},{9,8},{10,9... | collective-permute-start | bytes 98312 | tf_op jit(solution)/shard_map/ppermute | solution.py:172
  37.0 3.4 %copy-start.2 = (bf16[32,1024,128]{2,1,0:T(8,128)(2,1)S(1)}, bf16[32,1024,128]{2,1,0:T(8,128)(2,1)}, u32[]{:S(2)}) copy-start(bf16[32,1024,128]{2,1,0:T(8,128)(2,1)} %copy-done) | copy-start | bytes 25165828
  42.6 2.2 %copy-start.19 = (bf16[32,4096]{1,0:T(8,128)(2,1)}, bf16[32,4096]{1,0:T(8,128)(2,1)S(1)}, u32[]{:S(2)}) copy-start(bf16[32,4096]{1,0:T(8,128)(2,1)S(1)} %get-tuple-element.73.after.refs_6_) | copy-start | bytes 786436
  42.6 12.2 %collective-permute-start.8 = (bf16[32,4096]{1,0:T(8,128)(2,1)S(1)}, bf16[32,4096]{1,0:T(8,128)(2,1)S(1)}, u32[]{:S(2)}, u32[]{:S(2)}) collective-permute-start(bf16[32,4096]{1,0:T(8,128)(2,1)S(1)} %get-tuple-element.73.after.refs_6_), channel_id=1, source_target_pairs={{0,4},{4,8},{8,12},{12,16},{16,20},{20,24},{24,28},{28,0},{1,5},{5... | collective-permute-start | bytes 786440 | tf_op jit(solution)/shard_map/ppermute | solution.py:172
  44.9 1.3 collective-permute-start.10
  45.0 3.7 %collective-permute-start.11 = (bf16[32,512]{1,0:T(8,128)(2,1)S(1)}, bf16[32,512]{1,0:T(8,128)(2,1)S(1)}, u32[]{:S(2)}, u32[]{:S(2)}) collective-permute-start(bf16[32,512]{1,0:T(8,128)(2,1)S(1)} %get-tuple-element.75), channel_id=1, source_target_pairs={{0,3},{1,0},{2,1},{3,2},{4,7},{5,4},{6,5},{7,6},{8,11},{9,8},{10,9... | collective-permute-start | bytes 98312 | tf_op jit(solution)/shard_map/ppermute | solution.py:172
  48.6 3.4 %copy-start.3 = (bf16[32,1024,128]{2,1,0:T(8,128)(2,1)S(1)}, bf16[32,1024,128]{2,1,0:T(8,128)(2,1)}, u32[]{:S(2)}) copy-start(bf16[32,1024,128]{2,1,0:T(8,128)(2,1)} %copy-done) | copy-start | bytes 25165828
  54.3 12.7 %collective-permute-start.15 = (bf16[32,4096]{1,0:T(8,128)(2,1)S(1)}, bf16[32,4096]{1,0:T(8,128)(2,1)S(1)}, u32[]{:S(2)}, u32[]{:S(2)}) collective-permute-start(bf16[32,4096]{1,0:T(8,128)(2,1)S(1)} %get-tuple-element.77.after.refs_6_), channel_id=1, source_target_pairs={{0,4},{4,8},{8,12},{12,16},{16,20},{20,24},{24,28},{28,0},{1,5},{5... | collective-permute-start | bytes 786440 | tf_op jit(solution)/shard_map/ppermute | solution.py:172
  55.0 1.2 collective-permute-start.12
  55.0 3.4 %collective-permute-start.13 = (bf16[32,512]{1,0:T(8,128)(2,1)S(1)}, bf16[32,512]{1,0:T(8,128)(2,1)S(1)}, u32[]{:S(2)}, u32[]{:S(2)}) collective-permute-start(bf16[32,512]{1,0:T(8,128)(2,1)S(1)} %get-tuple-element.79), channel_id=1, source_target_pairs={{0,3},{1,0},{2,1},{3,2},{4,7},{5,4},{6,5},{7,6},{8,11},{9,8},{10,9... | collective-permute-start | bytes 98312 | tf_op jit(solution)/shard_map/ppermute | solution.py:172
  58.4 3.4 %copy-start.4 = (bf16[32,1024,128]{2,1,0:T(8,128)(2,1)S(1)}, bf16[32,1024,128]{2,1,0:T(8,128)(2,1)}, u32[]{:S(2)}) copy-start(bf16[32,1024,128]{2,1,0:T(8,128)(2,1)} %copy-done) | copy-start | bytes 25165828
  64.0 3.0 %copy-start.23 = (bf16[32,4096]{1,0:T(8,128)(2,1)}, bf16[32,4096]{1,0:T(8,128)(2,1)S(1)}, u32[]{:S(2)}) copy-start(bf16[32,4096]{1,0:T(8,128)(2,1)S(1)} %get-tuple-element.81.after.refs_6_) | copy-start | bytes 786436
  64.0 13.9 %collective-permute-start.14 = (bf16[32,4096]{1,0:T(8,128)(2,1)S(1)}, bf16[32,4096]{1,0:T(8,128)(2,1)S(1)}, u32[]{:S(2)}, u32[]{:S(2)}) collective-permute-start(bf16[32,4096]{1,0:T(8,128)(2,1)S(1)} %get-tuple-element.81.after.refs_6_), channel_id=1, source_target_pairs={{0,4},{4,8},{8,12},{12,16},{16,20},{20,24},{24,28},{28,0},{1,5},{5... | collective-permute-start | bytes 786440 | tf_op jit(solution)/shard_map/ppermute | solution.py:172
  67.0 1.3 collective-permute-start.16
  67.1 3.6 %collective-permute-start.17 = (bf16[32,512]{1,0:T(8,128)(2,1)S(1)}, bf16[32,512]{1,0:T(8,128)(2,1)S(1)}, u32[]{:S(2)}, u32[]{:S(2)}) collective-permute-start(bf16[32,512]{1,0:T(8,128)(2,1)S(1)} %get-tuple-element.83), channel_id=1, source_target_pairs={{0,3},{1,0},{2,1},{3,2},{4,7},{5,4},{6,5},{7,6},{8,11},{9,8},{10,9... | collective-permute-start | bytes 98312 | tf_op jit(solution)/shard_map/ppermute | solution.py:172
  70.8 3.4 %copy-start.5 = (bf16[32,1024,128]{2,1,0:T(8,128)(2,1)S(1)}, bf16[32,1024,128]{2,1,0:T(8,128)(2,1)}, u32[]{:S(2)}) copy-start(bf16[32,1024,128]{2,1,0:T(8,128)(2,1)} %copy-done) | copy-start | bytes 25165828
  76.4 13.0 %collective-permute-start.21 = (bf16[32,4096]{1,0:T(8,128)(2,1)S(1)}, bf16[32,4096]{1,0:T(8,128)(2,1)S(1)}, u32[]{:S(2)}, u32[]{:S(2)}) collective-permute-start(bf16[32,4096]{1,0:T(8,128)(2,1)S(1)} %get-tuple-element.85.after.refs_6_), channel_id=1, source_target_pairs={{0,4},{4,8},{8,12},{12,16},{16,20},{20,24},{24,28},{28,0},{1,5},{5... | collective-permute-start | bytes 786440 | tf_op jit(solution)/shard_map/ppermute | solution.py:172
  77.9 1.4 collective-permute-start.18
  78.2 3.7 %collective-permute-start.19 = (bf16[32,512]{1,0:T(8,128)(2,1)S(1)}, bf16[32,512]{1,0:T(8,128)(2,1)S(1)}, u32[]{:S(2)}, u32[]{:S(2)}) collective-permute-start(bf16[32,512]{1,0:T(8,128)(2,1)S(1)} %get-tuple-element.87), channel_id=1, source_target_pairs={{0,3},{1,0},{2,1},{3,2},{4,7},{5,4},{6,5},{7,6},{8,11},{9,8},{10,9... | collective-permute-start | bytes 98312 | tf_op jit(solution)/shard_map/ppermute | solution.py:172
  81.8 3.4 %copy-start.6 = (bf16[32,1024,128]{2,1,0:T(8,128)(2,1)S(1)}, bf16[32,1024,128]{2,1,0:T(8,128)(2,1)}, u32[]{:S(2)}) copy-start(bf16[32,1024,128]{2,1,0:T(8,128)(2,1)} %copy-done) | copy-start | bytes 25165828
  87.5 1.9 %copy-start.27 = (bf16[32,4096]{1,0:T(8,128)(2,1)}, bf16[32,4096]{1,0:T(8,128)(2,1)S(1)}, u32[]{:S(2)}) copy-start(bf16[32,4096]{1,0:T(8,128)(2,1)S(1)} %get-tuple-element.89.after.refs_6_) | copy-start | bytes 786436
  87.5 12.7 %collective-permute-start.20 = (bf16[32,4096]{1,0:T(8,128)(2,1)S(1)}, bf16[32,4096]{1,0:T(8,128)(2,1)S(1)}, u32[]{:S(2)}, u32[]{:S(2)}) collective-permute-start(bf16[32,4096]{1,0:T(8,128)(2,1)S(1)} %get-tuple-element.89.after.refs_6_), channel_id=1, source_target_pairs={{0,4},{4,8},{8,12},{12,16},{16,20},{20,24},{24,28},{28,0},{1,5},{5... | collective-permute-start | bytes 786440 | tf_op jit(solution)/shard_map/ppermute | solution.py:172
  89.4 1.3 collective-permute-start.22
  89.5 3.7 %collective-permute-start.23 = (bf16[32,512]{1,0:T(8,128)(2,1)S(1)}, bf16[32,512]{1,0:T(8,128)(2,1)S(1)}, u32[]{:S(2)}, u32[]{:S(2)}) collective-permute-start(bf16[32,512]{1,0:T(8,128)(2,1)S(1)} %get-tuple-element.91), channel_id=1, source_target_pairs={{0,3},{1,0},{2,1},{3,2},{4,7},{5,4},{6,5},{7,6},{8,11},{9,8},{10,9... | collective-permute-start | bytes 98312 | tf_op jit(solution)/shard_map/ppermute | solution.py:172
  93.2 3.4 %copy-start.7 = (bf16[32,1024,128]{2,1,0:T(8,128)(2,1)S(1)}, bf16[32,1024,128]{2,1,0:T(8,128)(2,1)}, u32[]{:S(2)}) copy-start(bf16[32,1024,128]{2,1,0:T(8,128)(2,1)} %copy-done) | copy-start | bytes 25165828
  98.8 13.2 %collective-permute-start.27 = (bf16[32,4096]{1,0:T(8,128)(2,1)S(1)}, bf16[32,4096]{1,0:T(8,128)(2,1)S(1)}, u32[]{:S(2)}, u32[]{:S(2)}) collective-permute-start(bf16[32,4096]{1,0:T(8,128)(2,1)S(1)} %get-tuple-element.93.after.refs_6_), channel_id=1, source_target_pairs={{0,4},{4,8},{8,12},{12,16},{16,20},{20,24},{24,28},{28,0},{1,5},{5... | collective-permute-start | bytes 786440 | tf_op jit(solution)/shard_map/ppermute | solution.py:172
  100.2 1.3 collective-permute-start.24
  100.3 3.7 %collective-permute-start.25 = (bf16[32,512]{1,0:T(8,128)(2,1)S(1)}, bf16[32,512]{1,0:T(8,128)(2,1)S(1)}, u32[]{:S(2)}, u32[]{:S(2)}) collective-permute-start(bf16[32,512]{1,0:T(8,128)(2,1)S(1)} %get-tuple-element.95), channel_id=1, source_target_pairs={{0,3},{1,0},{2,1},{3,2},{4,7},{5,4},{6,5},{7,6},{8,11},{9,8},{10,9... | collective-permute-start | bytes 98312 | tf_op jit(solution)/shard_map/ppermute | solution.py:172
  104.0 3.4 %copy-start.8 = (bf16[32,1024,128]{2,1,0:T(8,128)(2,1)S(1)}, bf16[32,1024,128]{2,1,0:T(8,128)(2,1)}, u32[]{:S(2)}) copy-start(bf16[32,1024,128]{2,1,0:T(8,128)(2,1)} %copy-done) | copy-start | bytes 25165828
  109.6 2.4 %copy-start.31 = (bf16[32,4096]{1,0:T(8,128)(2,1)}, bf16[32,4096]{1,0:T(8,128)(2,1)S(1)}, u32[]{:S(2)}) copy-start(bf16[32,4096]{1,0:T(8,128)(2,1)S(1)} %get-tuple-element.97.after.refs_6_) | copy-start | bytes 786436
  109.6 12.4 %collective-permute-start.26 = (bf16[32,4096]{1,0:T(8,128)(2,1)S(1)}, bf16[32,4096]{1,0:T(8,128)(2,1)S(1)}, u32[]{:S(2)}, u32[]{:S(2)}) collective-permute-start(bf16[32,4096]{1,0:T(8,128)(2,1)S(1)} %get-tuple-element.97.after.refs_6_), channel_id=1, source_target_pairs={{0,4},{4,8},{8,12},{12,16},{16,20},{20,24},{24,28},{28,0},{1,5},{5... | collective-permute-start | bytes 786440 | tf_op jit(solution)/shard_map/ppermute | solution.py:172
  112.0 1.3 collective-permute-start.28
  112.1 3.7 %collective-permute-start.29 = (bf16[32,512]{1,0:T(8,128)(2,1)S(1)}, bf16[32,512]{1,0:T(8,128)(2,1)S(1)}, u32[]{:S(2)}, u32[]{:S(2)}) collective-permute-start(bf16[32,512]{1,0:T(8,128)(2,1)S(1)} %get-tuple-element.99), channel_id=1, source_target_pairs={{0,3},{1,0},{2,1},{3,2},{4,7},{5,4},{6,5},{7,6},{8,11},{9,8},{10,9... | collective-permute-start | bytes 98312 | tf_op jit(solution)/shard_map/ppermute | solution.py:172
  115.8 3.4 %copy-start.9 = (bf16[32,1024,128]{2,1,0:T(8,128)(2,1)S(1)}, bf16[32,1024,128]{2,1,0:T(8,128)(2,1)}, u32[]{:S(2)}) copy-start(bf16[32,1024,128]{2,1,0:T(8,128)(2,1)} %copy-done) | copy-start | bytes 25165828
  121.4 11.4 %collective-permute-start.33 = (bf16[32,4096]{1,0:T(8,128)(2,1)S(1)}, bf16[32,4096]{1,0:T(8,128)(2,1)S(1)}, u32[]{:S(2)}, u32[]{:S(2)}) collective-permute-start(bf16[32,4096]{1,0:T(8,128)(2,1)S(1)} %get-tuple-element.101.after.refs_6_), channel_id=1, source_target_pairs={{0,4},{4,8},{8,12},{12,16},{16,20},{20,24},{24,28},{28,0},{1,5},{5... | collective-permute-start | bytes 786440 | tf_op jit(solution)/shard_map/ppermute | solution.py:172
  122.1 1.2 collective-permute-start.30
  122.1 3.7 %collective-permute-start.31 = (bf16[32,512]{1,0:T(8,128)(2,1)S(1)}, bf16[32,512]{1,0:T(8,128)(2,1)S(1)}, u32[]{:S(2)}, u32[]{:S(2)}) collective-permute-start(bf16[32,512]{1,0:T(8,128)(2,1)S(1)} %get-tuple-element.103), channel_id=1, source_target_pairs={{0,3},{1,0},{2,1},{3,2},{4,7},{5,4},{6,5},{7,6},{8,11},{9,8},{10,9... | collective-permute-start | bytes 98312 | tf_op jit(solution)/shard_map/ppermute | solution.py:172
  125.8 3.4 %copy-start.10 = (bf16[32,1024,128]{2,1,0:T(8,128)(2,1)S(1)}, bf16[32,1024,128]{2,1,0:T(8,128)(2,1)}, u32[]{:S(2)}) copy-start(bf16[32,1024,128]{2,1,0:T(8,128)(2,1)} %copy-done) | copy-start | bytes 25165828
  131.4 12.2 %collective-permute-start.32 = (bf16[32,4096]{1,0:T(8,128)(2,1)S(1)}, bf16[32,4096]{1,0:T(8,128)(2,1)S(1)}, u32[]{:S(2)}, u32[]{:S(2)}) collective-permute-start(bf16[32,4096]{1,0:T(8,128)(2,1)S(1)} %get-tuple-element.105.after.refs_6_), channel_id=1, source_target_pairs={{0,4},{4,8},{8,12},{12,16},{16,20},{20,24},{24,28},{28,0},{1,5},{5... | collective-permute-start | bytes 786440 | tf_op jit(solution)/shard_map/ppermute | solution.py:172
  132.9 1.3 collective-permute-start.34
  132.9 3.7 %collective-permute-start.35 = (bf16[32,512]{1,0:T(8,128)(2,1)S(1)}, bf16[32,512]{1,0:T(8,128)(2,1)S(1)}, u32[]{:S(2)}, u32[]{:S(2)}) collective-permute-start(bf16[32,512]{1,0:T(8,128)(2,1)S(1)} %get-tuple-element.107), channel_id=1, source_target_pairs={{0,3},{1,0},{2,1},{3,2},{4,7},{5,4},{6,5},{7,6},{8,11},{9,8},{10,9... | collective-permute-start | bytes 98312 | tf_op jit(solution)/shard_map/ppermute | solution.py:172
  136.6 3.4 %copy-start.11 = (bf16[32,1024,128]{2,1,0:T(8,128)(2,1)S(1)}, bf16[32,1024,128]{2,1,0:T(8,128)(2,1)}, u32[]{:S(2)}) copy-start(bf16[32,1024,128]{2,1,0:T(8,128)(2,1)} %copy-done) | copy-start | bytes 25165828
  142.3 11.5 %collective-permute-start.39 = (bf16[32,4096]{1,0:T(8,128)(2,1)S(1)}, bf16[32,4096]{1,0:T(8,128)(2,1)S(1)}, u32[]{:S(2)}, u32[]{:S(2)}) collective-permute-start(bf16[32,4096]{1,0:T(8,128)(2,1)S(1)} %get-tuple-element.109.after.refs_6_), channel_id=1, source_target_pairs={{0,4},{4,8},{8,12},{12,16},{16,20},{20,24},{24,28},{28,0},{1,5},{5... | collective-permute-start | bytes 786440 | tf_op jit(solution)/shard_map/ppermute | solution.py:172
  143.7 1.3 collective-permute-start.36
  143.8 3.7 %collective-permute-start.37 = (bf16[32,512]{1,0:T(8,128)(2,1)S(1)}, bf16[32,512]{1,0:T(8,128)(2,1)S(1)}, u32[]{:S(2)}, u32[]{:S(2)}) collective-permute-start(bf16[32,512]{1,0:T(8,128)(2,1)S(1)} %get-tuple-element.111), channel_id=1, source_target_pairs={{0,3},{1,0},{2,1},{3,2},{4,7},{5,4},{6,5},{7,6},{8,11},{9,8},{10,9... | collective-permute-start | bytes 98312 | tf_op jit(solution)/shard_map/ppermute | solution.py:172
  147.4 3.4 %copy-start.12 = (bf16[32,1024,128]{2,1,0:T(8,128)(2,1)S(1)}, bf16[32,1024,128]{2,1,0:T(8,128)(2,1)}, u32[]{:S(2)}) copy-start(bf16[32,1024,128]{2,1,0:T(8,128)(2,1)} %copy-done) | copy-start | bytes 25165828
  153.1 10.3 %collective-permute-start.38 = (bf16[32,4096]{1,0:T(8,128)(2,1)S(1)}, bf16[32,4096]{1,0:T(8,128)(2,1)S(1)}, u32[]{:S(2)}, u32[]{:S(2)}) collective-permute-start(bf16[32,4096]{1,0:T(8,128)(2,1)S(1)} %get-tuple-element.113.after.refs_6_), channel_id=1, source_target_pairs={{0,4},{4,8},{8,12},{12,16},{16,20},{20,24},{24,28},{28,0},{1,5},{5... | collective-permute-start | bytes 786440 | tf_op jit(solution)/shard_map/ppermute | solution.py:172
  153.8 1.2 collective-permute-start.40
  154.0 3.7 %collective-permute-start.41 = (bf16[32,512]{1,0:T(8,128)(2,1)S(1)}, bf16[32,512]{1,0:T(8,128)(2,1)S(1)}, u32[]{:S(2)}, u32[]{:S(2)}) collective-permute-start(bf16[32,512]{1,0:T(8,128)(2,1)S(1)} %get-tuple-element.115), channel_id=1, source_target_pairs={{0,3},{1,0},{2,1},{3,2},{4,7},{5,4},{6,5},{7,6},{8,11},{9,8},{10,9... | collective-permute-start | bytes 98312 | tf_op jit(solution)/shard_map/ppermute | solution.py:172
  157.7 3.4 %copy-start.13 = (bf16[32,1024,128]{2,1,0:T(8,128)(2,1)S(1)}, bf16[32,1024,128]{2,1,0:T(8,128)(2,1)}, u32[]{:S(2)}) copy-start(bf16[32,1024,128]{2,1,0:T(8,128)(2,1)} %copy-done) | copy-start | bytes 25165828
  163.4 2.3 %collective-permute-start.42 = (bf16[32,512]{1,0:T(8,128)(2,1)S(1)}, bf16[32,512]{1,0:T(8,128)(2,1)S(1)}, u32[]{:S(2)}, u32[]{:S(2)}) collective-permute-start(bf16[32,512]{1,0:T(8,128)(2,1)S(1)} %get-tuple-element.117), channel_id=1, source_target_pairs={{0,1},{1,2},{2,3},{3,0},{4,5},{5,6},{6,7},{7,4},{8,9},{9,10},{10,1... | collective-permute-start | bytes 98312 | tf_op jit(solution)/shard_map/ppermute | solution.py:172
  164.7 3.3 %collective-permute-start.43 = (bf16[32,512]{1,0:T(8,128)(2,1)S(1)}, bf16[32,512]{1,0:T(8,128)(2,1)S(1)}, u32[]{:S(2)}, u32[]{:S(2)}) collective-permute-start(bf16[32,512]{1,0:T(8,128)(2,1)S(1)} %get-tuple-element.118), channel_id=1, source_target_pairs={{0,3},{1,0},{2,1},{3,2},{4,7},{5,4},{6,5},{7,6},{8,11},{9,8},{10,9... | collective-permute-start | bytes 98312 | tf_op jit(solution)/shard_map/ppermute | solution.py:172
  168.0 3.4 %copy-start.14 = (bf16[32,1024,128]{2,1,0:T(8,128)(2,1)S(1)}, bf16[32,1024,128]{2,1,0:T(8,128)(2,1)}, u32[]{:S(2)}) copy-start(bf16[32,1024,128]{2,1,0:T(8,128)(2,1)} %copy-done) | copy-start | bytes 25165828
  (21 other events, 21.0 us)

commit v3 on v2

--- a/solution.py
+++ b/solution.py
@@ -155,6 +155,7 @@
         out_shape=(aval, aval),
         in_specs=[VMEM, ANY],
         out_specs=(VMEM, VMEM),
+        compiler_params=pltpu.CompilerParams(vmem_limit_bytes=1024 * 1024),
         name="edges",
     )(pltpu.with_memory_space_constraint(main, pltpu.VMEM), after)
 

time: 175 us -> 131 us (0.75); the launches traced: 173 us -> 131 us
  local copies, waits for them, and re-layouts: 61.6 us -> 3.24 us
  waiting for transfers between devices: 50.4 us -> 70.4 us
  starting transfers between devices: 33.8 us -> 30.2 us
    unnamed x82 -> x2, local copies, waits for them, and re-layouts: 60.5 us -> 2.19 us
    ppermute x44, waiting for transfers between devices: 50.4 us -> 70.4 us  [cycle(): lax.ppermute(values, axis, [(i, (i + shift) % count) for i in range(count)])]
    ppermute x44, starting transfers between devices: 33.8 us -> 30.2 us  [cycle(): lax.ppermute(values, axis, [(i, (i + shift) % count) for i in range(count)])]
  transfers between devices with their start and end apart: 44 -> 44, of which waited for: 29 -> 38; matrix products, arithmetic and copies ran while one was open for 1% -> 1% of each run, Pallas kernels for 13% -> 17%
where the time goes in v3:
time: 131 us
  waiting for transfers between devices  70.4 us (54%)
  starting transfers between devices  30.2 us (23%)
  Pallas kernels  26 us (20%)
  local copies, waits for them, and re-layouts  3.24 us (2%)
    ppermute x44, waiting for transfers between devices, cycle(): lax.ppermute(values, axis, [(i, (i + shift) % count) for i in range(count)])  70.4 us
    ppermute x44, starting transfers between devices, cycle(): lax.ppermute(values, axis, [(i, (i + shift) % count) for i in range(count)])  30.2 us
    pallas_call x16, Pallas kernels, apply_layer(): pl.pallas_call(body, out_shape=tuple(out_shape), in_specs=specs, out_spec...  22.3 us
    pallas_call x1, Pallas kernels, load(): pl.pallas_call(load_kernel, out_shape=tuple((pltpu.VMEM(a.shape, a.dtype)...  3.61 us
  transfers between devices with their start and end apart: 44, of which 38 were waited for; matrix products, arithmetic and copies ran while one was open for 1% of the time, Pallas kernels for 17%

profile of v3, /device:TPU:1, one launch (start us, length us, event | category | flops | bytes accessed | tf_op | source)
XLA Modules:
  0.0 131.1 jit_solution(13566981012655337306)
XLA Ops:
  0.9 2.7 %collective-permute-start = (bf16[64,512]{1,0:T(8,128)(2,1)S(1)}, bf16[64,512]{1,0:T(8,128)(2,1)S(1)}, u32[]{:S(2)}, u32[]{:S(2)}) collective-permute-start(bf16[64,512]{1,0:T(8,128)(2,1)S(1)} %get-tuple-element.120), channel_id=1, source_target_pairs={{0,1},{1,2},{2,3},{3,0},{4,5},{5,6},{6,7},{7,4},{8,9},{9,10},{10,1... | collective-permute-start | bytes 196616 | tf_op jit(solution)/shard_map/ppermute | solution.py:173
  4.4 3.6 %load.1 = (bf16[64,4096]{1,0:T(8,128)(2,1)S(1)}, bf16[32,1024,128]{2,1,0:T(8,128)(2,1)S(1)}, f32[1,4096]{1,0:T(1,128)S(1)}) custom-call(bf16[64,4096]{1,0:T(8,128)(2,1)} %state.1, bf16[32,1024,128]{2,1,0:T(8,128)(2,1)} %bitcast.2, f32[1,4096]{1,0:T(1,128)} %bias.1), custom_call_target="tpu_custom_call" | custom-call | bytes 8388608 | tf_op jit(solution)/shard_map/load/pallas_call | solution.py:31
  8.1 2.1 %layer_t0_r0.1.refs_6_ = bf16[32,4096]{1,0:T(8,128)(2,1)S(1)} custom-call(s32[257]{0:T(512)S(1)} %pad_add_fusion.refs_0_, bf16[64,4096]{1,0:T(8,128)(2,1)S(1)} %get-tuple-element.62.refs_1_, bf16[64,512]{1,0:T(8,128)(2,1)S(1)} %collective-permute-done.refs_2_, bf16[64,512]{1,0:T(8,128)(2,1)S(1)} %collective-permute-done.1.refs_3_, ...), custom_call_target="tpu_custom_call" | custom-call | flops 268435456 | bytes 8388608 | tf_op jit(solution)/shard_map/layer_t0_r0/pallas_call | solution.py:129
  10.1 1.3 collective-permute-start.3
  11.4 2.1 %layer_t0_r32.1 = (bf16[8,64,4096]{2,1,0:T(8,128)(2,1)}, bf16[32,4096]{1,0:T(8,128)(2,1)S(1)}) custom-call(s32[257]{0:T(512)S(1)} %pad_add_fusion.refs_0_, bf16[64,4096]{1,0:T(8,128)(2,1)S(1)} %get-tuple-element.62.refs_1_, bf16[64,512]{1,0:T(8,128)(2,1)S(1)} %collective-permute-done.refs_2_, bf16[64,512]{1,0:T(8,128)(2,1)S(1)} %collective-permute-done.1.refs_3_, ...), custom_call_target="tpu_custom_call" | custom-call | flops 268435456 | bytes 8388608 | tf_op jit(solution)/shard_map/layer_t0_r32/pallas_call | solution.py:129
  13.5 1.3 collective-permute-start.2
  14.8 5.8 %collective-permute-done.3.main.refs_1_ = bf16[32,4096]{1,0:T(8,128)(2,1)S(1)} collective-permute-done((bf16[32,4096]{1,0:T(8,128)(2,1)S(1)}, bf16[32,4096]{1,0:T(8,128)(2,1)S(1)}, u32[]{:S(2)}, u32[]{:S(2)}) %collective-permute-start.3) | collective-permute-done | bytes 262176 | tf_op jit(solution)/shard_map/ppermute | solution.py:173
  20.6 3.4 %collective-permute-start.4 = (bf16[32,512]{1,0:T(8,128)(2,1)S(1)}, bf16[32,512]{1,0:T(8,128)(2,1)S(1)}, u32[]{:S(2)}, u32[]{:S(2)}) collective-permute-start(bf16[32,512]{1,0:T(8,128)(2,1)S(1)} %get-tuple-element.66), channel_id=1, source_target_pairs={{0,1},{1,2},{2,3},{3,0},{4,5},{5,6},{6,7},{7,4},{8,9},{9,10},{10,1... | collective-permute-start | bytes 98312 | tf_op jit(solution)/shard_map/ppermute | solution.py:173
  23.9 1.0 collective-permute-done.4.refs_2_
  25.0 2.3 %collective-permute-done.5.refs_3_ = bf16[32,512]{1,0:T(8,128)(2,1)S(1)} collective-permute-done((bf16[32,512]{1,0:T(8,128)(2,1)S(1)}, bf16[32,512]{1,0:T(8,128)(2,1)S(1)}, u32[]{:S(2)}, u32[]{:S(2)}) %collective-permute-start.5) | collective-permute-done | bytes 32800 | tf_op jit(solution)/shard_map/ppermute | solution.py:173
  27.3 1.3 layer_t1_r0.1
  29.9 2.2 %collective-permute-done.7.refs_3_ = bf16[32,512]{1,0:T(8,128)(2,1)S(1)} collective-permute-done((bf16[32,512]{1,0:T(8,128)(2,1)S(1)}, bf16[32,512]{1,0:T(8,128)(2,1)S(1)}, u32[]{:S(2)}, u32[]{:S(2)}) %collective-permute-start.7) | collective-permute-done | bytes 32800 | tf_op jit(solution)/shard_map/ppermute | solution.py:173
  32.1 1.3 layer_t1_r32.1
  33.4 2.8 %collective-permute-start.8 = (bf16[32,4096]{1,0:T(8,128)(2,1)S(1)}, bf16[32,4096]{1,0:T(8,128)(2,1)S(1)}, u32[]{:S(2)}, u32[]{:S(2)}) collective-permute-start(bf16[32,4096]{1,0:T(8,128)(2,1)S(1)} %get-tuple-element.73.after.refs_6_), channel_id=1, source_target_pairs={{0,4},{4,8},{8,12},{12,16},{16,20},{20,24},{24,28},{28,0},{1,5},{5... | collective-permute-start | bytes 786440 | tf_op jit(solution)/shard_map/ppermute | solution.py:173
  36.1 2.3 %collective-permute-done.9.main.refs_1_ = bf16[32,4096]{1,0:T(8,128)(2,1)S(1)} collective-permute-done((bf16[32,4096]{1,0:T(8,128)(2,1)S(1)}, bf16[32,4096]{1,0:T(8,128)(2,1)S(1)}, u32[]{:S(2)}, u32[]{:S(2)}) %collective-permute-start.9) | collective-permute-done | bytes 262176 | tf_op jit(solution)/shard_map/ppermute | solution.py:173
  38.4 1.5 %collective-permute-start.10 = (bf16[32,512]{1,0:T(8,128)(2,1)S(1)}, bf16[32,512]{1,0:T(8,128)(2,1)S(1)}, u32[]{:S(2)}, u32[]{:S(2)}) collective-permute-start(bf16[32,512]{1,0:T(8,128)(2,1)S(1)} %get-tuple-element.74), channel_id=1, source_target_pairs={{0,1},{1,2},{2,3},{3,0},{4,5},{5,6},{6,7},{7,4},{8,9},{9,10},{10,1... | collective-permute-start | bytes 98312 | tf_op jit(solution)/shard_map/ppermute | solution.py:173
  39.9 1.0 collective-permute-done.10.refs_2_
  40.9 2.3 %collective-permute-done.11.refs_3_ = bf16[32,512]{1,0:T(8,128)(2,1)S(1)} collective-permute-done((bf16[32,512]{1,0:T(8,128)(2,1)S(1)}, bf16[32,512]{1,0:T(8,128)(2,1)S(1)}, u32[]{:S(2)}, u32[]{:S(2)}) %collective-permute-start.11) | collective-permute-done | bytes 32800 | tf_op jit(solution)/shard_map/ppermute | solution.py:173
  43.2 1.3 layer_t2_r0.1
  44.6 1.4 %collective-permute-start.12 = (bf16[32,512]{1,0:T(8,128)(2,1)S(1)}, bf16[32,512]{1,0:T(8,128)(2,1)S(1)}, u32[]{:S(2)}, u32[]{:S(2)}) collective-permute-start(bf16[32,512]{1,0:T(8,128)(2,1)S(1)} %get-tuple-element.78), channel_id=1, source_target_pairs={{0,1},{1,2},{2,3},{3,0},{4,5},{5,6},{6,7},{7,4},{8,9},{9,10},{10,1... | collective-permute-start | bytes 98312 | tf_op jit(solution)/shard_map/ppermute | solution.py:173
  46.0 1.0 collective-permute-done.12.refs_2_
  47.0 2.6 %collective-permute-done.13.refs_3_ = bf16[32,512]{1,0:T(8,128)(2,1)S(1)} collective-permute-done((bf16[32,512]{1,0:T(8,128)(2,1)S(1)}, bf16[32,512]{1,0:T(8,128)(2,1)S(1)}, u32[]{:S(2)}, u32[]{:S(2)}) %collective-permute-start.13) | collective-permute-done | bytes 32800 | tf_op jit(solution)/shard_map/ppermute | solution.py:173
  49.6 1.3 layer_t2_r32.1
  51.0 3.1 %collective-permute-done.15.main.refs_1_ = bf16[32,4096]{1,0:T(8,128)(2,1)S(1)} collective-permute-done((bf16[32,4096]{1,0:T(8,128)(2,1)S(1)}, bf16[32,4096]{1,0:T(8,128)(2,1)S(1)}, u32[]{:S(2)}, u32[]{:S(2)}) %collective-permute-start.15) | collective-permute-done | bytes 262176 | tf_op jit(solution)/shard_map/ppermute | solution.py:173
  54.1 1.9 %collective-permute-start.16 = (bf16[32,512]{1,0:T(8,128)(2,1)S(1)}, bf16[32,512]{1,0:T(8,128)(2,1)S(1)}, u32[]{:S(2)}, u32[]{:S(2)}) collective-permute-start(bf16[32,512]{1,0:T(8,128)(2,1)S(1)} %get-tuple-element.82), channel_id=1, source_target_pairs={{0,1},{1,2},{2,3},{3,0},{4,5},{5,6},{6,7},{7,4},{8,9},{9,10},{10,1... | collective-permute-start | bytes 98312 | tf_op jit(solution)/shard_map/ppermute | solution.py:173
  55.9 1.0 collective-permute-done.16.refs_2_
  57.0 2.3 %collective-permute-done.17.refs_3_ = bf16[32,512]{1,0:T(8,128)(2,1)S(1)} collective-permute-done((bf16[32,512]{1,0:T(8,128)(2,1)S(1)}, bf16[32,512]{1,0:T(8,128)(2,1)S(1)}, u32[]{:S(2)}, u32[]{:S(2)}) %collective-permute-start.17) | collective-permute-done | bytes 32800 | tf_op jit(solution)/shard_map/ppermute | solution.py:173
  59.3 1.3 layer_t3_r0.1
  60.7 1.2 collective-permute-start.18
  62.9 2.6 %collective-permute-done.19.refs_3_ = bf16[32,512]{1,0:T(8,128)(2,1)S(1)} collective-permute-done((bf16[32,512]{1,0:T(8,128)(2,1)S(1)}, bf16[32,512]{1,0:T(8,128)(2,1)S(1)}, u32[]{:S(2)}, u32[]{:S(2)}) %collective-permute-start.19) | collective-permute-done | bytes 32800 | tf_op jit(solution)/shard_map/ppermute | solution.py:173
  65.5 1.3 layer_t3_r32.1
  66.9 2.8 %collective-permute-done.21.main.refs_1_ = bf16[32,4096]{1,0:T(8,128)(2,1)S(1)} collective-permute-done((bf16[32,4096]{1,0:T(8,128)(2,1)S(1)}, bf16[32,4096]{1,0:T(8,128)(2,1)S(1)}, u32[]{:S(2)}, u32[]{:S(2)}) %collective-permute-start.21) | collective-permute-done | bytes 262176 | tf_op jit(solution)/shard_map/ppermute | solution.py:173
  69.7 1.9 %collective-permute-start.22 = (bf16[32,512]{1,0:T(8,128)(2,1)S(1)}, bf16[32,512]{1,0:T(8,128)(2,1)S(1)}, u32[]{:S(2)}, u32[]{:S(2)}) collective-permute-start(bf16[32,512]{1,0:T(8,128)(2,1)S(1)} %get-tuple-element.90), channel_id=1, source_target_pairs={{0,1},{1,2},{2,3},{3,0},{4,5},{5,6},{6,7},{7,4},{8,9},{9,10},{10,1... | collective-permute-start | bytes 98312 | tf_op jit(solution)/shard_map/ppermute | solution.py:173
  71.6 1.0 collective-permute-done.22.refs_2_
  72.6 2.3 %collective-permute-done.23.refs_3_ = bf16[32,512]{1,0:T(8,128)(2,1)S(1)} collective-permute-done((bf16[32,512]{1,0:T(8,128)(2,1)S(1)}, bf16[32,512]{1,0:T(8,128)(2,1)S(1)}, u32[]{:S(2)}, u32[]{:S(2)}) %collective-permute-start.23) | collective-permute-done | bytes 32800 | tf_op jit(solution)/shard_map/ppermute | solution.py:173
  74.9 1.3 layer_t4_r0.1
  76.3 1.9 %collective-permute-start.24 = (bf16[32,512]{1,0:T(8,128)(2,1)S(1)}, bf16[32,512]{1,0:T(8,128)(2,1)S(1)}, u32[]{:S(2)}, u32[]{:S(2)}) collective-permute-start(bf16[32,512]{1,0:T(8,128)(2,1)S(1)} %get-tuple-element.94), channel_id=1, source_target_pairs={{0,1},{1,2},{2,3},{3,0},{4,5},{5,6},{6,7},{7,4},{8,9},{9,10},{10,1... | collective-permute-start | bytes 98312 | tf_op jit(solution)/shard_map/ppermute | solution.py:173
  78.1 1.2 collective-permute-done.24.refs_2_
  79.3 2.5 %collective-permute-done.25.refs_3_ = bf16[32,512]{1,0:T(8,128)(2,1)S(1)} collective-permute-done((bf16[32,512]{1,0:T(8,128)(2,1)S(1)}, bf16[32,512]{1,0:T(8,128)(2,1)S(1)}, u32[]{:S(2)}, u32[]{:S(2)}) %collective-permute-start.25) | collective-permute-done | bytes 32800 | tf_op jit(solution)/shard_map/ppermute | solution.py:173
  81.8 1.3 layer_t4_r32.1
  83.1 2.2 %collective-permute-done.27.main.refs_1_ = bf16[32,4096]{1,0:T(8,128)(2,1)S(1)} collective-permute-done((bf16[32,4096]{1,0:T(8,128)(2,1)S(1)}, bf16[32,4096]{1,0:T(8,128)(2,1)S(1)}, u32[]{:S(2)}, u32[]{:S(2)}) %collective-permute-start.27) | collective-permute-done | bytes 262176 | tf_op jit(solution)/shard_map/ppermute | solution.py:173
  85.3 1.2 collective-permute-start.28
  87.5 2.6 %collective-permute-done.29.refs_3_ = bf16[32,512]{1,0:T(8,128)(2,1)S(1)} collective-permute-done((bf16[32,512]{1,0:T(8,128)(2,1)S(1)}, bf16[32,512]{1,0:T(8,128)(2,1)S(1)}, u32[]{:S(2)}, u32[]{:S(2)}) %collective-permute-start.29) | collective-permute-done | bytes 32800 | tf_op jit(solution)/shard_map/ppermute | solution.py:173
  90.2 1.3 layer_t5_r0.1
  92.3 1.9 %collective-permute-start.30 = (bf16[32,512]{1,0:T(8,128)(2,1)S(1)}, bf16[32,512]{1,0:T(8,128)(2,1)S(1)}, u32[]{:S(2)}, u32[]{:S(2)}) collective-permute-start(bf16[32,512]{1,0:T(8,128)(2,1)S(1)} %get-tuple-element.102), channel_id=1, source_target_pairs={{0,1},{1,2},{2,3},{3,0},{4,5},{5,6},{6,7},{7,4},{8,9},{9,10},{10,1... | collective-permute-start | bytes 98312 | tf_op jit(solution)/shard_map/ppermute | solution.py:173
  95.2 2.6 %collective-permute-done.31.refs_3_ = bf16[32,512]{1,0:T(8,128)(2,1)S(1)} collective-permute-done((bf16[32,512]{1,0:T(8,128)(2,1)S(1)}, bf16[32,512]{1,0:T(8,128)(2,1)S(1)}, u32[]{:S(2)}, u32[]{:S(2)}) %collective-permute-start.31) | collective-permute-done | bytes 32800 | tf_op jit(solution)/shard_map/ppermute | solution.py:173
  97.8 1.3 layer_t5_r32.1
  99.1 1.1 collective-permute-done.33.main.refs_1_
  100.3 1.6 %collective-permute-start.34 = (bf16[32,512]{1,0:T(8,128)(2,1)S(1)}, bf16[32,512]{1,0:T(8,128)(2,1)S(1)}, u32[]{:S(2)}, u32[]{:S(2)}) collective-permute-start(bf16[32,512]{1,0:T(8,128)(2,1)S(1)} %get-tuple-element.106), channel_id=1, source_target_pairs={{0,1},{1,2},{2,3},{3,0},{4,5},{5,6},{6,7},{7,4},{8,9},{9,10},{10,1... | collective-permute-start | bytes 98312 | tf_op jit(solution)/shard_map/ppermute | solution.py:173
  102.9 2.6 %collective-permute-done.35.refs_3_ = bf16[32,512]{1,0:T(8,128)(2,1)S(1)} collective-permute-done((bf16[32,512]{1,0:T(8,128)(2,1)S(1)}, bf16[32,512]{1,0:T(8,128)(2,1)S(1)}, u32[]{:S(2)}, u32[]{:S(2)}) %collective-permute-start.35) | collective-permute-done | bytes 32800 | tf_op jit(solution)/shard_map/ppermute | solution.py:173
  105.5 1.3 layer_t6_r0.1
  106.9 1.0 collective-permute-done.32.main.refs_1_
  107.9 1.2 collective-permute-start.36
  110.1 2.6 %collective-permute-done.37.refs_3_ = bf16[32,512]{1,0:T(8,128)(2,1)S(1)} collective-permute-done((bf16[32,512]{1,0:T(8,128)(2,1)S(1)}, bf16[32,512]{1,0:T(8,128)(2,1)S(1)}, u32[]{:S(2)}, u32[]{:S(2)}) %collective-permute-start.37) | collective-permute-done | bytes 32800 | tf_op jit(solution)/shard_map/ppermute | solution.py:173
  112.7 1.3 layer_t6_r32.1
  114.1 1.5 %collective-permute-done.39.main.refs_1_ = bf16[32,4096]{1,0:T(8,128)(2,1)S(1)} collective-permute-done((bf16[32,4096]{1,0:T(8,128)(2,1)S(1)}, bf16[32,4096]{1,0:T(8,128)(2,1)S(1)}, u32[]{:S(2)}, u32[]{:S(2)}) %collective-permute-start.39) | collective-permute-done | bytes 262176 | tf_op jit(solution)/shard_map/ppermute | solution.py:173
  116.4 1.2 collective-permute-done.40.refs_2_
  117.6 2.4 %collective-permute-done.41.refs_3_ = bf16[32,512]{1,0:T(8,128)(2,1)S(1)} collective-permute-done((bf16[32,512]{1,0:T(8,128)(2,1)S(1)}, bf16[32,512]{1,0:T(8,128)(2,1)S(1)}, u32[]{:S(2)}, u32[]{:S(2)}) %collective-permute-start.41) | collective-permute-done | bytes 32800 | tf_op jit(solution)/shard_map/ppermute | solution.py:173
  120.1 1.5 %layer_t7_r0.1.after.refs_6_ = bf16[8,64,4096]{2,1,0:T(8,128)(2,1)} custom-call(s32[257]{0:T(512)S(1)} %pad_add_fusion.refs_0_, bf16[32,4096]{1,0:T(8,128)(2,1)S(1)} %collective-permute-done.39.main.refs_1_, bf16[32,512]{1,0:T(8,128)(2,1)S(1)} %collective-permute-done.40.refs_2_, ...), custom_call_target="tpu_custom_call", output_to_operand_aliasing={{}: (7, {})} | custom-call | flops 268435456 | bytes 8388608 | tf_op jit(solution)/shard_map/layer_t7_r0/pallas_call | solution.py:129
  121.6 1.2 collective-permute-done.38.main.refs_1_
  122.8 2.2 %copy-done = bf16[8,64,4096]{2,1,0:T(8,128)(2,1)S(1)} copy-done((bf16[8,64,4096]{2,1,0:T(8,128)(2,1)S(1)}, bf16[8,64,4096]{2,1,0:T(8,128)(2,1)}, u32[]{:S(2)}) %copy-start) | copy-done | bytes 4194328
  125.0 1.3 collective-permute-start.42
  127.3 2.3 %collective-permute-done.43.refs_3_ = bf16[32,512]{1,0:T(8,128)(2,1)S(1)} collective-permute-done((bf16[32,512]{1,0:T(8,128)(2,1)S(1)}, bf16[32,512]{1,0:T(8,128)(2,1)S(1)}, u32[]{:S(2)}, u32[]{:S(2)}) %collective-permute-start.43) | collective-permute-done | bytes 32800 | tf_op jit(solution)/shard_map/ppermute | solution.py:173
  129.6 1.3 layer_t7_r32.1
  (63 shorter events, 11.5 us)
Async XLA Ops:
  0.9 7.2 %collective-permute-start = (bf16[64,512]{1,0:T(8,128)(2,1)S(1)}, bf16[64,512]{1,0:T(8,128)(2,1)S(1)}, u32[]{:S(2)}, u32[]{:S(2)}) collective-permute-start(bf16[64,512]{1,0:T(8,128)(2,1)S(1)} %get-tuple-element.120), channel_id=1, source_target_pairs={{0,1},{1,2},{2,3},{3,0},{4,5},{5,6},{6,7},{7,4},{8,9},{9,10},{10,1... | collective-permute-start | bytes 196616 | tf_op jit(solution)/shard_map/ppermute | solution.py:173
  3.5 4.5 %collective-permute-start.1 = (bf16[64,512]{1,0:T(8,128)(2,1)S(1)}, bf16[64,512]{1,0:T(8,128)(2,1)S(1)}, u32[]{:S(2)}, u32[]{:S(2)}) collective-permute-start(bf16[64,512]{1,0:T(8,128)(2,1)S(1)} %get-tuple-element.119), channel_id=1, source_target_pairs={{0,3},{1,0},{2,1},{3,2},{4,7},{5,4},{6,5},{7,6},{8,11},{9,8},{10,9... | collective-permute-start | bytes 196616 | tf_op jit(solution)/shard_map/ppermute | solution.py:173
  10.1 10.4 %collective-permute-start.3 = (bf16[32,4096]{1,0:T(8,128)(2,1)S(1)}, bf16[32,4096]{1,0:T(8,128)(2,1)S(1)}, u32[]{:S(2)}, u32[]{:S(2)}) collective-permute-start(bf16[32,4096]{1,0:T(8,128)(2,1)S(1)} %layer_t0_r0.1.refs_6_), channel_id=1, source_target_pairs={{0,4},{4,8},{8,12},{12,16},{16,20},{20,24},{24,28},{28,0},{1,5},{5... | collective-permute-start | bytes 786440 | tf_op jit(solution)/shard_map/ppermute | solution.py:173
  13.5 15.1 %collective-permute-start.2 = (bf16[32,4096]{1,0:T(8,128)(2,1)S(1)}, bf16[32,4096]{1,0:T(8,128)(2,1)S(1)}, u32[]{:S(2)}, u32[]{:S(2)}) collective-permute-start(bf16[32,4096]{1,0:T(8,128)(2,1)S(1)} %get-tuple-element.65.after.refs_6_), channel_id=1, source_target_pairs={{0,4},{4,8},{8,12},{12,16},{16,20},{20,24},{24,28},{28,0},{1,5},{5... | collective-permute-start | bytes 786440 | tf_op jit(solution)/shard_map/ppermute | solution.py:173
  20.6 4.4 %collective-permute-start.4 = (bf16[32,512]{1,0:T(8,128)(2,1)S(1)}, bf16[32,512]{1,0:T(8,128)(2,1)S(1)}, u32[]{:S(2)}, u32[]{:S(2)}) collective-permute-start(bf16[32,512]{1,0:T(8,128)(2,1)S(1)} %get-tuple-element.66), channel_id=1, source_target_pairs={{0,1},{1,2},{2,3},{3,0},{4,5},{5,6},{6,7},{7,4},{8,9},{9,10},{10,1... | collective-permute-start | bytes 98312 | tf_op jit(solution)/shard_map/ppermute | solution.py:173
  23.9 3.3 %collective-permute-start.5 = (bf16[32,512]{1,0:T(8,128)(2,1)S(1)}, bf16[32,512]{1,0:T(8,128)(2,1)S(1)}, u32[]{:S(2)}, u32[]{:S(2)}) collective-permute-start(bf16[32,512]{1,0:T(8,128)(2,1)S(1)} %get-tuple-element.67), channel_id=1, source_target_pairs={{0,3},{1,0},{2,1},{3,2},{4,7},{5,4},{6,5},{7,6},{8,11},{9,8},{10,9... | collective-permute-start | bytes 98312 | tf_op jit(solution)/shard_map/ppermute | solution.py:173
  28.6 9.9 %collective-permute-start.9 = (bf16[32,4096]{1,0:T(8,128)(2,1)S(1)}, bf16[32,4096]{1,0:T(8,128)(2,1)S(1)}, u32[]{:S(2)}, u32[]{:S(2)}) collective-permute-start(bf16[32,4096]{1,0:T(8,128)(2,1)S(1)} %get-tuple-element.69.after.refs_6_), channel_id=1, source_target_pairs={{0,4},{4,8},{8,12},{12,16},{16,20},{20,24},{24,28},{28,0},{1,5},{5... | collective-permute-start | bytes 786440 | tf_op jit(solution)/shard_map/ppermute | solution.py:173
  28.6 1.3 collective-permute-start.6
  28.7 3.4 %collective-permute-start.7 = (bf16[32,512]{1,0:T(8,128)(2,1)S(1)}, bf16[32,512]{1,0:T(8,128)(2,1)S(1)}, u32[]{:S(2)}, u32[]{:S(2)}) collective-permute-start(bf16[32,512]{1,0:T(8,128)(2,1)S(1)} %get-tuple-element.71), channel_id=1, source_target_pairs={{0,3},{1,0},{2,1},{3,2},{4,7},{5,4},{6,5},{7,6},{8,11},{9,8},{10,9... | collective-permute-start | bytes 98312 | tf_op jit(solution)/shard_map/ppermute | solution.py:173
  33.4 11.2 %collective-permute-start.8 = (bf16[32,4096]{1,0:T(8,128)(2,1)S(1)}, bf16[32,4096]{1,0:T(8,128)(2,1)S(1)}, u32[]{:S(2)}, u32[]{:S(2)}) collective-permute-start(bf16[32,4096]{1,0:T(8,128)(2,1)S(1)} %get-tuple-element.73.after.refs_6_), channel_id=1, source_target_pairs={{0,4},{4,8},{8,12},{12,16},{16,20},{20,24},{24,28},{28,0},{1,5},{5... | collective-permute-start | bytes 786440 | tf_op jit(solution)/shard_map/ppermute | solution.py:173
  38.4 2.5 %collective-permute-start.10 = (bf16[32,512]{1,0:T(8,128)(2,1)S(1)}, bf16[32,512]{1,0:T(8,128)(2,1)S(1)}, u32[]{:S(2)}, u32[]{:S(2)}) collective-permute-start(bf16[32,512]{1,0:T(8,128)(2,1)S(1)} %get-tuple-element.74), channel_id=1, source_target_pairs={{0,1},{1,2},{2,3},{3,0},{4,5},{5,6},{6,7},{7,4},{8,9},{9,10},{10,1... | collective-permute-start | bytes 98312 | tf_op jit(solution)/shard_map/ppermute | solution.py:173
  39.9 3.3 %collective-permute-start.11 = (bf16[32,512]{1,0:T(8,128)(2,1)S(1)}, bf16[32,512]{1,0:T(8,128)(2,1)S(1)}, u32[]{:S(2)}, u32[]{:S(2)}) collective-permute-start(bf16[32,512]{1,0:T(8,128)(2,1)S(1)} %get-tuple-element.75), channel_id=1, source_target_pairs={{0,3},{1,0},{2,1},{3,2},{4,7},{5,4},{6,5},{7,6},{8,11},{9,8},{10,9... | collective-permute-start | bytes 98312 | tf_op jit(solution)/shard_map/ppermute | solution.py:173
  44.5 9.6 %collective-permute-start.15 = (bf16[32,4096]{1,0:T(8,128)(2,1)S(1)}, bf16[32,4096]{1,0:T(8,128)(2,1)S(1)}, u32[]{:S(2)}, u32[]{:S(2)}) collective-permute-start(bf16[32,4096]{1,0:T(8,128)(2,1)S(1)} %get-tuple-element.77.after.refs_6_), channel_id=1, source_target_pairs={{0,4},{4,8},{8,12},{12,16},{16,20},{20,24},{24,28},{28,0},{1,5},{5... | collective-permute-start | bytes 786440 | tf_op jit(solution)/shard_map/ppermute | solution.py:173
  44.6 2.4 %collective-permute-start.12 = (bf16[32,512]{1,0:T(8,128)(2,1)S(1)}, bf16[32,512]{1,0:T(8,128)(2,1)S(1)}, u32[]{:S(2)}, u32[]{:S(2)}) collective-permute-start(bf16[32,512]{1,0:T(8,128)(2,1)S(1)} %get-tuple-element.78), channel_id=1, source_target_pairs={{0,1},{1,2},{2,3},{3,0},{4,5},{5,6},{6,7},{7,4},{8,9},{9,10},{10,1... | collective-permute-start | bytes 98312 | tf_op jit(solution)/shard_map/ppermute | solution.py:173
  46.0 3.6 %collective-permute-start.13 = (bf16[32,512]{1,0:T(8,128)(2,1)S(1)}, bf16[32,512]{1,0:T(8,128)(2,1)S(1)}, u32[]{:S(2)}, u32[]{:S(2)}) collective-permute-start(bf16[32,512]{1,0:T(8,128)(2,1)S(1)} %get-tuple-element.79), channel_id=1, source_target_pairs={{0,3},{1,0},{2,1},{3,2},{4,7},{5,4},{6,5},{7,6},{8,11},{9,8},{10,9... | collective-permute-start | bytes 98312 | tf_op jit(solution)/shard_map/ppermute | solution.py:173
  50.9 9.7 %collective-permute-start.14 = (bf16[32,4096]{1,0:T(8,128)(2,1)S(1)}, bf16[32,4096]{1,0:T(8,128)(2,1)S(1)}, u32[]{:S(2)}, u32[]{:S(2)}) collective-permute-start(bf16[32,4096]{1,0:T(8,128)(2,1)S(1)} %get-tuple-element.81.after.refs_6_), channel_id=1, source_target_pairs={{0,4},{4,8},{8,12},{12,16},{16,20},{20,24},{24,28},{28,0},{1,5},{5... | collective-permute-start | bytes 786440 | tf_op jit(solution)/shard_map/ppermute | solution.py:173
  54.1 2.9 %collective-permute-start.16 = (bf16[32,512]{1,0:T(8,128)(2,1)S(1)}, bf16[32,512]{1,0:T(8,128)(2,1)S(1)}, u32[]{:S(2)}, u32[]{:S(2)}) collective-permute-start(bf16[32,512]{1,0:T(8,128)(2,1)S(1)} %get-tuple-element.82), channel_id=1, source_target_pairs={{0,1},{1,2},{2,3},{3,0},{4,5},{5,6},{6,7},{7,4},{8,9},{9,10},{10,1... | collective-permute-start | bytes 98312 | tf_op jit(solution)/shard_map/ppermute | solution.py:173
  55.9 3.3 %collective-permute-start.17 = (bf16[32,512]{1,0:T(8,128)(2,1)S(1)}, bf16[32,512]{1,0:T(8,128)(2,1)S(1)}, u32[]{:S(2)}, u32[]{:S(2)}) collective-permute-start(bf16[32,512]{1,0:T(8,128)(2,1)S(1)} %get-tuple-element.83), channel_id=1, source_target_pairs={{0,3},{1,0},{2,1},{3,2},{4,7},{5,4},{6,5},{7,6},{8,11},{9,8},{10,9... | collective-permute-start | bytes 98312 | tf_op jit(solution)/shard_map/ppermute | solution.py:173
  60.6 9.1 %collective-permute-start.21 = (bf16[32,4096]{1,0:T(8,128)(2,1)S(1)}, bf16[32,4096]{1,0:T(8,128)(2,1)S(1)}, u32[]{:S(2)}, u32[]{:S(2)}) collective-permute-start(bf16[32,4096]{1,0:T(8,128)(2,1)S(1)} %get-tuple-element.85.after.refs_6_), channel_id=1, source_target_pairs={{0,4},{4,8},{8,12},{12,16},{16,20},{20,24},{24,28},{28,0},{1,5},{5... | collective-permute-start | bytes 786440 | tf_op jit(solution)/shard_map/ppermute | solution.py:173
  60.7 2.2 %collective-permute-start.18 = (bf16[32,512]{1,0:T(8,128)(2,1)S(1)}, bf16[32,512]{1,0:T(8,128)(2,1)S(1)}, u32[]{:S(2)}, u32[]{:S(2)}) collective-permute-start(bf16[32,512]{1,0:T(8,128)(2,1)S(1)} %get-tuple-element.86), channel_id=1, source_target_pairs={{0,1},{1,2},{2,3},{3,0},{4,5},{5,6},{6,7},{7,4},{8,9},{9,10},{10,1... | collective-permute-start | bytes 98312 | tf_op jit(solution)/shard_map/ppermute | solution.py:173
  61.9 3.6 %collective-permute-start.19 = (bf16[32,512]{1,0:T(8,128)(2,1)S(1)}, bf16[32,512]{1,0:T(8,128)(2,1)S(1)}, u32[]{:S(2)}, u32[]{:S(2)}) collective-permute-start(bf16[32,512]{1,0:T(8,128)(2,1)S(1)} %get-tuple-element.87), channel_id=1, source_target_pairs={{0,3},{1,0},{2,1},{3,2},{4,7},{5,4},{6,5},{7,6},{8,11},{9,8},{10,9... | collective-permute-start | bytes 98312 | tf_op jit(solution)/shard_map/ppermute | solution.py:173
  66.8 9.5 %collective-permute-start.20 = (bf16[32,4096]{1,0:T(8,128)(2,1)S(1)}, bf16[32,4096]{1,0:T(8,128)(2,1)S(1)}, u32[]{:S(2)}, u32[]{:S(2)}) collective-permute-start(bf16[32,4096]{1,0:T(8,128)(2,1)S(1)} %get-tuple-element.89.after.refs_6_), channel_id=1, source_target_pairs={{0,4},{4,8},{8,12},{12,16},{16,20},{20,24},{24,28},{28,0},{1,5},{5... | collective-permute-start | bytes 786440 | tf_op jit(solution)/shard_map/ppermute | solution.py:173
  69.7 2.9 %collective-permute-start.22 = (bf16[32,512]{1,0:T(8,128)(2,1)S(1)}, bf16[32,512]{1,0:T(8,128)(2,1)S(1)}, u32[]{:S(2)}, u32[]{:S(2)}) collective-permute-start(bf16[32,512]{1,0:T(8,128)(2,1)S(1)} %get-tuple-element.90), channel_id=1, source_target_pairs={{0,1},{1,2},{2,3},{3,0},{4,5},{5,6},{6,7},{7,4},{8,9},{9,10},{10,1... | collective-permute-start | bytes 98312 | tf_op jit(solution)/shard_map/ppermute | solution.py:173
  71.6 3.3 %collective-permute-start.23 = (bf16[32,512]{1,0:T(8,128)(2,1)S(1)}, bf16[32,512]{1,0:T(8,128)(2,1)S(1)}, u32[]{:S(2)}, u32[]{:S(2)}) collective-permute-start(bf16[32,512]{1,0:T(8,128)(2,1)S(1)} %get-tuple-element.91), channel_id=1, source_target_pairs={{0,3},{1,0},{2,1},{3,2},{4,7},{5,4},{6,5},{7,6},{8,11},{9,8},{10,9... | collective-permute-start | bytes 98312 | tf_op jit(solution)/shard_map/ppermute | solution.py:173
  76.2 9.1 %collective-permute-start.27 = (bf16[32,4096]{1,0:T(8,128)(2,1)S(1)}, bf16[32,4096]{1,0:T(8,128)(2,1)S(1)}, u32[]{:S(2)}, u32[]{:S(2)}) collective-permute-start(bf16[32,4096]{1,0:T(8,128)(2,1)S(1)} %get-tuple-element.93.after.refs_6_), channel_id=1, source_target_pairs={{0,4},{4,8},{8,12},{12,16},{16,20},{20,24},{24,28},{28,0},{1,5},{5... | collective-permute-start | bytes 786440 | tf_op jit(solution)/shard_map/ppermute | solution.py:173
  76.3 3.0 %collective-permute-start.24 = (bf16[32,512]{1,0:T(8,128)(2,1)S(1)}, bf16[32,512]{1,0:T(8,128)(2,1)S(1)}, u32[]{:S(2)}, u32[]{:S(2)}) collective-permute-start(bf16[32,512]{1,0:T(8,128)(2,1)S(1)} %get-tuple-element.94), channel_id=1, source_target_pairs={{0,1},{1,2},{2,3},{3,0},{4,5},{5,6},{6,7},{7,4},{8,9},{9,10},{10,1... | collective-permute-start | bytes 98312 | tf_op jit(solution)/shard_map/ppermute | solution.py:173
  78.1 3.6 %collective-permute-start.25 = (bf16[32,512]{1,0:T(8,128)(2,1)S(1)}, bf16[32,512]{1,0:T(8,128)(2,1)S(1)}, u32[]{:S(2)}, u32[]{:S(2)}) collective-permute-start(bf16[32,512]{1,0:T(8,128)(2,1)S(1)} %get-tuple-element.95), channel_id=1, source_target_pairs={{0,3},{1,0},{2,1},{3,2},{4,7},{5,4},{6,5},{7,6},{8,11},{9,8},{10,9... | collective-permute-start | bytes 98312 | tf_op jit(solution)/shard_map/ppermute | solution.py:173
  83.0 9.2 %collective-permute-start.26 = (bf16[32,4096]{1,0:T(8,128)(2,1)S(1)}, bf16[32,4096]{1,0:T(8,128)(2,1)S(1)}, u32[]{:S(2)}, u32[]{:S(2)}) collective-permute-start(bf16[32,4096]{1,0:T(8,128)(2,1)S(1)} %get-tuple-element.97.after.refs_6_), channel_id=1, source_target_pairs={{0,4},{4,8},{8,12},{12,16},{16,20},{20,24},{24,28},{28,0},{1,5},{5... | collective-permute-start | bytes 786440 | tf_op jit(solution)/shard_map/ppermute | solution.py:173
  85.3 2.2 %collective-permute-start.28 = (bf16[32,512]{1,0:T(8,128)(2,1)S(1)}, bf16[32,512]{1,0:T(8,128)(2,1)S(1)}, u32[]{:S(2)}, u32[]{:S(2)}) collective-permute-start(bf16[32,512]{1,0:T(8,128)(2,1)S(1)} %get-tuple-element.98), channel_id=1, source_target_pairs={{0,1},{1,2},{2,3},{3,0},{4,5},{5,6},{6,7},{7,4},{8,9},{9,10},{10,1... | collective-permute-start | bytes 98312 | tf_op jit(solution)/shard_map/ppermute | solution.py:173
  86.5 3.6 %collective-permute-start.29 = (bf16[32,512]{1,0:T(8,128)(2,1)S(1)}, bf16[32,512]{1,0:T(8,128)(2,1)S(1)}, u32[]{:S(2)}, u32[]{:S(2)}) collective-permute-start(bf16[32,512]{1,0:T(8,128)(2,1)S(1)} %get-tuple-element.99), channel_id=1, source_target_pairs={{0,3},{1,0},{2,1},{3,2},{4,7},{5,4},{6,5},{7,6},{8,11},{9,8},{10,9... | collective-permute-start | bytes 98312 | tf_op jit(solution)/shard_map/ppermute | solution.py:173
  91.4 8.8 %collective-permute-start.33 = (bf16[32,4096]{1,0:T(8,128)(2,1)S(1)}, bf16[32,4096]{1,0:T(8,128)(2,1)S(1)}, u32[]{:S(2)}, u32[]{:S(2)}) collective-permute-start(bf16[32,4096]{1,0:T(8,128)(2,1)S(1)} %get-tuple-element.101.after.refs_6_), channel_id=1, source_target_pairs={{0,4},{4,8},{8,12},{12,16},{16,20},{20,24},{24,28},{28,0},{1,5},{5... | collective-permute-start | bytes 786440 | tf_op jit(solution)/shard_map/ppermute | solution.py:173
  92.3 2.9 %collective-permute-start.30 = (bf16[32,512]{1,0:T(8,128)(2,1)S(1)}, bf16[32,512]{1,0:T(8,128)(2,1)S(1)}, u32[]{:S(2)}, u32[]{:S(2)}) collective-permute-start(bf16[32,512]{1,0:T(8,128)(2,1)S(1)} %get-tuple-element.102), channel_id=1, source_target_pairs={{0,1},{1,2},{2,3},{3,0},{4,5},{5,6},{6,7},{7,4},{8,9},{9,10},{10,1... | collective-permute-start | bytes 98312 | tf_op jit(solution)/shard_map/ppermute | solution.py:173
  94.2 3.6 %collective-permute-start.31 = (bf16[32,512]{1,0:T(8,128)(2,1)S(1)}, bf16[32,512]{1,0:T(8,128)(2,1)S(1)}, u32[]{:S(2)}, u32[]{:S(2)}) collective-permute-start(bf16[32,512]{1,0:T(8,128)(2,1)S(1)} %get-tuple-element.103), channel_id=1, source_target_pairs={{0,3},{1,0},{2,1},{3,2},{4,7},{5,4},{6,5},{7,6},{8,11},{9,8},{10,9... | collective-permute-start | bytes 98312 | tf_op jit(solution)/shard_map/ppermute | solution.py:173
  99.1 8.8 %collective-permute-start.32 = (bf16[32,4096]{1,0:T(8,128)(2,1)S(1)}, bf16[32,4096]{1,0:T(8,128)(2,1)S(1)}, u32[]{:S(2)}, u32[]{:S(2)}) collective-permute-start(bf16[32,4096]{1,0:T(8,128)(2,1)S(1)} %get-tuple-element.105.after.refs_6_), channel_id=1, source_target_pairs={{0,4},{4,8},{8,12},{12,16},{16,20},{20,24},{24,28},{28,0},{1,5},{5... | collective-permute-start | bytes 786440 | tf_op jit(solution)/shard_map/ppermute | solution.py:173
  100.3 2.6 %collective-permute-start.34 = (bf16[32,512]{1,0:T(8,128)(2,1)S(1)}, bf16[32,512]{1,0:T(8,128)(2,1)S(1)}, u32[]{:S(2)}, u32[]{:S(2)}) collective-permute-start(bf16[32,512]{1,0:T(8,128)(2,1)S(1)} %get-tuple-element.106), channel_id=1, source_target_pairs={{0,1},{1,2},{2,3},{3,0},{4,5},{5,6},{6,7},{7,4},{8,9},{9,10},{10,1... | collective-permute-start | bytes 98312 | tf_op jit(solution)/shard_map/ppermute | solution.py:173
  101.9 3.6 %collective-permute-start.35 = (bf16[32,512]{1,0:T(8,128)(2,1)S(1)}, bf16[32,512]{1,0:T(8,128)(2,1)S(1)}, u32[]{:S(2)}, u32[]{:S(2)}) collective-permute-start(bf16[32,512]{1,0:T(8,128)(2,1)S(1)} %get-tuple-element.107), channel_id=1, source_target_pairs={{0,3},{1,0},{2,1},{3,2},{4,7},{5,4},{6,5},{7,6},{8,11},{9,8},{10,9... | collective-permute-start | bytes 98312 | tf_op jit(solution)/shard_map/ppermute | solution.py:173
  106.8 8.8 %collective-permute-start.39 = (bf16[32,4096]{1,0:T(8,128)(2,1)S(1)}, bf16[32,4096]{1,0:T(8,128)(2,1)S(1)}, u32[]{:S(2)}, u32[]{:S(2)}) collective-permute-start(bf16[32,4096]{1,0:T(8,128)(2,1)S(1)} %get-tuple-element.109.after.refs_6_), channel_id=1, source_target_pairs={{0,4},{4,8},{8,12},{12,16},{16,20},{20,24},{24,28},{28,0},{1,5},{5... | collective-permute-start | bytes 786440 | tf_op jit(solution)/shard_map/ppermute | solution.py:173
  107.9 2.2 %collective-permute-start.36 = (bf16[32,512]{1,0:T(8,128)(2,1)S(1)}, bf16[32,512]{1,0:T(8,128)(2,1)S(1)}, u32[]{:S(2)}, u32[]{:S(2)}) collective-permute-start(bf16[32,512]{1,0:T(8,128)(2,1)S(1)} %get-tuple-element.110), channel_id=1, source_target_pairs={{0,1},{1,2},{2,3},{3,0},{4,5},{5,6},{6,7},{7,4},{8,9},{9,10},{10,1... | collective-permute-start | bytes 98312 | tf_op jit(solution)/shard_map/ppermute | solution.py:173
  109.1 3.6 %collective-permute-start.37 = (bf16[32,512]{1,0:T(8,128)(2,1)S(1)}, bf16[32,512]{1,0:T(8,128)(2,1)S(1)}, u32[]{:S(2)}, u32[]{:S(2)}) collective-permute-start(bf16[32,512]{1,0:T(8,128)(2,1)S(1)} %get-tuple-element.111), channel_id=1, source_target_pairs={{0,3},{1,0},{2,1},{3,2},{4,7},{5,4},{6,5},{7,6},{8,11},{9,8},{10,9... | collective-permute-start | bytes 98312 | tf_op jit(solution)/shard_map/ppermute | solution.py:173
  114.0 8.8 %collective-permute-start.38 = (bf16[32,4096]{1,0:T(8,128)(2,1)S(1)}, bf16[32,4096]{1,0:T(8,128)(2,1)S(1)}, u32[]{:S(2)}, u32[]{:S(2)}) collective-permute-start(bf16[32,4096]{1,0:T(8,128)(2,1)S(1)} %get-tuple-element.113.after.refs_6_), channel_id=1, source_target_pairs={{0,4},{4,8},{8,12},{12,16},{16,20},{20,24},{24,28},{28,0},{1,5},{5... | collective-permute-start | bytes 786440 | tf_op jit(solution)/shard_map/ppermute | solution.py:173
  115.6 2.0 %collective-permute-start.40 = (bf16[32,512]{1,0:T(8,128)(2,1)S(1)}, bf16[32,512]{1,0:T(8,128)(2,1)S(1)}, u32[]{:S(2)}, u32[]{:S(2)}) collective-permute-start(bf16[32,512]{1,0:T(8,128)(2,1)S(1)} %get-tuple-element.114), channel_id=1, source_target_pairs={{0,1},{1,2},{2,3},{3,0},{4,5},{5,6},{6,7},{7,4},{8,9},{9,10},{10,1... | collective-permute-start | bytes 98312 | tf_op jit(solution)/shard_map/ppermute | solution.py:173
  116.4 3.6 %collective-permute-start.41 = (bf16[32,512]{1,0:T(8,128)(2,1)S(1)}, bf16[32,512]{1,0:T(8,128)(2,1)S(1)}, u32[]{:S(2)}, u32[]{:S(2)}) collective-permute-start(bf16[32,512]{1,0:T(8,128)(2,1)S(1)} %get-tuple-element.115), channel_id=1, source_target_pairs={{0,3},{1,0},{2,1},{3,2},{4,7},{5,4},{6,5},{7,6},{8,11},{9,8},{10,9... | collective-permute-start | bytes 98312 | tf_op jit(solution)/shard_map/ppermute | solution.py:173
  122.8 2.2 %copy-start = (bf16[8,64,4096]{2,1,0:T(8,128)(2,1)S(1)}, bf16[8,64,4096]{2,1,0:T(8,128)(2,1)}, u32[]{:S(2)}) copy-start(bf16[8,64,4096]{2,1,0:T(8,128)(2,1)} %layer_t7_r0.1.after.refs_6_) | copy-start | bytes 12582916
  125.0 2.3 %collective-permute-start.42 = (bf16[32,512]{1,0:T(8,128)(2,1)S(1)}, bf16[32,512]{1,0:T(8,128)(2,1)S(1)}, u32[]{:S(2)}, u32[]{:S(2)}) collective-permute-start(bf16[32,512]{1,0:T(8,128)(2,1)S(1)} %get-tuple-element.117), channel_id=1, source_target_pairs={{0,1},{1,2},{2,3},{3,0},{4,5},{5,6},{6,7},{7,4},{8,9},{9,10},{10,1... | collective-permute-start | bytes 98312 | tf_op jit(solution)/shard_map/ppermute | solution.py:173
  126.3 3.3 %collective-permute-start.43 = (bf16[32,512]{1,0:T(8,128)(2,1)S(1)}, bf16[32,512]{1,0:T(8,128)(2,1)S(1)}, u32[]{:S(2)}, u32[]{:S(2)}) collective-permute-start(bf16[32,512]{1,0:T(8,128)(2,1)S(1)} %get-tuple-element.118), channel_id=1, source_target_pairs={{0,3},{1,0},{2,1},{3,2},{4,7},{5,4},{6,5},{7,6},{8,11},{9,8},{10,9... | collective-permute-start | bytes 98312 | tf_op jit(solution)/shard_map/ppermute | solution.py:173

commit v4 on v2

v4 whole, which is shorter than its diff:
```python
import functools

import jax
import jax.numpy as jnp
from jax import lax
from jax.experimental import pallas as pl
from jax.experimental.pallas import tpu as pltpu
from jax.sharding import PartitionSpec as P

BLK = 128
HALO = 4
TICKS = 8
CHUNKS = 2
VMEM = pl.BlockSpec(memory_space=pltpu.VMEM)
SMEM = pl.BlockSpec(memory_space=pltpu.SMEM)
ANY = pl.BlockSpec(memory_space=pl.ANY)


def load_kernel(blks, state, w, bias, indices, state_out, w_out, bias_out, meta, raw, sems):
    copies = [
        pltpu.make_async_copy(src, dst, sems.at[i])
        for i, (src, dst) in enumerate(((indices, raw), (state, state_out), (bias, bias_out), (w, w_out)))
    ]
    for copy in copies:
        copy.start()
    brs, nzb = indices.shape
    columns = brs * blks
    start = lax.axis_index("blk") * brs - HALO
    meta[brs * nzb] = lax.axis_index("section")
    copies[0].wait()

    @pl.loop(0, brs)
    def _(i):
        for k in range(nzb):
            col = raw[i, k] - start
            col = jnp.where(col < 0, col + columns, col)
            meta[i * nzb + k] = jnp.where(col >= columns, col - columns, col) * BLK

    for copy in copies[1:]:
        copy.wait()


def load(blks, state, w, bias, indices):
    arrays = (state, w, bias)
    return pl.pallas_call(
        functools.partial(load_kernel, blks),
        out_shape=(
            *(pltpu.VMEM(a.shape, a.dtype) for a in arrays),
            pltpu.SMEM((indices.size + 1,), jnp.int32),
        ),
        in_specs=[ANY] * 4,
        out_specs=(VMEM,) * 3 + (SMEM,),
        scratch_shapes=[pltpu.SMEM(indices.shape, jnp.int32), pltpu.SemaphoreType.DMA((4,))],
        compiler_params=pltpu.CompilerParams(vmem_limit_bytes=16 * 1024 * 1024),
        cost_estimate=pl.CostEstimate(flops=0, bytes_accessed=w.size * 2, transcendentals=0),
        name="load",
    )(*(pltpu.with_memory_space_constraint(a, pltpu.HBM) for a in (*arrays, indices)))


def layer_kernel(tick, src_row, rows, brs, nzb, own_slot, prev_slot, aliased, *refs):
    refs = list(refs)
    meta, main, low, high, w, bias = refs[:6]
    del refs[:6]
    prev = refs.pop(0) if prev_slot is not None else None
    if aliased:
        refs.pop(0)
    emitted = refs.pop(0) if prev_slot is not None or own_slot is not None else None
    left = right = None
    if own_slot is None:
        out, left, right, xbuf, sems = refs
    else:
        out, xbuf, sems = refs
    edge = HALO * BLK
    width = brs * BLK

    def write(src, slot, first, count, sem):
        where = (slice(None), pl.ds(first * BLK, count * BLK))
        slot_tick, row = slot
        return pltpu.make_async_copy(
            src.at[where], emitted.at[slot_tick, pl.ds(row, rows), pl.ds(first * BLK, count * BLK)], sem
        )

    pieces = 4
    own = []
    if own_slot is not None:
        own = [write(out, own_slot, n * brs // pieces, brs // pieces, sems.at[1 + n]) for n in range(pieces)]
    if prev is not None:
        before = write(prev, prev_slot, 0, brs, sems.at[0])
        before.start()
    live = meta[brs * nzb] >= tick

    @pl.when(live)
    def _():
        src = pl.ds(src_row, rows)
        xbuf[:, 0:edge] = low[src, :]
        xbuf[:, edge : edge + width] = main[src, :]
        xbuf[:, edge + width : edge + width + edge] = high[src, :]
        for i in range(brs):
            picked = jnp.concatenate(
                [xbuf[:, pl.ds(pl.multiple_of(meta[i * nzb + k], BLK), BLK)] for k in range(nzb)], axis=1
            )
            cols = pl.ds(i * BLK, BLK)
            summed = jnp.dot(picked, w[i], preferred_element_type=jnp.float32) + bias[:, cols]
            made = jnp.maximum(summed, 0.0).astype(jnp.bfloat16)
            out[:, cols] = made
            if left is not None and i < HALO:
                left[:, cols] = made
            if right is not None and i >= brs - HALO:
                right[:, pl.ds((i - brs + HALO) * BLK, BLK)] = made
            if own and (i + 1) % (brs // pieces) == 0:
                own[i // (brs // pieces)].start()

    @pl.when(jnp.logical_not(live))
    def _():
        out[...] = jnp.zeros_like(out)
        if left is not None:
            left[...] = jnp.zeros_like(left)
            right[...] = jnp.zeros_like(right)
        for copy in own:
            copy.start()

    if prev is not None:
        before.wait()
    for copy in own:
        copy.wait()


def apply_layer(tick, src_row, row, rows, last, operands, prev, prev_slot, emitted, emitted_aval):
    meta, main, low, high, w, bias = operands
    brs, depth = w.shape[:2]
    nzb = depth // BLK
    width = brs * BLK
    edge = HALO * BLK
    args = [
        pltpu.with_memory_space_constraint(meta, pltpu.SMEM),
        *(pltpu.with_memory_space_constraint(a, pltpu.VMEM) for a in (main, low, high, w, bias)),
    ]
    specs = [SMEM] + [VMEM] * 5
    out_shape = []
    out_specs = []
    scratch = [
        pltpu.VMEM((rows, width + 2 * edge), jnp.bfloat16),
        pltpu.SemaphoreType.DMA((5,)),
    ]
    aliases = {}
    if prev is not None:
        args.append(pltpu.with_memory_space_constraint(prev, pltpu.VMEM))
        specs.append(VMEM)
    if emitted is not None:
        aliases = {len(args): 0}
        args.append(emitted)
        specs.append(ANY)
    if prev is not None or last:
        out_shape.append(emitted_aval)
        out_specs.append(ANY)
    if last:
        scratch.insert(0, pltpu.VMEM((rows, width), jnp.bfloat16))
    else:
        out_shape += [pltpu.VMEM((rows, cols), jnp.bfloat16) for cols in (width, edge, edge)]
        out_specs += [VMEM] * 3
    body = functools.partial(
        layer_kernel, tick, src_row, rows, brs, nzb, (tick, row) if last else None, prev_slot, emitted is not None
    )
    return pl.pallas_call(
        body,
        out_shape=tuple(out_shape),
        in_specs=specs,
        out_specs=tuple(out_specs),
        scratch_shapes=scratch,
        input_output_aliases=aliases,
        compiler_params=pltpu.CompilerParams(vmem_limit_bytes=8 * 1024 * 1024),
        cost_estimate=pl.CostEstimate(
            flops=20 * rows * brs * nzb * BLK * BLK, bytes_accessed=20 * w.size, transcendentals=0
        ),
        name=f"layer_t{tick}_r{row}",
    )(*args)


def shards(sections, blks, pending_groups, coefficient_tiles, source_block_indices, additive_offsets):
    block_rows, nzb = coefficient_tiles.shape[1:3]
    height, width = pending_groups.shape
    rows = height // CHUNKS
    edge = HALO * BLK
    emitted_aval = jax.ShapeDtypeStruct((TICKS, height, width), jnp.bfloat16)

    def hop(values, step, shift):
        pairs = [
            (s * blks + i, (s + step) % sections * blks + (i + shift) % blks)
            for s in range(sections)
            for i in range(blks)
        ]
        return lax.ppermute(values, ("section", "blk"), pairs)

    low = hop(pending_groups[:, width - edge :], 0, 1)
    high = hop(pending_groups[:, :edge], 0, -1)
    state, w, bias, meta = load(
        blks,
        pending_groups,
        coefficient_tiles.reshape(block_rows, nzb * BLK, BLK),
        additive_offsets,
        source_block_indices[0],
    )
    parts = [(state, low, high, c * rows) for c in range(CHUNKS)]
    emitted = prev = prev_slot = None
    for tick in range(TICKS):
        last = tick + 1 == TICKS
        for c in range(CHUNKS):
            main, low, high, src_row = parts[c]
            outs = list(
                apply_layer(
                    tick, src_row, c * rows, rows, last, (meta, main, low, high, w, bias), prev, prev_slot, emitted, emitted_aval
                )
            )
            if prev is not None or last:
                emitted = outs.pop(0)
            prev = prev_slot = None
            if not last:
                prev, left, right = outs
                prev_slot = (tick, c * rows)
                parts[c] = (hop(prev, 1, 0), hop(right, 1, 1), hop(left, 1, -1), 0)
    return emitted


def solution(mesh):
    in_specs = (
        P("section", "blk"),
        P("section", "blk", None, None, None),
        P("section", "blk", None),
        P("section", "blk"),
    )
    out_specs = P(None, "section", "blk")
    body = functools.partial(shards, mesh.shape["section"], mesh.shape["blk"])
    return jax.shard_map(body, mesh=mesh, in_specs=in_specs, out_specs=out_specs, check_vma=False)
```

time: 175 us -> 119 us (0.68)
  local copies, waits for them, and re-layouts: 61.6 us -> 2.25 us
  waiting for transfers between devices: 50.4 us -> 63.5 us
  Pallas kernels: 25.8 us -> 17.1 us
    unnamed x82 -> x1, local copies, waits for them, and re-layouts: 60.5 us -> 1.37 us
    ppermute x44, waiting for transfers between devices: 50.4 us -> 63.5 us  [hop(): return lax.ppermute(values, ('section', 'blk'), pairs)]
    pallas_call x16, Pallas kernels: 22.1 us -> 13.5 us  [apply_layer(): pl.pallas_call(body, out_shape=tuple(out_shape), in_specs=specs, out_spec...]
    pallas_call x15 -> x1, Pallas kernels: 3.69 us -> 3.62 us  [load(): pl.pallas_call(functools.partial(load_kernel, blks), out_shape=(*(pltpu.V...]
  transfers between devices with their start and end apart: 44 -> 44, of which waited for: 29 -> 27; matrix products, arithmetic and copies ran while one was open for 1% -> 1% of each run, Pallas kernels for 13% -> 13%
where the time goes in v4:
time: 119 us
  waiting for transfers between devices  63.5 us (53%)
  starting transfers between devices  35.3 us (30%)
  Pallas kernels  17.1 us (14%)
  local copies, waits for them, and re-layouts  2.25 us (2%)
    ppermute x44, waiting for transfers between devices, hop(): return lax.ppermute(values, ('section', 'blk'), pairs)  63.5 us
    ppermute x44, starting transfers between devices, hop(): return lax.ppermute(values, ('section', 'blk'), pairs)  35.3 us
    pallas_call x16, Pallas kernels, apply_layer(): pl.pallas_call(body, out_shape=tuple(out_shape), in_specs=specs, out_spec...  13.5 us
    pallas_call x1, Pallas kernels, load(): pl.pallas_call(functools.partial(load_kernel, blks), out_shape=(*(pltpu.V...  3.62 us
  transfers between devices with their start and end apart: 44, of which 27 were waited for; matrix products, arithmetic and copies ran while one was open for 1% of the time, Pallas kernels for 13%

profile of v4, /device:TPU:1, one launch (start us, length us, event | category | flops | bytes accessed | tf_op | source)
XLA Modules:
  0.0 118.6 jit_solution(12565586496677832764)
XLA Ops:
  0.0 0.9 fusion
  0.9 2.7 %collective-permute-start = (bf16[64,512]{1,0:T(8,128)(2,1)S(1)}, bf16[64,512]{1,0:T(8,128)(2,1)S(1)}, u32[]{:S(2)}, u32[]{:S(2)}) collective-permute-start(bf16[64,512]{1,0:T(8,128)(2,1)S(1)} %get-tuple-element.124), channel_id=1, source_target_pairs={{0,1},{1,2},{2,3},{3,0},{4,5},{5,6},{6,7},{7,4},{8,9},{9,10},{10,1... | collective-permute-start | bytes 196616 | tf_op jit(solution)/shard_map/ppermute | solution.py:192
  3.5 1.4 %copy.19 = s32[1,32,8]{2,1,0:T(8,128)} copy(s32[1,32,8]{1,2,0:T(8,128)} %param.6) | data formatting | bytes 2048 | tf_op args[2]
  4.9 3.6 %load.1 = (bf16[64,4096]{1,0:T(8,128)(2,1)S(1)}, bf16[32,1024,128]{2,1,0:T(8,128)(2,1)S(1)}, f32[1,4096]{1,0:T(1,128)S(1)}, s32[257]{0:T(512)S(4)}) custom-call(bf16[64,4096]{1,0:T(8,128)(2,1)} %state.1, bf16[32,1024,128]{2,1,0:T(8,128)(2,1)} %bitcast.2, f32[1,4096]{1,0:T(1,128)} %bias.1, s32[32,8]{1,0:T(8,128)} %bitcast.3), custom_call_target="tpu_custom_call" | custom-call | bytes 8388608 | tf_op jit(solution)/shard_map/load/pallas_call | solution.py:45
  8.6 1.5 %layer_t0_r0.1 = (bf16[32,4096]{1,0:T(8,128)(2,1)S(1)}, bf16[32,512]{1,0:T(8,128)(2,1)S(1)}, bf16[32,512]{1,0:T(8,128)(2,1)S(1)}) custom-call(s32[257]{0:T(512)S(4)} %get-tuple-element.64.refs_0_, bf16[64,4096]{1,0:T(8,128)(2,1)S(1)} %get-tuple-element.65.refs_1_, bf16[64,512]{1,0:T(8,128)(2,1)S(1)} %collective-permute-done.refs_2_, ...), custom_call_target="tpu_custom_call" | custom-call | flops 2684354560 | bytes 83886080 | tf_op jit(solution)/shard_map/layer_t0_r0/pallas_call | solution.py:164
  10.0 1.3 %collective-permute-start.5 = (bf16[32,4096]{1,0:T(8,128)(2,1)S(1)}, bf16[32,4096]{1,0:T(8,128)(2,1)S(1)}, u32[]{:S(2)}, u32[]{:S(2)}) collective-permute-start(bf16[32,4096]{1,0:T(8,128)(2,1)S(1)} %get-tuple-element.68.refs_6_), channel_id=1, source_target_pairs={{0,4},{1,5},{2,6},{3,7},{4,8},{5,9},{6,10},{7,11},{8,12},{9,13},{1... | collective-permute-start | bytes 786440 | tf_op jit(solution)/shard_map/ppermute | solution.py:192
  11.3 3.0 %collective-permute-start.6 = (bf16[32,512]{1,0:T(8,128)(2,1)S(1)}, bf16[32,512]{1,0:T(8,128)(2,1)S(1)}, u32[]{:S(2)}, u32[]{:S(2)}) collective-permute-start(bf16[32,512]{1,0:T(8,128)(2,1)S(1)} %get-tuple-element.72), channel_id=1, source_target_pairs={{0,5},{1,6},{2,7},{3,4},{4,9},{5,10},{6,11},{7,8},{8,13},{9,14},{1... | collective-permute-start | bytes 98312 | tf_op jit(solution)/shard_map/ppermute | solution.py:192
  14.3 1.5 %layer_t0_r32.1 = (bf16[8,64,4096]{2,1,0:T(8,128)(2,1)}, bf16[32,4096]{1,0:T(8,128)(2,1)S(1)}, bf16[32,512]{1,0:T(8,128)(2,1)S(1)}, bf16[32,512]{1,0:T(8,128)(2,1)S(1)}) custom-call(s32[257]{0:T(512)S(4)} %get-tuple-element.64.refs_0_, bf16[64,4096]{1,0:T(8,128)(2,1)S(1)} %get-tuple-element.65.refs_1_, bf16[64,512]{1,0:T(8,128)(2,1)S(1)} %collective-permute-done.refs_2_, ...), custom_call_target="tpu_custom_call" | custom-call | flops 2684354560 | bytes 83886080 | tf_op jit(solution)/shard_map/layer_t0_r32/pallas_call | solution.py:164
  15.8 1.3 %collective-permute-start.2 = (bf16[32,4096]{1,0:T(8,128)(2,1)S(1)}, bf16[32,4096]{1,0:T(8,128)(2,1)S(1)}, u32[]{:S(2)}, u32[]{:S(2)}) collective-permute-start(bf16[32,4096]{1,0:T(8,128)(2,1)S(1)} %get-tuple-element.69.refs_6_), channel_id=1, source_target_pairs={{0,4},{1,5},{2,6},{3,7},{4,8},{5,9},{6,10},{7,11},{8,12},{9,13},{1... | collective-permute-start | bytes 786440 | tf_op jit(solution)/shard_map/ppermute | solution.py:192
  17.1 4.0 %collective-permute-start.3 = (bf16[32,512]{1,0:T(8,128)(2,1)S(1)}, bf16[32,512]{1,0:T(8,128)(2,1)S(1)}, u32[]{:S(2)}, u32[]{:S(2)}) collective-permute-start(bf16[32,512]{1,0:T(8,128)(2,1)S(1)} %get-tuple-element.70), channel_id=1, source_target_pairs={{0,5},{1,6},{2,7},{3,4},{4,9},{5,10},{6,11},{7,8},{8,13},{9,14},{1... | collective-permute-start | bytes 98312 | tf_op jit(solution)/shard_map/ppermute | solution.py:192
  21.0 1.5 %collective-permute-done.6.refs_2_ = bf16[32,512]{1,0:T(8,128)(2,1)S(1)} collective-permute-done((bf16[32,512]{1,0:T(8,128)(2,1)S(1)}, bf16[32,512]{1,0:T(8,128)(2,1)S(1)}, u32[]{:S(2)}, u32[]{:S(2)}) %collective-permute-start.6) | collective-permute-done | bytes 32800 | tf_op jit(solution)/shard_map/ppermute | solution.py:192
  22.5 1.6 %collective-permute-done.7.refs_3_ = bf16[32,512]{1,0:T(8,128)(2,1)S(1)} collective-permute-done((bf16[32,512]{1,0:T(8,128)(2,1)S(1)}, bf16[32,512]{1,0:T(8,128)(2,1)S(1)}, u32[]{:S(2)}, u32[]{:S(2)}) %collective-permute-start.7) | collective-permute-done | bytes 32800 | tf_op jit(solution)/shard_map/ppermute | solution.py:192
  24.2 0.7 layer_t1_r0.1
  25.0 2.1 %collective-permute-start.12 = (bf16[32,512]{1,0:T(8,128)(2,1)S(1)}, bf16[32,512]{1,0:T(8,128)(2,1)S(1)}, u32[]{:S(2)}, u32[]{:S(2)}) collective-permute-start(bf16[32,512]{1,0:T(8,128)(2,1)S(1)} %get-tuple-element.80), channel_id=1, source_target_pairs={{0,5},{1,6},{2,7},{3,4},{4,9},{5,10},{6,11},{7,8},{8,13},{9,14},{1... | collective-permute-start | bytes 98312 | tf_op jit(solution)/shard_map/ppermute | solution.py:192
  27.1 2.4 %collective-permute-done.3.refs_2_ = bf16[32,512]{1,0:T(8,128)(2,1)S(1)} collective-permute-done((bf16[32,512]{1,0:T(8,128)(2,1)S(1)}, bf16[32,512]{1,0:T(8,128)(2,1)S(1)}, u32[]{:S(2)}, u32[]{:S(2)}) %collective-permute-start.3) | collective-permute-done | bytes 32800 | tf_op jit(solution)/shard_map/ppermute | solution.py:192
  29.5 0.3 collective-permute-done.4.refs_3_
  29.8 0.7 layer_t1_r32.1
  30.6 0.5 collective-permute-start.8
  31.0 3.9 %collective-permute-start.10 = (bf16[32,512]{1,0:T(8,128)(2,1)S(1)}, bf16[32,512]{1,0:T(8,128)(2,1)S(1)}, u32[]{:S(2)}, u32[]{:S(2)}) collective-permute-start(bf16[32,512]{1,0:T(8,128)(2,1)S(1)} %get-tuple-element.79), channel_id=1, source_target_pairs={{0,7},{1,4},{2,5},{3,6},{4,11},{5,8},{6,9},{7,10},{8,15},{9,12},{1... | collective-permute-start | bytes 98312 | tf_op jit(solution)/shard_map/ppermute | solution.py:192
  34.9 2.1 %collective-permute-done.12.refs_2_ = bf16[32,512]{1,0:T(8,128)(2,1)S(1)} collective-permute-done((bf16[32,512]{1,0:T(8,128)(2,1)S(1)}, bf16[32,512]{1,0:T(8,128)(2,1)S(1)}, u32[]{:S(2)}, u32[]{:S(2)}) %collective-permute-start.12) | collective-permute-done | bytes 32800 | tf_op jit(solution)/shard_map/ppermute | solution.py:192
  37.0 1.0 collective-permute-done.13.refs_3_
  38.1 0.7 layer_t2_r0.1
  38.9 1.1 collective-permute-start.18
  40.0 4.8 %collective-permute-done.10.refs_3_ = bf16[32,512]{1,0:T(8,128)(2,1)S(1)} collective-permute-done((bf16[32,512]{1,0:T(8,128)(2,1)S(1)}, bf16[32,512]{1,0:T(8,128)(2,1)S(1)}, u32[]{:S(2)}, u32[]{:S(2)}) %collective-permute-start.10) | collective-permute-done | bytes 32800 | tf_op jit(solution)/shard_map/ppermute | solution.py:192
  44.8 0.8 layer_t2_r32.1
  45.6 2.4 %collective-permute-start.15 = (bf16[32,512]{1,0:T(8,128)(2,1)S(1)}, bf16[32,512]{1,0:T(8,128)(2,1)S(1)}, u32[]{:S(2)}, u32[]{:S(2)}) collective-permute-start(bf16[32,512]{1,0:T(8,128)(2,1)S(1)} %get-tuple-element.86), channel_id=1, source_target_pairs={{0,5},{1,6},{2,7},{3,4},{4,9},{5,10},{6,11},{7,8},{8,13},{9,14},{1... | collective-permute-start | bytes 98312 | tf_op jit(solution)/shard_map/ppermute | solution.py:192
  48.0 2.8 %collective-permute-done.18.refs_2_ = bf16[32,512]{1,0:T(8,128)(2,1)S(1)} collective-permute-done((bf16[32,512]{1,0:T(8,128)(2,1)S(1)}, bf16[32,512]{1,0:T(8,128)(2,1)S(1)}, u32[]{:S(2)}, u32[]{:S(2)}) %collective-permute-start.18) | collective-permute-done | bytes 32800 | tf_op jit(solution)/shard_map/ppermute | solution.py:192
  50.8 1.7 %collective-permute-done.19.refs_3_ = bf16[32,512]{1,0:T(8,128)(2,1)S(1)} collective-permute-done((bf16[32,512]{1,0:T(8,128)(2,1)S(1)}, bf16[32,512]{1,0:T(8,128)(2,1)S(1)}, u32[]{:S(2)}, u32[]{:S(2)}) %collective-permute-start.19) | collective-permute-done | bytes 32800 | tf_op jit(solution)/shard_map/ppermute | solution.py:192
  52.5 0.7 layer_t3_r0.1
  53.4 2.0 %collective-permute-start.24 = (bf16[32,512]{1,0:T(8,128)(2,1)S(1)}, bf16[32,512]{1,0:T(8,128)(2,1)S(1)}, u32[]{:S(2)}, u32[]{:S(2)}) collective-permute-start(bf16[32,512]{1,0:T(8,128)(2,1)S(1)} %get-tuple-element.96), channel_id=1, source_target_pairs={{0,5},{1,6},{2,7},{3,4},{4,9},{5,10},{6,11},{7,8},{8,13},{9,14},{1... | collective-permute-start | bytes 98312 | tf_op jit(solution)/shard_map/ppermute | solution.py:192
  55.4 3.5 %collective-permute-done.15.refs_2_ = bf16[32,512]{1,0:T(8,128)(2,1)S(1)} collective-permute-done((bf16[32,512]{1,0:T(8,128)(2,1)S(1)}, bf16[32,512]{1,0:T(8,128)(2,1)S(1)}, u32[]{:S(2)}, u32[]{:S(2)}) %collective-permute-start.15) | collective-permute-done | bytes 32800 | tf_op jit(solution)/shard_map/ppermute | solution.py:192
  58.9 1.0 collective-permute-done.16.refs_3_
  59.9 0.7 layer_t3_r32.1
  60.7 1.3 %collective-permute-start.21 = (bf16[32,512]{1,0:T(8,128)(2,1)S(1)}, bf16[32,512]{1,0:T(8,128)(2,1)S(1)}, u32[]{:S(2)}, u32[]{:S(2)}) collective-permute-start(bf16[32,512]{1,0:T(8,128)(2,1)S(1)} %get-tuple-element.94), channel_id=1, source_target_pairs={{0,5},{1,6},{2,7},{3,4},{4,9},{5,10},{6,11},{7,8},{8,13},{9,14},{1... | collective-permute-start | bytes 98312 | tf_op jit(solution)/shard_map/ppermute | solution.py:192
  62.1 3.8 %collective-permute-done.24.refs_2_ = bf16[32,512]{1,0:T(8,128)(2,1)S(1)} collective-permute-done((bf16[32,512]{1,0:T(8,128)(2,1)S(1)}, bf16[32,512]{1,0:T(8,128)(2,1)S(1)}, u32[]{:S(2)}, u32[]{:S(2)}) %collective-permute-start.24) | collective-permute-done | bytes 32800 | tf_op jit(solution)/shard_map/ppermute | solution.py:192
  65.9 1.2 %collective-permute-done.25.refs_3_ = bf16[32,512]{1,0:T(8,128)(2,1)S(1)} collective-permute-done((bf16[32,512]{1,0:T(8,128)(2,1)S(1)}, bf16[32,512]{1,0:T(8,128)(2,1)S(1)}, u32[]{:S(2)}, u32[]{:S(2)}) %collective-permute-start.25) | collective-permute-done | bytes 32800 | tf_op jit(solution)/shard_map/ppermute | solution.py:192
  67.1 0.7 layer_t4_r0.1
  67.9 1.4 %collective-permute-start.30 = (bf16[32,512]{1,0:T(8,128)(2,1)S(1)}, bf16[32,512]{1,0:T(8,128)(2,1)S(1)}, u32[]{:S(2)}, u32[]{:S(2)}) collective-permute-start(bf16[32,512]{1,0:T(8,128)(2,1)S(1)} %get-tuple-element.104), channel_id=1, source_target_pairs={{0,5},{1,6},{2,7},{3,4},{4,9},{5,10},{6,11},{7,8},{8,13},{9,14},{1... | collective-permute-start | bytes 98312 | tf_op jit(solution)/shard_map/ppermute | solution.py:192
  69.4 4.1 %collective-permute-done.21.refs_2_ = bf16[32,512]{1,0:T(8,128)(2,1)S(1)} collective-permute-done((bf16[32,512]{1,0:T(8,128)(2,1)S(1)}, bf16[32,512]{1,0:T(8,128)(2,1)S(1)}, u32[]{:S(2)}, u32[]{:S(2)}) %collective-permute-start.21) | collective-permute-done | bytes 32800 | tf_op jit(solution)/shard_map/ppermute | solution.py:192
  73.5 1.0 collective-permute-done.22.refs_3_
  74.5 0.7 layer_t4_r32.1
  75.3 1.4 %collective-permute-start.27 = (bf16[32,512]{1,0:T(8,128)(2,1)S(1)}, bf16[32,512]{1,0:T(8,128)(2,1)S(1)}, u32[]{:S(2)}, u32[]{:S(2)}) collective-permute-start(bf16[32,512]{1,0:T(8,128)(2,1)S(1)} %get-tuple-element.102), channel_id=1, source_target_pairs={{0,5},{1,6},{2,7},{3,4},{4,9},{5,10},{6,11},{7,8},{8,13},{9,14},{1... | collective-permute-start | bytes 98312 | tf_op jit(solution)/shard_map/ppermute | solution.py:192
  76.7 3.8 %collective-permute-done.30.refs_2_ = bf16[32,512]{1,0:T(8,128)(2,1)S(1)} collective-permute-done((bf16[32,512]{1,0:T(8,128)(2,1)S(1)}, bf16[32,512]{1,0:T(8,128)(2,1)S(1)}, u32[]{:S(2)}, u32[]{:S(2)}) %collective-permute-start.30) | collective-permute-done | bytes 32800 | tf_op jit(solution)/shard_map/ppermute | solution.py:192
  80.5 1.2 collective-permute-done.31.refs_3_
  81.7 0.7 layer_t5_r0.1
  82.5 1.5 %collective-permute-start.36 = (bf16[32,512]{1,0:T(8,128)(2,1)S(1)}, bf16[32,512]{1,0:T(8,128)(2,1)S(1)}, u32[]{:S(2)}, u32[]{:S(2)}) collective-permute-start(bf16[32,512]{1,0:T(8,128)(2,1)S(1)} %get-tuple-element.112), channel_id=1, source_target_pairs={{0,5},{1,6},{2,7},{3,4},{4,9},{5,10},{6,11},{7,8},{8,13},{9,14},{1... | collective-permute-start | bytes 98312 | tf_op jit(solution)/shard_map/ppermute | solution.py:192
  84.0 4.0 %collective-permute-done.27.refs_2_ = bf16[32,512]{1,0:T(8,128)(2,1)S(1)} collective-permute-done((bf16[32,512]{1,0:T(8,128)(2,1)S(1)}, bf16[32,512]{1,0:T(8,128)(2,1)S(1)}, u32[]{:S(2)}, u32[]{:S(2)}) %collective-permute-start.27) | collective-permute-done | bytes 32800 | tf_op jit(solution)/shard_map/ppermute | solution.py:192
  88.0 1.0 collective-permute-done.28.refs_3_
  89.0 0.7 layer_t5_r32.1
  89.8 1.5 %collective-permute-start.33 = (bf16[32,512]{1,0:T(8,128)(2,1)S(1)}, bf16[32,512]{1,0:T(8,128)(2,1)S(1)}, u32[]{:S(2)}, u32[]{:S(2)}) collective-permute-start(bf16[32,512]{1,0:T(8,128)(2,1)S(1)} %get-tuple-element.110), channel_id=1, source_target_pairs={{0,5},{1,6},{2,7},{3,4},{4,9},{5,10},{6,11},{7,8},{8,13},{9,14},{1... | collective-permute-start | bytes 98312 | tf_op jit(solution)/shard_map/ppermute | solution.py:192
  91.3 3.7 %collective-permute-done.36.refs_2_ = bf16[32,512]{1,0:T(8,128)(2,1)S(1)} collective-permute-done((bf16[32,512]{1,0:T(8,128)(2,1)S(1)}, bf16[32,512]{1,0:T(8,128)(2,1)S(1)}, u32[]{:S(2)}, u32[]{:S(2)}) %collective-permute-start.36) | collective-permute-done | bytes 32800 | tf_op jit(solution)/shard_map/ppermute | solution.py:192
  95.1 1.2 %collective-permute-done.37.refs_3_ = bf16[32,512]{1,0:T(8,128)(2,1)S(1)} collective-permute-done((bf16[32,512]{1,0:T(8,128)(2,1)S(1)}, bf16[32,512]{1,0:T(8,128)(2,1)S(1)}, u32[]{:S(2)}, u32[]{:S(2)}) %collective-permute-start.37) | collective-permute-done | bytes 32800 | tf_op jit(solution)/shard_map/ppermute | solution.py:192
  96.3 0.7 layer_t6_r0.1
  97.1 1.5 %collective-permute-start.42 = (bf16[32,512]{1,0:T(8,128)(2,1)S(1)}, bf16[32,512]{1,0:T(8,128)(2,1)S(1)}, u32[]{:S(2)}, u32[]{:S(2)}) collective-permute-start(bf16[32,512]{1,0:T(8,128)(2,1)S(1)} %get-tuple-element.120), channel_id=1, source_target_pairs={{0,5},{1,6},{2,7},{3,4},{4,9},{5,10},{6,11},{7,8},{8,13},{9,14},{1... | collective-permute-start | bytes 98312 | tf_op jit(solution)/shard_map/ppermute | solution.py:192
  98.7 3.9 %collective-permute-done.33.refs_2_ = bf16[32,512]{1,0:T(8,128)(2,1)S(1)} collective-permute-done((bf16[32,512]{1,0:T(8,128)(2,1)S(1)}, bf16[32,512]{1,0:T(8,128)(2,1)S(1)}, u32[]{:S(2)}, u32[]{:S(2)}) %collective-permute-start.33) | collective-permute-done | bytes 32800 | tf_op jit(solution)/shard_map/ppermute | solution.py:192
  102.5 0.9 collective-permute-done.34.refs_3_
  103.5 0.7 layer_t6_r32.1
  104.3 1.7 %collective-permute-start.39 = (bf16[32,512]{1,0:T(8,128)(2,1)S(1)}, bf16[32,512]{1,0:T(8,128)(2,1)S(1)}, u32[]{:S(2)}, u32[]{:S(2)}) collective-permute-start(bf16[32,512]{1,0:T(8,128)(2,1)S(1)} %get-tuple-element.118), channel_id=1, source_target_pairs={{0,5},{1,6},{2,7},{3,4},{4,9},{5,10},{6,11},{7,8},{8,13},{9,14},{1... | collective-permute-start | bytes 98312 | tf_op jit(solution)/shard_map/ppermute | solution.py:192
  106.0 3.7 %collective-permute-done.42.refs_2_ = bf16[32,512]{1,0:T(8,128)(2,1)S(1)} collective-permute-done((bf16[32,512]{1,0:T(8,128)(2,1)S(1)}, bf16[32,512]{1,0:T(8,128)(2,1)S(1)}, u32[]{:S(2)}, u32[]{:S(2)}) %collective-permute-start.42) | collective-permute-done | bytes 32800 | tf_op jit(solution)/shard_map/ppermute | solution.py:192
  109.7 1.2 collective-permute-done.43.refs_3_
  110.9 0.8 layer_t7_r0.1.refs_6_
  111.7 5.3 %collective-permute-done.39.refs_2_ = bf16[32,512]{1,0:T(8,128)(2,1)S(1)} collective-permute-done((bf16[32,512]{1,0:T(8,128)(2,1)S(1)}, bf16[32,512]{1,0:T(8,128)(2,1)S(1)}, u32[]{:S(2)}, u32[]{:S(2)}) %collective-permute-start.39) | collective-permute-done | bytes 32800 | tf_op jit(solution)/shard_map/ppermute | solution.py:192
  117.0 0.6 collective-permute-done.40.refs_3_
  117.6 0.8 layer_t7_r32.1
  (43 shorter events, 0.7 us)
Async XLA Ops:
  0.9 7.7 %collective-permute-start = (bf16[64,512]{1,0:T(8,128)(2,1)S(1)}, bf16[64,512]{1,0:T(8,128)(2,1)S(1)}, u32[]{:S(2)}, u32[]{:S(2)}) collective-permute-start(bf16[64,512]{1,0:T(8,128)(2,1)S(1)} %get-tuple-element.124), channel_id=1, source_target_pairs={{0,1},{1,2},{2,3},{3,0},{4,5},{5,6},{6,7},{7,4},{8,9},{9,10},{10,1... | collective-permute-start | bytes 196616 | tf_op jit(solution)/shard_map/ppermute | solution.py:192
  3.5 5.0 %collective-permute-start.1 = (bf16[64,512]{1,0:T(8,128)(2,1)S(1)}, bf16[64,512]{1,0:T(8,128)(2,1)S(1)}, u32[]{:S(2)}, u32[]{:S(2)}) collective-permute-start(bf16[64,512]{1,0:T(8,128)(2,1)S(1)} %get-tuple-element.123), channel_id=1, source_target_pairs={{0,3},{1,0},{2,1},{3,2},{4,7},{5,4},{6,5},{7,6},{8,11},{9,8},{10,9... | collective-permute-start | bytes 196616 | tf_op jit(solution)/shard_map/ppermute | solution.py:192
  10.0 14.1 %collective-permute-start.5 = (bf16[32,4096]{1,0:T(8,128)(2,1)S(1)}, bf16[32,4096]{1,0:T(8,128)(2,1)S(1)}, u32[]{:S(2)}, u32[]{:S(2)}) collective-permute-start(bf16[32,4096]{1,0:T(8,128)(2,1)S(1)} %get-tuple-element.68.refs_6_), channel_id=1, source_target_pairs={{0,4},{1,5},{2,6},{3,7},{4,8},{5,9},{6,10},{7,11},{8,12},{9,13},{1... | collective-permute-start | bytes 786440 | tf_op jit(solution)/shard_map/ppermute | solution.py:192
  11.3 11.2 %collective-permute-start.6 = (bf16[32,512]{1,0:T(8,128)(2,1)S(1)}, bf16[32,512]{1,0:T(8,128)(2,1)S(1)}, u32[]{:S(2)}, u32[]{:S(2)}) collective-permute-start(bf16[32,512]{1,0:T(8,128)(2,1)S(1)} %get-tuple-element.72), channel_id=1, source_target_pairs={{0,5},{1,6},{2,7},{3,4},{4,9},{5,10},{6,11},{7,8},{8,13},{9,14},{1... | collective-permute-start | bytes 98312 | tf_op jit(solution)/shard_map/ppermute | solution.py:192
  14.3 9.9 %collective-permute-start.7 = (bf16[32,512]{1,0:T(8,128)(2,1)S(1)}, bf16[32,512]{1,0:T(8,128)(2,1)S(1)}, u32[]{:S(2)}, u32[]{:S(2)}) collective-permute-start(bf16[32,512]{1,0:T(8,128)(2,1)S(1)} %get-tuple-element.73), channel_id=1, source_target_pairs={{0,7},{1,4},{2,5},{3,6},{4,11},{5,8},{6,9},{7,10},{8,15},{9,12},{1... | collective-permute-start | bytes 98312 | tf_op jit(solution)/shard_map/ppermute | solution.py:192
  15.8 14.0 %collective-permute-start.2 = (bf16[32,4096]{1,0:T(8,128)(2,1)S(1)}, bf16[32,4096]{1,0:T(8,128)(2,1)S(1)}, u32[]{:S(2)}, u32[]{:S(2)}) collective-permute-start(bf16[32,4096]{1,0:T(8,128)(2,1)S(1)} %get-tuple-element.69.refs_6_), channel_id=1, source_target_pairs={{0,4},{1,5},{2,6},{3,7},{4,8},{5,9},{6,10},{7,11},{8,12},{9,13},{1... | collective-permute-start | bytes 786440 | tf_op jit(solution)/shard_map/ppermute | solution.py:192
  17.1 12.4 %collective-permute-start.3 = (bf16[32,512]{1,0:T(8,128)(2,1)S(1)}, bf16[32,512]{1,0:T(8,128)(2,1)S(1)}, u32[]{:S(2)}, u32[]{:S(2)}) collective-permute-start(bf16[32,512]{1,0:T(8,128)(2,1)S(1)} %get-tuple-element.70), channel_id=1, source_target_pairs={{0,5},{1,6},{2,7},{3,4},{4,9},{5,10},{6,11},{7,8},{8,13},{9,14},{1... | collective-permute-start | bytes 98312 | tf_op jit(solution)/shard_map/ppermute | solution.py:192
  22.5 7.3 %collective-permute-start.4 = (bf16[32,512]{1,0:T(8,128)(2,1)S(1)}, bf16[32,512]{1,0:T(8,128)(2,1)S(1)}, u32[]{:S(2)}, u32[]{:S(2)}) collective-permute-start(bf16[32,512]{1,0:T(8,128)(2,1)S(1)} %get-tuple-element.71), channel_id=1, source_target_pairs={{0,7},{1,4},{2,5},{3,6},{4,11},{5,8},{6,9},{7,10},{8,15},{9,12},{1... | collective-permute-start | bytes 98312 | tf_op jit(solution)/shard_map/ppermute | solution.py:192
  24.9 13.1 %collective-permute-start.11 = (bf16[32,4096]{1,0:T(8,128)(2,1)S(1)}, bf16[32,4096]{1,0:T(8,128)(2,1)S(1)}, u32[]{:S(2)}, u32[]{:S(2)}) collective-permute-start(bf16[32,4096]{1,0:T(8,128)(2,1)S(1)} %get-tuple-element.75.refs_6_), channel_id=1, source_target_pairs={{0,4},{1,5},{2,6},{3,7},{4,8},{5,9},{6,10},{7,11},{8,12},{9,13},{1... | collective-permute-start | bytes 786440 | tf_op jit(solution)/shard_map/ppermute | solution.py:192
  25.0 12.0 %collective-permute-start.12 = (bf16[32,512]{1,0:T(8,128)(2,1)S(1)}, bf16[32,512]{1,0:T(8,128)(2,1)S(1)}, u32[]{:S(2)}, u32[]{:S(2)}) collective-permute-start(bf16[32,512]{1,0:T(8,128)(2,1)S(1)} %get-tuple-element.80), channel_id=1, source_target_pairs={{0,5},{1,6},{2,7},{3,4},{4,9},{5,10},{6,11},{7,8},{8,13},{9,14},{1... | collective-permute-start | bytes 98312 | tf_op jit(solution)/shard_map/ppermute | solution.py:192
  29.5 8.6 %collective-permute-start.13 = (bf16[32,512]{1,0:T(8,128)(2,1)S(1)}, bf16[32,512]{1,0:T(8,128)(2,1)S(1)}, u32[]{:S(2)}, u32[]{:S(2)}) collective-permute-start(bf16[32,512]{1,0:T(8,128)(2,1)S(1)} %get-tuple-element.81), channel_id=1, source_target_pairs={{0,7},{1,4},{2,5},{3,6},{4,11},{5,8},{6,9},{7,10},{8,15},{9,12},{1... | collective-permute-start | bytes 98312 | tf_op jit(solution)/shard_map/ppermute | solution.py:192
  30.6 14.2 %collective-permute-start.8 = (bf16[32,4096]{1,0:T(8,128)(2,1)S(1)}, bf16[32,4096]{1,0:T(8,128)(2,1)S(1)}, u32[]{:S(2)}, u32[]{:S(2)}) collective-permute-start(bf16[32,4096]{1,0:T(8,128)(2,1)S(1)} %get-tuple-element.77.refs_6_), channel_id=1, source_target_pairs={{0,4},{1,5},{2,6},{3,7},{4,8},{5,9},{6,10},{7,11},{8,12},{9,13},{1... | collective-permute-start | bytes 786440 | tf_op jit(solution)/shard_map/ppermute | solution.py:192
  31.0 13.7 %collective-permute-start.10 = (bf16[32,512]{1,0:T(8,128)(2,1)S(1)}, bf16[32,512]{1,0:T(8,128)(2,1)S(1)}, u32[]{:S(2)}, u32[]{:S(2)}) collective-permute-start(bf16[32,512]{1,0:T(8,128)(2,1)S(1)} %get-tuple-element.79), channel_id=1, source_target_pairs={{0,7},{1,4},{2,5},{3,6},{4,11},{5,8},{6,9},{7,10},{8,15},{9,12},{1... | collective-permute-start | bytes 98312 | tf_op jit(solution)/shard_map/ppermute | solution.py:192
  37.0 7.7 %collective-permute-start.9 = (bf16[32,512]{1,0:T(8,128)(2,1)S(1)}, bf16[32,512]{1,0:T(8,128)(2,1)S(1)}, u32[]{:S(2)}, u32[]{:S(2)}) collective-permute-start(bf16[32,512]{1,0:T(8,128)(2,1)S(1)} %get-tuple-element.78), channel_id=1, source_target_pairs={{0,5},{1,6},{2,7},{3,4},{4,9},{5,10},{6,11},{7,8},{8,13},{9,14},{1... | collective-permute-start | bytes 98312 | tf_op jit(solution)/shard_map/ppermute | solution.py:192
  38.8 13.7 %collective-permute-start.17 = (bf16[32,4096]{1,0:T(8,128)(2,1)S(1)}, bf16[32,4096]{1,0:T(8,128)(2,1)S(1)}, u32[]{:S(2)}, u32[]{:S(2)}) collective-permute-start(bf16[32,4096]{1,0:T(8,128)(2,1)S(1)} %get-tuple-element.83.refs_6_), channel_id=1, source_target_pairs={{0,4},{1,5},{2,6},{3,7},{4,8},{5,9},{6,10},{7,11},{8,12},{9,13},{1... | collective-permute-start | bytes 786440 | tf_op jit(solution)/shard_map/ppermute | solution.py:192
  38.9 11.9 %collective-permute-start.18 = (bf16[32,512]{1,0:T(8,128)(2,1)S(1)}, bf16[32,512]{1,0:T(8,128)(2,1)S(1)}, u32[]{:S(2)}, u32[]{:S(2)}) collective-permute-start(bf16[32,512]{1,0:T(8,128)(2,1)S(1)} %get-tuple-element.88), channel_id=1, source_target_pairs={{0,5},{1,6},{2,7},{3,4},{4,9},{5,10},{6,11},{7,8},{8,13},{9,14},{1... | collective-permute-start | bytes 98312 | tf_op jit(solution)/shard_map/ppermute | solution.py:192
  44.8 7.8 %collective-permute-start.19 = (bf16[32,512]{1,0:T(8,128)(2,1)S(1)}, bf16[32,512]{1,0:T(8,128)(2,1)S(1)}, u32[]{:S(2)}, u32[]{:S(2)}) collective-permute-start(bf16[32,512]{1,0:T(8,128)(2,1)S(1)} %get-tuple-element.89), channel_id=1, source_target_pairs={{0,7},{1,4},{2,5},{3,6},{4,11},{5,8},{6,9},{7,10},{8,15},{9,12},{1... | collective-permute-start | bytes 98312 | tf_op jit(solution)/shard_map/ppermute | solution.py:192
  45.6 14.4 %collective-permute-start.14 = (bf16[32,4096]{1,0:T(8,128)(2,1)S(1)}, bf16[32,4096]{1,0:T(8,128)(2,1)S(1)}, u32[]{:S(2)}, u32[]{:S(2)}) collective-permute-start(bf16[32,4096]{1,0:T(8,128)(2,1)S(1)} %get-tuple-element.85.refs_6_), channel_id=1, source_target_pairs={{0,4},{1,5},{2,6},{3,7},{4,8},{5,9},{6,10},{7,11},{8,12},{9,13},{1... | collective-permute-start | bytes 786440 | tf_op jit(solution)/shard_map/ppermute | solution.py:192
  45.6 13.3 %collective-permute-start.15 = (bf16[32,512]{1,0:T(8,128)(2,1)S(1)}, bf16[32,512]{1,0:T(8,128)(2,1)S(1)}, u32[]{:S(2)}, u32[]{:S(2)}) collective-permute-start(bf16[32,512]{1,0:T(8,128)(2,1)S(1)} %get-tuple-element.86), channel_id=1, source_target_pairs={{0,5},{1,6},{2,7},{3,4},{4,9},{5,10},{6,11},{7,8},{8,13},{9,14},{1... | collective-permute-start | bytes 98312 | tf_op jit(solution)/shard_map/ppermute | solution.py:192
  50.8 9.1 %collective-permute-start.16 = (bf16[32,512]{1,0:T(8,128)(2,1)S(1)}, bf16[32,512]{1,0:T(8,128)(2,1)S(1)}, u32[]{:S(2)}, u32[]{:S(2)}) collective-permute-start(bf16[32,512]{1,0:T(8,128)(2,1)S(1)} %get-tuple-element.87), channel_id=1, source_target_pairs={{0,7},{1,4},{2,5},{3,6},{4,11},{5,8},{6,9},{7,10},{8,15},{9,12},{1... | collective-permute-start | bytes 98312 | tf_op jit(solution)/shard_map/ppermute | solution.py:192
  53.3 13.8 %collective-permute-start.23 = (bf16[32,4096]{1,0:T(8,128)(2,1)S(1)}, bf16[32,4096]{1,0:T(8,128)(2,1)S(1)}, u32[]{:S(2)}, u32[]{:S(2)}) collective-permute-start(bf16[32,4096]{1,0:T(8,128)(2,1)S(1)} %get-tuple-element.91.refs_6_), channel_id=1, source_target_pairs={{0,4},{1,5},{2,6},{3,7},{4,8},{5,9},{6,10},{7,11},{8,12},{9,13},{1... | collective-permute-start | bytes 786440 | tf_op jit(solution)/shard_map/ppermute | solution.py:192
  53.4 12.5 %collective-permute-start.24 = (bf16[32,512]{1,0:T(8,128)(2,1)S(1)}, bf16[32,512]{1,0:T(8,128)(2,1)S(1)}, u32[]{:S(2)}, u32[]{:S(2)}) collective-permute-start(bf16[32,512]{1,0:T(8,128)(2,1)S(1)} %get-tuple-element.96), channel_id=1, source_target_pairs={{0,5},{1,6},{2,7},{3,4},{4,9},{5,10},{6,11},{7,8},{8,13},{9,14},{1... | collective-permute-start | bytes 98312 | tf_op jit(solution)/shard_map/ppermute | solution.py:192
  58.9 8.2 %collective-permute-start.25 = (bf16[32,512]{1,0:T(8,128)(2,1)S(1)}, bf16[32,512]{1,0:T(8,128)(2,1)S(1)}, u32[]{:S(2)}, u32[]{:S(2)}) collective-permute-start(bf16[32,512]{1,0:T(8,128)(2,1)S(1)} %get-tuple-element.97), channel_id=1, source_target_pairs={{0,7},{1,4},{2,5},{3,6},{4,11},{5,8},{6,9},{7,10},{8,15},{9,12},{1... | collective-permute-start | bytes 98312 | tf_op jit(solution)/shard_map/ppermute | solution.py:192
  60.7 13.8 %collective-permute-start.20 = (bf16[32,4096]{1,0:T(8,128)(2,1)S(1)}, bf16[32,4096]{1,0:T(8,128)(2,1)S(1)}, u32[]{:S(2)}, u32[]{:S(2)}) collective-permute-start(bf16[32,4096]{1,0:T(8,128)(2,1)S(1)} %get-tuple-element.93.refs_6_), channel_id=1, source_target_pairs={{0,4},{1,5},{2,6},{3,7},{4,8},{5,9},{6,10},{7,11},{8,12},{9,13},{1... | collective-permute-start | bytes 786440 | tf_op jit(solution)/shard_map/ppermute | solution.py:192
  60.7 12.7 %collective-permute-start.21 = (bf16[32,512]{1,0:T(8,128)(2,1)S(1)}, bf16[32,512]{1,0:T(8,128)(2,1)S(1)}, u32[]{:S(2)}, u32[]{:S(2)}) collective-permute-start(bf16[32,512]{1,0:T(8,128)(2,1)S(1)} %get-tuple-element.94), channel_id=1, source_target_pairs={{0,5},{1,6},{2,7},{3,4},{4,9},{5,10},{6,11},{7,8},{8,13},{9,14},{1... | collective-permute-start | bytes 98312 | tf_op jit(solution)/shard_map/ppermute | solution.py:192
  65.9 8.6 %collective-permute-start.22 = (bf16[32,512]{1,0:T(8,128)(2,1)S(1)}, bf16[32,512]{1,0:T(8,128)(2,1)S(1)}, u32[]{:S(2)}, u32[]{:S(2)}) collective-permute-start(bf16[32,512]{1,0:T(8,128)(2,1)S(1)} %get-tuple-element.95), channel_id=1, source_target_pairs={{0,7},{1,4},{2,5},{3,6},{4,11},{5,8},{6,9},{7,10},{8,15},{9,12},{1... | collective-permute-start | bytes 98312 | tf_op jit(solution)/shard_map/ppermute | solution.py:192
  67.9 13.8 %collective-permute-start.29 = (bf16[32,4096]{1,0:T(8,128)(2,1)S(1)}, bf16[32,4096]{1,0:T(8,128)(2,1)S(1)}, u32[]{:S(2)}, u32[]{:S(2)}) collective-permute-start(bf16[32,4096]{1,0:T(8,128)(2,1)S(1)} %get-tuple-element.99.refs_6_), channel_id=1, source_target_pairs={{0,4},{1,5},{2,6},{3,7},{4,8},{5,9},{6,10},{7,11},{8,12},{9,13},{1... | collective-permute-start | bytes 786440 | tf_op jit(solution)/shard_map/ppermute | solution.py:192
  67.9 12.6 %collective-permute-start.30 = (bf16[32,512]{1,0:T(8,128)(2,1)S(1)}, bf16[32,512]{1,0:T(8,128)(2,1)S(1)}, u32[]{:S(2)}, u32[]{:S(2)}) collective-permute-start(bf16[32,512]{1,0:T(8,128)(2,1)S(1)} %get-tuple-element.104), channel_id=1, source_target_pairs={{0,5},{1,6},{2,7},{3,4},{4,9},{5,10},{6,11},{7,8},{8,13},{9,14},{1... | collective-permute-start | bytes 98312 | tf_op jit(solution)/shard_map/ppermute | solution.py:192
  73.5 8.2 %collective-permute-start.31 = (bf16[32,512]{1,0:T(8,128)(2,1)S(1)}, bf16[32,512]{1,0:T(8,128)(2,1)S(1)}, u32[]{:S(2)}, u32[]{:S(2)}) collective-permute-start(bf16[32,512]{1,0:T(8,128)(2,1)S(1)} %get-tuple-element.105), channel_id=1, source_target_pairs={{0,7},{1,4},{2,5},{3,6},{4,11},{5,8},{6,9},{7,10},{8,15},{9,12},{1... | collective-permute-start | bytes 98312 | tf_op jit(solution)/shard_map/ppermute | solution.py:192
  75.2 13.8 %collective-permute-start.26 = (bf16[32,4096]{1,0:T(8,128)(2,1)S(1)}, bf16[32,4096]{1,0:T(8,128)(2,1)S(1)}, u32[]{:S(2)}, u32[]{:S(2)}) collective-permute-start(bf16[32,4096]{1,0:T(8,128)(2,1)S(1)} %get-tuple-element.101.refs_6_), channel_id=1, source_target_pairs={{0,4},{1,5},{2,6},{3,7},{4,8},{5,9},{6,10},{7,11},{8,12},{9,13},{1... | collective-permute-start | bytes 786440 | tf_op jit(solution)/shard_map/ppermute | solution.py:192
  75.3 12.7 %collective-permute-start.27 = (bf16[32,512]{1,0:T(8,128)(2,1)S(1)}, bf16[32,512]{1,0:T(8,128)(2,1)S(1)}, u32[]{:S(2)}, u32[]{:S(2)}) collective-permute-start(bf16[32,512]{1,0:T(8,128)(2,1)S(1)} %get-tuple-element.102), channel_id=1, source_target_pairs={{0,5},{1,6},{2,7},{3,4},{4,9},{5,10},{6,11},{7,8},{8,13},{9,14},{1... | collective-permute-start | bytes 98312 | tf_op jit(solution)/shard_map/ppermute | solution.py:192
  80.5 8.5 %collective-permute-start.28 = (bf16[32,512]{1,0:T(8,128)(2,1)S(1)}, bf16[32,512]{1,0:T(8,128)(2,1)S(1)}, u32[]{:S(2)}, u32[]{:S(2)}) collective-permute-start(bf16[32,512]{1,0:T(8,128)(2,1)S(1)} %get-tuple-element.103), channel_id=1, source_target_pairs={{0,7},{1,4},{2,5},{3,6},{4,11},{5,8},{6,9},{7,10},{8,15},{9,12},{1... | collective-permute-start | bytes 98312 | tf_op jit(solution)/shard_map/ppermute | solution.py:192
  82.4 13.9 %collective-permute-start.35 = (bf16[32,4096]{1,0:T(8,128)(2,1)S(1)}, bf16[32,4096]{1,0:T(8,128)(2,1)S(1)}, u32[]{:S(2)}, u32[]{:S(2)}) collective-permute-start(bf16[32,4096]{1,0:T(8,128)(2,1)S(1)} %get-tuple-element.107.refs_6_), channel_id=1, source_target_pairs={{0,4},{1,5},{2,6},{3,7},{4,8},{5,9},{6,10},{7,11},{8,12},{9,13},{1... | collective-permute-start | bytes 786440 | tf_op jit(solution)/shard_map/ppermute | solution.py:192
  82.5 12.6 %collective-permute-start.36 = (bf16[32,512]{1,0:T(8,128)(2,1)S(1)}, bf16[32,512]{1,0:T(8,128)(2,1)S(1)}, u32[]{:S(2)}, u32[]{:S(2)}) collective-permute-start(bf16[32,512]{1,0:T(8,128)(2,1)S(1)} %get-tuple-element.112), channel_id=1, source_target_pairs={{0,5},{1,6},{2,7},{3,4},{4,9},{5,10},{6,11},{7,8},{8,13},{9,14},{1... | collective-permute-start | bytes 98312 | tf_op jit(solution)/shard_map/ppermute | solution.py:192
  88.0 8.3 %collective-permute-start.37 = (bf16[32,512]{1,0:T(8,128)(2,1)S(1)}, bf16[32,512]{1,0:T(8,128)(2,1)S(1)}, u32[]{:S(2)}, u32[]{:S(2)}) collective-permute-start(bf16[32,512]{1,0:T(8,128)(2,1)S(1)} %get-tuple-element.113), channel_id=1, source_target_pairs={{0,7},{1,4},{2,5},{3,6},{4,11},{5,8},{6,9},{7,10},{8,15},{9,12},{1... | collective-permute-start | bytes 98312 | tf_op jit(solution)/shard_map/ppermute | solution.py:192
  89.7 13.7 %collective-permute-start.32 = (bf16[32,4096]{1,0:T(8,128)(2,1)S(1)}, bf16[32,4096]{1,0:T(8,128)(2,1)S(1)}, u32[]{:S(2)}, u32[]{:S(2)}) collective-permute-start(bf16[32,4096]{1,0:T(8,128)(2,1)S(1)} %get-tuple-element.109.refs_6_), channel_id=1, source_target_pairs={{0,4},{1,5},{2,6},{3,7},{4,8},{5,9},{6,10},{7,11},{8,12},{9,13},{1... | collective-permute-start | bytes 786440 | tf_op jit(solution)/shard_map/ppermute | solution.py:192
  89.8 12.7 %collective-permute-start.33 = (bf16[32,512]{1,0:T(8,128)(2,1)S(1)}, bf16[32,512]{1,0:T(8,128)(2,1)S(1)}, u32[]{:S(2)}, u32[]{:S(2)}) collective-permute-start(bf16[32,512]{1,0:T(8,128)(2,1)S(1)} %get-tuple-element.110), channel_id=1, source_target_pairs={{0,5},{1,6},{2,7},{3,4},{4,9},{5,10},{6,11},{7,8},{8,13},{9,14},{1... | collective-permute-start | bytes 98312 | tf_op jit(solution)/shard_map/ppermute | solution.py:192
  95.1 8.4 %collective-permute-start.34 = (bf16[32,512]{1,0:T(8,128)(2,1)S(1)}, bf16[32,512]{1,0:T(8,128)(2,1)S(1)}, u32[]{:S(2)}, u32[]{:S(2)}) collective-permute-start(bf16[32,512]{1,0:T(8,128)(2,1)S(1)} %get-tuple-element.111), channel_id=1, source_target_pairs={{0,7},{1,4},{2,5},{3,6},{4,11},{5,8},{6,9},{7,10},{8,15},{9,12},{1... | collective-permute-start | bytes 98312 | tf_op jit(solution)/shard_map/ppermute | solution.py:192
  97.0 13.8 %collective-permute-start.41 = (bf16[32,4096]{1,0:T(8,128)(2,1)S(1)}, bf16[32,4096]{1,0:T(8,128)(2,1)S(1)}, u32[]{:S(2)}, u32[]{:S(2)}) collective-permute-start(bf16[32,4096]{1,0:T(8,128)(2,1)S(1)} %get-tuple-element.115.refs_6_), channel_id=1, source_target_pairs={{0,4},{1,5},{2,6},{3,7},{4,8},{5,9},{6,10},{7,11},{8,12},{9,13},{1... | collective-permute-start | bytes 786440 | tf_op jit(solution)/shard_map/ppermute | solution.py:192
  97.1 12.6 %collective-permute-start.42 = (bf16[32,512]{1,0:T(8,128)(2,1)S(1)}, bf16[32,512]{1,0:T(8,128)(2,1)S(1)}, u32[]{:S(2)}, u32[]{:S(2)}) collective-permute-start(bf16[32,512]{1,0:T(8,128)(2,1)S(1)} %get-tuple-element.120), channel_id=1, source_target_pairs={{0,5},{1,6},{2,7},{3,4},{4,9},{5,10},{6,11},{7,8},{8,13},{9,14},{1... | collective-permute-start | bytes 98312 | tf_op jit(solution)/shard_map/ppermute | solution.py:192
  102.5 8.3 %collective-permute-start.43 = (bf16[32,512]{1,0:T(8,128)(2,1)S(1)}, bf16[32,512]{1,0:T(8,128)(2,1)S(1)}, u32[]{:S(2)}, u32[]{:S(2)}) collective-permute-start(bf16[32,512]{1,0:T(8,128)(2,1)S(1)} %get-tuple-element.121), channel_id=1, source_target_pairs={{0,7},{1,4},{2,5},{3,6},{4,11},{5,8},{6,9},{7,10},{8,15},{9,12},{1... | collective-permute-start | bytes 98312 | tf_op jit(solution)/shard_map/ppermute | solution.py:192
  104.2 13.4 %collective-permute-start.38 = (bf16[32,4096]{1,0:T(8,128)(2,1)S(1)}, bf16[32,4096]{1,0:T(8,128)(2,1)S(1)}, u32[]{:S(2)}, u32[]{:S(2)}) collective-permute-start(bf16[32,4096]{1,0:T(8,128)(2,1)S(1)} %get-tuple-element.117.refs_6_), channel_id=1, source_target_pairs={{0,4},{1,5},{2,6},{3,7},{4,8},{5,9},{6,10},{7,11},{8,12},{9,13},{1... | collective-permute-start | bytes 786440 | tf_op jit(solution)/shard_map/ppermute | solution.py:192
  104.3 12.7 %collective-permute-start.39 = (bf16[32,512]{1,0:T(8,128)(2,1)S(1)}, bf16[32,512]{1,0:T(8,128)(2,1)S(1)}, u32[]{:S(2)}, u32[]{:S(2)}) collective-permute-start(bf16[32,512]{1,0:T(8,128)(2,1)S(1)} %get-tuple-element.118), channel_id=1, source_target_pairs={{0,5},{1,6},{2,7},{3,4},{4,9},{5,10},{6,11},{7,8},{8,13},{9,14},{1... | collective-permute-start | bytes 98312 | tf_op jit(solution)/shard_map/ppermute | solution.py:192
  109.7 7.9 %collective-permute-start.40 = (bf16[32,512]{1,0:T(8,128)(2,1)S(1)}, bf16[32,512]{1,0:T(8,128)(2,1)S(1)}, u32[]{:S(2)}, u32[]{:S(2)}) collective-permute-start(bf16[32,512]{1,0:T(8,128)(2,1)S(1)} %get-tuple-element.119), channel_id=1, source_target_pairs={{0,7},{1,4},{2,5},{3,6},{4,11},{5,8},{6,9},{7,10},{8,15},{9,12},{1... | collective-permute-start | bytes 98312 | tf_op jit(solution)/shard_map/ppermute | solution.py:192

commit v5 on v4

--- a/solution.py
+++ b/solution.py
@@ -23,16 +23,17 @@
     ]
     for copy in copies:
         copy.start()
-    brs, nzb = indices.shape
+    nzb, brs = indices.shape
     columns = brs * blks
     start = lax.axis_index("blk") * brs - HALO
     meta[brs * nzb] = lax.axis_index("section")
+    meta[brs * nzb + 1] = lax.axis_index("blk") % 2
     copies[0].wait()
 
     @pl.loop(0, brs)
     def _(i):
         for k in range(nzb):
-            col = raw[i, k] - start
+            col = raw[k, i] - start
             col = jnp.where(col < 0, col + columns, col)
             meta[i * nzb + k] = jnp.where(col >= columns, col - columns, col) * BLK
 
@@ -46,7 +47,7 @@
         functools.partial(load_kernel, blks),
         out_shape=(
             *(pltpu.VMEM(a.shape, a.dtype) for a in arrays),
-            pltpu.SMEM((indices.size + 1,), jnp.int32),
+            pltpu.SMEM((indices.size + 2,), jnp.int32),
         ),
         in_specs=[ANY] * 4,
         out_specs=(VMEM,) * 3 + (SMEM,),
@@ -59,15 +60,17 @@
 
 def layer_kernel(tick, src_row, rows, brs, nzb, own_slot, prev_slot, aliased, *refs):
     refs = list(refs)
-    meta, main, low, high, w, bias = refs[:6]
+    meta, main, across, inside, w, bias = refs[:6]
     del refs[:6]
-    prev = refs.pop(0) if prev_slot is not None else None
+    prev = None
+    if prev_slot is not None:
+        prev = refs.pop(0)
     if aliased:
         refs.pop(0)
     emitted = refs.pop(0) if prev_slot is not None or own_slot is not None else None
-    left = right = None
+    outer = None
     if own_slot is None:
-        out, left, right, xbuf, sems = refs
+        out, outer, xbuf, sems = refs
     else:
         out, xbuf, sems = refs
     edge = HALO * BLK
@@ -88,13 +91,14 @@
         before = write(prev, prev_slot, 0, brs, sems.at[0])
         before.start()
     live = meta[brs * nzb] >= tick
+    odd = meta[brs * nzb + 1]
 
     @pl.when(live)
     def _():
         src = pl.ds(src_row, rows)
-        xbuf[:, 0:edge] = low[src, :]
         xbuf[:, edge : edge + width] = main[src, :]
-        xbuf[:, edge + width : edge + width + edge] = high[src, :]
+        xbuf[:, pl.ds(pl.multiple_of(odd * (edge + width), BLK), edge)] = across[src, :]
+        xbuf[:, pl.ds(pl.multiple_of((1 - odd) * (edge + width), BLK), edge)] = inside[src, :]
         for i in range(brs):
             picked = jnp.concatenate(
                 [xbuf[:, pl.ds(pl.multiple_of(meta[i * nzb + k], BLK), BLK)] for k in range(nzb)], axis=1
@@ -103,19 +107,16 @@
             summed = jnp.dot(picked, w[i], preferred_element_type=jnp.float32) + bias[:, cols]
             made = jnp.maximum(summed, 0.0).astype(jnp.bfloat16)
             out[:, cols] = made
-            if left is not None and i < HALO:
-                left[:, cols] = made
-            if right is not None and i >= brs - HALO:
-                right[:, pl.ds((i - brs + HALO) * BLK, BLK)] = made
             if own and (i + 1) % (brs // pieces) == 0:
                 own[i // (brs // pieces)].start()
+        if outer is not None:
+            outer[...] = out[:, pl.ds(pl.multiple_of(odd * (width - edge), BLK), edge)]
 
     @pl.when(jnp.logical_not(live))
     def _():
         out[...] = jnp.zeros_like(out)
-        if left is not None:
-            left[...] = jnp.zeros_like(left)
-            right[...] = jnp.zeros_like(right)
+        if outer is not None:
+            outer[...] = jnp.zeros_like(outer)
         for copy in own:
             copy.start()
 
@@ -126,14 +127,14 @@
 
 
 def apply_layer(tick, src_row, row, rows, last, operands, prev, prev_slot, emitted, emitted_aval):
-    meta, main, low, high, w, bias = operands
+    meta, main, across, inside, w, bias = operands
     brs, depth = w.shape[:2]
     nzb = depth // BLK
     width = brs * BLK
     edge = HALO * BLK
     args = [
         pltpu.with_memory_space_constraint(meta, pltpu.SMEM),
-        *(pltpu.with_memory_space_constraint(a, pltpu.VMEM) for a in (main, low, high, w, bias)),
+        *(pltpu.with_memory_space_constraint(a, pltpu.VMEM) for a in (main, across, inside, w, bias)),
     ]
     specs = [SMEM] + [VMEM] * 5
     out_shape = []
@@ -156,8 +157,8 @@
     if last:
         scratch.insert(0, pltpu.VMEM((rows, width), jnp.bfloat16))
     else:
-        out_shape += [pltpu.VMEM((rows, cols), jnp.bfloat16) for cols in (width, edge, edge)]
-        out_specs += [VMEM] * 3
+        out_shape += [pltpu.VMEM((rows, cols), jnp.bfloat16) for cols in (width, edge)]
+        out_specs += [VMEM] * 2
     body = functools.partial(
         layer_kernel, tick, src_row, rows, brs, nzb, (tick, row) if last else None, prev_slot, emitted is not None
     )
@@ -170,10 +171,32 @@
         input_output_aliases=aliases,
         compiler_params=pltpu.CompilerParams(vmem_limit_bytes=8 * 1024 * 1024),
         cost_estimate=pl.CostEstimate(
-            flops=20 * rows * brs * nzb * BLK * BLK, bytes_accessed=20 * w.size, transcendentals=0
+            flops=14 * rows * brs * nzb * BLK * BLK, bytes_accessed=14 * w.size, transcendentals=0
         ),
         name=f"layer_t{tick}_r{row}",
     )(*args)
+
+
+def edge_kernel(meta, main, after, edge):
+    del after
+    odd = meta[meta.shape[0] - 1]
+    width = main.shape[1]
+    edge[...] = main[:, pl.ds(pl.multiple_of((1 - odd) * (width - HALO * BLK), BLK), HALO * BLK)]
+
+
+def inner_edge(meta, main, after):
+    return pl.pallas_call(
+        edge_kernel,
+        out_shape=pltpu.VMEM((main.shape[0], HALO * BLK), main.dtype),
+        in_specs=[SMEM, VMEM, ANY],
+        out_specs=VMEM,
+        compiler_params=pltpu.CompilerParams(vmem_limit_bytes=1024 * 1024),
+        name="edge",
+    )(
+        pltpu.with_memory_space_constraint(meta, pltpu.SMEM),
+        pltpu.with_memory_space_constraint(main, pltpu.VMEM),
+        after,
+    )
 
 
 def shards(sections, blks, pending_groups, coefficient_tiles, source_block_indices, additive_offsets):
@@ -183,41 +206,54 @@
     edge = HALO * BLK
     emitted_aval = jax.ShapeDtypeStruct((TICKS, height, width), jnp.bfloat16)
 
-    def hop(values, step, shift):
+    def hop(values, step, place):
         pairs = [
-            (s * blks + i, (s + step) % sections * blks + (i + shift) % blks)
+            (s * blks + i, (s + step) % sections * blks + place(i) % blks)
             for s in range(sections)
             for i in range(blks)
         ]
         return lax.ppermute(values, ("section", "blk"), pairs)
 
-    low = hop(pending_groups[:, width - edge :], 0, 1)
-    high = hop(pending_groups[:, :edge], 0, -1)
+    def across(i):
+        return i + 1 if i % 2 else i - 1
+
+    def inside(i):
+        return i - 1 if i % 2 else i + 1
+
+    odd = lax.axis_index("blk") % 2
+    outer = lax.dynamic_slice_in_dim(pending_groups, odd * (width - edge), edge, axis=1)
+    inner = lax.dynamic_slice_in_dim(pending_groups, (1 - odd) * (width - edge), edge, axis=1)
+    far, near = hop(outer, 0, across), hop(inner, 0, inside)
     state, w, bias, meta = load(
         blks,
         pending_groups,
         coefficient_tiles.reshape(block_rows, nzb * BLK, BLK),
         additive_offsets,
-        source_block_indices[0],
-    )
-    parts = [(state, low, high, c * rows) for c in range(CHUNKS)]
-    emitted = prev = prev_slot = None
+        source_block_indices[0].T,
+    )
+    parts = [(state, far)] * CHUNKS
+    emitted = prev = sent = prev_slot = None
     for tick in range(TICKS):
         last = tick + 1 == TICKS
         for c in range(CHUNKS):
-            main, low, high, src_row = parts[c]
+            main, far = parts[c]
+            src_row = c * rows
+            if tick > 0:
+                near = hop(inner_edge(meta, main, emitted if sent is None else sent), 0, inside)
+                src_row = 0
             outs = list(
                 apply_layer(
-                    tick, src_row, c * rows, rows, last, (meta, main, low, high, w, bias), prev, prev_slot, emitted, emitted_aval
+                    tick, src_row, c * rows, rows, last, (meta, main, far, near, w, bias), prev, prev_slot, emitted, emitted_aval
                 )
             )
             if prev is not None or last:
                 emitted = outs.pop(0)
             prev = prev_slot = None
             if not last:
-                prev, left, right = outs
+                prev, outer = outs
                 prev_slot = (tick, c * rows)
-                parts[c] = (hop(prev, 1, 0), hop(right, 1, 1), hop(left, 1, -1), 0)
+                sent = hop(outer, 1, across)
+                parts[c] = (hop(prev, 1, lambda i: i), sent)
     return emitted
 
 

time: 119 us -> 153 us (1.29)
  waiting for transfers between devices: 63.5 us -> 119 us
  starting transfers between devices: 35.3 us -> 13.6 us
    ppermute x44, waiting for transfers between devices: 63.5 us -> 119 us  [hop(): return lax.ppermute(values, ('section', 'blk'), pairs)]
    ppermute x44, starting transfers between devices: 35.3 us -> 13.6 us  [hop(): return lax.ppermute(values, ('section', 'blk'), pairs)]
  transfers between devices with their start and end apart: 44 -> 44, of which waited for: 27 -> 26; matrix products, arithmetic and copies ran while one was open for 1% -> 0% of each run, Pallas kernels for 13% -> 10%
where the time goes in v5:
time: 153 us; the launch traced here: 151 us
  waiting for transfers between devices  119 us (78%)
  Pallas kernels  17.2 us (11%)
  starting transfers between devices  13.6 us (9%)
    ppermute x44, waiting for transfers between devices, hop(): return lax.ppermute(values, ('section', 'blk'), pairs)  119 us
    ppermute x44, starting transfers between devices, hop(): return lax.ppermute(values, ('section', 'blk'), pairs)  13.6 us
    pallas_call x16, Pallas kernels, apply_layer(): pl.pallas_call(body, out_shape=tuple(out_shape), in_specs=specs, out_spec...  13.5 us
    pallas_call x1, Pallas kernels, load(): pl.pallas_call(functools.partial(load_kernel, blks), out_shape=(*(pltpu.V...  3.62 us
  transfers between devices with their start and end apart: 44, of which 26 were waited for; matrix products, arithmetic and copies ran while one was open for 0% of the time, Pallas kernels for 10%

profile of v5, /device:TPU:1, one launch (start us, length us, event | category | flops | bytes accessed | tf_op | source)
XLA Modules:
  0.0 151.5 jit_solution(4574539322650413490)
XLA Ops:
  0.0 0.9 constant_dynamic-slice_fusion
  0.9 2.7 %collective-permute-start = (bf16[64,512]{1,0:T(8,128)(2,1)S(1)}, bf16[64,512]{1,0:T(8,128)(2,1)S(1)}, u32[]{:S(2)}, u32[]{:S(2)}) collective-permute-start(bf16[64,512]{1,0:T(8,128)(2,1)S(1)} %get-tuple-element.96), channel_id=1, source_target_pairs={{0,3},{1,2},{2,1},{3,0},{4,7},{5,6},{6,5},{7,4},{8,11},{9,10},{10,... | collective-permute-start | bytes 196616 | tf_op jit(solution)/shard_map/ppermute | solution.py:215
  3.6 3.6 %load.1 = (bf16[64,4096]{1,0:T(8,128)(2,1)S(1)}, bf16[32,1024,128]{2,1,0:T(8,128)(2,1)S(1)}, f32[1,4096]{1,0:T(1,128)S(1)}, s32[258]{0:T(512)S(4)}) custom-call(bf16[64,4096]{1,0:T(8,128)(2,1)} %state.1, bf16[32,1024,128]{2,1,0:T(8,128)(2,1)} %bitcast.4, f32[1,4096]{1,0:T(1,128)} %bias.1, s32[8,32]{1,0:T(8,128)} %bitcast.5), custom_call_target="tpu_custom_call" | custom-call | bytes 8388608 | tf_op jit(solution)/shard_map/load/pallas_call | solution.py:46
  7.2 1.5 layer_t0_r0.1
  8.7 1.3 collective-permute-start.4
  10.0 1.5 layer_t0_r32.1
  11.5 2.0 %collective-permute-start.3 = (bf16[32,512]{1,0:T(8,128)(2,1)S(1)}, bf16[32,512]{1,0:T(8,128)(2,1)S(1)}, u32[]{:S(2)}, u32[]{:S(2)}) collective-permute-start(bf16[32,512]{1,0:T(8,128)(2,1)S(1)} %get-tuple-element.56), channel_id=1, source_target_pairs={{0,7},{1,6},{2,5},{3,4},{4,11},{5,10},{6,9},{7,8},{8,15},{9,14},{1... | collective-permute-start | bytes 98312 | tf_op jit(solution)/shard_map/ppermute | solution.py:215
  13.5 1.3 collective-permute-start.2
  14.7 2.0 %collective-permute-start.5 = (bf16[32,512]{1,0:T(8,128)(2,1)S(1)}, bf16[32,512]{1,0:T(8,128)(2,1)S(1)}, u32[]{:S(2)}, u32[]{:S(2)}) collective-permute-start(bf16[32,512]{1,0:T(8,128)(2,1)S(1)} %get-tuple-element.57), channel_id=1, source_target_pairs={{0,7},{1,6},{2,5},{3,4},{4,11},{5,10},{6,9},{7,8},{8,15},{9,14},{1... | collective-permute-start | bytes 98312 | tf_op jit(solution)/shard_map/ppermute | solution.py:215
  16.7 4.6 %collective-permute-done.3.after.refs_2_ = bf16[32,512]{1,0:T(8,128)(2,1)S(1)} collective-permute-done((bf16[32,512]{1,0:T(8,128)(2,1)S(1)}, bf16[32,512]{1,0:T(8,128)(2,1)S(1)}, u32[]{:S(2)}, u32[]{:S(2)}) %collective-permute-start.3) | collective-permute-done | bytes 32800 | tf_op jit(solution)/shard_map/ppermute | solution.py:215
  21.3 5.8 %collective-permute-done.5.refs_2_ = bf16[32,512]{1,0:T(8,128)(2,1)S(1)} collective-permute-done((bf16[32,512]{1,0:T(8,128)(2,1)S(1)}, bf16[32,512]{1,0:T(8,128)(2,1)S(1)}, u32[]{:S(2)}, u32[]{:S(2)}) %collective-permute-start.5) | collective-permute-done | bytes 32800 | tf_op jit(solution)/shard_map/ppermute | solution.py:215
  27.1 0.7 layer_t1_r0.1
  27.8 0.1 collective-permute-start.7
  27.9 1.6 %collective-permute-start.11 = (bf16[32,4096]{1,0:T(8,128)(2,1)S(1)}, bf16[32,4096]{1,0:T(8,128)(2,1)S(1)}, u32[]{:S(2)}, u32[]{:S(2)}) collective-permute-start(bf16[32,4096]{1,0:T(8,128)(2,1)S(1)} %get-tuple-element.60.refs_6_), channel_id=1, source_target_pairs={{0,4},{1,5},{2,6},{3,7},{4,8},{5,9},{6,10},{7,11},{8,12},{9,13},{1... | collective-permute-start | bytes 786440 | tf_op jit(solution)/shard_map/ppermute | solution.py:215
  29.5 5.9 %collective-permute-done.7.after.refs_2_ = bf16[32,512]{1,0:T(8,128)(2,1)S(1)} collective-permute-done((bf16[32,512]{1,0:T(8,128)(2,1)S(1)}, bf16[32,512]{1,0:T(8,128)(2,1)S(1)}, u32[]{:S(2)}, u32[]{:S(2)}) %collective-permute-start.7) | collective-permute-done | bytes 32800 | tf_op jit(solution)/shard_map/ppermute | solution.py:215
  35.4 1.2 collective-permute-done.8.refs_3_
  36.6 0.7 layer_t1_r32.1
  37.4 0.1 collective-permute-start.10
  37.5 0.8 collective-permute-start.9
  38.3 6.7 %collective-permute-done.10.after.refs_2_ = bf16[32,512]{1,0:T(8,128)(2,1)S(1)} collective-permute-done((bf16[32,512]{1,0:T(8,128)(2,1)S(1)}, bf16[32,512]{1,0:T(8,128)(2,1)S(1)}, u32[]{:S(2)}, u32[]{:S(2)}) %collective-permute-start.10) | collective-permute-done | bytes 32800 | tf_op jit(solution)/shard_map/ppermute | solution.py:215
  45.0 1.2 collective-permute-done.12.refs_3_
  46.2 0.7 layer_t2_r0.1
  47.0 0.1 collective-permute-start.13
  47.1 0.1 collective-permute-start.17
  47.1 7.5 %collective-permute-done.13.after.refs_2_ = bf16[32,512]{1,0:T(8,128)(2,1)S(1)} collective-permute-done((bf16[32,512]{1,0:T(8,128)(2,1)S(1)}, bf16[32,512]{1,0:T(8,128)(2,1)S(1)}, u32[]{:S(2)}, u32[]{:S(2)}) %collective-permute-start.13) | collective-permute-done | bytes 32800 | tf_op jit(solution)/shard_map/ppermute | solution.py:215
  54.6 1.2 collective-permute-done.14.refs_3_
  55.8 0.7 layer_t2_r32.1
  56.6 0.1 collective-permute-start.16
  56.6 0.1 collective-permute-start.15
  56.7 7.5 %collective-permute-done.16.after.refs_2_ = bf16[32,512]{1,0:T(8,128)(2,1)S(1)} collective-permute-done((bf16[32,512]{1,0:T(8,128)(2,1)S(1)}, bf16[32,512]{1,0:T(8,128)(2,1)S(1)}, u32[]{:S(2)}, u32[]{:S(2)}) %collective-permute-start.16) | collective-permute-done | bytes 32800 | tf_op jit(solution)/shard_map/ppermute | solution.py:215
  64.2 1.2 collective-permute-done.18.refs_3_
  65.4 0.7 layer_t3_r0.1
  66.2 0.1 collective-permute-start.19
  66.2 0.1 collective-permute-start.23
  66.3 7.5 %collective-permute-done.19.after.refs_2_ = bf16[32,512]{1,0:T(8,128)(2,1)S(1)} collective-permute-done((bf16[32,512]{1,0:T(8,128)(2,1)S(1)}, bf16[32,512]{1,0:T(8,128)(2,1)S(1)}, u32[]{:S(2)}, u32[]{:S(2)}) %collective-permute-start.19) | collective-permute-done | bytes 32800 | tf_op jit(solution)/shard_map/ppermute | solution.py:215
  73.8 1.2 collective-permute-done.20.refs_3_
  75.0 0.7 layer_t3_r32.1
  75.9 7.5 %collective-permute-done.22.after.refs_2_ = bf16[32,512]{1,0:T(8,128)(2,1)S(1)} collective-permute-done((bf16[32,512]{1,0:T(8,128)(2,1)S(1)}, bf16[32,512]{1,0:T(8,128)(2,1)S(1)}, u32[]{:S(2)}, u32[]{:S(2)}) %collective-permute-start.22) | collective-permute-done | bytes 32800 | tf_op jit(solution)/shard_map/ppermute | solution.py:215
  83.4 1.2 collective-permute-done.24.refs_3_
  84.6 0.7 layer_t4_r0.1
  85.4 0.1 collective-permute-start.25
  85.5 7.5 %collective-permute-done.25.after.refs_2_ = bf16[32,512]{1,0:T(8,128)(2,1)S(1)} collective-permute-done((bf16[32,512]{1,0:T(8,128)(2,1)S(1)}, bf16[32,512]{1,0:T(8,128)(2,1)S(1)}, u32[]{:S(2)}, u32[]{:S(2)}) %collective-permute-start.25) | collective-permute-done | bytes 32800 | tf_op jit(solution)/shard_map/ppermute | solution.py:215
  93.0 1.2 collective-permute-done.26.refs_3_
  94.2 0.7 layer_t4_r32.1
  95.0 0.1 collective-permute-start.28
  95.1 7.5 %collective-permute-done.28.after.refs_2_ = bf16[32,512]{1,0:T(8,128)(2,1)S(1)} collective-permute-done((bf16[32,512]{1,0:T(8,128)(2,1)S(1)}, bf16[32,512]{1,0:T(8,128)(2,1)S(1)}, u32[]{:S(2)}, u32[]{:S(2)}) %collective-permute-start.28) | collective-permute-done | bytes 32800 | tf_op jit(solution)/shard_map/ppermute | solution.py:215
  102.6 1.2 collective-permute-done.30.refs_3_
  103.8 0.7 layer_t5_r0.1
  104.7 7.5 %collective-permute-done.31.after.refs_2_ = bf16[32,512]{1,0:T(8,128)(2,1)S(1)} collective-permute-done((bf16[32,512]{1,0:T(8,128)(2,1)S(1)}, bf16[32,512]{1,0:T(8,128)(2,1)S(1)}, u32[]{:S(2)}, u32[]{:S(2)}) %collective-permute-start.31) | collective-permute-done | bytes 32800 | tf_op jit(solution)/shard_map/ppermute | solution.py:215
  112.2 1.2 collective-permute-done.32.refs_3_
  113.4 0.7 layer_t5_r32.1
  114.3 7.5 %collective-permute-done.34.after.refs_2_ = bf16[32,512]{1,0:T(8,128)(2,1)S(1)} collective-permute-done((bf16[32,512]{1,0:T(8,128)(2,1)S(1)}, bf16[32,512]{1,0:T(8,128)(2,1)S(1)}, u32[]{:S(2)}, u32[]{:S(2)}) %collective-permute-start.34) | collective-permute-done | bytes 32800 | tf_op jit(solution)/shard_map/ppermute | solution.py:215
  121.8 1.2 collective-permute-done.36.refs_3_
  123.0 0.7 layer_t6_r0.1
  123.8 6.9 %collective-permute-done.37.after.refs_2_ = bf16[32,512]{1,0:T(8,128)(2,1)S(1)} collective-permute-done((bf16[32,512]{1,0:T(8,128)(2,1)S(1)}, bf16[32,512]{1,0:T(8,128)(2,1)S(1)}, u32[]{:S(2)}, u32[]{:S(2)}) %collective-permute-start.37) | collective-permute-done | bytes 32800 | tf_op jit(solution)/shard_map/ppermute | solution.py:215
  130.7 0.2 collective-permute-start.38
  130.9 1.0 collective-permute-done.38.refs_3_
  131.9 0.7 layer_t6_r32.1
  132.8 15.6 %collective-permute-done.40.after.refs_2_ = bf16[32,512]{1,0:T(8,128)(2,1)S(1)} collective-permute-done((bf16[32,512]{1,0:T(8,128)(2,1)S(1)}, bf16[32,512]{1,0:T(8,128)(2,1)S(1)}, u32[]{:S(2)}, u32[]{:S(2)}) %collective-permute-start.40) | collective-permute-done | bytes 32800 | tf_op jit(solution)/shard_map/ppermute | solution.py:215
  148.5 0.1 collective-permute-start.43
  148.6 0.4 collective-permute-start.41
  149.0 0.7 collective-permute-done.43.refs_3_
  149.7 0.8 layer_t7_r0.1.refs_6_
  150.5 0.8 layer_t7_r32.1
  (56 shorter events, 0.8 us)
Async XLA Ops:
  0.9 6.3 %collective-permute-start = (bf16[64,512]{1,0:T(8,128)(2,1)S(1)}, bf16[64,512]{1,0:T(8,128)(2,1)S(1)}, u32[]{:S(2)}, u32[]{:S(2)}) collective-permute-start(bf16[64,512]{1,0:T(8,128)(2,1)S(1)} %get-tuple-element.96), channel_id=1, source_target_pairs={{0,3},{1,2},{2,1},{3,0},{4,7},{5,6},{6,5},{7,4},{8,11},{9,10},{10,... | collective-permute-start | bytes 196616 | tf_op jit(solution)/shard_map/ppermute | solution.py:215
  3.6 3.6 %collective-permute-start.1 = (bf16[64,512]{1,0:T(8,128)(2,1)S(1)}, bf16[64,512]{1,0:T(8,128)(2,1)S(1)}, u32[]{:S(2)}, u32[]{:S(2)}) collective-permute-start(bf16[64,512]{1,0:T(8,128)(2,1)S(1)} %get-tuple-element.95), channel_id=1, source_target_pairs={{0,1},{1,0},{2,3},{3,2},{4,5},{5,4},{6,7},{7,6},{8,9},{9,8},{10,11... | collective-permute-start | bytes 196616 | tf_op jit(solution)/shard_map/ppermute | solution.py:215
  8.7 12.6 %collective-permute-start.4 = (bf16[32,4096]{1,0:T(8,128)(2,1)S(1)}, bf16[32,4096]{1,0:T(8,128)(2,1)S(1)}, u32[]{:S(2)}, u32[]{:S(2)}) collective-permute-start(bf16[32,4096]{1,0:T(8,128)(2,1)S(1)} %get-tuple-element.54.refs_6_), channel_id=1, source_target_pairs={{0,4},{1,5},{2,6},{3,7},{4,8},{5,9},{6,10},{7,11},{8,12},{9,13},{1... | collective-permute-start | bytes 786440 | tf_op jit(solution)/shard_map/ppermute | solution.py:215
  11.5 9.8 %collective-permute-start.3 = (bf16[32,512]{1,0:T(8,128)(2,1)S(1)}, bf16[32,512]{1,0:T(8,128)(2,1)S(1)}, u32[]{:S(2)}, u32[]{:S(2)}) collective-permute-start(bf16[32,512]{1,0:T(8,128)(2,1)S(1)} %get-tuple-element.56), channel_id=1, source_target_pairs={{0,7},{1,6},{2,5},{3,4},{4,11},{5,10},{6,9},{7,8},{8,15},{9,14},{1... | collective-permute-start | bytes 98312 | tf_op jit(solution)/shard_map/ppermute | solution.py:215
  13.5 16.0 %collective-permute-start.2 = (bf16[32,4096]{1,0:T(8,128)(2,1)S(1)}, bf16[32,4096]{1,0:T(8,128)(2,1)S(1)}, u32[]{:S(2)}, u32[]{:S(2)}) collective-permute-start(bf16[32,4096]{1,0:T(8,128)(2,1)S(1)} %get-tuple-element.55.refs_6_), channel_id=1, source_target_pairs={{0,4},{1,5},{2,6},{3,7},{4,8},{5,9},{6,10},{7,11},{8,12},{9,13},{1... | collective-permute-start | bytes 786440 | tf_op jit(solution)/shard_map/ppermute | solution.py:215
  14.7 12.3 %collective-permute-start.5 = (bf16[32,512]{1,0:T(8,128)(2,1)S(1)}, bf16[32,512]{1,0:T(8,128)(2,1)S(1)}, u32[]{:S(2)}, u32[]{:S(2)}) collective-permute-start(bf16[32,512]{1,0:T(8,128)(2,1)S(1)} %get-tuple-element.57), channel_id=1, source_target_pairs={{0,7},{1,6},{2,5},{3,4},{4,11},{5,10},{6,9},{7,8},{8,15},{9,14},{1... | collective-permute-start | bytes 98312 | tf_op jit(solution)/shard_map/ppermute | solution.py:215
  21.3 5.8 %collective-permute-start.6 = (bf16[32,512]{1,0:T(8,128)(2,1)S(1)}, bf16[32,512]{1,0:T(8,128)(2,1)S(1)}, u32[]{:S(2)}, u32[]{:S(2)}) collective-permute-start(bf16[32,512]{1,0:T(8,128)(2,1)S(1)} %edge.14), channel_id=1, source_target_pairs={{0,1},{1,0},{2,3},{3,2},{4,5},{5,4},{6,7},{7,6},{8,9},{9,8},{10,11... | collective-permute-start | bytes 98312 | tf_op jit(solution)/shard_map/ppermute | solution.py:215
  27.8 7.6 %collective-permute-start.7 = (bf16[32,512]{1,0:T(8,128)(2,1)S(1)}, bf16[32,512]{1,0:T(8,128)(2,1)S(1)}, u32[]{:S(2)}, u32[]{:S(2)}) collective-permute-start(bf16[32,512]{1,0:T(8,128)(2,1)S(1)} %get-tuple-element.59), channel_id=1, source_target_pairs={{0,7},{1,6},{2,5},{3,4},{4,11},{5,10},{6,9},{7,8},{8,15},{9,14},{1... | collective-permute-start | bytes 98312 | tf_op jit(solution)/shard_map/ppermute | solution.py:215
  27.9 17.1 %collective-permute-start.11 = (bf16[32,4096]{1,0:T(8,128)(2,1)S(1)}, bf16[32,4096]{1,0:T(8,128)(2,1)S(1)}, u32[]{:S(2)}, u32[]{:S(2)}) collective-permute-start(bf16[32,4096]{1,0:T(8,128)(2,1)S(1)} %get-tuple-element.60.refs_6_), channel_id=1, source_target_pairs={{0,4},{1,5},{2,6},{3,7},{4,8},{5,9},{6,10},{7,11},{8,12},{9,13},{1... | collective-permute-start | bytes 786440 | tf_op jit(solution)/shard_map/ppermute | solution.py:215
  35.4 1.2 collective-permute-start.8
  37.4 7.6 %collective-permute-start.10 = (bf16[32,512]{1,0:T(8,128)(2,1)S(1)}, bf16[32,512]{1,0:T(8,128)(2,1)S(1)}, u32[]{:S(2)}, u32[]{:S(2)}) collective-permute-start(bf16[32,512]{1,0:T(8,128)(2,1)S(1)} %get-tuple-element.63), channel_id=1, source_target_pairs={{0,7},{1,6},{2,5},{3,4},{4,11},{5,10},{6,9},{7,8},{8,15},{9,14},{1... | collective-permute-start | bytes 98312 | tf_op jit(solution)/shard_map/ppermute | solution.py:215
  37.5 17.2 %collective-permute-start.9 = (bf16[32,4096]{1,0:T(8,128)(2,1)S(1)}, bf16[32,4096]{1,0:T(8,128)(2,1)S(1)}, u32[]{:S(2)}, u32[]{:S(2)}) collective-permute-start(bf16[32,4096]{1,0:T(8,128)(2,1)S(1)} %get-tuple-element.62.refs_6_), channel_id=1, source_target_pairs={{0,4},{1,5},{2,6},{3,7},{4,8},{5,9},{6,10},{7,11},{8,12},{9,13},{1... | collective-permute-start | bytes 786440 | tf_op jit(solution)/shard_map/ppermute | solution.py:215
  45.0 1.2 collective-permute-start.12
  47.0 7.6 %collective-permute-start.13 = (bf16[32,512]{1,0:T(8,128)(2,1)S(1)}, bf16[32,512]{1,0:T(8,128)(2,1)S(1)}, u32[]{:S(2)}, u32[]{:S(2)}) collective-permute-start(bf16[32,512]{1,0:T(8,128)(2,1)S(1)} %get-tuple-element.65), channel_id=1, source_target_pairs={{0,7},{1,6},{2,5},{3,4},{4,11},{5,10},{6,9},{7,8},{8,15},{9,14},{1... | collective-permute-start | bytes 98312 | tf_op jit(solution)/shard_map/ppermute | solution.py:215
  47.1 17.2 %collective-permute-start.17 = (bf16[32,4096]{1,0:T(8,128)(2,1)S(1)}, bf16[32,4096]{1,0:T(8,128)(2,1)S(1)}, u32[]{:S(2)}, u32[]{:S(2)}) collective-permute-start(bf16[32,4096]{1,0:T(8,128)(2,1)S(1)} %get-tuple-element.66.refs_6_), channel_id=1, source_target_pairs={{0,4},{1,5},{2,6},{3,7},{4,8},{5,9},{6,10},{7,11},{8,12},{9,13},{1... | collective-permute-start | bytes 786440 | tf_op jit(solution)/shard_map/ppermute | solution.py:215
  54.6 1.2 collective-permute-start.14
  56.6 7.6 %collective-permute-start.16 = (bf16[32,512]{1,0:T(8,128)(2,1)S(1)}, bf16[32,512]{1,0:T(8,128)(2,1)S(1)}, u32[]{:S(2)}, u32[]{:S(2)}) collective-permute-start(bf16[32,512]{1,0:T(8,128)(2,1)S(1)} %get-tuple-element.69), channel_id=1, source_target_pairs={{0,7},{1,6},{2,5},{3,4},{4,11},{5,10},{6,9},{7,8},{8,15},{9,14},{1... | collective-permute-start | bytes 98312 | tf_op jit(solution)/shard_map/ppermute | solution.py:215
  56.6 17.2 %collective-permute-start.15 = (bf16[32,4096]{1,0:T(8,128)(2,1)S(1)}, bf16[32,4096]{1,0:T(8,128)(2,1)S(1)}, u32[]{:S(2)}, u32[]{:S(2)}) collective-permute-start(bf16[32,4096]{1,0:T(8,128)(2,1)S(1)} %get-tuple-element.68.refs_6_), channel_id=1, source_target_pairs={{0,4},{1,5},{2,6},{3,7},{4,8},{5,9},{6,10},{7,11},{8,12},{9,13},{1... | collective-permute-start | bytes 786440 | tf_op jit(solution)/shard_map/ppermute | solution.py:215
  64.2 1.2 collective-permute-start.18
  66.2 7.6 %collective-permute-start.19 = (bf16[32,512]{1,0:T(8,128)(2,1)S(1)}, bf16[32,512]{1,0:T(8,128)(2,1)S(1)}, u32[]{:S(2)}, u32[]{:S(2)}) collective-permute-start(bf16[32,512]{1,0:T(8,128)(2,1)S(1)} %get-tuple-element.71), channel_id=1, source_target_pairs={{0,7},{1,6},{2,5},{3,4},{4,11},{5,10},{6,9},{7,8},{8,15},{9,14},{1... | collective-permute-start | bytes 98312 | tf_op jit(solution)/shard_map/ppermute | solution.py:215
  66.2 17.2 %collective-permute-start.23 = (bf16[32,4096]{1,0:T(8,128)(2,1)S(1)}, bf16[32,4096]{1,0:T(8,128)(2,1)S(1)}, u32[]{:S(2)}, u32[]{:S(2)}) collective-permute-start(bf16[32,4096]{1,0:T(8,128)(2,1)S(1)} %get-tuple-element.72.refs_6_), channel_id=1, source_target_pairs={{0,4},{1,5},{2,6},{3,7},{4,8},{5,9},{6,10},{7,11},{8,12},{9,13},{1... | collective-permute-start | bytes 786440 | tf_op jit(solution)/shard_map/ppermute | solution.py:215
  73.8 1.2 collective-permute-start.20
  75.8 7.6 %collective-permute-start.22 = (bf16[32,512]{1,0:T(8,128)(2,1)S(1)}, bf16[32,512]{1,0:T(8,128)(2,1)S(1)}, u32[]{:S(2)}, u32[]{:S(2)}) collective-permute-start(bf16[32,512]{1,0:T(8,128)(2,1)S(1)} %get-tuple-element.75), channel_id=1, source_target_pairs={{0,7},{1,6},{2,5},{3,4},{4,11},{5,10},{6,9},{7,8},{8,15},{9,14},{1... | collective-permute-start | bytes 98312 | tf_op jit(solution)/shard_map/ppermute | solution.py:215
  75.8 17.2 %collective-permute-start.21 = (bf16[32,4096]{1,0:T(8,128)(2,1)S(1)}, bf16[32,4096]{1,0:T(8,128)(2,1)S(1)}, u32[]{:S(2)}, u32[]{:S(2)}) collective-permute-start(bf16[32,4096]{1,0:T(8,128)(2,1)S(1)} %get-tuple-element.74.refs_6_), channel_id=1, source_target_pairs={{0,4},{1,5},{2,6},{3,7},{4,8},{5,9},{6,10},{7,11},{8,12},{9,13},{1... | collective-permute-start | bytes 786440 | tf_op jit(solution)/shard_map/ppermute | solution.py:215
  83.4 1.2 collective-permute-start.24
  85.4 7.6 %collective-permute-start.25 = (bf16[32,512]{1,0:T(8,128)(2,1)S(1)}, bf16[32,512]{1,0:T(8,128)(2,1)S(1)}, u32[]{:S(2)}, u32[]{:S(2)}) collective-permute-start(bf16[32,512]{1,0:T(8,128)(2,1)S(1)} %get-tuple-element.77), channel_id=1, source_target_pairs={{0,7},{1,6},{2,5},{3,4},{4,11},{5,10},{6,9},{7,8},{8,15},{9,14},{1... | collective-permute-start | bytes 98312 | tf_op jit(solution)/shard_map/ppermute | solution.py:215
  85.4 17.2 %collective-permute-start.29 = (bf16[32,4096]{1,0:T(8,128)(2,1)S(1)}, bf16[32,4096]{1,0:T(8,128)(2,1)S(1)}, u32[]{:S(2)}, u32[]{:S(2)}) collective-permute-start(bf16[32,4096]{1,0:T(8,128)(2,1)S(1)} %get-tuple-element.78.refs_6_), channel_id=1, source_target_pairs={{0,4},{1,5},{2,6},{3,7},{4,8},{5,9},{6,10},{7,11},{8,12},{9,13},{1... | collective-permute-start | bytes 786440 | tf_op jit(solution)/shard_map/ppermute | solution.py:215
  93.0 1.2 collective-permute-start.26
  95.0 7.6 %collective-permute-start.28 = (bf16[32,512]{1,0:T(8,128)(2,1)S(1)}, bf16[32,512]{1,0:T(8,128)(2,1)S(1)}, u32[]{:S(2)}, u32[]{:S(2)}) collective-permute-start(bf16[32,512]{1,0:T(8,128)(2,1)S(1)} %get-tuple-element.81), channel_id=1, source_target_pairs={{0,7},{1,6},{2,5},{3,4},{4,11},{5,10},{6,9},{7,8},{8,15},{9,14},{1... | collective-permute-start | bytes 98312 | tf_op jit(solution)/shard_map/ppermute | solution.py:215
  95.0 17.2 %collective-permute-start.27 = (bf16[32,4096]{1,0:T(8,128)(2,1)S(1)}, bf16[32,4096]{1,0:T(8,128)(2,1)S(1)}, u32[]{:S(2)}, u32[]{:S(2)}) collective-permute-start(bf16[32,4096]{1,0:T(8,128)(2,1)S(1)} %get-tuple-element.80.refs_6_), channel_id=1, source_target_pairs={{0,4},{1,5},{2,6},{3,7},{4,8},{5,9},{6,10},{7,11},{8,12},{9,13},{1... | collective-permute-start | bytes 786440 | tf_op jit(solution)/shard_map/ppermute | solution.py:215
  102.6 1.2 collective-permute-start.30
  104.5 7.6 %collective-permute-start.31 = (bf16[32,512]{1,0:T(8,128)(2,1)S(1)}, bf16[32,512]{1,0:T(8,128)(2,1)S(1)}, u32[]{:S(2)}, u32[]{:S(2)}) collective-permute-start(bf16[32,512]{1,0:T(8,128)(2,1)S(1)} %get-tuple-element.83), channel_id=1, source_target_pairs={{0,7},{1,6},{2,5},{3,4},{4,11},{5,10},{6,9},{7,8},{8,15},{9,14},{1... | collective-permute-start | bytes 98312 | tf_op jit(solution)/shard_map/ppermute | solution.py:215
  104.6 17.2 %collective-permute-start.35 = (bf16[32,4096]{1,0:T(8,128)(2,1)S(1)}, bf16[32,4096]{1,0:T(8,128)(2,1)S(1)}, u32[]{:S(2)}, u32[]{:S(2)}) collective-permute-start(bf16[32,4096]{1,0:T(8,128)(2,1)S(1)} %get-tuple-element.84.refs_6_), channel_id=1, source_target_pairs={{0,4},{1,5},{2,6},{3,7},{4,8},{5,9},{6,10},{7,11},{8,12},{9,13},{1... | collective-permute-start | bytes 786440 | tf_op jit(solution)/shard_map/ppermute | solution.py:215
  112.2 1.2 collective-permute-start.32
  114.1 7.6 %collective-permute-start.34 = (bf16[32,512]{1,0:T(8,128)(2,1)S(1)}, bf16[32,512]{1,0:T(8,128)(2,1)S(1)}, u32[]{:S(2)}, u32[]{:S(2)}) collective-permute-start(bf16[32,512]{1,0:T(8,128)(2,1)S(1)} %get-tuple-element.87), channel_id=1, source_target_pairs={{0,7},{1,6},{2,5},{3,4},{4,11},{5,10},{6,9},{7,8},{8,15},{9,14},{1... | collective-permute-start | bytes 98312 | tf_op jit(solution)/shard_map/ppermute | solution.py:215
  114.2 16.5 %collective-permute-start.33 = (bf16[32,4096]{1,0:T(8,128)(2,1)S(1)}, bf16[32,4096]{1,0:T(8,128)(2,1)S(1)}, u32[]{:S(2)}, u32[]{:S(2)}) collective-permute-start(bf16[32,4096]{1,0:T(8,128)(2,1)S(1)} %get-tuple-element.86.refs_6_), channel_id=1, source_target_pairs={{0,4},{1,5},{2,6},{3,7},{4,8},{5,9},{6,10},{7,11},{8,12},{9,13},{1... | collective-permute-start | bytes 786440 | tf_op jit(solution)/shard_map/ppermute | solution.py:215
  121.8 1.2 collective-permute-start.36
  123.7 7.0 %collective-permute-start.37 = (bf16[32,512]{1,0:T(8,128)(2,1)S(1)}, bf16[32,512]{1,0:T(8,128)(2,1)S(1)}, u32[]{:S(2)}, u32[]{:S(2)}) collective-permute-start(bf16[32,512]{1,0:T(8,128)(2,1)S(1)} %get-tuple-element.89), channel_id=1, source_target_pairs={{0,7},{1,6},{2,5},{3,4},{4,11},{5,10},{6,9},{7,8},{8,15},{9,14},{1... | collective-permute-start | bytes 98312 | tf_op jit(solution)/shard_map/ppermute | solution.py:215
  130.7 1.2 collective-permute-start.38
  130.9 17.6 %collective-permute-start.42 = (bf16[32,4096]{1,0:T(8,128)(2,1)S(1)}, bf16[32,4096]{1,0:T(8,128)(2,1)S(1)}, u32[]{:S(2)}, u32[]{:S(2)}) collective-permute-start(bf16[32,4096]{1,0:T(8,128)(2,1)S(1)} %get-tuple-element.90.refs_6_), channel_id=1, source_target_pairs={{0,4},{1,5},{2,6},{3,7},{4,8},{5,9},{6,10},{7,11},{8,12},{9,13},{1... | collective-permute-start | bytes 786440 | tf_op jit(solution)/shard_map/ppermute | solution.py:215
  132.7 15.9 %collective-permute-start.39 = (bf16[32,4096]{1,0:T(8,128)(2,1)S(1)}, bf16[32,4096]{1,0:T(8,128)(2,1)S(1)}, u32[]{:S(2)}, u32[]{:S(2)}) collective-permute-start(bf16[32,4096]{1,0:T(8,128)(2,1)S(1)} %get-tuple-element.92.refs_6_), channel_id=1, source_target_pairs={{0,4},{1,5},{2,6},{3,7},{4,8},{5,9},{6,10},{7,11},{8,12},{9,13},{1... | collective-permute-start | bytes 786440 | tf_op jit(solution)/shard_map/ppermute | solution.py:215
  132.8 15.7 %collective-permute-start.40 = (bf16[32,512]{1,0:T(8,128)(2,1)S(1)}, bf16[32,512]{1,0:T(8,128)(2,1)S(1)}, u32[]{:S(2)}, u32[]{:S(2)}) collective-permute-start(bf16[32,512]{1,0:T(8,128)(2,1)S(1)} %get-tuple-element.93), channel_id=1, source_target_pairs={{0,7},{1,6},{2,5},{3,4},{4,11},{5,10},{6,9},{7,8},{8,15},{9,14},{1... | collective-permute-start | bytes 98312 | tf_op jit(solution)/shard_map/ppermute | solution.py:215
  148.5 1.2 collective-permute-start.43
  148.6 2.0 %collective-permute-start.41 = (bf16[32,512]{1,0:T(8,128)(2,1)S(1)}, bf16[32,512]{1,0:T(8,128)(2,1)S(1)}, u32[]{:S(2)}, u32[]{:S(2)}) collective-permute-start(bf16[32,512]{1,0:T(8,128)(2,1)S(1)} %edge.26), channel_id=1, source_target_pairs={{0,1},{1,0},{2,3},{3,2},{4,5},{5,4},{6,7},{7,6},{8,9},{9,8},{10,11... | collective-permute-start | bytes 98312 | tf_op jit(solution)/shard_map/ppermute | solution.py:215

commit v6 on v5

--- a/solution.py
+++ b/solution.py
@@ -171,30 +171,31 @@
         input_output_aliases=aliases,
         compiler_params=pltpu.CompilerParams(vmem_limit_bytes=8 * 1024 * 1024),
         cost_estimate=pl.CostEstimate(
-            flops=14 * rows * brs * nzb * BLK * BLK, bytes_accessed=14 * w.size, transcendentals=0
+            flops=18 * rows * brs * nzb * BLK * BLK, bytes_accessed=18 * w.size, transcendentals=0
         ),
         name=f"layer_t{tick}_r{row}",
     )(*args)
 
 
-def edge_kernel(meta, main, after, edge):
-    del after
+def edge_kernel(meta, main, far, after, edge):
+    del far, after
     odd = meta[meta.shape[0] - 1]
     width = main.shape[1]
     edge[...] = main[:, pl.ds(pl.multiple_of((1 - odd) * (width - HALO * BLK), BLK), HALO * BLK)]
 
 
-def inner_edge(meta, main, after):
+def inner_edge(meta, main, far, after):
     return pl.pallas_call(
         edge_kernel,
         out_shape=pltpu.VMEM((main.shape[0], HALO * BLK), main.dtype),
-        in_specs=[SMEM, VMEM, ANY],
+        in_specs=[SMEM, VMEM, ANY, ANY],
         out_specs=VMEM,
         compiler_params=pltpu.CompilerParams(vmem_limit_bytes=1024 * 1024),
         name="edge",
     )(
         pltpu.with_memory_space_constraint(meta, pltpu.SMEM),
         pltpu.with_memory_space_constraint(main, pltpu.VMEM),
+        far,
         after,
     )
 
@@ -232,14 +233,14 @@
         source_block_indices[0].T,
     )
     parts = [(state, far)] * CHUNKS
-    emitted = prev = sent = prev_slot = None
+    emitted = prev = prev_slot = made = None
     for tick in range(TICKS):
         last = tick + 1 == TICKS
         for c in range(CHUNKS):
             main, far = parts[c]
             src_row = c * rows
             if tick > 0:
-                near = hop(inner_edge(meta, main, emitted if sent is None else sent), 0, inside)
+                near = hop(inner_edge(meta, main, far, made), 0, inside)
                 src_row = 0
             outs = list(
                 apply_layer(
@@ -251,9 +252,9 @@
             prev = prev_slot = None
             if not last:
                 prev, outer = outs
+                made = prev
                 prev_slot = (tick, c * rows)
-                sent = hop(outer, 1, across)
-                parts[c] = (hop(prev, 1, lambda i: i), sent)
+                parts[c] = (hop(prev, 1, lambda i: i), hop(outer, 1, across))
     return emitted
 
 

time: 153 us -> 124 us (0.81)
  waiting for transfers between devices: 119 us -> 91.2 us
    ppermute x44, waiting for transfers between devices: 119 us -> 91.2 us  [hop(): return lax.ppermute(values, ('section', 'blk'), pairs)]
  transfers between devices with their start and end apart: 44 -> 44, of which waited for: 26 -> 27; matrix products, arithmetic and copies ran while one was open for 0% -> 0% of each run, Pallas kernels for 10% -> 12%
where the time goes in v6:
time: 124 us
  waiting for transfers between devices  91.2 us (74%)
  Pallas kernels  17.1 us (14%)
  starting transfers between devices  14.1 us (11%)
    ppermute x44, waiting for transfers between devices, hop(): return lax.ppermute(values, ('section', 'blk'), pairs)  91.2 us
    ppermute x44, starting transfers between devices, hop(): return lax.ppermute(values, ('section', 'blk'), pairs)  14.1 us
    pallas_call x16, Pallas kernels, apply_layer(): pl.pallas_call(body, out_shape=tuple(out_shape), in_specs=specs, out_spec...  13.5 us
    pallas_call x1, Pallas kernels, load(): pl.pallas_call(functools.partial(load_kernel, blks), out_shape=(*(pltpu.V...  3.62 us
  transfers between devices with their start and end apart: 44, of which 27 were waited for; matrix products, arithmetic and copies ran while one was open for 0% of the time, Pallas kernels for 12%

profile of v6, /device:TPU:1, one launch (start us, length us, event | category | flops | bytes accessed | tf_op | source)
XLA Modules:
  0.0 123.7 jit_solution(8194717773722225713)
XLA Ops:
  0.0 0.9 constant_dynamic-slice_fusion
  0.9 2.7 %collective-permute-start = (bf16[64,512]{1,0:T(8,128)(2,1)S(1)}, bf16[64,512]{1,0:T(8,128)(2,1)S(1)}, u32[]{:S(2)}, u32[]{:S(2)}) collective-permute-start(bf16[64,512]{1,0:T(8,128)(2,1)S(1)} %get-tuple-element.96), channel_id=1, source_target_pairs={{0,3},{1,2},{2,1},{3,0},{4,7},{5,6},{6,5},{7,4},{8,11},{9,10},{10,... | collective-permute-start | bytes 196616 | tf_op jit(solution)/shard_map/ppermute | solution.py:216
  3.6 3.6 %load.1 = (bf16[64,4096]{1,0:T(8,128)(2,1)S(1)}, bf16[32,1024,128]{2,1,0:T(8,128)(2,1)S(1)}, f32[1,4096]{1,0:T(1,128)S(1)}, s32[258]{0:T(512)S(4)}) custom-call(bf16[64,4096]{1,0:T(8,128)(2,1)} %state.1, bf16[32,1024,128]{2,1,0:T(8,128)(2,1)} %bitcast.4, f32[1,4096]{1,0:T(1,128)} %bias.1, s32[8,32]{1,0:T(8,128)} %bitcast.5), custom_call_target="tpu_custom_call" | custom-call | bytes 8388608 | tf_op jit(solution)/shard_map/load/pallas_call | solution.py:46
  7.2 1.5 %layer_t0_r0.1 = (bf16[32,4096]{1,0:T(8,128)(2,1)S(1)}, bf16[32,512]{1,0:T(8,128)(2,1)S(1)}) custom-call(s32[258]{0:T(512)S(4)} %get-tuple-element.50.refs_0_.meta, bf16[64,4096]{1,0:T(8,128)(2,1)S(1)} %get-tuple-element.51.refs_1_, bf16[64,512]{1,0:T(8,128)(2,1)S(1)} %collective-permute-done.refs_2_, bf16[64,512]{1,0:T(8,128)(2,1)S(1)} %collective-permute-done.1.refs_3_, ...), custom_call_target="tpu_custom_call" | custom-call | flops 2415919104 | bytes 75497472 | tf_op jit(solution)/shard_map/layer_t0_r0/pallas_call | solution.py:165
  8.7 1.3 %collective-permute-start.4 = (bf16[32,4096]{1,0:T(8,128)(2,1)S(1)}, bf16[32,4096]{1,0:T(8,128)(2,1)S(1)}, u32[]{:S(2)}, u32[]{:S(2)}) collective-permute-start(bf16[32,4096]{1,0:T(8,128)(2,1)S(1)} %get-tuple-element.54.refs_6_), channel_id=1, source_target_pairs={{0,4},{1,5},{2,6},{3,7},{4,8},{5,9},{6,10},{7,11},{8,12},{9,13},{1... | collective-permute-start | bytes 786440 | tf_op jit(solution)/shard_map/ppermute | solution.py:216
  10.0 2.0 %collective-permute-start.5 = (bf16[32,512]{1,0:T(8,128)(2,1)S(1)}, bf16[32,512]{1,0:T(8,128)(2,1)S(1)}, u32[]{:S(2)}, u32[]{:S(2)}) collective-permute-start(bf16[32,512]{1,0:T(8,128)(2,1)S(1)} %get-tuple-element.57), channel_id=1, source_target_pairs={{0,7},{1,6},{2,5},{3,4},{4,11},{5,10},{6,9},{7,8},{8,15},{9,14},{1... | collective-permute-start | bytes 98312 | tf_op jit(solution)/shard_map/ppermute | solution.py:216
  11.9 1.5 %layer_t0_r32.1 = (bf16[8,64,4096]{2,1,0:T(8,128)(2,1)}, bf16[32,4096]{1,0:T(8,128)(2,1)S(1)}, bf16[32,512]{1,0:T(8,128)(2,1)S(1)}) custom-call(s32[258]{0:T(512)S(4)} %get-tuple-element.50.refs_0_.meta, bf16[64,4096]{1,0:T(8,128)(2,1)S(1)} %get-tuple-element.51.refs_1_, bf16[64,512]{1,0:T(8,128)(2,1)S(1)} %collective-permute-done.refs_2_, ...), custom_call_target="tpu_custom_call" | custom-call | flops 2415919104 | bytes 75497472 | tf_op jit(solution)/shard_map/layer_t0_r32/pallas_call | solution.py:165
  13.4 1.3 %collective-permute-start.2 = (bf16[32,4096]{1,0:T(8,128)(2,1)S(1)}, bf16[32,4096]{1,0:T(8,128)(2,1)S(1)}, u32[]{:S(2)}, u32[]{:S(2)}) collective-permute-start(bf16[32,4096]{1,0:T(8,128)(2,1)S(1)} %get-tuple-element.55.after.refs_6_), channel_id=1, source_target_pairs={{0,4},{1,5},{2,6},{3,7},{4,8},{5,9},{6,10},{7,11},{8,12},{9,13},{1... | collective-permute-start | bytes 786440 | tf_op jit(solution)/shard_map/ppermute | solution.py:216
  14.7 6.6 %collective-permute-done.5.far.refs_2_ = bf16[32,512]{1,0:T(8,128)(2,1)S(1)} collective-permute-done((bf16[32,512]{1,0:T(8,128)(2,1)S(1)}, bf16[32,512]{1,0:T(8,128)(2,1)S(1)}, u32[]{:S(2)}, u32[]{:S(2)}) %collective-permute-start.5) | collective-permute-done | bytes 32800 | tf_op jit(solution)/shard_map/ppermute | solution.py:216
  21.3 0.1 collective-permute-start.3
  21.4 1.1 collective-permute-done.6.refs_3_
  22.5 0.7 layer_t1_r0.1
  23.3 1.8 %collective-permute-start.10 = (bf16[32,4096]{1,0:T(8,128)(2,1)S(1)}, bf16[32,4096]{1,0:T(8,128)(2,1)S(1)}, u32[]{:S(2)}, u32[]{:S(2)}) collective-permute-start(bf16[32,4096]{1,0:T(8,128)(2,1)S(1)} %get-tuple-element.59.after.refs_6_), channel_id=1, source_target_pairs={{0,4},{1,5},{2,6},{3,7},{4,8},{5,9},{6,10},{7,11},{8,12},{9,13},{1... | collective-permute-start | bytes 786440 | tf_op jit(solution)/shard_map/ppermute | solution.py:216
  25.1 3.4 %collective-permute-done.3.far.refs_2_ = bf16[32,512]{1,0:T(8,128)(2,1)S(1)} collective-permute-done((bf16[32,512]{1,0:T(8,128)(2,1)S(1)}, bf16[32,512]{1,0:T(8,128)(2,1)S(1)}, u32[]{:S(2)}, u32[]{:S(2)}) %collective-permute-start.3) | collective-permute-done | bytes 32800 | tf_op jit(solution)/shard_map/ppermute | solution.py:216
  28.5 0.4 collective-permute-start.7
  28.9 0.9 collective-permute-done.7.refs_3_
  29.7 0.7 layer_t1_r32.1
  30.5 0.1 collective-permute-start.8
  30.6 5.3 %collective-permute-done.11.far.refs_2_ = bf16[32,512]{1,0:T(8,128)(2,1)S(1)} collective-permute-done((bf16[32,512]{1,0:T(8,128)(2,1)S(1)}, bf16[32,512]{1,0:T(8,128)(2,1)S(1)}, u32[]{:S(2)}, u32[]{:S(2)}) %collective-permute-start.11) | collective-permute-done | bytes 32800 | tf_op jit(solution)/shard_map/ppermute | solution.py:216
  35.8 0.3 collective-permute-start.12
  36.2 0.9 collective-permute-done.12.refs_3_
  37.0 0.7 layer_t2_r0.1
  37.9 5.3 %collective-permute-done.9.far.refs_2_ = bf16[32,512]{1,0:T(8,128)(2,1)S(1)} collective-permute-done((bf16[32,512]{1,0:T(8,128)(2,1)S(1)}, bf16[32,512]{1,0:T(8,128)(2,1)S(1)}, u32[]{:S(2)}, u32[]{:S(2)}) %collective-permute-start.9) | collective-permute-done | bytes 32800 | tf_op jit(solution)/shard_map/ppermute | solution.py:216
  43.1 0.3 collective-permute-start.13
  43.5 0.9 collective-permute-done.13.refs_3_
  44.4 0.7 layer_t2_r32.1
  45.2 5.3 %collective-permute-done.17.far.refs_2_ = bf16[32,512]{1,0:T(8,128)(2,1)S(1)} collective-permute-done((bf16[32,512]{1,0:T(8,128)(2,1)S(1)}, bf16[32,512]{1,0:T(8,128)(2,1)S(1)}, u32[]{:S(2)}, u32[]{:S(2)}) %collective-permute-start.17) | collective-permute-done | bytes 32800 | tf_op jit(solution)/shard_map/ppermute | solution.py:216
  50.5 0.4 collective-permute-start.18
  50.9 0.9 collective-permute-done.18.refs_3_
  51.7 0.7 layer_t3_r0.1
  52.6 5.3 %collective-permute-done.15.far.refs_2_ = bf16[32,512]{1,0:T(8,128)(2,1)S(1)} collective-permute-done((bf16[32,512]{1,0:T(8,128)(2,1)S(1)}, bf16[32,512]{1,0:T(8,128)(2,1)S(1)}, u32[]{:S(2)}, u32[]{:S(2)}) %collective-permute-start.15) | collective-permute-done | bytes 32800 | tf_op jit(solution)/shard_map/ppermute | solution.py:216
  57.8 0.3 collective-permute-start.19
  58.1 0.9 collective-permute-done.19.refs_3_
  59.0 0.7 layer_t3_r32.1
  59.9 5.3 %collective-permute-done.23.far.refs_2_ = bf16[32,512]{1,0:T(8,128)(2,1)S(1)} collective-permute-done((bf16[32,512]{1,0:T(8,128)(2,1)S(1)}, bf16[32,512]{1,0:T(8,128)(2,1)S(1)}, u32[]{:S(2)}, u32[]{:S(2)}) %collective-permute-start.23) | collective-permute-done | bytes 32800 | tf_op jit(solution)/shard_map/ppermute | solution.py:216
  65.1 0.4 collective-permute-start.24
  65.5 0.9 collective-permute-done.24.refs_3_
  66.4 0.7 layer_t4_r0.1
  67.2 5.3 %collective-permute-done.21.far.refs_2_ = bf16[32,512]{1,0:T(8,128)(2,1)S(1)} collective-permute-done((bf16[32,512]{1,0:T(8,128)(2,1)S(1)}, bf16[32,512]{1,0:T(8,128)(2,1)S(1)}, u32[]{:S(2)}, u32[]{:S(2)}) %collective-permute-start.21) | collective-permute-done | bytes 32800 | tf_op jit(solution)/shard_map/ppermute | solution.py:216
  72.5 0.3 collective-permute-start.25
  72.8 0.9 collective-permute-done.25.refs_3_
  73.7 0.7 layer_t4_r32.1
  74.5 5.3 %collective-permute-done.29.far.refs_2_ = bf16[32,512]{1,0:T(8,128)(2,1)S(1)} collective-permute-done((bf16[32,512]{1,0:T(8,128)(2,1)S(1)}, bf16[32,512]{1,0:T(8,128)(2,1)S(1)}, u32[]{:S(2)}, u32[]{:S(2)}) %collective-permute-start.29) | collective-permute-done | bytes 32800 | tf_op jit(solution)/shard_map/ppermute | solution.py:216
  79.8 0.4 collective-permute-start.30
  80.2 0.9 collective-permute-done.30.refs_3_
  81.1 0.7 layer_t5_r0.1
  81.9 5.3 %collective-permute-done.27.far.refs_2_ = bf16[32,512]{1,0:T(8,128)(2,1)S(1)} collective-permute-done((bf16[32,512]{1,0:T(8,128)(2,1)S(1)}, bf16[32,512]{1,0:T(8,128)(2,1)S(1)}, u32[]{:S(2)}, u32[]{:S(2)}) %collective-permute-start.27) | collective-permute-done | bytes 32800 | tf_op jit(solution)/shard_map/ppermute | solution.py:216
  87.1 0.3 collective-permute-start.31
  87.5 0.9 collective-permute-done.31.refs_3_
  88.4 0.7 layer_t5_r32.1
  89.2 5.3 %collective-permute-done.35.far.refs_2_ = bf16[32,512]{1,0:T(8,128)(2,1)S(1)} collective-permute-done((bf16[32,512]{1,0:T(8,128)(2,1)S(1)}, bf16[32,512]{1,0:T(8,128)(2,1)S(1)}, u32[]{:S(2)}, u32[]{:S(2)}) %collective-permute-start.35) | collective-permute-done | bytes 32800 | tf_op jit(solution)/shard_map/ppermute | solution.py:216
  94.5 0.4 collective-permute-start.36
  94.9 0.9 collective-permute-done.36.refs_3_
  95.7 0.7 layer_t6_r0.1
  96.5 5.3 %collective-permute-done.33.far.refs_2_ = bf16[32,512]{1,0:T(8,128)(2,1)S(1)} collective-permute-done((bf16[32,512]{1,0:T(8,128)(2,1)S(1)}, bf16[32,512]{1,0:T(8,128)(2,1)S(1)}, u32[]{:S(2)}, u32[]{:S(2)}) %collective-permute-start.33) | collective-permute-done | bytes 32800 | tf_op jit(solution)/shard_map/ppermute | solution.py:216
  101.8 0.3 collective-permute-start.37
  102.1 0.9 collective-permute-done.37.refs_3_
  103.0 0.7 layer_t6_r32.1
  104.0 16.8 %collective-permute-done.42.far.refs_2_ = bf16[32,512]{1,0:T(8,128)(2,1)S(1)} collective-permute-done((bf16[32,512]{1,0:T(8,128)(2,1)S(1)}, bf16[32,512]{1,0:T(8,128)(2,1)S(1)}, u32[]{:S(2)}, u32[]{:S(2)}) %collective-permute-start.42) | collective-permute-done | bytes 32800 | tf_op jit(solution)/shard_map/ppermute | solution.py:216
  120.8 0.2 collective-permute-done.39.far.refs_2_
  121.0 0.3 collective-permute-start.40
  121.3 0.6 collective-permute-done.43.refs_3_
  122.0 0.8 layer_t7_r0.1.refs_6_
  122.8 0.8 layer_t7_r32.1
  (56 shorter events, 0.8 us)
Async XLA Ops:
  0.9 6.3 %collective-permute-start = (bf16[64,512]{1,0:T(8,128)(2,1)S(1)}, bf16[64,512]{1,0:T(8,128)(2,1)S(1)}, u32[]{:S(2)}, u32[]{:S(2)}) collective-permute-start(bf16[64,512]{1,0:T(8,128)(2,1)S(1)} %get-tuple-element.96), channel_id=1, source_target_pairs={{0,3},{1,2},{2,1},{3,0},{4,7},{5,6},{6,5},{7,4},{8,11},{9,10},{10,... | collective-permute-start | bytes 196616 | tf_op jit(solution)/shard_map/ppermute | solution.py:216
  3.6 3.6 %collective-permute-start.1 = (bf16[64,512]{1,0:T(8,128)(2,1)S(1)}, bf16[64,512]{1,0:T(8,128)(2,1)S(1)}, u32[]{:S(2)}, u32[]{:S(2)}) collective-permute-start(bf16[64,512]{1,0:T(8,128)(2,1)S(1)} %get-tuple-element.95), channel_id=1, source_target_pairs={{0,1},{1,0},{2,3},{3,2},{4,5},{5,4},{6,7},{7,6},{8,9},{9,8},{10,11... | collective-permute-start | bytes 196616 | tf_op jit(solution)/shard_map/ppermute | solution.py:216
  8.7 12.6 %collective-permute-start.4 = (bf16[32,4096]{1,0:T(8,128)(2,1)S(1)}, bf16[32,4096]{1,0:T(8,128)(2,1)S(1)}, u32[]{:S(2)}, u32[]{:S(2)}) collective-permute-start(bf16[32,4096]{1,0:T(8,128)(2,1)S(1)} %get-tuple-element.54.refs_6_), channel_id=1, source_target_pairs={{0,4},{1,5},{2,6},{3,7},{4,8},{5,9},{6,10},{7,11},{8,12},{9,13},{1... | collective-permute-start | bytes 786440 | tf_op jit(solution)/shard_map/ppermute | solution.py:216
  10.0 11.3 %collective-permute-start.5 = (bf16[32,512]{1,0:T(8,128)(2,1)S(1)}, bf16[32,512]{1,0:T(8,128)(2,1)S(1)}, u32[]{:S(2)}, u32[]{:S(2)}) collective-permute-start(bf16[32,512]{1,0:T(8,128)(2,1)S(1)} %get-tuple-element.57), channel_id=1, source_target_pairs={{0,7},{1,6},{2,5},{3,4},{4,11},{5,10},{6,9},{7,8},{8,15},{9,14},{1... | collective-permute-start | bytes 98312 | tf_op jit(solution)/shard_map/ppermute | solution.py:216
  13.4 15.1 %collective-permute-start.2 = (bf16[32,4096]{1,0:T(8,128)(2,1)S(1)}, bf16[32,4096]{1,0:T(8,128)(2,1)S(1)}, u32[]{:S(2)}, u32[]{:S(2)}) collective-permute-start(bf16[32,4096]{1,0:T(8,128)(2,1)S(1)} %get-tuple-element.55.after.refs_6_), channel_id=1, source_target_pairs={{0,4},{1,5},{2,6},{3,7},{4,8},{5,9},{6,10},{7,11},{8,12},{9,13},{1... | collective-permute-start | bytes 786440 | tf_op jit(solution)/shard_map/ppermute | solution.py:216
  21.3 1.2 collective-permute-start.6
  21.3 7.2 %collective-permute-start.3 = (bf16[32,512]{1,0:T(8,128)(2,1)S(1)}, bf16[32,512]{1,0:T(8,128)(2,1)S(1)}, u32[]{:S(2)}, u32[]{:S(2)}) collective-permute-start(bf16[32,512]{1,0:T(8,128)(2,1)S(1)} %get-tuple-element.56), channel_id=1, source_target_pairs={{0,7},{1,6},{2,5},{3,4},{4,11},{5,10},{6,9},{7,8},{8,15},{9,14},{1... | collective-permute-start | bytes 98312 | tf_op jit(solution)/shard_map/ppermute | solution.py:216
  23.3 12.6 %collective-permute-start.10 = (bf16[32,4096]{1,0:T(8,128)(2,1)S(1)}, bf16[32,4096]{1,0:T(8,128)(2,1)S(1)}, u32[]{:S(2)}, u32[]{:S(2)}) collective-permute-start(bf16[32,4096]{1,0:T(8,128)(2,1)S(1)} %get-tuple-element.59.after.refs_6_), channel_id=1, source_target_pairs={{0,4},{1,5},{2,6},{3,7},{4,8},{5,9},{6,10},{7,11},{8,12},{9,13},{1... | collective-permute-start | bytes 786440 | tf_op jit(solution)/shard_map/ppermute | solution.py:216
  28.5 1.3 %collective-permute-start.7 = (bf16[32,512]{1,0:T(8,128)(2,1)S(1)}, bf16[32,512]{1,0:T(8,128)(2,1)S(1)}, u32[]{:S(2)}, u32[]{:S(2)}) collective-permute-start(bf16[32,512]{1,0:T(8,128)(2,1)S(1)} %edge.15), channel_id=1, source_target_pairs={{0,1},{1,0},{2,3},{3,2},{4,5},{5,4},{6,7},{7,6},{8,9},{9,8},{10,11... | collective-permute-start | bytes 98312 | tf_op jit(solution)/shard_map/ppermute | solution.py:216
  28.9 6.9 %collective-permute-start.11 = (bf16[32,512]{1,0:T(8,128)(2,1)S(1)}, bf16[32,512]{1,0:T(8,128)(2,1)S(1)}, u32[]{:S(2)}, u32[]{:S(2)}) collective-permute-start(bf16[32,512]{1,0:T(8,128)(2,1)S(1)} %get-tuple-element.63), channel_id=1, source_target_pairs={{0,7},{1,6},{2,5},{3,4},{4,11},{5,10},{6,9},{7,8},{8,15},{9,14},{1... | collective-permute-start | bytes 98312 | tf_op jit(solution)/shard_map/ppermute | solution.py:216
  30.5 12.7 %collective-permute-start.8 = (bf16[32,4096]{1,0:T(8,128)(2,1)S(1)}, bf16[32,4096]{1,0:T(8,128)(2,1)S(1)}, u32[]{:S(2)}, u32[]{:S(2)}) collective-permute-start(bf16[32,4096]{1,0:T(8,128)(2,1)S(1)} %get-tuple-element.61.after.refs_6_), channel_id=1, source_target_pairs={{0,4},{1,5},{2,6},{3,7},{4,8},{5,9},{6,10},{7,11},{8,12},{9,13},{1... | collective-permute-start | bytes 786440 | tf_op jit(solution)/shard_map/ppermute | solution.py:216
  35.8 1.2 collective-permute-start.12
  36.2 7.0 %collective-permute-start.9 = (bf16[32,512]{1,0:T(8,128)(2,1)S(1)}, bf16[32,512]{1,0:T(8,128)(2,1)S(1)}, u32[]{:S(2)}, u32[]{:S(2)}) collective-permute-start(bf16[32,512]{1,0:T(8,128)(2,1)S(1)} %get-tuple-element.62), channel_id=1, source_target_pairs={{0,7},{1,6},{2,5},{3,4},{4,11},{5,10},{6,9},{7,8},{8,15},{9,14},{1... | collective-permute-start | bytes 98312 | tf_op jit(solution)/shard_map/ppermute | solution.py:216
  37.8 12.7 %collective-permute-start.16 = (bf16[32,4096]{1,0:T(8,128)(2,1)S(1)}, bf16[32,4096]{1,0:T(8,128)(2,1)S(1)}, u32[]{:S(2)}, u32[]{:S(2)}) collective-permute-start(bf16[32,4096]{1,0:T(8,128)(2,1)S(1)} %get-tuple-element.65.after.refs_6_), channel_id=1, source_target_pairs={{0,4},{1,5},{2,6},{3,7},{4,8},{5,9},{6,10},{7,11},{8,12},{9,13},{1... | collective-permute-start | bytes 786440 | tf_op jit(solution)/shard_map/ppermute | solution.py:216
  43.1 1.2 collective-permute-start.13
  43.5 7.0 %collective-permute-start.17 = (bf16[32,512]{1,0:T(8,128)(2,1)S(1)}, bf16[32,512]{1,0:T(8,128)(2,1)S(1)}, u32[]{:S(2)}, u32[]{:S(2)}) collective-permute-start(bf16[32,512]{1,0:T(8,128)(2,1)S(1)} %get-tuple-element.69), channel_id=1, source_target_pairs={{0,7},{1,6},{2,5},{3,4},{4,11},{5,10},{6,9},{7,8},{8,15},{9,14},{1... | collective-permute-start | bytes 98312 | tf_op jit(solution)/shard_map/ppermute | solution.py:216
  45.1 12.7 %collective-permute-start.14 = (bf16[32,4096]{1,0:T(8,128)(2,1)S(1)}, bf16[32,4096]{1,0:T(8,128)(2,1)S(1)}, u32[]{:S(2)}, u32[]{:S(2)}) collective-permute-start(bf16[32,4096]{1,0:T(8,128)(2,1)S(1)} %get-tuple-element.67.after.refs_6_), channel_id=1, source_target_pairs={{0,4},{1,5},{2,6},{3,7},{4,8},{5,9},{6,10},{7,11},{8,12},{9,13},{1... | collective-permute-start | bytes 786440 | tf_op jit(solution)/shard_map/ppermute | solution.py:216
  50.5 1.3 %collective-permute-start.18 = (bf16[32,512]{1,0:T(8,128)(2,1)S(1)}, bf16[32,512]{1,0:T(8,128)(2,1)S(1)}, u32[]{:S(2)}, u32[]{:S(2)}) collective-permute-start(bf16[32,512]{1,0:T(8,128)(2,1)S(1)} %edge.18), channel_id=1, source_target_pairs={{0,1},{1,0},{2,3},{3,2},{4,5},{5,4},{6,7},{7,6},{8,9},{9,8},{10,11... | collective-permute-start | bytes 98312 | tf_op jit(solution)/shard_map/ppermute | solution.py:216
  50.9 6.9 %collective-permute-start.15 = (bf16[32,512]{1,0:T(8,128)(2,1)S(1)}, bf16[32,512]{1,0:T(8,128)(2,1)S(1)}, u32[]{:S(2)}, u32[]{:S(2)}) collective-permute-start(bf16[32,512]{1,0:T(8,128)(2,1)S(1)} %get-tuple-element.68), channel_id=1, source_target_pairs={{0,7},{1,6},{2,5},{3,4},{4,11},{5,10},{6,9},{7,8},{8,15},{9,14},{1... | collective-permute-start | bytes 98312 | tf_op jit(solution)/shard_map/ppermute | solution.py:216
  52.5 12.6 %collective-permute-start.22 = (bf16[32,4096]{1,0:T(8,128)(2,1)S(1)}, bf16[32,4096]{1,0:T(8,128)(2,1)S(1)}, u32[]{:S(2)}, u32[]{:S(2)}) collective-permute-start(bf16[32,4096]{1,0:T(8,128)(2,1)S(1)} %get-tuple-element.71.after.refs_6_), channel_id=1, source_target_pairs={{0,4},{1,5},{2,6},{3,7},{4,8},{5,9},{6,10},{7,11},{8,12},{9,13},{1... | collective-permute-start | bytes 786440 | tf_op jit(solution)/shard_map/ppermute | solution.py:216
  57.8 1.2 collective-permute-start.19
  58.1 7.0 %collective-permute-start.23 = (bf16[32,512]{1,0:T(8,128)(2,1)S(1)}, bf16[32,512]{1,0:T(8,128)(2,1)S(1)}, u32[]{:S(2)}, u32[]{:S(2)}) collective-permute-start(bf16[32,512]{1,0:T(8,128)(2,1)S(1)} %get-tuple-element.75), channel_id=1, source_target_pairs={{0,7},{1,6},{2,5},{3,4},{4,11},{5,10},{6,9},{7,8},{8,15},{9,14},{1... | collective-permute-start | bytes 98312 | tf_op jit(solution)/shard_map/ppermute | solution.py:216
  59.8 12.7 %collective-permute-start.20 = (bf16[32,4096]{1,0:T(8,128)(2,1)S(1)}, bf16[32,4096]{1,0:T(8,128)(2,1)S(1)}, u32[]{:S(2)}, u32[]{:S(2)}) collective-permute-start(bf16[32,4096]{1,0:T(8,128)(2,1)S(1)} %get-tuple-element.73.after.refs_6_), channel_id=1, source_target_pairs={{0,4},{1,5},{2,6},{3,7},{4,8},{5,9},{6,10},{7,11},{8,12},{9,13},{1... | collective-permute-start | bytes 786440 | tf_op jit(solution)/shard_map/ppermute | solution.py:216
  65.1 1.3 %collective-permute-start.24 = (bf16[32,512]{1,0:T(8,128)(2,1)S(1)}, bf16[32,512]{1,0:T(8,128)(2,1)S(1)}, u32[]{:S(2)}, u32[]{:S(2)}) collective-permute-start(bf16[32,512]{1,0:T(8,128)(2,1)S(1)} %edge.20), channel_id=1, source_target_pairs={{0,1},{1,0},{2,3},{3,2},{4,5},{5,4},{6,7},{7,6},{8,9},{9,8},{10,11... | collective-permute-start | bytes 98312 | tf_op jit(solution)/shard_map/ppermute | solution.py:216
  65.5 6.9 %collective-permute-start.21 = (bf16[32,512]{1,0:T(8,128)(2,1)S(1)}, bf16[32,512]{1,0:T(8,128)(2,1)S(1)}, u32[]{:S(2)}, u32[]{:S(2)}) collective-permute-start(bf16[32,512]{1,0:T(8,128)(2,1)S(1)} %get-tuple-element.74), channel_id=1, source_target_pairs={{0,7},{1,6},{2,5},{3,4},{4,11},{5,10},{6,9},{7,8},{8,15},{9,14},{1... | collective-permute-start | bytes 98312 | tf_op jit(solution)/shard_map/ppermute | solution.py:216
  67.2 12.6 %collective-permute-start.28 = (bf16[32,4096]{1,0:T(8,128)(2,1)S(1)}, bf16[32,4096]{1,0:T(8,128)(2,1)S(1)}, u32[]{:S(2)}, u32[]{:S(2)}) collective-permute-start(bf16[32,4096]{1,0:T(8,128)(2,1)S(1)} %get-tuple-element.77.after.refs_6_), channel_id=1, source_target_pairs={{0,4},{1,5},{2,6},{3,7},{4,8},{5,9},{6,10},{7,11},{8,12},{9,13},{1... | collective-permute-start | bytes 786440 | tf_op jit(solution)/shard_map/ppermute | solution.py:216
  72.5 1.2 collective-permute-start.25
  72.8 7.0 %collective-permute-start.29 = (bf16[32,512]{1,0:T(8,128)(2,1)S(1)}, bf16[32,512]{1,0:T(8,128)(2,1)S(1)}, u32[]{:S(2)}, u32[]{:S(2)}) collective-permute-start(bf16[32,512]{1,0:T(8,128)(2,1)S(1)} %get-tuple-element.81), channel_id=1, source_target_pairs={{0,7},{1,6},{2,5},{3,4},{4,11},{5,10},{6,9},{7,8},{8,15},{9,14},{1... | collective-permute-start | bytes 98312 | tf_op jit(solution)/shard_map/ppermute | solution.py:216
  74.4 12.7 %collective-permute-start.26 = (bf16[32,4096]{1,0:T(8,128)(2,1)S(1)}, bf16[32,4096]{1,0:T(8,128)(2,1)S(1)}, u32[]{:S(2)}, u32[]{:S(2)}) collective-permute-start(bf16[32,4096]{1,0:T(8,128)(2,1)S(1)} %get-tuple-element.79.after.refs_6_), channel_id=1, source_target_pairs={{0,4},{1,5},{2,6},{3,7},{4,8},{5,9},{6,10},{7,11},{8,12},{9,13},{1... | collective-permute-start | bytes 786440 | tf_op jit(solution)/shard_map/ppermute | solution.py:216
  79.8 1.3 %collective-permute-start.30 = (bf16[32,512]{1,0:T(8,128)(2,1)S(1)}, bf16[32,512]{1,0:T(8,128)(2,1)S(1)}, u32[]{:S(2)}, u32[]{:S(2)}) collective-permute-start(bf16[32,512]{1,0:T(8,128)(2,1)S(1)} %edge.22), channel_id=1, source_target_pairs={{0,1},{1,0},{2,3},{3,2},{4,5},{5,4},{6,7},{7,6},{8,9},{9,8},{10,11... | collective-permute-start | bytes 98312 | tf_op jit(solution)/shard_map/ppermute | solution.py:216
  80.2 6.9 %collective-permute-start.27 = (bf16[32,512]{1,0:T(8,128)(2,1)S(1)}, bf16[32,512]{1,0:T(8,128)(2,1)S(1)}, u32[]{:S(2)}, u32[]{:S(2)}) collective-permute-start(bf16[32,512]{1,0:T(8,128)(2,1)S(1)} %get-tuple-element.80), channel_id=1, source_target_pairs={{0,7},{1,6},{2,5},{3,4},{4,11},{5,10},{6,9},{7,8},{8,15},{9,14},{1... | collective-permute-start | bytes 98312 | tf_op jit(solution)/shard_map/ppermute | solution.py:216
  81.8 12.6 %collective-permute-start.34 = (bf16[32,4096]{1,0:T(8,128)(2,1)S(1)}, bf16[32,4096]{1,0:T(8,128)(2,1)S(1)}, u32[]{:S(2)}, u32[]{:S(2)}) collective-permute-start(bf16[32,4096]{1,0:T(8,128)(2,1)S(1)} %get-tuple-element.83.after.refs_6_), channel_id=1, source_target_pairs={{0,4},{1,5},{2,6},{3,7},{4,8},{5,9},{6,10},{7,11},{8,12},{9,13},{1... | collective-permute-start | bytes 786440 | tf_op jit(solution)/shard_map/ppermute | solution.py:216
  87.1 1.2 collective-permute-start.31
  87.5 7.0 %collective-permute-start.35 = (bf16[32,512]{1,0:T(8,128)(2,1)S(1)}, bf16[32,512]{1,0:T(8,128)(2,1)S(1)}, u32[]{:S(2)}, u32[]{:S(2)}) collective-permute-start(bf16[32,512]{1,0:T(8,128)(2,1)S(1)} %get-tuple-element.87), channel_id=1, source_target_pairs={{0,7},{1,6},{2,5},{3,4},{4,11},{5,10},{6,9},{7,8},{8,15},{9,14},{1... | collective-permute-start | bytes 98312 | tf_op jit(solution)/shard_map/ppermute | solution.py:216
  89.1 12.7 %collective-permute-start.32 = (bf16[32,4096]{1,0:T(8,128)(2,1)S(1)}, bf16[32,4096]{1,0:T(8,128)(2,1)S(1)}, u32[]{:S(2)}, u32[]{:S(2)}) collective-permute-start(bf16[32,4096]{1,0:T(8,128)(2,1)S(1)} %get-tuple-element.85.after.refs_6_), channel_id=1, source_target_pairs={{0,4},{1,5},{2,6},{3,7},{4,8},{5,9},{6,10},{7,11},{8,12},{9,13},{1... | collective-permute-start | bytes 786440 | tf_op jit(solution)/shard_map/ppermute | solution.py:216
  94.5 1.3 %collective-permute-start.36 = (bf16[32,512]{1,0:T(8,128)(2,1)S(1)}, bf16[32,512]{1,0:T(8,128)(2,1)S(1)}, u32[]{:S(2)}, u32[]{:S(2)}) collective-permute-start(bf16[32,512]{1,0:T(8,128)(2,1)S(1)} %edge.24), channel_id=1, source_target_pairs={{0,1},{1,0},{2,3},{3,2},{4,5},{5,4},{6,7},{7,6},{8,9},{9,8},{10,11... | collective-permute-start | bytes 98312 | tf_op jit(solution)/shard_map/ppermute | solution.py:216
  94.9 6.9 %collective-permute-start.33 = (bf16[32,512]{1,0:T(8,128)(2,1)S(1)}, bf16[32,512]{1,0:T(8,128)(2,1)S(1)}, u32[]{:S(2)}, u32[]{:S(2)}) collective-permute-start(bf16[32,512]{1,0:T(8,128)(2,1)S(1)} %get-tuple-element.86), channel_id=1, source_target_pairs={{0,7},{1,6},{2,5},{3,4},{4,11},{5,10},{6,9},{7,8},{8,15},{9,14},{1... | collective-permute-start | bytes 98312 | tf_op jit(solution)/shard_map/ppermute | solution.py:216
  101.8 1.2 collective-permute-start.37
  102.1 18.6 %collective-permute-start.41 = (bf16[32,4096]{1,0:T(8,128)(2,1)S(1)}, bf16[32,4096]{1,0:T(8,128)(2,1)S(1)}, u32[]{:S(2)}, u32[]{:S(2)}) collective-permute-start(bf16[32,4096]{1,0:T(8,128)(2,1)S(1)} %get-tuple-element.89.after.refs_6_), channel_id=1, source_target_pairs={{0,4},{1,5},{2,6},{3,7},{4,8},{5,9},{6,10},{7,11},{8,12},{9,13},{1... | collective-permute-start | bytes 786440 | tf_op jit(solution)/shard_map/ppermute | solution.py:216
  103.8 17.2 %collective-permute-start.38 = (bf16[32,4096]{1,0:T(8,128)(2,1)S(1)}, bf16[32,4096]{1,0:T(8,128)(2,1)S(1)}, u32[]{:S(2)}, u32[]{:S(2)}) collective-permute-start(bf16[32,4096]{1,0:T(8,128)(2,1)S(1)} %get-tuple-element.91.after.refs_6_), channel_id=1, source_target_pairs={{0,4},{1,5},{2,6},{3,7},{4,8},{5,9},{6,10},{7,11},{8,12},{9,13},{1... | collective-permute-start | bytes 786440 | tf_op jit(solution)/shard_map/ppermute | solution.py:216
  103.8 16.9 %collective-permute-start.42 = (bf16[32,512]{1,0:T(8,128)(2,1)S(1)}, bf16[32,512]{1,0:T(8,128)(2,1)S(1)}, u32[]{:S(2)}, u32[]{:S(2)}) collective-permute-start(bf16[32,512]{1,0:T(8,128)(2,1)S(1)} %get-tuple-element.93), channel_id=1, source_target_pairs={{0,7},{1,6},{2,5},{3,4},{4,11},{5,10},{6,9},{7,8},{8,15},{9,14},{1... | collective-permute-start | bytes 98312 | tf_op jit(solution)/shard_map/ppermute | solution.py:216
  103.9 17.1 %collective-permute-start.39 = (bf16[32,512]{1,0:T(8,128)(2,1)S(1)}, bf16[32,512]{1,0:T(8,128)(2,1)S(1)}, u32[]{:S(2)}, u32[]{:S(2)}) collective-permute-start(bf16[32,512]{1,0:T(8,128)(2,1)S(1)} %get-tuple-element.92), channel_id=1, source_target_pairs={{0,7},{1,6},{2,5},{3,4},{4,11},{5,10},{6,9},{7,8},{8,15},{9,14},{1... | collective-permute-start | bytes 98312 | tf_op jit(solution)/shard_map/ppermute | solution.py:216
  120.7 1.2 collective-permute-start.43
  121.0 1.8 %collective-permute-start.40 = (bf16[32,512]{1,0:T(8,128)(2,1)S(1)}, bf16[32,512]{1,0:T(8,128)(2,1)S(1)}, u32[]{:S(2)}, u32[]{:S(2)}) collective-permute-start(bf16[32,512]{1,0:T(8,128)(2,1)S(1)} %edge.26), channel_id=1, source_target_pairs={{0,1},{1,0},{2,3},{3,2},{4,5},{5,4},{6,7},{7,6},{8,9},{9,8},{10,11... | collective-permute-start | bytes 98312 | tf_op jit(solution)/shard_map/ppermute | solution.py:216

commit v7 on v6

--- a/solution.py
+++ b/solution.py
@@ -207,13 +207,19 @@
     edge = HALO * BLK
     emitted_aval = jax.ShapeDtypeStruct((TICKS, height, width), jnp.bfloat16)
 
-    def hop(values, step, place):
-        pairs = [
-            (s * blks + i, (s + step) % sections * blks + place(i) % blks)
-            for s in range(sections)
-            for i in range(blks)
-        ]
+    def hop(values, place, tick=None):
+        pairs = []
+        for s in range(sections):
+            target = s
+            if tick is not None and s >= tick:
+                target = s + 1 if s + 1 < sections else tick
+            for i in range(blks):
+                moved = place(i) % blks if tick is None or s >= tick else i
+                pairs.append((s * blks + i, target * blks + moved))
         return lax.ppermute(values, ("section", "blk"), pairs)
+
+    def same(i):
+        return i
 
     def across(i):
         return i + 1 if i % 2 else i - 1
@@ -224,7 +230,7 @@
     odd = lax.axis_index("blk") % 2
     outer = lax.dynamic_slice_in_dim(pending_groups, odd * (width - edge), edge, axis=1)
     inner = lax.dynamic_slice_in_dim(pending_groups, (1 - odd) * (width - edge), edge, axis=1)
-    far, near = hop(outer, 0, across), hop(inner, 0, inside)
+    far, near = hop(outer, across), hop(inner, inside)
     state, w, bias, meta = load(
         blks,
         pending_groups,
@@ -240,7 +246,7 @@
             main, far = parts[c]
             src_row = c * rows
             if tick > 0:
-                near = hop(inner_edge(meta, main, far, made), 0, inside)
+                near = hop(inner_edge(meta, main, far, made), inside)
                 src_row = 0
             outs = list(
                 apply_layer(
@@ -254,7 +260,7 @@
                 prev, outer = outs
                 made = prev
                 prev_slot = (tick, c * rows)
-                parts[c] = (hop(prev, 1, lambda i: i), hop(outer, 1, across))
+                parts[c] = (hop(prev, same, tick), hop(outer, across, tick))
     return emitted
 
 

time: 124 us -> 134 us (1.081)
  the two profiles are of different devices: /device:TPU:1 before, /device:TPU:29 now
where the time goes in v7:
time: 134 us; the launch traced here: 133 us
  starting transfers between devices  92.1 us (69%)
  Pallas kernels  29.1 us (22%)
  waiting for transfers between devices  10.2 us (8%)
    ppermute x44, starting transfers between devices, hop(): return lax.ppermute(values, ('section', 'blk'), pairs)  92.1 us
    pallas_call x16, Pallas kernels, apply_layer(): pl.pallas_call(body, out_shape=tuple(out_shape), in_specs=specs, out_spec...  25.4 us
    ppermute x44, waiting for transfers between devices, hop(): return lax.ppermute(values, ('section', 'blk'), pairs)  10.2 us
    pallas_call x1, Pallas kernels, load(): pl.pallas_call(functools.partial(load_kernel, blks), out_shape=(*(pltpu.V...  3.62 us
  transfers between devices with their start and end apart: 44, of which 7 were waited for; matrix products, arithmetic and copies ran while one was open for 0% of the time, Pallas kernels for 19%

profile of v7, /device:TPU:29, one launch (start us, length us, event | category | flops | bytes accessed | tf_op | source)
XLA Modules:
  0.0 133.1 jit_solution(14631670782200502723)
XLA Ops:
  0.0 0.9 constant_dynamic-slice_fusion
  0.9 1.8 %collective-permute-start = (bf16[64,512]{1,0:T(8,128)(2,1)S(1)}, bf16[64,512]{1,0:T(8,128)(2,1)S(1)}, u32[]{:S(2)}, u32[]{:S(2)}) collective-permute-start(bf16[64,512]{1,0:T(8,128)(2,1)S(1)} %get-tuple-element.96), channel_id=1, source_target_pairs={{0,3},{1,2},{2,1},{3,0},{4,7},{5,6},{6,5},{7,4},{8,11},{9,10},{10,... | collective-permute-start | bytes 196616 | tf_op jit(solution)/shard_map/ppermute | solution.py:219
  2.7 3.6 %load.1 = (bf16[64,4096]{1,0:T(8,128)(2,1)S(1)}, bf16[32,1024,128]{2,1,0:T(8,128)(2,1)S(1)}, f32[1,4096]{1,0:T(1,128)S(1)}, s32[258]{0:T(512)S(4)}) custom-call(bf16[64,4096]{1,0:T(8,128)(2,1)} %state.1, bf16[32,1024,128]{2,1,0:T(8,128)(2,1)} %bitcast.4, f32[1,4096]{1,0:T(1,128)} %bias.1, s32[8,32]{1,0:T(8,128)} %bitcast.5), custom_call_target="tpu_custom_call" | custom-call | bytes 8388608 | tf_op jit(solution)/shard_map/load/pallas_call | solution.py:46
  6.4 1.5 %layer_t0_r0.1 = (bf16[32,4096]{1,0:T(8,128)(2,1)S(1)}, bf16[32,512]{1,0:T(8,128)(2,1)S(1)}) custom-call(s32[258]{0:T(512)S(4)} %get-tuple-element.50.refs_0_.meta, bf16[64,4096]{1,0:T(8,128)(2,1)S(1)} %get-tuple-element.51.refs_1_, bf16[64,512]{1,0:T(8,128)(2,1)S(1)} %collective-permute-done.refs_2_, bf16[64,512]{1,0:T(8,128)(2,1)S(1)} %collective-permute-done.1.refs_3_, ...), custom_call_target="tpu_custom_call" | custom-call | flops 2415919104 | bytes 75497472 | tf_op jit(solution)/shard_map/layer_t0_r0/pallas_call | solution.py:165
  7.9 1.8 %collective-permute-start.5 = (bf16[32,512]{1,0:T(8,128)(2,1)S(1)}, bf16[32,512]{1,0:T(8,128)(2,1)S(1)}, u32[]{:S(2)}, u32[]{:S(2)}) collective-permute-start(bf16[32,512]{1,0:T(8,128)(2,1)S(1)} %get-tuple-element.57), channel_id=1, source_target_pairs={{0,7},{1,6},{2,5},{3,4},{4,11},{5,10},{6,9},{7,8},{8,15},{9,14},{1... | collective-permute-start | bytes 98312 | tf_op jit(solution)/shard_map/ppermute | solution.py:219
  9.8 1.5 %layer_t0_r32.1 = (bf16[8,64,4096]{2,1,0:T(8,128)(2,1)}, bf16[32,4096]{1,0:T(8,128)(2,1)S(1)}, bf16[32,512]{1,0:T(8,128)(2,1)S(1)}) custom-call(s32[258]{0:T(512)S(4)} %get-tuple-element.50.refs_0_.meta, bf16[64,4096]{1,0:T(8,128)(2,1)S(1)} %get-tuple-element.51.refs_1_, bf16[64,512]{1,0:T(8,128)(2,1)S(1)} %collective-permute-done.refs_2_, ...), custom_call_target="tpu_custom_call" | custom-call | flops 2415919104 | bytes 75497472 | tf_op jit(solution)/shard_map/layer_t0_r32/pallas_call | solution.py:165
  11.2 1.3 collective-permute-start.2
  12.5 1.4 %collective-permute-done.5.far.refs_2_ = bf16[32,512]{1,0:T(8,128)(2,1)S(1)} collective-permute-done((bf16[32,512]{1,0:T(8,128)(2,1)S(1)}, bf16[32,512]{1,0:T(8,128)(2,1)S(1)}, u32[]{:S(2)}, u32[]{:S(2)}) %collective-permute-start.5) | collective-permute-done | bytes 32800 | tf_op jit(solution)/shard_map/ppermute | solution.py:219
  13.9 2.0 %collective-permute-done.4.main.refs_1_ = bf16[32,4096]{1,0:T(8,128)(2,1)S(1)} collective-permute-done((bf16[32,4096]{1,0:T(8,128)(2,1)S(1)}, bf16[32,4096]{1,0:T(8,128)(2,1)S(1)}, u32[]{:S(2)}, u32[]{:S(2)}) %collective-permute-start.4) | collective-permute-done | bytes 262176 | tf_op jit(solution)/shard_map/ppermute | solution.py:219
  16.0 2.3 %collective-permute-start.6 = (bf16[32,512]{1,0:T(8,128)(2,1)S(1)}, bf16[32,512]{1,0:T(8,128)(2,1)S(1)}, u32[]{:S(2)}, u32[]{:S(2)}) collective-permute-start(bf16[32,512]{1,0:T(8,128)(2,1)S(1)} %edge.14), channel_id=1, source_target_pairs={{0,1},{1,0},{2,3},{3,2},{4,5},{5,4},{6,7},{7,6},{8,9},{9,8},{10,11... | collective-permute-start | bytes 98312 | tf_op jit(solution)/shard_map/ppermute | solution.py:219
  18.3 3.5 %collective-permute-start.3 = (bf16[32,512]{1,0:T(8,128)(2,1)S(1)}, bf16[32,512]{1,0:T(8,128)(2,1)S(1)}, u32[]{:S(2)}, u32[]{:S(2)}) collective-permute-start(bf16[32,512]{1,0:T(8,128)(2,1)S(1)} %get-tuple-element.56), channel_id=1, source_target_pairs={{0,7},{1,6},{2,5},{3,4},{4,11},{5,10},{6,9},{7,8},{8,15},{9,14},{1... | collective-permute-start | bytes 98312 | tf_op jit(solution)/shard_map/ppermute | solution.py:219
  21.8 1.5 %layer_t1_r0.1 = (bf16[8,64,4096]{2,1,0:T(8,128)(2,1)}, bf16[32,4096]{1,0:T(8,128)(2,1)S(1)}, bf16[32,512]{1,0:T(8,128)(2,1)S(1)}) custom-call(s32[258]{0:T(512)S(4)} %get-tuple-element.50.refs_0_.meta, bf16[32,4096]{1,0:T(8,128)(2,1)S(1)} %collective-permute-done.4.main.refs_1_, ...), custom_call_target="tpu_custom_call", output_to_operand_aliasing={{0}: (7, {})} | custom-call | flops 2415919104 | bytes 75497472 | tf_op jit(solution)/shard_map/layer_t1_r0/pallas_call | solution.py:165
  23.3 1.9 %collective-permute-start.10 = (bf16[32,4096]{1,0:T(8,128)(2,1)S(1)}, bf16[32,4096]{1,0:T(8,128)(2,1)S(1)}, u32[]{:S(2)}, u32[]{:S(2)}) collective-permute-start(bf16[32,4096]{1,0:T(8,128)(2,1)S(1)} %get-tuple-element.59.after.refs_6_), channel_id=1, source_target_pairs={{0,0},{1,1},{2,2},{3,3},{4,8},{5,9},{6,10},{7,11},{8,12},{9,13},{1... | collective-permute-start | bytes 786440 | tf_op jit(solution)/shard_map/ppermute | solution.py:219
  25.4 2.6 %collective-permute-start.11 = (bf16[32,512]{1,0:T(8,128)(2,1)S(1)}, bf16[32,512]{1,0:T(8,128)(2,1)S(1)}, u32[]{:S(2)}, u32[]{:S(2)}) collective-permute-start(bf16[32,512]{1,0:T(8,128)(2,1)S(1)} %get-tuple-element.63), channel_id=1, source_target_pairs={{0,0},{1,1},{2,2},{3,3},{4,11},{5,10},{6,9},{7,8},{8,15},{9,14},{1... | collective-permute-start | bytes 98312 | tf_op jit(solution)/shard_map/ppermute | solution.py:219
  28.0 1.5 %layer_t1_r32.1 = (bf16[8,64,4096]{2,1,0:T(8,128)(2,1)}, bf16[32,4096]{1,0:T(8,128)(2,1)S(1)}, bf16[32,512]{1,0:T(8,128)(2,1)S(1)}) custom-call(s32[258]{0:T(512)S(4)} %get-tuple-element.50.refs_0_.meta, bf16[32,4096]{1,0:T(8,128)(2,1)S(1)} %collective-permute-done.2.main.refs_1_, ...), custom_call_target="tpu_custom_call", output_to_operand_aliasing={{0}: (7, {})} | custom-call | flops 2415919104 | bytes 75497472 | tf_op jit(solution)/shard_map/layer_t1_r32/pallas_call | solution.py:165
  29.5 3.3 %collective-permute-start.8 = (bf16[32,4096]{1,0:T(8,128)(2,1)S(1)}, bf16[32,4096]{1,0:T(8,128)(2,1)S(1)}, u32[]{:S(2)}, u32[]{:S(2)}) collective-permute-start(bf16[32,4096]{1,0:T(8,128)(2,1)S(1)} %get-tuple-element.61.after.refs_6_), channel_id=1, source_target_pairs={{0,0},{1,1},{2,2},{3,3},{4,8},{5,9},{6,10},{7,11},{8,12},{9,13},{1... | collective-permute-start | bytes 786440 | tf_op jit(solution)/shard_map/ppermute | solution.py:219
  32.8 0.9 collective-permute-done.10.main.refs_1_
  33.8 0.9 collective-permute-start.12
  34.6 4.4 %collective-permute-start.9 = (bf16[32,512]{1,0:T(8,128)(2,1)S(1)}, bf16[32,512]{1,0:T(8,128)(2,1)S(1)}, u32[]{:S(2)}, u32[]{:S(2)}) collective-permute-start(bf16[32,512]{1,0:T(8,128)(2,1)S(1)} %get-tuple-element.62), channel_id=1, source_target_pairs={{0,0},{1,1},{2,2},{3,3},{4,11},{5,10},{6,9},{7,8},{8,15},{9,14},{1... | collective-permute-start | bytes 98312 | tf_op jit(solution)/shard_map/ppermute | solution.py:219
  39.0 1.5 %layer_t2_r0.1 = (bf16[8,64,4096]{2,1,0:T(8,128)(2,1)}, bf16[32,4096]{1,0:T(8,128)(2,1)S(1)}, bf16[32,512]{1,0:T(8,128)(2,1)S(1)}) custom-call(s32[258]{0:T(512)S(4)} %get-tuple-element.50.refs_0_.meta, bf16[32,4096]{1,0:T(8,128)(2,1)S(1)} %collective-permute-done.10.main.refs_1_, ...), custom_call_target="tpu_custom_call", output_to_operand_aliasing={{0}: (7, {})} | custom-call | flops 2415919104 | bytes 75497472 | tf_op jit(solution)/shard_map/layer_t2_r0/pallas_call | solution.py:165
  40.5 1.9 %collective-permute-start.16 = (bf16[32,4096]{1,0:T(8,128)(2,1)S(1)}, bf16[32,4096]{1,0:T(8,128)(2,1)S(1)}, u32[]{:S(2)}, u32[]{:S(2)}) collective-permute-start(bf16[32,4096]{1,0:T(8,128)(2,1)S(1)} %get-tuple-element.65.after.refs_6_), channel_id=1, source_target_pairs={{0,0},{1,1},{2,2},{3,3},{4,4},{5,5},{6,6},{7,7},{8,12},{9,13},{10,... | collective-permute-start | bytes 786440 | tf_op jit(solution)/shard_map/ppermute | solution.py:219
  42.5 0.4 collective-permute-start.13
  42.9 3.7 %collective-permute-start.17 = (bf16[32,512]{1,0:T(8,128)(2,1)S(1)}, bf16[32,512]{1,0:T(8,128)(2,1)S(1)}, u32[]{:S(2)}, u32[]{:S(2)}) collective-permute-start(bf16[32,512]{1,0:T(8,128)(2,1)S(1)} %get-tuple-element.69), channel_id=1, source_target_pairs={{0,0},{1,1},{2,2},{3,3},{4,4},{5,5},{6,6},{7,7},{8,15},{9,14},{10,... | collective-permute-start | bytes 98312 | tf_op jit(solution)/shard_map/ppermute | solution.py:219
  46.6 1.5 %layer_t2_r32.1 = (bf16[8,64,4096]{2,1,0:T(8,128)(2,1)}, bf16[32,4096]{1,0:T(8,128)(2,1)S(1)}, bf16[32,512]{1,0:T(8,128)(2,1)S(1)}) custom-call(s32[258]{0:T(512)S(4)} %get-tuple-element.50.refs_0_.meta, bf16[32,4096]{1,0:T(8,128)(2,1)S(1)} %collective-permute-done.8.main.refs_1_, ...), custom_call_target="tpu_custom_call", output_to_operand_aliasing={{0}: (7, {})} | custom-call | flops 2415919104 | bytes 75497472 | tf_op jit(solution)/shard_map/layer_t2_r32/pallas_call | solution.py:165
  48.1 2.2 %collective-permute-start.14 = (bf16[32,4096]{1,0:T(8,128)(2,1)S(1)}, bf16[32,4096]{1,0:T(8,128)(2,1)S(1)}, u32[]{:S(2)}, u32[]{:S(2)}) collective-permute-start(bf16[32,4096]{1,0:T(8,128)(2,1)S(1)} %get-tuple-element.67.after.refs_6_), channel_id=1, source_target_pairs={{0,0},{1,1},{2,2},{3,3},{4,4},{5,5},{6,6},{7,7},{8,12},{9,13},{10,... | collective-permute-start | bytes 786440 | tf_op jit(solution)/shard_map/ppermute | solution.py:219
  50.3 0.3 collective-permute-done.16.main.refs_1_
  50.6 1.2 collective-permute-start.18
  51.8 4.3 %collective-permute-start.15 = (bf16[32,512]{1,0:T(8,128)(2,1)S(1)}, bf16[32,512]{1,0:T(8,128)(2,1)S(1)}, u32[]{:S(2)}, u32[]{:S(2)}) collective-permute-start(bf16[32,512]{1,0:T(8,128)(2,1)S(1)} %get-tuple-element.68), channel_id=1, source_target_pairs={{0,0},{1,1},{2,2},{3,3},{4,4},{5,5},{6,6},{7,7},{8,15},{9,14},{10,... | collective-permute-start | bytes 98312 | tf_op jit(solution)/shard_map/ppermute | solution.py:219
  56.2 1.5 %layer_t3_r0.1 = (bf16[8,64,4096]{2,1,0:T(8,128)(2,1)}, bf16[32,4096]{1,0:T(8,128)(2,1)S(1)}, bf16[32,512]{1,0:T(8,128)(2,1)S(1)}) custom-call(s32[258]{0:T(512)S(4)} %get-tuple-element.50.refs_0_.meta, bf16[32,4096]{1,0:T(8,128)(2,1)S(1)} %collective-permute-done.16.main.refs_1_, ...), custom_call_target="tpu_custom_call", output_to_operand_aliasing={{0}: (7, {})} | custom-call | flops 2415919104 | bytes 75497472 | tf_op jit(solution)/shard_map/layer_t3_r0/pallas_call | solution.py:165
  57.7 2.8 %collective-permute-start.22 = (bf16[32,4096]{1,0:T(8,128)(2,1)S(1)}, bf16[32,4096]{1,0:T(8,128)(2,1)S(1)}, u32[]{:S(2)}, u32[]{:S(2)}) collective-permute-start(bf16[32,4096]{1,0:T(8,128)(2,1)S(1)} %get-tuple-element.71.after.refs_6_), channel_id=1, source_target_pairs={{0,0},{1,1},{2,2},{3,3},{4,4},{5,5},{6,6},{7,7},{8,8},{9,9},{10,10... | collective-permute-start | bytes 786440 | tf_op jit(solution)/shard_map/ppermute | solution.py:219
  60.5 0.8 collective-permute-start.19
  61.3 1.9 %collective-permute-start.23 = (bf16[32,512]{1,0:T(8,128)(2,1)S(1)}, bf16[32,512]{1,0:T(8,128)(2,1)S(1)}, u32[]{:S(2)}, u32[]{:S(2)}) collective-permute-start(bf16[32,512]{1,0:T(8,128)(2,1)S(1)} %get-tuple-element.75), channel_id=1, source_target_pairs={{0,0},{1,1},{2,2},{3,3},{4,4},{5,5},{6,6},{7,7},{8,8},{9,9},{10,10... | collective-permute-start | bytes 98312 | tf_op jit(solution)/shard_map/ppermute | solution.py:219
  63.2 1.7 %layer_t3_r32.1 = (bf16[8,64,4096]{2,1,0:T(8,128)(2,1)}, bf16[32,4096]{1,0:T(8,128)(2,1)S(1)}, bf16[32,512]{1,0:T(8,128)(2,1)S(1)}) custom-call(s32[258]{0:T(512)S(4)} %get-tuple-element.50.refs_0_.meta, bf16[32,4096]{1,0:T(8,128)(2,1)S(1)} %collective-permute-done.14.main.refs_1_, ...), custom_call_target="tpu_custom_call", output_to_operand_aliasing={{0}: (7, {})} | custom-call | flops 2415919104 | bytes 75497472 | tf_op jit(solution)/shard_map/layer_t3_r32/pallas_call | solution.py:165
  64.9 3.4 %collective-permute-start.20 = (bf16[32,4096]{1,0:T(8,128)(2,1)S(1)}, bf16[32,4096]{1,0:T(8,128)(2,1)S(1)}, u32[]{:S(2)}, u32[]{:S(2)}) collective-permute-start(bf16[32,4096]{1,0:T(8,128)(2,1)S(1)} %get-tuple-element.73.after.refs_6_), channel_id=1, source_target_pairs={{0,0},{1,1},{2,2},{3,3},{4,4},{5,5},{6,6},{7,7},{8,8},{9,9},{10,10... | collective-permute-start | bytes 786440 | tf_op jit(solution)/shard_map/ppermute | solution.py:219
  68.4 0.8 collective-permute-start.24
  69.2 4.0 %collective-permute-start.21 = (bf16[32,512]{1,0:T(8,128)(2,1)S(1)}, bf16[32,512]{1,0:T(8,128)(2,1)S(1)}, u32[]{:S(2)}, u32[]{:S(2)}) collective-permute-start(bf16[32,512]{1,0:T(8,128)(2,1)S(1)} %get-tuple-element.74), channel_id=1, source_target_pairs={{0,0},{1,1},{2,2},{3,3},{4,4},{5,5},{6,6},{7,7},{8,8},{9,9},{10,10... | collective-permute-start | bytes 98312 | tf_op jit(solution)/shard_map/ppermute | solution.py:219
  73.3 1.5 %layer_t4_r0.1 = (bf16[8,64,4096]{2,1,0:T(8,128)(2,1)}, bf16[32,4096]{1,0:T(8,128)(2,1)S(1)}, bf16[32,512]{1,0:T(8,128)(2,1)S(1)}) custom-call(s32[258]{0:T(512)S(4)} %get-tuple-element.50.refs_0_.meta, bf16[32,4096]{1,0:T(8,128)(2,1)S(1)} %collective-permute-done.22.main.refs_1_, ...), custom_call_target="tpu_custom_call", output_to_operand_aliasing={{0}: (7, {})} | custom-call | flops 2415919104 | bytes 75497472 | tf_op jit(solution)/shard_map/layer_t4_r0/pallas_call | solution.py:165
  74.8 2.8 %collective-permute-start.28 = (bf16[32,4096]{1,0:T(8,128)(2,1)S(1)}, bf16[32,4096]{1,0:T(8,128)(2,1)S(1)}, u32[]{:S(2)}, u32[]{:S(2)}) collective-permute-start(bf16[32,4096]{1,0:T(8,128)(2,1)S(1)} %get-tuple-element.77.after.refs_6_), channel_id=1, source_target_pairs={{0,0},{1,1},{2,2},{3,3},{4,4},{5,5},{6,6},{7,7},{8,8},{9,9},{10,10... | collective-permute-start | bytes 786440 | tf_op jit(solution)/shard_map/ppermute | solution.py:219
  77.6 0.8 collective-permute-start.25
  78.4 2.5 %collective-permute-start.29 = (bf16[32,512]{1,0:T(8,128)(2,1)S(1)}, bf16[32,512]{1,0:T(8,128)(2,1)S(1)}, u32[]{:S(2)}, u32[]{:S(2)}) collective-permute-start(bf16[32,512]{1,0:T(8,128)(2,1)S(1)} %get-tuple-element.81), channel_id=1, source_target_pairs={{0,0},{1,1},{2,2},{3,3},{4,4},{5,5},{6,6},{7,7},{8,8},{9,9},{10,10... | collective-permute-start | bytes 98312 | tf_op jit(solution)/shard_map/ppermute | solution.py:219
  80.9 1.5 %layer_t4_r32.1 = (bf16[8,64,4096]{2,1,0:T(8,128)(2,1)}, bf16[32,4096]{1,0:T(8,128)(2,1)S(1)}, bf16[32,512]{1,0:T(8,128)(2,1)S(1)}) custom-call(s32[258]{0:T(512)S(4)} %get-tuple-element.50.refs_0_.meta, bf16[32,4096]{1,0:T(8,128)(2,1)S(1)} %collective-permute-done.20.main.refs_1_, ...), custom_call_target="tpu_custom_call", output_to_operand_aliasing={{0}: (7, {})} | custom-call | flops 2415919104 | bytes 75497472 | tf_op jit(solution)/shard_map/layer_t4_r32/pallas_call | solution.py:165
  82.4 2.8 %collective-permute-start.26 = (bf16[32,4096]{1,0:T(8,128)(2,1)S(1)}, bf16[32,4096]{1,0:T(8,128)(2,1)S(1)}, u32[]{:S(2)}, u32[]{:S(2)}) collective-permute-start(bf16[32,4096]{1,0:T(8,128)(2,1)S(1)} %get-tuple-element.79.after.refs_6_), channel_id=1, source_target_pairs={{0,0},{1,1},{2,2},{3,3},{4,4},{5,5},{6,6},{7,7},{8,8},{9,9},{10,10... | collective-permute-start | bytes 786440 | tf_op jit(solution)/shard_map/ppermute | solution.py:219
  85.3 0.8 collective-permute-start.30
  86.1 4.2 %collective-permute-start.27 = (bf16[32,512]{1,0:T(8,128)(2,1)S(1)}, bf16[32,512]{1,0:T(8,128)(2,1)S(1)}, u32[]{:S(2)}, u32[]{:S(2)}) collective-permute-start(bf16[32,512]{1,0:T(8,128)(2,1)S(1)} %get-tuple-element.80), channel_id=1, source_target_pairs={{0,0},{1,1},{2,2},{3,3},{4,4},{5,5},{6,6},{7,7},{8,8},{9,9},{10,10... | collective-permute-start | bytes 98312 | tf_op jit(solution)/shard_map/ppermute | solution.py:219
  90.4 1.5 %layer_t5_r0.1 = (bf16[8,64,4096]{2,1,0:T(8,128)(2,1)}, bf16[32,4096]{1,0:T(8,128)(2,1)S(1)}, bf16[32,512]{1,0:T(8,128)(2,1)S(1)}) custom-call(s32[258]{0:T(512)S(4)} %get-tuple-element.50.refs_0_.meta, bf16[32,4096]{1,0:T(8,128)(2,1)S(1)} %collective-permute-done.28.main.refs_1_, ...), custom_call_target="tpu_custom_call", output_to_operand_aliasing={{0}: (7, {})} | custom-call | flops 2415919104 | bytes 75497472 | tf_op jit(solution)/shard_map/layer_t5_r0/pallas_call | solution.py:165
  91.9 2.5 %collective-permute-start.34 = (bf16[32,4096]{1,0:T(8,128)(2,1)S(1)}, bf16[32,4096]{1,0:T(8,128)(2,1)S(1)}, u32[]{:S(2)}, u32[]{:S(2)}) collective-permute-start(bf16[32,4096]{1,0:T(8,128)(2,1)S(1)} %get-tuple-element.83.after.refs_6_), channel_id=1, source_target_pairs={{0,0},{1,1},{2,2},{3,3},{4,4},{5,5},{6,6},{7,7},{8,8},{9,9},{10,10... | collective-permute-start | bytes 786440 | tf_op jit(solution)/shard_map/ppermute | solution.py:219
  94.4 0.4 collective-permute-start.31
  94.8 2.9 %collective-permute-start.35 = (bf16[32,512]{1,0:T(8,128)(2,1)S(1)}, bf16[32,512]{1,0:T(8,128)(2,1)S(1)}, u32[]{:S(2)}, u32[]{:S(2)}) collective-permute-start(bf16[32,512]{1,0:T(8,128)(2,1)S(1)} %get-tuple-element.87), channel_id=1, source_target_pairs={{0,0},{1,1},{2,2},{3,3},{4,4},{5,5},{6,6},{7,7},{8,8},{9,9},{10,10... | collective-permute-start | bytes 98312 | tf_op jit(solution)/shard_map/ppermute | solution.py:219
  97.7 1.5 %layer_t5_r32.1 = (bf16[8,64,4096]{2,1,0:T(8,128)(2,1)}, bf16[32,4096]{1,0:T(8,128)(2,1)S(1)}, bf16[32,512]{1,0:T(8,128)(2,1)S(1)}) custom-call(s32[258]{0:T(512)S(4)} %get-tuple-element.50.refs_0_.meta, bf16[32,4096]{1,0:T(8,128)(2,1)S(1)} %collective-permute-done.26.main.refs_1_, ...), custom_call_target="tpu_custom_call", output_to_operand_aliasing={{0}: (7, {})} | custom-call | flops 2415919104 | bytes 75497472 | tf_op jit(solution)/shard_map/layer_t5_r32/pallas_call | solution.py:165
  99.2 3.3 %collective-permute-start.32 = (bf16[32,4096]{1,0:T(8,128)(2,1)S(1)}, bf16[32,4096]{1,0:T(8,128)(2,1)S(1)}, u32[]{:S(2)}, u32[]{:S(2)}) collective-permute-start(bf16[32,4096]{1,0:T(8,128)(2,1)S(1)} %get-tuple-element.85.after.refs_6_), channel_id=1, source_target_pairs={{0,0},{1,1},{2,2},{3,3},{4,4},{5,5},{6,6},{7,7},{8,8},{9,9},{10,10... | collective-permute-start | bytes 786440 | tf_op jit(solution)/shard_map/ppermute | solution.py:219
  102.6 0.9 collective-permute-start.36
  103.5 2.8 %collective-permute-start.33 = (bf16[32,512]{1,0:T(8,128)(2,1)S(1)}, bf16[32,512]{1,0:T(8,128)(2,1)S(1)}, u32[]{:S(2)}, u32[]{:S(2)}) collective-permute-start(bf16[32,512]{1,0:T(8,128)(2,1)S(1)} %get-tuple-element.86), channel_id=1, source_target_pairs={{0,0},{1,1},{2,2},{3,3},{4,4},{5,5},{6,6},{7,7},{8,8},{9,9},{10,10... | collective-permute-start | bytes 98312 | tf_op jit(solution)/shard_map/ppermute | solution.py:219
  106.3 1.5 %layer_t6_r0.1 = (bf16[8,64,4096]{2,1,0:T(8,128)(2,1)}, bf16[32,4096]{1,0:T(8,128)(2,1)S(1)}, bf16[32,512]{1,0:T(8,128)(2,1)S(1)}) custom-call(s32[258]{0:T(512)S(4)} %get-tuple-element.50.refs_0_.meta, bf16[32,4096]{1,0:T(8,128)(2,1)S(1)} %collective-permute-done.34.main.refs_1_, ...), custom_call_target="tpu_custom_call", output_to_operand_aliasing={{0}: (7, {})} | custom-call | flops 2415919104 | bytes 75497472 | tf_op jit(solution)/shard_map/layer_t6_r0/pallas_call | solution.py:165
  107.8 1.8 %collective-permute-done.33.far.refs_2_ = bf16[32,512]{1,0:T(8,128)(2,1)S(1)} collective-permute-done((bf16[32,512]{1,0:T(8,128)(2,1)S(1)}, bf16[32,512]{1,0:T(8,128)(2,1)S(1)}, u32[]{:S(2)}, u32[]{:S(2)}) %collective-permute-start.33) | collective-permute-done | bytes 32800 | tf_op jit(solution)/shard_map/ppermute | solution.py:219
  109.6 0.9 collective-permute-start.37
  110.5 3.8 %collective-permute-start.41 = (bf16[32,4096]{1,0:T(8,128)(2,1)S(1)}, bf16[32,4096]{1,0:T(8,128)(2,1)S(1)}, u32[]{:S(2)}, u32[]{:S(2)}) collective-permute-start(bf16[32,4096]{1,0:T(8,128)(2,1)S(1)} %get-tuple-element.89.after.refs_6_), channel_id=1, source_target_pairs={{0,0},{1,1},{2,2},{3,3},{4,4},{5,5},{6,6},{7,7},{8,8},{9,9},{10,10... | collective-permute-start | bytes 786440 | tf_op jit(solution)/shard_map/ppermute | solution.py:219
  114.3 1.5 %layer_t6_r32.1 = (bf16[8,64,4096]{2,1,0:T(8,128)(2,1)}, bf16[32,4096]{1,0:T(8,128)(2,1)S(1)}, bf16[32,512]{1,0:T(8,128)(2,1)S(1)}) custom-call(s32[258]{0:T(512)S(4)} %get-tuple-element.50.refs_0_.meta, bf16[32,4096]{1,0:T(8,128)(2,1)S(1)} %collective-permute-done.32.main.refs_1_, ...), custom_call_target="tpu_custom_call", output_to_operand_aliasing={{0}: (7, {})} | custom-call | flops 2415919104 | bytes 75497472 | tf_op jit(solution)/shard_map/layer_t6_r32/pallas_call | solution.py:165
  115.8 1.9 %collective-permute-start.38 = (bf16[32,4096]{1,0:T(8,128)(2,1)S(1)}, bf16[32,4096]{1,0:T(8,128)(2,1)S(1)}, u32[]{:S(2)}, u32[]{:S(2)}) collective-permute-start(bf16[32,4096]{1,0:T(8,128)(2,1)S(1)} %get-tuple-element.91.after.refs_6_), channel_id=1, source_target_pairs={{0,0},{1,1},{2,2},{3,3},{4,4},{5,5},{6,6},{7,7},{8,8},{9,9},{10,10... | collective-permute-start | bytes 786440 | tf_op jit(solution)/shard_map/ppermute | solution.py:219
  117.8 4.5 %collective-permute-start.42 = (bf16[32,512]{1,0:T(8,128)(2,1)S(1)}, bf16[32,512]{1,0:T(8,128)(2,1)S(1)}, u32[]{:S(2)}, u32[]{:S(2)}) collective-permute-start(bf16[32,512]{1,0:T(8,128)(2,1)S(1)} %get-tuple-element.93), channel_id=1, source_target_pairs={{0,0},{1,1},{2,2},{3,3},{4,4},{5,5},{6,6},{7,7},{8,8},{9,9},{10,10... | collective-permute-start | bytes 98312 | tf_op jit(solution)/shard_map/ppermute | solution.py:219
  122.3 1.9 %collective-permute-start.39 = (bf16[32,512]{1,0:T(8,128)(2,1)S(1)}, bf16[32,512]{1,0:T(8,128)(2,1)S(1)}, u32[]{:S(2)}, u32[]{:S(2)}) collective-permute-start(bf16[32,512]{1,0:T(8,128)(2,1)S(1)} %get-tuple-element.92), channel_id=1, source_target_pairs={{0,0},{1,1},{2,2},{3,3},{4,4},{5,5},{6,6},{7,7},{8,8},{9,9},{10,10... | collective-permute-start | bytes 98312 | tf_op jit(solution)/shard_map/ppermute | solution.py:219
  124.3 0.6 collective-permute-start.43
  124.9 3.5 %collective-permute-done.39.far.refs_2_ = bf16[32,512]{1,0:T(8,128)(2,1)S(1)} collective-permute-done((bf16[32,512]{1,0:T(8,128)(2,1)S(1)}, bf16[32,512]{1,0:T(8,128)(2,1)S(1)}, u32[]{:S(2)}, u32[]{:S(2)}) %collective-permute-start.39) | collective-permute-done | bytes 32800 | tf_op jit(solution)/shard_map/ppermute | solution.py:219
  128.4 2.3 %layer_t7_r0.1.refs_6_ = bf16[8,64,4096]{2,1,0:T(8,128)(2,1)} custom-call(s32[258]{0:T(512)S(4)} %get-tuple-element.50.refs_0_.meta, bf16[32,4096]{1,0:T(8,128)(2,1)S(1)} %collective-permute-done.41.main.refs_1_, bf16[32,512]{1,0:T(8,128)(2,1)S(1)} %collective-permute-done.42.far.refs_2_, ...), custom_call_target="tpu_custom_call", output_to_operand_aliasing={{}: (7, {})} | custom-call | flops 2415919104 | bytes 75497472 | tf_op jit(solution)/shard_map/layer_t7_r0/pallas_call | solution.py:165
  130.8 2.1 %layer_t7_r32.1 = bf16[8,64,4096]{2,1,0:T(8,128)(2,1)} custom-call(s32[258]{0:T(512)S(4)} %get-tuple-element.50.refs_0_.meta, bf16[32,4096]{1,0:T(8,128)(2,1)S(1)} %collective-permute-done.38.main.refs_1_, bf16[32,512]{1,0:T(8,128)(2,1)S(1)} %collective-permute-done.39.far.refs_2_, ...), custom_call_target="tpu_custom_call", output_to_operand_aliasing={{}: (6, {})} | custom-call | flops 2415919104 | bytes 75497472 | tf_op jit(solution)/shard_map/layer_t7_r32/pallas_call | solution.py:165
  (56 shorter events, 0.5 us)
Async XLA Ops:
  0.9 5.5 %collective-permute-start = (bf16[64,512]{1,0:T(8,128)(2,1)S(1)}, bf16[64,512]{1,0:T(8,128)(2,1)S(1)}, u32[]{:S(2)}, u32[]{:S(2)}) collective-permute-start(bf16[64,512]{1,0:T(8,128)(2,1)S(1)} %get-tuple-element.96), channel_id=1, source_target_pairs={{0,3},{1,2},{2,1},{3,0},{4,7},{5,6},{6,5},{7,4},{8,11},{9,10},{10,... | collective-permute-start | bytes 196616 | tf_op jit(solution)/shard_map/ppermute | solution.py:219
  2.7 3.6 %collective-permute-start.1 = (bf16[64,512]{1,0:T(8,128)(2,1)S(1)}, bf16[64,512]{1,0:T(8,128)(2,1)S(1)}, u32[]{:S(2)}, u32[]{:S(2)}) collective-permute-start(bf16[64,512]{1,0:T(8,128)(2,1)S(1)} %get-tuple-element.95), channel_id=1, source_target_pairs={{0,1},{1,0},{2,3},{3,2},{4,5},{5,4},{6,7},{7,6},{8,9},{9,8},{10,11... | collective-permute-start | bytes 196616 | tf_op jit(solution)/shard_map/ppermute | solution.py:219
  7.9 8.1 %collective-permute-start.4 = (bf16[32,4096]{1,0:T(8,128)(2,1)S(1)}, bf16[32,4096]{1,0:T(8,128)(2,1)S(1)}, u32[]{:S(2)}, u32[]{:S(2)}) collective-permute-start(bf16[32,4096]{1,0:T(8,128)(2,1)S(1)} %get-tuple-element.54.refs_6_), channel_id=1, source_target_pairs={{0,4},{1,5},{2,6},{3,7},{4,8},{5,9},{6,10},{7,11},{8,12},{9,13},{1... | collective-permute-start | bytes 786440 | tf_op jit(solution)/shard_map/ppermute | solution.py:219
  7.9 6.0 %collective-permute-start.5 = (bf16[32,512]{1,0:T(8,128)(2,1)S(1)}, bf16[32,512]{1,0:T(8,128)(2,1)S(1)}, u32[]{:S(2)}, u32[]{:S(2)}) collective-permute-start(bf16[32,512]{1,0:T(8,128)(2,1)S(1)} %get-tuple-element.57), channel_id=1, source_target_pairs={{0,7},{1,6},{2,5},{3,4},{4,11},{5,10},{6,9},{7,8},{8,15},{9,14},{1... | collective-permute-start | bytes 98312 | tf_op jit(solution)/shard_map/ppermute | solution.py:219
  11.2 14.0 %collective-permute-start.2 = (bf16[32,4096]{1,0:T(8,128)(2,1)S(1)}, bf16[32,4096]{1,0:T(8,128)(2,1)S(1)}, u32[]{:S(2)}, u32[]{:S(2)}) collective-permute-start(bf16[32,4096]{1,0:T(8,128)(2,1)S(1)} %get-tuple-element.55.after.refs_6_), channel_id=1, source_target_pairs={{0,4},{1,5},{2,6},{3,7},{4,8},{5,9},{6,10},{7,11},{8,12},{9,13},{1... | collective-permute-start | bytes 786440 | tf_op jit(solution)/shard_map/ppermute | solution.py:219
  16.0 5.8 %collective-permute-start.6 = (bf16[32,512]{1,0:T(8,128)(2,1)S(1)}, bf16[32,512]{1,0:T(8,128)(2,1)S(1)}, u32[]{:S(2)}, u32[]{:S(2)}) collective-permute-start(bf16[32,512]{1,0:T(8,128)(2,1)S(1)} %edge.14), channel_id=1, source_target_pairs={{0,1},{1,0},{2,3},{3,2},{4,5},{5,4},{6,7},{7,6},{8,9},{9,8},{10,11... | collective-permute-start | bytes 98312 | tf_op jit(solution)/shard_map/ppermute | solution.py:219
  18.3 6.9 %collective-permute-start.3 = (bf16[32,512]{1,0:T(8,128)(2,1)S(1)}, bf16[32,512]{1,0:T(8,128)(2,1)S(1)}, u32[]{:S(2)}, u32[]{:S(2)}) collective-permute-start(bf16[32,512]{1,0:T(8,128)(2,1)S(1)} %get-tuple-element.56), channel_id=1, source_target_pairs={{0,7},{1,6},{2,5},{3,4},{4,11},{5,10},{6,9},{7,8},{8,15},{9,14},{1... | collective-permute-start | bytes 98312 | tf_op jit(solution)/shard_map/ppermute | solution.py:219
  23.3 10.5 %collective-permute-start.10 = (bf16[32,4096]{1,0:T(8,128)(2,1)S(1)}, bf16[32,4096]{1,0:T(8,128)(2,1)S(1)}, u32[]{:S(2)}, u32[]{:S(2)}) collective-permute-start(bf16[32,4096]{1,0:T(8,128)(2,1)S(1)} %get-tuple-element.59.after.refs_6_), channel_id=1, source_target_pairs={{0,0},{1,1},{2,2},{3,3},{4,8},{5,9},{6,10},{7,11},{8,12},{9,13},{1... | collective-permute-start | bytes 786440 | tf_op jit(solution)/shard_map/ppermute | solution.py:219
  25.3 2.8 %collective-permute-start.7 = (bf16[32,512]{1,0:T(8,128)(2,1)S(1)}, bf16[32,512]{1,0:T(8,128)(2,1)S(1)}, u32[]{:S(2)}, u32[]{:S(2)}) collective-permute-start(bf16[32,512]{1,0:T(8,128)(2,1)S(1)} %edge.15), channel_id=1, source_target_pairs={{0,1},{1,0},{2,3},{3,2},{4,5},{5,4},{6,7},{7,6},{8,9},{9,8},{10,11... | collective-permute-start | bytes 98312 | tf_op jit(solution)/shard_map/ppermute | solution.py:219
  25.4 7.4 %collective-permute-start.11 = (bf16[32,512]{1,0:T(8,128)(2,1)S(1)}, bf16[32,512]{1,0:T(8,128)(2,1)S(1)}, u32[]{:S(2)}, u32[]{:S(2)}) collective-permute-start(bf16[32,512]{1,0:T(8,128)(2,1)S(1)} %get-tuple-element.63), channel_id=1, source_target_pairs={{0,0},{1,1},{2,2},{3,3},{4,11},{5,10},{6,9},{7,8},{8,15},{9,14},{1... | collective-permute-start | bytes 98312 | tf_op jit(solution)/shard_map/ppermute | solution.py:219
  29.5 12.9 %collective-permute-start.8 = (bf16[32,4096]{1,0:T(8,128)(2,1)S(1)}, bf16[32,4096]{1,0:T(8,128)(2,1)S(1)}, u32[]{:S(2)}, u32[]{:S(2)}) collective-permute-start(bf16[32,4096]{1,0:T(8,128)(2,1)S(1)} %get-tuple-element.61.after.refs_6_), channel_id=1, source_target_pairs={{0,0},{1,1},{2,2},{3,3},{4,8},{5,9},{6,10},{7,11},{8,12},{9,13},{1... | collective-permute-start | bytes 786440 | tf_op jit(solution)/shard_map/ppermute | solution.py:219
  33.8 5.3 %collective-permute-start.12 = (bf16[32,512]{1,0:T(8,128)(2,1)S(1)}, bf16[32,512]{1,0:T(8,128)(2,1)S(1)}, u32[]{:S(2)}, u32[]{:S(2)}) collective-permute-start(bf16[32,512]{1,0:T(8,128)(2,1)S(1)} %edge.16), channel_id=1, source_target_pairs={{0,1},{1,0},{2,3},{3,2},{4,5},{5,4},{6,7},{7,6},{8,9},{9,8},{10,11... | collective-permute-start | bytes 98312 | tf_op jit(solution)/shard_map/ppermute | solution.py:219
  34.6 7.8 %collective-permute-start.9 = (bf16[32,512]{1,0:T(8,128)(2,1)S(1)}, bf16[32,512]{1,0:T(8,128)(2,1)S(1)}, u32[]{:S(2)}, u32[]{:S(2)}) collective-permute-start(bf16[32,512]{1,0:T(8,128)(2,1)S(1)} %get-tuple-element.62), channel_id=1, source_target_pairs={{0,0},{1,1},{2,2},{3,3},{4,11},{5,10},{6,9},{7,8},{8,15},{9,14},{1... | collective-permute-start | bytes 98312 | tf_op jit(solution)/shard_map/ppermute | solution.py:219
  40.5 10.1 %collective-permute-start.16 = (bf16[32,4096]{1,0:T(8,128)(2,1)S(1)}, bf16[32,4096]{1,0:T(8,128)(2,1)S(1)}, u32[]{:S(2)}, u32[]{:S(2)}) collective-permute-start(bf16[32,4096]{1,0:T(8,128)(2,1)S(1)} %get-tuple-element.65.after.refs_6_), channel_id=1, source_target_pairs={{0,0},{1,1},{2,2},{3,3},{4,4},{5,5},{6,6},{7,7},{8,12},{9,13},{10,... | collective-permute-start | bytes 786440 | tf_op jit(solution)/shard_map/ppermute | solution.py:219
  42.5 4.1 %collective-permute-start.13 = (bf16[32,512]{1,0:T(8,128)(2,1)S(1)}, bf16[32,512]{1,0:T(8,128)(2,1)S(1)}, u32[]{:S(2)}, u32[]{:S(2)}) collective-permute-start(bf16[32,512]{1,0:T(8,128)(2,1)S(1)} %edge.17), channel_id=1, source_target_pairs={{0,1},{1,0},{2,3},{3,2},{4,5},{5,4},{6,7},{7,6},{8,9},{9,8},{10,11... | collective-permute-start | bytes 98312 | tf_op jit(solution)/shard_map/ppermute | solution.py:219
  42.9 7.4 %collective-permute-start.17 = (bf16[32,512]{1,0:T(8,128)(2,1)S(1)}, bf16[32,512]{1,0:T(8,128)(2,1)S(1)}, u32[]{:S(2)}, u32[]{:S(2)}) collective-permute-start(bf16[32,512]{1,0:T(8,128)(2,1)S(1)} %get-tuple-element.69), channel_id=1, source_target_pairs={{0,0},{1,1},{2,2},{3,3},{4,4},{5,5},{6,6},{7,7},{8,15},{9,14},{10,... | collective-permute-start | bytes 98312 | tf_op jit(solution)/shard_map/ppermute | solution.py:219
  48.1 12.3 %collective-permute-start.14 = (bf16[32,4096]{1,0:T(8,128)(2,1)S(1)}, bf16[32,4096]{1,0:T(8,128)(2,1)S(1)}, u32[]{:S(2)}, u32[]{:S(2)}) collective-permute-start(bf16[32,4096]{1,0:T(8,128)(2,1)S(1)} %get-tuple-element.67.after.refs_6_), channel_id=1, source_target_pairs={{0,0},{1,1},{2,2},{3,3},{4,4},{5,5},{6,6},{7,7},{8,12},{9,13},{10,... | collective-permute-start | bytes 786440 | tf_op jit(solution)/shard_map/ppermute | solution.py:219
  50.6 5.5 %collective-permute-start.18 = (bf16[32,512]{1,0:T(8,128)(2,1)S(1)}, bf16[32,512]{1,0:T(8,128)(2,1)S(1)}, u32[]{:S(2)}, u32[]{:S(2)}) collective-permute-start(bf16[32,512]{1,0:T(8,128)(2,1)S(1)} %edge.18), channel_id=1, source_target_pairs={{0,1},{1,0},{2,3},{3,2},{4,5},{5,4},{6,7},{7,6},{8,9},{9,8},{10,11... | collective-permute-start | bytes 98312 | tf_op jit(solution)/shard_map/ppermute | solution.py:219
  51.8 8.6 %collective-permute-start.15 = (bf16[32,512]{1,0:T(8,128)(2,1)S(1)}, bf16[32,512]{1,0:T(8,128)(2,1)S(1)}, u32[]{:S(2)}, u32[]{:S(2)}) collective-permute-start(bf16[32,512]{1,0:T(8,128)(2,1)S(1)} %get-tuple-element.68), channel_id=1, source_target_pairs={{0,0},{1,1},{2,2},{3,3},{4,4},{5,5},{6,6},{7,7},{8,15},{9,14},{10,... | collective-permute-start | bytes 98312 | tf_op jit(solution)/shard_map/ppermute | solution.py:219
  57.7 10.7 %collective-permute-start.22 = (bf16[32,4096]{1,0:T(8,128)(2,1)S(1)}, bf16[32,4096]{1,0:T(8,128)(2,1)S(1)}, u32[]{:S(2)}, u32[]{:S(2)}) collective-permute-start(bf16[32,4096]{1,0:T(8,128)(2,1)S(1)} %get-tuple-element.71.after.refs_6_), channel_id=1, source_target_pairs={{0,0},{1,1},{2,2},{3,3},{4,4},{5,5},{6,6},{7,7},{8,8},{9,9},{10,10... | collective-permute-start | bytes 786440 | tf_op jit(solution)/shard_map/ppermute | solution.py:219
  60.5 2.8 %collective-permute-start.19 = (bf16[32,512]{1,0:T(8,128)(2,1)S(1)}, bf16[32,512]{1,0:T(8,128)(2,1)S(1)}, u32[]{:S(2)}, u32[]{:S(2)}) collective-permute-start(bf16[32,512]{1,0:T(8,128)(2,1)S(1)} %edge.19), channel_id=1, source_target_pairs={{0,1},{1,0},{2,3},{3,2},{4,5},{5,4},{6,7},{7,6},{8,9},{9,8},{10,11... | collective-permute-start | bytes 98312 | tf_op jit(solution)/shard_map/ppermute | solution.py:219
  61.3 7.0 %collective-permute-start.23 = (bf16[32,512]{1,0:T(8,128)(2,1)S(1)}, bf16[32,512]{1,0:T(8,128)(2,1)S(1)}, u32[]{:S(2)}, u32[]{:S(2)}) collective-permute-start(bf16[32,512]{1,0:T(8,128)(2,1)S(1)} %get-tuple-element.75), channel_id=1, source_target_pairs={{0,0},{1,1},{2,2},{3,3},{4,4},{5,5},{6,6},{7,7},{8,8},{9,9},{10,10... | collective-permute-start | bytes 98312 | tf_op jit(solution)/shard_map/ppermute | solution.py:219
  64.9 12.6 %collective-permute-start.20 = (bf16[32,4096]{1,0:T(8,128)(2,1)S(1)}, bf16[32,4096]{1,0:T(8,128)(2,1)S(1)}, u32[]{:S(2)}, u32[]{:S(2)}) collective-permute-start(bf16[32,4096]{1,0:T(8,128)(2,1)S(1)} %get-tuple-element.73.after.refs_6_), channel_id=1, source_target_pairs={{0,0},{1,1},{2,2},{3,3},{4,4},{5,5},{6,6},{7,7},{8,8},{9,9},{10,10... | collective-permute-start | bytes 786440 | tf_op jit(solution)/shard_map/ppermute | solution.py:219
  68.4 4.9 %collective-permute-start.24 = (bf16[32,512]{1,0:T(8,128)(2,1)S(1)}, bf16[32,512]{1,0:T(8,128)(2,1)S(1)}, u32[]{:S(2)}, u32[]{:S(2)}) collective-permute-start(bf16[32,512]{1,0:T(8,128)(2,1)S(1)} %edge.20), channel_id=1, source_target_pairs={{0,1},{1,0},{2,3},{3,2},{4,5},{5,4},{6,7},{7,6},{8,9},{9,8},{10,11... | collective-permute-start | bytes 98312 | tf_op jit(solution)/shard_map/ppermute | solution.py:219
  69.2 8.3 %collective-permute-start.21 = (bf16[32,512]{1,0:T(8,128)(2,1)S(1)}, bf16[32,512]{1,0:T(8,128)(2,1)S(1)}, u32[]{:S(2)}, u32[]{:S(2)}) collective-permute-start(bf16[32,512]{1,0:T(8,128)(2,1)S(1)} %get-tuple-element.74), channel_id=1, source_target_pairs={{0,0},{1,1},{2,2},{3,3},{4,4},{5,5},{6,6},{7,7},{8,8},{9,9},{10,10... | collective-permute-start | bytes 98312 | tf_op jit(solution)/shard_map/ppermute | solution.py:219
  74.8 10.5 %collective-permute-start.28 = (bf16[32,4096]{1,0:T(8,128)(2,1)S(1)}, bf16[32,4096]{1,0:T(8,128)(2,1)S(1)}, u32[]{:S(2)}, u32[]{:S(2)}) collective-permute-start(bf16[32,4096]{1,0:T(8,128)(2,1)S(1)} %get-tuple-element.77.after.refs_6_), channel_id=1, source_target_pairs={{0,0},{1,1},{2,2},{3,3},{4,4},{5,5},{6,6},{7,7},{8,8},{9,9},{10,10... | collective-permute-start | bytes 786440 | tf_op jit(solution)/shard_map/ppermute | solution.py:219
  77.6 3.3 %collective-permute-start.25 = (bf16[32,512]{1,0:T(8,128)(2,1)S(1)}, bf16[32,512]{1,0:T(8,128)(2,1)S(1)}, u32[]{:S(2)}, u32[]{:S(2)}) collective-permute-start(bf16[32,512]{1,0:T(8,128)(2,1)S(1)} %edge.21), channel_id=1, source_target_pairs={{0,1},{1,0},{2,3},{3,2},{4,5},{5,4},{6,7},{7,6},{8,9},{9,8},{10,11... | collective-permute-start | bytes 98312 | tf_op jit(solution)/shard_map/ppermute | solution.py:219
  78.4 6.8 %collective-permute-start.29 = (bf16[32,512]{1,0:T(8,128)(2,1)S(1)}, bf16[32,512]{1,0:T(8,128)(2,1)S(1)}, u32[]{:S(2)}, u32[]{:S(2)}) collective-permute-start(bf16[32,512]{1,0:T(8,128)(2,1)S(1)} %get-tuple-element.81), channel_id=1, source_target_pairs={{0,0},{1,1},{2,2},{3,3},{4,4},{5,5},{6,6},{7,7},{8,8},{9,9},{10,10... | collective-permute-start | bytes 98312 | tf_op jit(solution)/shard_map/ppermute | solution.py:219
  82.4 12.0 %collective-permute-start.26 = (bf16[32,4096]{1,0:T(8,128)(2,1)S(1)}, bf16[32,4096]{1,0:T(8,128)(2,1)S(1)}, u32[]{:S(2)}, u32[]{:S(2)}) collective-permute-start(bf16[32,4096]{1,0:T(8,128)(2,1)S(1)} %get-tuple-element.79.after.refs_6_), channel_id=1, source_target_pairs={{0,0},{1,1},{2,2},{3,3},{4,4},{5,5},{6,6},{7,7},{8,8},{9,9},{10,10... | collective-permute-start | bytes 786440 | tf_op jit(solution)/shard_map/ppermute | solution.py:219
  85.3 5.1 %collective-permute-start.30 = (bf16[32,512]{1,0:T(8,128)(2,1)S(1)}, bf16[32,512]{1,0:T(8,128)(2,1)S(1)}, u32[]{:S(2)}, u32[]{:S(2)}) collective-permute-start(bf16[32,512]{1,0:T(8,128)(2,1)S(1)} %edge.22), channel_id=1, source_target_pairs={{0,1},{1,0},{2,3},{3,2},{4,5},{5,4},{6,7},{7,6},{8,9},{9,8},{10,11... | collective-permute-start | bytes 98312 | tf_op jit(solution)/shard_map/ppermute | solution.py:219
  86.1 8.3 %collective-permute-start.27 = (bf16[32,512]{1,0:T(8,128)(2,1)S(1)}, bf16[32,512]{1,0:T(8,128)(2,1)S(1)}, u32[]{:S(2)}, u32[]{:S(2)}) collective-permute-start(bf16[32,512]{1,0:T(8,128)(2,1)S(1)} %get-tuple-element.80), channel_id=1, source_target_pairs={{0,0},{1,1},{2,2},{3,3},{4,4},{5,5},{6,6},{7,7},{8,8},{9,9},{10,10... | collective-permute-start | bytes 98312 | tf_op jit(solution)/shard_map/ppermute | solution.py:219
  91.9 10.7 %collective-permute-start.34 = (bf16[32,4096]{1,0:T(8,128)(2,1)S(1)}, bf16[32,4096]{1,0:T(8,128)(2,1)S(1)}, u32[]{:S(2)}, u32[]{:S(2)}) collective-permute-start(bf16[32,4096]{1,0:T(8,128)(2,1)S(1)} %get-tuple-element.83.after.refs_6_), channel_id=1, source_target_pairs={{0,0},{1,1},{2,2},{3,3},{4,4},{5,5},{6,6},{7,7},{8,8},{9,9},{10,10... | collective-permute-start | bytes 786440 | tf_op jit(solution)/shard_map/ppermute | solution.py:219
  94.4 3.3 %collective-permute-start.31 = (bf16[32,512]{1,0:T(8,128)(2,1)S(1)}, bf16[32,512]{1,0:T(8,128)(2,1)S(1)}, u32[]{:S(2)}, u32[]{:S(2)}) collective-permute-start(bf16[32,512]{1,0:T(8,128)(2,1)S(1)} %edge.23), channel_id=1, source_target_pairs={{0,1},{1,0},{2,3},{3,2},{4,5},{5,4},{6,7},{7,6},{8,9},{9,8},{10,11... | collective-permute-start | bytes 98312 | tf_op jit(solution)/shard_map/ppermute | solution.py:219
  94.8 7.8 %collective-permute-start.35 = (bf16[32,512]{1,0:T(8,128)(2,1)S(1)}, bf16[32,512]{1,0:T(8,128)(2,1)S(1)}, u32[]{:S(2)}, u32[]{:S(2)}) collective-permute-start(bf16[32,512]{1,0:T(8,128)(2,1)S(1)} %get-tuple-element.87), channel_id=1, source_target_pairs={{0,0},{1,1},{2,2},{3,3},{4,4},{5,5},{6,6},{7,7},{8,8},{9,9},{10,10... | collective-permute-start | bytes 98312 | tf_op jit(solution)/shard_map/ppermute | solution.py:219
  99.2 10.4 %collective-permute-start.32 = (bf16[32,4096]{1,0:T(8,128)(2,1)S(1)}, bf16[32,4096]{1,0:T(8,128)(2,1)S(1)}, u32[]{:S(2)}, u32[]{:S(2)}) collective-permute-start(bf16[32,4096]{1,0:T(8,128)(2,1)S(1)} %get-tuple-element.85.after.refs_6_), channel_id=1, source_target_pairs={{0,0},{1,1},{2,2},{3,3},{4,4},{5,5},{6,6},{7,7},{8,8},{9,9},{10,10... | collective-permute-start | bytes 786440 | tf_op jit(solution)/shard_map/ppermute | solution.py:219
  102.6 3.7 %collective-permute-start.36 = (bf16[32,512]{1,0:T(8,128)(2,1)S(1)}, bf16[32,512]{1,0:T(8,128)(2,1)S(1)}, u32[]{:S(2)}, u32[]{:S(2)}) collective-permute-start(bf16[32,512]{1,0:T(8,128)(2,1)S(1)} %edge.24), channel_id=1, source_target_pairs={{0,1},{1,0},{2,3},{3,2},{4,5},{5,4},{6,7},{7,6},{8,9},{9,8},{10,11... | collective-permute-start | bytes 98312 | tf_op jit(solution)/shard_map/ppermute | solution.py:219
  103.5 6.2 %collective-permute-start.33 = (bf16[32,512]{1,0:T(8,128)(2,1)S(1)}, bf16[32,512]{1,0:T(8,128)(2,1)S(1)}, u32[]{:S(2)}, u32[]{:S(2)}) collective-permute-start(bf16[32,512]{1,0:T(8,128)(2,1)S(1)} %get-tuple-element.86), channel_id=1, source_target_pairs={{0,0},{1,1},{2,2},{3,3},{4,4},{5,5},{6,6},{7,7},{8,8},{9,9},{10,10... | collective-permute-start | bytes 98312 | tf_op jit(solution)/shard_map/ppermute | solution.py:219
  109.6 4.7 %collective-permute-start.37 = (bf16[32,512]{1,0:T(8,128)(2,1)S(1)}, bf16[32,512]{1,0:T(8,128)(2,1)S(1)}, u32[]{:S(2)}, u32[]{:S(2)}) collective-permute-start(bf16[32,512]{1,0:T(8,128)(2,1)S(1)} %edge.25), channel_id=1, source_target_pairs={{0,1},{1,0},{2,3},{3,2},{4,5},{5,4},{6,7},{7,6},{8,9},{9,8},{10,11... | collective-permute-start | bytes 98312 | tf_op jit(solution)/shard_map/ppermute | solution.py:219
  110.5 13.8 %collective-permute-start.41 = (bf16[32,4096]{1,0:T(8,128)(2,1)S(1)}, bf16[32,4096]{1,0:T(8,128)(2,1)S(1)}, u32[]{:S(2)}, u32[]{:S(2)}) collective-permute-start(bf16[32,4096]{1,0:T(8,128)(2,1)S(1)} %get-tuple-element.89.after.refs_6_), channel_id=1, source_target_pairs={{0,0},{1,1},{2,2},{3,3},{4,4},{5,5},{6,6},{7,7},{8,8},{9,9},{10,10... | collective-permute-start | bytes 786440 | tf_op jit(solution)/shard_map/ppermute | solution.py:219
  115.8 12.6 %collective-permute-start.38 = (bf16[32,4096]{1,0:T(8,128)(2,1)S(1)}, bf16[32,4096]{1,0:T(8,128)(2,1)S(1)}, u32[]{:S(2)}, u32[]{:S(2)}) collective-permute-start(bf16[32,4096]{1,0:T(8,128)(2,1)S(1)} %get-tuple-element.91.after.refs_6_), channel_id=1, source_target_pairs={{0,0},{1,1},{2,2},{3,3},{4,4},{5,5},{6,6},{7,7},{8,8},{9,9},{10,10... | collective-permute-start | bytes 786440 | tf_op jit(solution)/shard_map/ppermute | solution.py:219
  117.8 6.5 %collective-permute-start.42 = (bf16[32,512]{1,0:T(8,128)(2,1)S(1)}, bf16[32,512]{1,0:T(8,128)(2,1)S(1)}, u32[]{:S(2)}, u32[]{:S(2)}) collective-permute-start(bf16[32,512]{1,0:T(8,128)(2,1)S(1)} %get-tuple-element.93), channel_id=1, source_target_pairs={{0,0},{1,1},{2,2},{3,3},{4,4},{5,5},{6,6},{7,7},{8,8},{9,9},{10,10... | collective-permute-start | bytes 98312 | tf_op jit(solution)/shard_map/ppermute | solution.py:219
  122.3 6.1 %collective-permute-start.39 = (bf16[32,512]{1,0:T(8,128)(2,1)S(1)}, bf16[32,512]{1,0:T(8,128)(2,1)S(1)}, u32[]{:S(2)}, u32[]{:S(2)}) collective-permute-start(bf16[32,512]{1,0:T(8,128)(2,1)S(1)} %get-tuple-element.92), channel_id=1, source_target_pairs={{0,0},{1,1},{2,2},{3,3},{4,4},{5,5},{6,6},{7,7},{8,8},{9,9},{10,10... | collective-permute-start | bytes 98312 | tf_op jit(solution)/shard_map/ppermute | solution.py:219
  124.3 4.1 %collective-permute-start.43 = (bf16[32,512]{1,0:T(8,128)(2,1)S(1)}, bf16[32,512]{1,0:T(8,128)(2,1)S(1)}, u32[]{:S(2)}, u32[]{:S(2)}) collective-permute-start(bf16[32,512]{1,0:T(8,128)(2,1)S(1)} %edge.27), channel_id=1, source_target_pairs={{0,1},{1,0},{2,3},{3,2},{4,5},{5,4},{6,7},{7,6},{8,9},{9,8},{10,11... | collective-permute-start | bytes 98312 | tf_op jit(solution)/shard_map/ppermute | solution.py:219
  128.4 2.4 %collective-permute-start.40 = (bf16[32,512]{1,0:T(8,128)(2,1)S(1)}, bf16[32,512]{1,0:T(8,128)(2,1)S(1)}, u32[]{:S(2)}, u32[]{:S(2)}) collective-permute-start(bf16[32,512]{1,0:T(8,128)(2,1)S(1)} %edge.26), channel_id=1, source_target_pairs={{0,1},{1,0},{2,3},{3,2},{4,5},{5,4},{6,7},{7,6},{8,9},{9,8},{10,11... | collective-permute-start | bytes 98312 | tf_op jit(solution)/shard_map/ppermute | solution.py:219

commit v8 on v4

--- a/solution.py
+++ b/solution.py
@@ -19,11 +19,13 @@
 def load_kernel(blks, state, w, bias, indices, state_out, w_out, bias_out, meta, raw, sems):
     copies = [
         pltpu.make_async_copy(src, dst, sems.at[i])
-        for i, (src, dst) in enumerate(((indices, raw), (state, state_out), (bias, bias_out), (w, w_out)))
+        for i, (src, dst) in enumerate(
+            ((indices, raw), (state, state_out), (bias, bias_out), (w.at[: w_out.shape[0]], w_out))
+        )
     ]
     for copy in copies:
         copy.start()
-    brs, nzb = indices.shape
+    nzb, brs = indices.shape
     columns = brs * blks
     start = lax.axis_index("blk") * brs - HALO
     meta[brs * nzb] = lax.axis_index("section")
@@ -32,7 +34,7 @@
     @pl.loop(0, brs)
     def _(i):
         for k in range(nzb):
-            col = raw[i, k] - start
+            col = raw[k, i] - start
             col = jnp.where(col < 0, col + columns, col)
             meta[i * nzb + k] = jnp.where(col >= columns, col - columns, col) * BLK
 
@@ -45,7 +47,9 @@
     return pl.pallas_call(
         functools.partial(load_kernel, blks),
         out_shape=(
-            *(pltpu.VMEM(a.shape, a.dtype) for a in arrays),
+            pltpu.VMEM(state.shape, state.dtype),
+            pltpu.VMEM((w.shape[0] // 2, *w.shape[1:]), w.dtype),
+            pltpu.VMEM(bias.shape, bias.dtype),
             pltpu.SMEM((indices.size + 1,), jnp.int32),
         ),
         in_specs=[ANY] * 4,
@@ -59,14 +63,21 @@
 
 def layer_kernel(tick, src_row, rows, brs, nzb, own_slot, prev_slot, aliased, *refs):
     refs = list(refs)
-    meta, main, low, high, w, bias = refs[:6]
-    del refs[:6]
+    meta, main, low, high, w_early, w_late, bias = refs[:7]
+    del refs[:7]
     prev = refs.pop(0) if prev_slot is not None else None
     if aliased:
         refs.pop(0)
     emitted = refs.pop(0) if prev_slot is not None or own_slot is not None else None
     left = right = None
-    if own_slot is None:
+    late = None
+    early = w_early.shape[0]
+    if prev_slot is None and own_slot is None:
+        out, left, right, loaded, xbuf, sems = refs
+        late = pltpu.make_async_copy(w_late.at[early:], loaded, sems.at[0])
+        w_late = loaded
+        late.start()
+    elif own_slot is None:
         out, left, right, xbuf, sems = refs
     else:
         out, xbuf, sems = refs
@@ -89,18 +100,20 @@
         before.start()
     live = meta[brs * nzb] >= tick
 
-    @pl.when(live)
-    def _():
+    def compute():
         src = pl.ds(src_row, rows)
         xbuf[:, 0:edge] = low[src, :]
         xbuf[:, edge : edge + width] = main[src, :]
         xbuf[:, edge + width : edge + width + edge] = high[src, :]
         for i in range(brs):
+            if late is not None and i == early:
+                late.wait()
             picked = jnp.concatenate(
                 [xbuf[:, pl.ds(pl.multiple_of(meta[i * nzb + k], BLK), BLK)] for k in range(nzb)], axis=1
             )
             cols = pl.ds(i * BLK, BLK)
-            summed = jnp.dot(picked, w[i], preferred_element_type=jnp.float32) + bias[:, cols]
+            w = w_early[i] if i < early else w_late[i - early]
+            summed = jnp.dot(picked, w, preferred_element_type=jnp.float32) + bias[:, cols]
             made = jnp.maximum(summed, 0.0).astype(jnp.bfloat16)
             out[:, cols] = made
             if left is not None and i < HALO:
@@ -110,8 +123,7 @@
             if own and (i + 1) % (brs // pieces) == 0:
                 own[i // (brs // pieces)].start()
 
-    @pl.when(jnp.logical_not(live))
-    def _():
+    def clear():
         out[...] = jnp.zeros_like(out)
         if left is not None:
             left[...] = jnp.zeros_like(left)
@@ -119,6 +131,11 @@
         for copy in own:
             copy.start()
 
+    if tick == 0:
+        compute()
+    else:
+        pl.when(live)(compute)
+        pl.when(jnp.logical_not(live))(clear)
     if prev is not None:
         before.wait()
     for copy in own:
@@ -126,16 +143,21 @@
 
 
 def apply_layer(tick, src_row, row, rows, last, operands, prev, prev_slot, emitted, emitted_aval):
-    meta, main, low, high, w, bias = operands
-    brs, depth = w.shape[:2]
+    meta, main, low, high, w_early, w_late, bias = operands
+    depth = w_early.shape[1]
+    brs = bias.shape[1] // BLK
     nzb = depth // BLK
     width = brs * BLK
     edge = HALO * BLK
     args = [
         pltpu.with_memory_space_constraint(meta, pltpu.SMEM),
-        *(pltpu.with_memory_space_constraint(a, pltpu.VMEM) for a in (main, low, high, w, bias)),
+        *(pltpu.with_memory_space_constraint(a, pltpu.VMEM) for a in (main, low, high, w_early)),
+        pltpu.with_memory_space_constraint(w_late, pltpu.VMEM if prev is not None or last else pltpu.HBM),
+        pltpu.with_memory_space_constraint(bias, pltpu.VMEM),
     ]
-    specs = [SMEM] + [VMEM] * 5
+    specs = [SMEM] + [VMEM] * 6
+    if prev is None and not last:
+        specs[5] = ANY
     out_shape = []
     out_specs = []
     scratch = [
@@ -158,6 +180,9 @@
     else:
         out_shape += [pltpu.VMEM((rows, cols), jnp.bfloat16) for cols in (width, edge, edge)]
         out_specs += [VMEM] * 3
+    if prev is None and not last:
+        out_shape.append(pltpu.VMEM((brs - w_early.shape[0], depth, BLK), w_early.dtype))
+        out_specs.append(VMEM)
     body = functools.partial(
         layer_kernel, tick, src_row, rows, brs, nzb, (tick, row) if last else None, prev_slot, emitted is not None
     )
@@ -170,7 +195,7 @@
         input_output_aliases=aliases,
         compiler_params=pltpu.CompilerParams(vmem_limit_bytes=8 * 1024 * 1024),
         cost_estimate=pl.CostEstimate(
-            flops=20 * rows * brs * nzb * BLK * BLK, bytes_accessed=20 * w.size, transcendentals=0
+            flops=20 * rows * brs * nzb * BLK * BLK, bytes_accessed=40 * w_early.size, transcendentals=0
         ),
         name=f"layer_t{tick}_r{row}",
     )(*args)
@@ -193,12 +218,13 @@
 
     low = hop(pending_groups[:, width - edge :], 0, 1)
     high = hop(pending_groups[:, :edge], 0, -1)
-    state, w, bias, meta = load(
+    w_late = coefficient_tiles.reshape(block_rows, nzb * BLK, BLK)
+    state, w_early, bias, meta = load(
         blks,
         pending_groups,
-        coefficient_tiles.reshape(block_rows, nzb * BLK, BLK),
+        w_late,
         additive_offsets,
-        source_block_indices[0],
+        source_block_indices[0].T,
     )
     parts = [(state, low, high, c * rows) for c in range(CHUNKS)]
     emitted = prev = prev_slot = None
@@ -208,11 +234,13 @@
             main, low, high, src_row = parts[c]
             outs = list(
                 apply_layer(
-                    tick, src_row, c * rows, rows, last, (meta, main, low, high, w, bias), prev, prev_slot, emitted, emitted_aval
+                    tick, src_row, c * rows, rows, last, (meta, main, low, high, w_early, w_late, bias), prev, prev_slot, emitted, emitted_aval
                 )
             )
             if prev is not None or last:
                 emitted = outs.pop(0)
+            if tick == 0 and c == 0:
+                w_late = outs.pop()
             prev = prev_slot = None
             if not last:
                 prev, left, right = outs

time: 119 us -> 119 us (level)
  waiting for transfers between devices: 63.5 us -> 66.1 us
  starting transfers between devices: 35.3 us -> 33.2 us
  Pallas kernels: 17.1 us -> 18.6 us
  local copies, waits for them, and re-layouts: 2.25 us -> 0.88 us
    pallas_call x16, Pallas kernels: 13.5 us -> 16.2 us  [apply_layer(): pl.pallas_call(body, out_shape=tuple(out_shape), in_specs=specs, out_spec...]
    ppermute x44, waiting for transfers between devices: 63.5 us -> 66.1 us  [hop(): return lax.ppermute(values, ('section', 'blk'), pairs)]
    ppermute x44, starting transfers between devices: 35.3 us -> 33.2 us  [hop(): return lax.ppermute(values, ('section', 'blk'), pairs)]
    unnamed x1 -> x0, local copies, waits for them, and re-layouts: 1.37 us -> none
    pallas_call x1, Pallas kernels: 3.62 us -> 2.41 us  [load(): pl.pallas_call(functools.partial(load_kernel, blks), out_shape=(pltpu.VME...]
  transfers between devices with their start and end apart: 44 -> 44, of which waited for: 27 -> 29; matrix products, arithmetic and copies ran while one was open for 1% -> 0% of each run, Pallas kernels for 13% -> 12%
where the time goes in v8:
time: 119 us
  waiting for transfers between devices  66.1 us (56%)
  starting transfers between devices  33.2 us (28%)
  Pallas kernels  18.6 us (16%)
    ppermute x44, waiting for transfers between devices, hop(): return lax.ppermute(values, ('section', 'blk'), pairs)  66.1 us
    ppermute x44, starting transfers between devices, hop(): return lax.ppermute(values, ('section', 'blk'), pairs)  33.2 us
    pallas_call x16, Pallas kernels, apply_layer(): pl.pallas_call(body, out_shape=tuple(out_shape), in_specs=specs, out_spec...  16.2 us
    pallas_call x1, Pallas kernels, load(): pl.pallas_call(functools.partial(load_kernel, blks), out_shape=(pltpu.VME...  2.41 us
  transfers between devices with their start and end apart: 44, of which 29 were waited for; matrix products, arithmetic and copies ran while one was open for 0% of the time, Pallas kernels for 12%

profile of v8, /device:TPU:1, one launch (start us, length us, event | category | flops | bytes accessed | tf_op | source)
XLA Modules:
  0.0 119.3 jit_solution(1790792971134905275)
XLA Ops:
  0.0 0.9 fusion
  0.9 2.7 %collective-permute-start = (bf16[64,512]{1,0:T(8,128)(2,1)S(1)}, bf16[64,512]{1,0:T(8,128)(2,1)S(1)}, u32[]{:S(2)}, u32[]{:S(2)}) collective-permute-start(bf16[64,512]{1,0:T(8,128)(2,1)S(1)} %get-tuple-element.126), channel_id=1, source_target_pairs={{0,1},{1,2},{2,3},{3,0},{4,5},{5,6},{6,7},{7,4},{8,9},{9,10},{10,1... | collective-permute-start | bytes 196616 | tf_op jit(solution)/shard_map/ppermute | solution.py:217
  3.5 2.4 %load.1 = (bf16[64,4096]{1,0:T(8,128)(2,1)S(1)}, bf16[16,1024,128]{2,1,0:T(8,128)(2,1)S(1)}, f32[1,4096]{1,0:T(1,128)S(1)}, s32[257]{0:T(512)S(4)}) custom-call(bf16[64,4096]{1,0:T(8,128)(2,1)} %state.1, bf16[32,1024,128]{2,1,0:T(8,128)(2,1)} %bitcast.4, f32[1,4096]{1,0:T(1,128)} %bias.1, s32[8,32]{1,0:T(8,128)} %bitcast.6), custom_call_target="tpu_custom_call" | custom-call | bytes 8388608 | tf_op jit(solution)/shard_map/load/pallas_call | solution.py:47
  6.0 1.3 %collective-permute-done.1.refs_3_ = bf16[64,512]{1,0:T(8,128)(2,1)S(1)} collective-permute-done((bf16[64,512]{1,0:T(8,128)(2,1)S(1)}, bf16[64,512]{1,0:T(8,128)(2,1)S(1)}, u32[]{:S(2)}, u32[]{:S(2)}) %collective-permute-start.1) | collective-permute-done | bytes 65568 | tf_op jit(solution)/shard_map/ppermute | solution.py:217
  7.2 3.7 %layer_t0_r0.1 = (bf16[32,4096]{1,0:T(8,128)(2,1)S(1)}, bf16[32,512]{1,0:T(8,128)(2,1)S(1)}, bf16[32,512]{1,0:T(8,128)(2,1)S(1)}, bf16[16,1024,128]{2,1,0:T(8,128)(2,1)S(1)}) custom-call(s32[257]{0:T(512)S(4)} %get-tuple-element.65.refs_0_, bf16[64,4096]{1,0:T(8,128)(2,1)S(1)} %get-tuple-element.66.refs_1_, ...), custom_call_target="tpu_custom_call" | custom-call | flops 2684354560 | bytes 83886080 | tf_op jit(solution)/shard_map/layer_t0_r0/pallas_call | solution.py:189
  10.9 1.3 %collective-permute-start.5 = (bf16[32,4096]{1,0:T(8,128)(2,1)S(1)}, bf16[32,4096]{1,0:T(8,128)(2,1)S(1)}, u32[]{:S(2)}, u32[]{:S(2)}) collective-permute-start(bf16[32,4096]{1,0:T(8,128)(2,1)S(1)} %get-tuple-element.70.refs_7_), channel_id=1, source_target_pairs={{0,4},{1,5},{2,6},{3,7},{4,8},{5,9},{6,10},{7,11},{8,12},{9,13},{1... | collective-permute-start | bytes 786440 | tf_op jit(solution)/shard_map/ppermute | solution.py:217
  12.2 1.7 %collective-permute-start.6 = (bf16[32,512]{1,0:T(8,128)(2,1)S(1)}, bf16[32,512]{1,0:T(8,128)(2,1)S(1)}, u32[]{:S(2)}, u32[]{:S(2)}) collective-permute-start(bf16[32,512]{1,0:T(8,128)(2,1)S(1)} %get-tuple-element.74), channel_id=1, source_target_pairs={{0,5},{1,6},{2,7},{3,4},{4,9},{5,10},{6,11},{7,8},{8,13},{9,14},{1... | collective-permute-start | bytes 98312 | tf_op jit(solution)/shard_map/ppermute | solution.py:217
  13.9 1.0 collective-permute-start.7
  15.0 2.0 %layer_t0_r32.1 = (bf16[8,64,4096]{2,1,0:T(8,128)(2,1)}, bf16[32,4096]{1,0:T(8,128)(2,1)S(1)}, bf16[32,512]{1,0:T(8,128)(2,1)S(1)}, bf16[32,512]{1,0:T(8,128)(2,1)S(1)}) custom-call(s32[257]{0:T(512)S(4)} %get-tuple-element.65.refs_0_, bf16[64,4096]{1,0:T(8,128)(2,1)S(1)} %get-tuple-element.66.refs_1_, bf16[64,512]{1,0:T(8,128)(2,1)S(1)} %collective-permute-done.refs_2_, ...), custom_call_target="tpu_custom_call" | custom-call | flops 2684354560 | bytes 83886080 | tf_op jit(solution)/shard_map/layer_t0_r32/pallas_call | solution.py:189
  17.0 1.3 %collective-permute-start.2 = (bf16[32,4096]{1,0:T(8,128)(2,1)S(1)}, bf16[32,4096]{1,0:T(8,128)(2,1)S(1)}, u32[]{:S(2)}, u32[]{:S(2)}) collective-permute-start(bf16[32,4096]{1,0:T(8,128)(2,1)S(1)} %get-tuple-element.71.refs_7_), channel_id=1, source_target_pairs={{0,4},{1,5},{2,6},{3,7},{4,8},{5,9},{6,10},{7,11},{8,12},{9,13},{1... | collective-permute-start | bytes 786440 | tf_op jit(solution)/shard_map/ppermute | solution.py:217
  18.3 2.9 %collective-permute-start.3 = (bf16[32,512]{1,0:T(8,128)(2,1)S(1)}, bf16[32,512]{1,0:T(8,128)(2,1)S(1)}, u32[]{:S(2)}, u32[]{:S(2)}) collective-permute-start(bf16[32,512]{1,0:T(8,128)(2,1)S(1)} %get-tuple-element.72), channel_id=1, source_target_pairs={{0,5},{1,6},{2,7},{3,4},{4,9},{5,10},{6,11},{7,8},{8,13},{9,14},{1... | collective-permute-start | bytes 98312 | tf_op jit(solution)/shard_map/ppermute | solution.py:217
  21.2 0.9 collective-permute-done.6.refs_2_
  22.1 2.2 %collective-permute-done.7.refs_3_ = bf16[32,512]{1,0:T(8,128)(2,1)S(1)} collective-permute-done((bf16[32,512]{1,0:T(8,128)(2,1)S(1)}, bf16[32,512]{1,0:T(8,128)(2,1)S(1)}, u32[]{:S(2)}, u32[]{:S(2)}) %collective-permute-start.7) | collective-permute-done | bytes 32800 | tf_op jit(solution)/shard_map/ppermute | solution.py:217
  24.3 0.7 layer_t1_r0.1
  25.1 2.0 %collective-permute-start.12 = (bf16[32,512]{1,0:T(8,128)(2,1)S(1)}, bf16[32,512]{1,0:T(8,128)(2,1)S(1)}, u32[]{:S(2)}, u32[]{:S(2)}) collective-permute-start(bf16[32,512]{1,0:T(8,128)(2,1)S(1)} %get-tuple-element.82), channel_id=1, source_target_pairs={{0,5},{1,6},{2,7},{3,4},{4,9},{5,10},{6,11},{7,8},{8,13},{9,14},{1... | collective-permute-start | bytes 98312 | tf_op jit(solution)/shard_map/ppermute | solution.py:217
  27.1 2.7 %collective-permute-done.3.refs_2_ = bf16[32,512]{1,0:T(8,128)(2,1)S(1)} collective-permute-done((bf16[32,512]{1,0:T(8,128)(2,1)S(1)}, bf16[32,512]{1,0:T(8,128)(2,1)S(1)}, u32[]{:S(2)}, u32[]{:S(2)}) %collective-permute-start.3) | collective-permute-done | bytes 32800 | tf_op jit(solution)/shard_map/ppermute | solution.py:217
  29.8 0.7 collective-permute-done.4.refs_3_
  30.5 0.7 layer_t1_r32.1
  31.7 2.5 %collective-permute-start.10 = (bf16[32,512]{1,0:T(8,128)(2,1)S(1)}, bf16[32,512]{1,0:T(8,128)(2,1)S(1)}, u32[]{:S(2)}, u32[]{:S(2)}) collective-permute-start(bf16[32,512]{1,0:T(8,128)(2,1)S(1)} %get-tuple-element.81), channel_id=1, source_target_pairs={{0,7},{1,4},{2,5},{3,6},{4,11},{5,8},{6,9},{7,10},{8,15},{9,12},{1... | collective-permute-start | bytes 98312 | tf_op jit(solution)/shard_map/ppermute | solution.py:217
  34.3 3.4 %collective-permute-done.12.refs_2_ = bf16[32,512]{1,0:T(8,128)(2,1)S(1)} collective-permute-done((bf16[32,512]{1,0:T(8,128)(2,1)S(1)}, bf16[32,512]{1,0:T(8,128)(2,1)S(1)}, u32[]{:S(2)}, u32[]{:S(2)}) %collective-permute-start.12) | collective-permute-done | bytes 32800 | tf_op jit(solution)/shard_map/ppermute | solution.py:217
  37.7 0.7 collective-permute-done.13.refs_3_
  38.4 0.7 layer_t2_r0.1
  39.1 0.7 collective-permute-start.17
  39.9 1.0 collective-permute-start.18
  40.9 3.9 %collective-permute-done.10.refs_3_ = bf16[32,512]{1,0:T(8,128)(2,1)S(1)} collective-permute-done((bf16[32,512]{1,0:T(8,128)(2,1)S(1)}, bf16[32,512]{1,0:T(8,128)(2,1)S(1)}, u32[]{:S(2)}, u32[]{:S(2)}) %collective-permute-start.10) | collective-permute-done | bytes 32800 | tf_op jit(solution)/shard_map/ppermute | solution.py:217
  45.0 0.7 layer_t2_r32.1
  45.7 0.5 collective-permute-start.14
  46.3 2.8 %collective-permute-start.15 = (bf16[32,512]{1,0:T(8,128)(2,1)S(1)}, bf16[32,512]{1,0:T(8,128)(2,1)S(1)}, u32[]{:S(2)}, u32[]{:S(2)}) collective-permute-start(bf16[32,512]{1,0:T(8,128)(2,1)S(1)} %get-tuple-element.88), channel_id=1, source_target_pairs={{0,5},{1,6},{2,7},{3,4},{4,9},{5,10},{6,11},{7,8},{8,13},{9,14},{1... | collective-permute-start | bytes 98312 | tf_op jit(solution)/shard_map/ppermute | solution.py:217
  49.1 3.4 %collective-permute-done.18.refs_2_ = bf16[32,512]{1,0:T(8,128)(2,1)S(1)} collective-permute-done((bf16[32,512]{1,0:T(8,128)(2,1)S(1)}, bf16[32,512]{1,0:T(8,128)(2,1)S(1)}, u32[]{:S(2)}, u32[]{:S(2)}) %collective-permute-start.18) | collective-permute-done | bytes 32800 | tf_op jit(solution)/shard_map/ppermute | solution.py:217
  52.8 0.7 layer_t3_r0.1
  53.6 2.5 %collective-permute-start.24 = (bf16[32,512]{1,0:T(8,128)(2,1)S(1)}, bf16[32,512]{1,0:T(8,128)(2,1)S(1)}, u32[]{:S(2)}, u32[]{:S(2)}) collective-permute-start(bf16[32,512]{1,0:T(8,128)(2,1)S(1)} %get-tuple-element.98), channel_id=1, source_target_pairs={{0,5},{1,6},{2,7},{3,4},{4,9},{5,10},{6,11},{7,8},{8,13},{9,14},{1... | collective-permute-start | bytes 98312 | tf_op jit(solution)/shard_map/ppermute | solution.py:217
  56.1 3.3 %collective-permute-done.15.refs_2_ = bf16[32,512]{1,0:T(8,128)(2,1)S(1)} collective-permute-done((bf16[32,512]{1,0:T(8,128)(2,1)S(1)}, bf16[32,512]{1,0:T(8,128)(2,1)S(1)}, u32[]{:S(2)}, u32[]{:S(2)}) %collective-permute-start.15) | collective-permute-done | bytes 32800 | tf_op jit(solution)/shard_map/ppermute | solution.py:217
  59.9 0.7 layer_t3_r32.1
  60.8 1.9 %collective-permute-start.21 = (bf16[32,512]{1,0:T(8,128)(2,1)S(1)}, bf16[32,512]{1,0:T(8,128)(2,1)S(1)}, u32[]{:S(2)}, u32[]{:S(2)}) collective-permute-start(bf16[32,512]{1,0:T(8,128)(2,1)S(1)} %get-tuple-element.96), channel_id=1, source_target_pairs={{0,5},{1,6},{2,7},{3,4},{4,9},{5,10},{6,11},{7,8},{8,13},{9,14},{1... | collective-permute-start | bytes 98312 | tf_op jit(solution)/shard_map/ppermute | solution.py:217
  62.7 3.4 %collective-permute-done.24.refs_2_ = bf16[32,512]{1,0:T(8,128)(2,1)S(1)} collective-permute-done((bf16[32,512]{1,0:T(8,128)(2,1)S(1)}, bf16[32,512]{1,0:T(8,128)(2,1)S(1)}, u32[]{:S(2)}, u32[]{:S(2)}) %collective-permute-start.24) | collective-permute-done | bytes 32800 | tf_op jit(solution)/shard_map/ppermute | solution.py:217
  66.1 1.6 %collective-permute-done.25.refs_3_ = bf16[32,512]{1,0:T(8,128)(2,1)S(1)} collective-permute-done((bf16[32,512]{1,0:T(8,128)(2,1)S(1)}, bf16[32,512]{1,0:T(8,128)(2,1)S(1)}, u32[]{:S(2)}, u32[]{:S(2)}) %collective-permute-start.25) | collective-permute-done | bytes 32800 | tf_op jit(solution)/shard_map/ppermute | solution.py:217
  67.7 0.7 layer_t4_r0.1
  68.6 1.0 collective-permute-start.30
  69.6 4.2 %collective-permute-done.21.refs_2_ = bf16[32,512]{1,0:T(8,128)(2,1)S(1)} collective-permute-done((bf16[32,512]{1,0:T(8,128)(2,1)S(1)}, bf16[32,512]{1,0:T(8,128)(2,1)S(1)}, u32[]{:S(2)}, u32[]{:S(2)}) %collective-permute-start.21) | collective-permute-done | bytes 32800 | tf_op jit(solution)/shard_map/ppermute | solution.py:217
  73.7 0.9 collective-permute-done.22.refs_3_
  74.7 0.7 layer_t4_r32.1
  75.5 1.4 %collective-permute-start.27 = (bf16[32,512]{1,0:T(8,128)(2,1)S(1)}, bf16[32,512]{1,0:T(8,128)(2,1)S(1)}, u32[]{:S(2)}, u32[]{:S(2)}) collective-permute-start(bf16[32,512]{1,0:T(8,128)(2,1)S(1)} %get-tuple-element.104), channel_id=1, source_target_pairs={{0,5},{1,6},{2,7},{3,4},{4,9},{5,10},{6,11},{7,8},{8,13},{9,14},{1... | collective-permute-start | bytes 98312 | tf_op jit(solution)/shard_map/ppermute | solution.py:217
  76.9 4.2 %collective-permute-done.30.refs_2_ = bf16[32,512]{1,0:T(8,128)(2,1)S(1)} collective-permute-done((bf16[32,512]{1,0:T(8,128)(2,1)S(1)}, bf16[32,512]{1,0:T(8,128)(2,1)S(1)}, u32[]{:S(2)}, u32[]{:S(2)}) %collective-permute-start.30) | collective-permute-done | bytes 32800 | tf_op jit(solution)/shard_map/ppermute | solution.py:217
  81.1 0.9 collective-permute-done.31.refs_3_
  82.0 0.7 layer_t5_r0.1
  82.8 1.4 %collective-permute-start.36 = (bf16[32,512]{1,0:T(8,128)(2,1)S(1)}, bf16[32,512]{1,0:T(8,128)(2,1)S(1)}, u32[]{:S(2)}, u32[]{:S(2)}) collective-permute-start(bf16[32,512]{1,0:T(8,128)(2,1)S(1)} %get-tuple-element.114), channel_id=1, source_target_pairs={{0,5},{1,6},{2,7},{3,4},{4,9},{5,10},{6,11},{7,8},{8,13},{9,14},{1... | collective-permute-start | bytes 98312 | tf_op jit(solution)/shard_map/ppermute | solution.py:217
  84.2 4.4 %collective-permute-done.27.refs_2_ = bf16[32,512]{1,0:T(8,128)(2,1)S(1)} collective-permute-done((bf16[32,512]{1,0:T(8,128)(2,1)S(1)}, bf16[32,512]{1,0:T(8,128)(2,1)S(1)}, u32[]{:S(2)}, u32[]{:S(2)}) %collective-permute-start.27) | collective-permute-done | bytes 32800 | tf_op jit(solution)/shard_map/ppermute | solution.py:217
  88.6 0.9 collective-permute-done.28.refs_3_
  89.6 0.7 layer_t5_r32.1
  90.4 1.1 collective-permute-start.33
  91.5 3.8 %collective-permute-done.36.refs_2_ = bf16[32,512]{1,0:T(8,128)(2,1)S(1)} collective-permute-done((bf16[32,512]{1,0:T(8,128)(2,1)S(1)}, bf16[32,512]{1,0:T(8,128)(2,1)S(1)}, u32[]{:S(2)}, u32[]{:S(2)}) %collective-permute-start.36) | collective-permute-done | bytes 32800 | tf_op jit(solution)/shard_map/ppermute | solution.py:217
  95.3 1.6 %collective-permute-done.37.refs_3_ = bf16[32,512]{1,0:T(8,128)(2,1)S(1)} collective-permute-done((bf16[32,512]{1,0:T(8,128)(2,1)S(1)}, bf16[32,512]{1,0:T(8,128)(2,1)S(1)}, u32[]{:S(2)}, u32[]{:S(2)}) %collective-permute-start.37) | collective-permute-done | bytes 32800 | tf_op jit(solution)/shard_map/ppermute | solution.py:217
  96.9 0.7 layer_t6_r0.1
  97.7 1.1 collective-permute-start.42
  98.8 4.2 %collective-permute-done.33.refs_2_ = bf16[32,512]{1,0:T(8,128)(2,1)S(1)} collective-permute-done((bf16[32,512]{1,0:T(8,128)(2,1)S(1)}, bf16[32,512]{1,0:T(8,128)(2,1)S(1)}, u32[]{:S(2)}, u32[]{:S(2)}) %collective-permute-start.33) | collective-permute-done | bytes 32800 | tf_op jit(solution)/shard_map/ppermute | solution.py:217
  103.0 0.9 collective-permute-done.34.refs_3_
  103.9 0.7 layer_t6_r32.1
  104.7 1.3 %collective-permute-start.39 = (bf16[32,512]{1,0:T(8,128)(2,1)S(1)}, bf16[32,512]{1,0:T(8,128)(2,1)S(1)}, u32[]{:S(2)}, u32[]{:S(2)}) collective-permute-start(bf16[32,512]{1,0:T(8,128)(2,1)S(1)} %get-tuple-element.120), channel_id=1, source_target_pairs={{0,5},{1,6},{2,7},{3,4},{4,9},{5,10},{6,11},{7,8},{8,13},{9,14},{1... | collective-permute-start | bytes 98312 | tf_op jit(solution)/shard_map/ppermute | solution.py:217
  106.0 4.2 %collective-permute-done.42.refs_2_ = bf16[32,512]{1,0:T(8,128)(2,1)S(1)} collective-permute-done((bf16[32,512]{1,0:T(8,128)(2,1)S(1)}, bf16[32,512]{1,0:T(8,128)(2,1)S(1)}, u32[]{:S(2)}, u32[]{:S(2)}) %collective-permute-start.42) | collective-permute-done | bytes 32800 | tf_op jit(solution)/shard_map/ppermute | solution.py:217
  110.2 0.9 collective-permute-done.43.refs_3_
  111.2 0.8 layer_t7_r0.1.refs_7_
  112.0 5.8 %collective-permute-done.39.refs_2_ = bf16[32,512]{1,0:T(8,128)(2,1)S(1)} collective-permute-done((bf16[32,512]{1,0:T(8,128)(2,1)S(1)}, bf16[32,512]{1,0:T(8,128)(2,1)S(1)}, u32[]{:S(2)}, u32[]{:S(2)}) %collective-permute-start.39) | collective-permute-done | bytes 32800 | tf_op jit(solution)/shard_map/ppermute | solution.py:217
  117.8 0.5 collective-permute-done.40.refs_3_
  118.3 0.8 layer_t7_r32.1
  (42 shorter events, 2.1 us)
Async XLA Ops:
  0.9 5.1 %collective-permute-start = (bf16[64,512]{1,0:T(8,128)(2,1)S(1)}, bf16[64,512]{1,0:T(8,128)(2,1)S(1)}, u32[]{:S(2)}, u32[]{:S(2)}) collective-permute-start(bf16[64,512]{1,0:T(8,128)(2,1)S(1)} %get-tuple-element.126), channel_id=1, source_target_pairs={{0,1},{1,2},{2,3},{3,0},{4,5},{5,6},{6,7},{7,4},{8,9},{9,10},{10,1... | collective-permute-start | bytes 196616 | tf_op jit(solution)/shard_map/ppermute | solution.py:217
  3.5 3.7 %collective-permute-start.1 = (bf16[64,512]{1,0:T(8,128)(2,1)S(1)}, bf16[64,512]{1,0:T(8,128)(2,1)S(1)}, u32[]{:S(2)}, u32[]{:S(2)}) collective-permute-start(bf16[64,512]{1,0:T(8,128)(2,1)S(1)} %get-tuple-element.125), channel_id=1, source_target_pairs={{0,3},{1,0},{2,1},{3,2},{4,7},{5,4},{6,5},{7,6},{8,11},{9,8},{10,9... | collective-permute-start | bytes 196616 | tf_op jit(solution)/shard_map/ppermute | solution.py:217
  10.9 13.4 %collective-permute-start.5 = (bf16[32,4096]{1,0:T(8,128)(2,1)S(1)}, bf16[32,4096]{1,0:T(8,128)(2,1)S(1)}, u32[]{:S(2)}, u32[]{:S(2)}) collective-permute-start(bf16[32,4096]{1,0:T(8,128)(2,1)S(1)} %get-tuple-element.70.refs_7_), channel_id=1, source_target_pairs={{0,4},{1,5},{2,6},{3,7},{4,8},{5,9},{6,10},{7,11},{8,12},{9,13},{1... | collective-permute-start | bytes 786440 | tf_op jit(solution)/shard_map/ppermute | solution.py:217
  12.2 9.9 %collective-permute-start.6 = (bf16[32,512]{1,0:T(8,128)(2,1)S(1)}, bf16[32,512]{1,0:T(8,128)(2,1)S(1)}, u32[]{:S(2)}, u32[]{:S(2)}) collective-permute-start(bf16[32,512]{1,0:T(8,128)(2,1)S(1)} %get-tuple-element.74), channel_id=1, source_target_pairs={{0,5},{1,6},{2,7},{3,4},{4,9},{5,10},{6,11},{7,8},{8,13},{9,14},{1... | collective-permute-start | bytes 98312 | tf_op jit(solution)/shard_map/ppermute | solution.py:217
  13.9 10.4 %collective-permute-start.7 = (bf16[32,512]{1,0:T(8,128)(2,1)S(1)}, bf16[32,512]{1,0:T(8,128)(2,1)S(1)}, u32[]{:S(2)}, u32[]{:S(2)}) collective-permute-start(bf16[32,512]{1,0:T(8,128)(2,1)S(1)} %get-tuple-element.75), channel_id=1, source_target_pairs={{0,7},{1,4},{2,5},{3,6},{4,11},{5,8},{6,9},{7,10},{8,15},{9,12},{1... | collective-permute-start | bytes 98312 | tf_op jit(solution)/shard_map/ppermute | solution.py:217
  17.0 13.5 %collective-permute-start.2 = (bf16[32,4096]{1,0:T(8,128)(2,1)S(1)}, bf16[32,4096]{1,0:T(8,128)(2,1)S(1)}, u32[]{:S(2)}, u32[]{:S(2)}) collective-permute-start(bf16[32,4096]{1,0:T(8,128)(2,1)S(1)} %get-tuple-element.71.refs_7_), channel_id=1, source_target_pairs={{0,4},{1,5},{2,6},{3,7},{4,8},{5,9},{6,10},{7,11},{8,12},{9,13},{1... | collective-permute-start | bytes 786440 | tf_op jit(solution)/shard_map/ppermute | solution.py:217
  18.3 11.5 %collective-permute-start.3 = (bf16[32,512]{1,0:T(8,128)(2,1)S(1)}, bf16[32,512]{1,0:T(8,128)(2,1)S(1)}, u32[]{:S(2)}, u32[]{:S(2)}) collective-permute-start(bf16[32,512]{1,0:T(8,128)(2,1)S(1)} %get-tuple-element.72), channel_id=1, source_target_pairs={{0,5},{1,6},{2,7},{3,4},{4,9},{5,10},{6,11},{7,8},{8,13},{9,14},{1... | collective-permute-start | bytes 98312 | tf_op jit(solution)/shard_map/ppermute | solution.py:217
  22.1 8.4 %collective-permute-start.4 = (bf16[32,512]{1,0:T(8,128)(2,1)S(1)}, bf16[32,512]{1,0:T(8,128)(2,1)S(1)}, u32[]{:S(2)}, u32[]{:S(2)}) collective-permute-start(bf16[32,512]{1,0:T(8,128)(2,1)S(1)} %get-tuple-element.73), channel_id=1, source_target_pairs={{0,7},{1,4},{2,5},{3,6},{4,11},{5,8},{6,9},{7,10},{8,15},{9,12},{1... | collective-permute-start | bytes 98312 | tf_op jit(solution)/shard_map/ppermute | solution.py:217
  25.1 13.3 %collective-permute-start.11 = (bf16[32,4096]{1,0:T(8,128)(2,1)S(1)}, bf16[32,4096]{1,0:T(8,128)(2,1)S(1)}, u32[]{:S(2)}, u32[]{:S(2)}) collective-permute-start(bf16[32,4096]{1,0:T(8,128)(2,1)S(1)} %get-tuple-element.77.refs_7_), channel_id=1, source_target_pairs={{0,4},{1,5},{2,6},{3,7},{4,8},{5,9},{6,10},{7,11},{8,12},{9,13},{1... | collective-permute-start | bytes 786440 | tf_op jit(solution)/shard_map/ppermute | solution.py:217
  25.1 12.6 %collective-permute-start.12 = (bf16[32,512]{1,0:T(8,128)(2,1)S(1)}, bf16[32,512]{1,0:T(8,128)(2,1)S(1)}, u32[]{:S(2)}, u32[]{:S(2)}) collective-permute-start(bf16[32,512]{1,0:T(8,128)(2,1)S(1)} %get-tuple-element.82), channel_id=1, source_target_pairs={{0,5},{1,6},{2,7},{3,4},{4,9},{5,10},{6,11},{7,8},{8,13},{9,14},{1... | collective-permute-start | bytes 98312 | tf_op jit(solution)/shard_map/ppermute | solution.py:217
  29.8 8.6 %collective-permute-start.13 = (bf16[32,512]{1,0:T(8,128)(2,1)S(1)}, bf16[32,512]{1,0:T(8,128)(2,1)S(1)}, u32[]{:S(2)}, u32[]{:S(2)}) collective-permute-start(bf16[32,512]{1,0:T(8,128)(2,1)S(1)} %get-tuple-element.83), channel_id=1, source_target_pairs={{0,7},{1,4},{2,5},{3,6},{4,11},{5,8},{6,9},{7,10},{8,15},{9,12},{1... | collective-permute-start | bytes 98312 | tf_op jit(solution)/shard_map/ppermute | solution.py:217
  31.3 13.7 %collective-permute-start.8 = (bf16[32,4096]{1,0:T(8,128)(2,1)S(1)}, bf16[32,4096]{1,0:T(8,128)(2,1)S(1)}, u32[]{:S(2)}, u32[]{:S(2)}) collective-permute-start(bf16[32,4096]{1,0:T(8,128)(2,1)S(1)} %get-tuple-element.79.refs_7_), channel_id=1, source_target_pairs={{0,4},{1,5},{2,6},{3,7},{4,8},{5,9},{6,10},{7,11},{8,12},{9,13},{1... | collective-permute-start | bytes 786440 | tf_op jit(solution)/shard_map/ppermute | solution.py:217
  31.7 13.1 %collective-permute-start.10 = (bf16[32,512]{1,0:T(8,128)(2,1)S(1)}, bf16[32,512]{1,0:T(8,128)(2,1)S(1)}, u32[]{:S(2)}, u32[]{:S(2)}) collective-permute-start(bf16[32,512]{1,0:T(8,128)(2,1)S(1)} %get-tuple-element.81), channel_id=1, source_target_pairs={{0,7},{1,4},{2,5},{3,6},{4,11},{5,8},{6,9},{7,10},{8,15},{9,12},{1... | collective-permute-start | bytes 98312 | tf_op jit(solution)/shard_map/ppermute | solution.py:217
  37.7 7.3 %collective-permute-start.9 = (bf16[32,512]{1,0:T(8,128)(2,1)S(1)}, bf16[32,512]{1,0:T(8,128)(2,1)S(1)}, u32[]{:S(2)}, u32[]{:S(2)}) collective-permute-start(bf16[32,512]{1,0:T(8,128)(2,1)S(1)} %get-tuple-element.80), channel_id=1, source_target_pairs={{0,5},{1,6},{2,7},{3,4},{4,9},{5,10},{6,11},{7,8},{8,13},{9,14},{1... | collective-permute-start | bytes 98312 | tf_op jit(solution)/shard_map/ppermute | solution.py:217
  39.1 13.7 %collective-permute-start.17 = (bf16[32,4096]{1,0:T(8,128)(2,1)S(1)}, bf16[32,4096]{1,0:T(8,128)(2,1)S(1)}, u32[]{:S(2)}, u32[]{:S(2)}) collective-permute-start(bf16[32,4096]{1,0:T(8,128)(2,1)S(1)} %get-tuple-element.85.refs_7_), channel_id=1, source_target_pairs={{0,4},{1,5},{2,6},{3,7},{4,8},{5,9},{6,10},{7,11},{8,12},{9,13},{1... | collective-permute-start | bytes 786440 | tf_op jit(solution)/shard_map/ppermute | solution.py:217
  39.9 12.6 %collective-permute-start.18 = (bf16[32,512]{1,0:T(8,128)(2,1)S(1)}, bf16[32,512]{1,0:T(8,128)(2,1)S(1)}, u32[]{:S(2)}, u32[]{:S(2)}) collective-permute-start(bf16[32,512]{1,0:T(8,128)(2,1)S(1)} %get-tuple-element.90), channel_id=1, source_target_pairs={{0,5},{1,6},{2,7},{3,4},{4,9},{5,10},{6,11},{7,8},{8,13},{9,14},{1... | collective-permute-start | bytes 98312 | tf_op jit(solution)/shard_map/ppermute | solution.py:217
  44.8 8.0 %collective-permute-start.19 = (bf16[32,512]{1,0:T(8,128)(2,1)S(1)}, bf16[32,512]{1,0:T(8,128)(2,1)S(1)}, u32[]{:S(2)}, u32[]{:S(2)}) collective-permute-start(bf16[32,512]{1,0:T(8,128)(2,1)S(1)} %get-tuple-element.91), channel_id=1, source_target_pairs={{0,7},{1,4},{2,5},{3,6},{4,11},{5,8},{6,9},{7,10},{8,15},{9,12},{1... | collective-permute-start | bytes 98312 | tf_op jit(solution)/shard_map/ppermute | solution.py:217
  45.7 14.2 %collective-permute-start.14 = (bf16[32,4096]{1,0:T(8,128)(2,1)S(1)}, bf16[32,4096]{1,0:T(8,128)(2,1)S(1)}, u32[]{:S(2)}, u32[]{:S(2)}) collective-permute-start(bf16[32,4096]{1,0:T(8,128)(2,1)S(1)} %get-tuple-element.87.refs_7_), channel_id=1, source_target_pairs={{0,4},{1,5},{2,6},{3,7},{4,8},{5,9},{6,10},{7,11},{8,12},{9,13},{1... | collective-permute-start | bytes 786440 | tf_op jit(solution)/shard_map/ppermute | solution.py:217
  46.3 13.2 %collective-permute-start.15 = (bf16[32,512]{1,0:T(8,128)(2,1)S(1)}, bf16[32,512]{1,0:T(8,128)(2,1)S(1)}, u32[]{:S(2)}, u32[]{:S(2)}) collective-permute-start(bf16[32,512]{1,0:T(8,128)(2,1)S(1)} %get-tuple-element.88), channel_id=1, source_target_pairs={{0,5},{1,6},{2,7},{3,4},{4,9},{5,10},{6,11},{7,8},{8,13},{9,14},{1... | collective-permute-start | bytes 98312 | tf_op jit(solution)/shard_map/ppermute | solution.py:217
  52.4 7.5 %collective-permute-start.16 = (bf16[32,512]{1,0:T(8,128)(2,1)S(1)}, bf16[32,512]{1,0:T(8,128)(2,1)S(1)}, u32[]{:S(2)}, u32[]{:S(2)}) collective-permute-start(bf16[32,512]{1,0:T(8,128)(2,1)S(1)} %get-tuple-element.89), channel_id=1, source_target_pairs={{0,7},{1,4},{2,5},{3,6},{4,11},{5,8},{6,9},{7,10},{8,15},{9,12},{1... | collective-permute-start | bytes 98312 | tf_op jit(solution)/shard_map/ppermute | solution.py:217
  53.6 14.2 %collective-permute-start.23 = (bf16[32,4096]{1,0:T(8,128)(2,1)S(1)}, bf16[32,4096]{1,0:T(8,128)(2,1)S(1)}, u32[]{:S(2)}, u32[]{:S(2)}) collective-permute-start(bf16[32,4096]{1,0:T(8,128)(2,1)S(1)} %get-tuple-element.93.refs_7_), channel_id=1, source_target_pairs={{0,4},{1,5},{2,6},{3,7},{4,8},{5,9},{6,10},{7,11},{8,12},{9,13},{1... | collective-permute-start | bytes 786440 | tf_op jit(solution)/shard_map/ppermute | solution.py:217
  53.6 12.5 %collective-permute-start.24 = (bf16[32,512]{1,0:T(8,128)(2,1)S(1)}, bf16[32,512]{1,0:T(8,128)(2,1)S(1)}, u32[]{:S(2)}, u32[]{:S(2)}) collective-permute-start(bf16[32,512]{1,0:T(8,128)(2,1)S(1)} %get-tuple-element.98), channel_id=1, source_target_pairs={{0,5},{1,6},{2,7},{3,4},{4,9},{5,10},{6,11},{7,8},{8,13},{9,14},{1... | collective-permute-start | bytes 98312 | tf_op jit(solution)/shard_map/ppermute | solution.py:217
  59.4 8.3 %collective-permute-start.25 = (bf16[32,512]{1,0:T(8,128)(2,1)S(1)}, bf16[32,512]{1,0:T(8,128)(2,1)S(1)}, u32[]{:S(2)}, u32[]{:S(2)}) collective-permute-start(bf16[32,512]{1,0:T(8,128)(2,1)S(1)} %get-tuple-element.99), channel_id=1, source_target_pairs={{0,7},{1,4},{2,5},{3,6},{4,11},{5,8},{6,9},{7,10},{8,15},{9,12},{1... | collective-permute-start | bytes 98312 | tf_op jit(solution)/shard_map/ppermute | solution.py:217
  60.7 14.0 %collective-permute-start.20 = (bf16[32,4096]{1,0:T(8,128)(2,1)S(1)}, bf16[32,4096]{1,0:T(8,128)(2,1)S(1)}, u32[]{:S(2)}, u32[]{:S(2)}) collective-permute-start(bf16[32,4096]{1,0:T(8,128)(2,1)S(1)} %get-tuple-element.95.refs_7_), channel_id=1, source_target_pairs={{0,4},{1,5},{2,6},{3,7},{4,8},{5,9},{6,10},{7,11},{8,12},{9,13},{1... | collective-permute-start | bytes 786440 | tf_op jit(solution)/shard_map/ppermute | solution.py:217
  60.8 13.0 %collective-permute-start.21 = (bf16[32,512]{1,0:T(8,128)(2,1)S(1)}, bf16[32,512]{1,0:T(8,128)(2,1)S(1)}, u32[]{:S(2)}, u32[]{:S(2)}) collective-permute-start(bf16[32,512]{1,0:T(8,128)(2,1)S(1)} %get-tuple-element.96), channel_id=1, source_target_pairs={{0,5},{1,6},{2,7},{3,4},{4,9},{5,10},{6,11},{7,8},{8,13},{9,14},{1... | collective-permute-start | bytes 98312 | tf_op jit(solution)/shard_map/ppermute | solution.py:217
  66.1 8.6 %collective-permute-start.22 = (bf16[32,512]{1,0:T(8,128)(2,1)S(1)}, bf16[32,512]{1,0:T(8,128)(2,1)S(1)}, u32[]{:S(2)}, u32[]{:S(2)}) collective-permute-start(bf16[32,512]{1,0:T(8,128)(2,1)S(1)} %get-tuple-element.97), channel_id=1, source_target_pairs={{0,7},{1,4},{2,5},{3,6},{4,11},{5,8},{6,9},{7,10},{8,15},{9,12},{1... | collective-permute-start | bytes 98312 | tf_op jit(solution)/shard_map/ppermute | solution.py:217
  68.5 13.5 %collective-permute-start.29 = (bf16[32,4096]{1,0:T(8,128)(2,1)S(1)}, bf16[32,4096]{1,0:T(8,128)(2,1)S(1)}, u32[]{:S(2)}, u32[]{:S(2)}) collective-permute-start(bf16[32,4096]{1,0:T(8,128)(2,1)S(1)} %get-tuple-element.101.refs_7_), channel_id=1, source_target_pairs={{0,4},{1,5},{2,6},{3,7},{4,8},{5,9},{6,10},{7,11},{8,12},{9,13},{1... | collective-permute-start | bytes 786440 | tf_op jit(solution)/shard_map/ppermute | solution.py:217
  68.6 12.5 %collective-permute-start.30 = (bf16[32,512]{1,0:T(8,128)(2,1)S(1)}, bf16[32,512]{1,0:T(8,128)(2,1)S(1)}, u32[]{:S(2)}, u32[]{:S(2)}) collective-permute-start(bf16[32,512]{1,0:T(8,128)(2,1)S(1)} %get-tuple-element.106), channel_id=1, source_target_pairs={{0,5},{1,6},{2,7},{3,4},{4,9},{5,10},{6,11},{7,8},{8,13},{9,14},{1... | collective-permute-start | bytes 98312 | tf_op jit(solution)/shard_map/ppermute | solution.py:217
  73.7 8.2 %collective-permute-start.31 = (bf16[32,512]{1,0:T(8,128)(2,1)S(1)}, bf16[32,512]{1,0:T(8,128)(2,1)S(1)}, u32[]{:S(2)}, u32[]{:S(2)}) collective-permute-start(bf16[32,512]{1,0:T(8,128)(2,1)S(1)} %get-tuple-element.107), channel_id=1, source_target_pairs={{0,7},{1,4},{2,5},{3,6},{4,11},{5,8},{6,9},{7,10},{8,15},{9,12},{1... | collective-permute-start | bytes 98312 | tf_op jit(solution)/shard_map/ppermute | solution.py:217
  75.4 14.1 %collective-permute-start.26 = (bf16[32,4096]{1,0:T(8,128)(2,1)S(1)}, bf16[32,4096]{1,0:T(8,128)(2,1)S(1)}, u32[]{:S(2)}, u32[]{:S(2)}) collective-permute-start(bf16[32,4096]{1,0:T(8,128)(2,1)S(1)} %get-tuple-element.103.refs_7_), channel_id=1, source_target_pairs={{0,4},{1,5},{2,6},{3,7},{4,8},{5,9},{6,10},{7,11},{8,12},{9,13},{1... | collective-permute-start | bytes 786440 | tf_op jit(solution)/shard_map/ppermute | solution.py:217
  75.5 13.1 %collective-permute-start.27 = (bf16[32,512]{1,0:T(8,128)(2,1)S(1)}, bf16[32,512]{1,0:T(8,128)(2,1)S(1)}, u32[]{:S(2)}, u32[]{:S(2)}) collective-permute-start(bf16[32,512]{1,0:T(8,128)(2,1)S(1)} %get-tuple-element.104), channel_id=1, source_target_pairs={{0,5},{1,6},{2,7},{3,4},{4,9},{5,10},{6,11},{7,8},{8,13},{9,14},{1... | collective-permute-start | bytes 98312 | tf_op jit(solution)/shard_map/ppermute | solution.py:217
  81.1 8.5 %collective-permute-start.28 = (bf16[32,512]{1,0:T(8,128)(2,1)S(1)}, bf16[32,512]{1,0:T(8,128)(2,1)S(1)}, u32[]{:S(2)}, u32[]{:S(2)}) collective-permute-start(bf16[32,512]{1,0:T(8,128)(2,1)S(1)} %get-tuple-element.105), channel_id=1, source_target_pairs={{0,7},{1,4},{2,5},{3,6},{4,11},{5,8},{6,9},{7,10},{8,15},{9,12},{1... | collective-permute-start | bytes 98312 | tf_op jit(solution)/shard_map/ppermute | solution.py:217
  82.7 14.2 %collective-permute-start.35 = (bf16[32,4096]{1,0:T(8,128)(2,1)S(1)}, bf16[32,4096]{1,0:T(8,128)(2,1)S(1)}, u32[]{:S(2)}, u32[]{:S(2)}) collective-permute-start(bf16[32,4096]{1,0:T(8,128)(2,1)S(1)} %get-tuple-element.109.refs_7_), channel_id=1, source_target_pairs={{0,4},{1,5},{2,6},{3,7},{4,8},{5,9},{6,10},{7,11},{8,12},{9,13},{1... | collective-permute-start | bytes 786440 | tf_op jit(solution)/shard_map/ppermute | solution.py:217
  82.8 12.5 %collective-permute-start.36 = (bf16[32,512]{1,0:T(8,128)(2,1)S(1)}, bf16[32,512]{1,0:T(8,128)(2,1)S(1)}, u32[]{:S(2)}, u32[]{:S(2)}) collective-permute-start(bf16[32,512]{1,0:T(8,128)(2,1)S(1)} %get-tuple-element.114), channel_id=1, source_target_pairs={{0,5},{1,6},{2,7},{3,4},{4,9},{5,10},{6,11},{7,8},{8,13},{9,14},{1... | collective-permute-start | bytes 98312 | tf_op jit(solution)/shard_map/ppermute | solution.py:217
  88.6 8.3 %collective-permute-start.37 = (bf16[32,512]{1,0:T(8,128)(2,1)S(1)}, bf16[32,512]{1,0:T(8,128)(2,1)S(1)}, u32[]{:S(2)}, u32[]{:S(2)}) collective-permute-start(bf16[32,512]{1,0:T(8,128)(2,1)S(1)} %get-tuple-element.115), channel_id=1, source_target_pairs={{0,7},{1,4},{2,5},{3,6},{4,11},{5,8},{6,9},{7,10},{8,15},{9,12},{1... | collective-permute-start | bytes 98312 | tf_op jit(solution)/shard_map/ppermute | solution.py:217
  90.3 13.6 %collective-permute-start.32 = (bf16[32,4096]{1,0:T(8,128)(2,1)S(1)}, bf16[32,4096]{1,0:T(8,128)(2,1)S(1)}, u32[]{:S(2)}, u32[]{:S(2)}) collective-permute-start(bf16[32,4096]{1,0:T(8,128)(2,1)S(1)} %get-tuple-element.111.refs_7_), channel_id=1, source_target_pairs={{0,4},{1,5},{2,6},{3,7},{4,8},{5,9},{6,10},{7,11},{8,12},{9,13},{1... | collective-permute-start | bytes 786440 | tf_op jit(solution)/shard_map/ppermute | solution.py:217
  90.4 12.7 %collective-permute-start.33 = (bf16[32,512]{1,0:T(8,128)(2,1)S(1)}, bf16[32,512]{1,0:T(8,128)(2,1)S(1)}, u32[]{:S(2)}, u32[]{:S(2)}) collective-permute-start(bf16[32,512]{1,0:T(8,128)(2,1)S(1)} %get-tuple-element.112), channel_id=1, source_target_pairs={{0,5},{1,6},{2,7},{3,4},{4,9},{5,10},{6,11},{7,8},{8,13},{9,14},{1... | collective-permute-start | bytes 98312 | tf_op jit(solution)/shard_map/ppermute | solution.py:217
  95.3 8.6 %collective-permute-start.34 = (bf16[32,512]{1,0:T(8,128)(2,1)S(1)}, bf16[32,512]{1,0:T(8,128)(2,1)S(1)}, u32[]{:S(2)}, u32[]{:S(2)}) collective-permute-start(bf16[32,512]{1,0:T(8,128)(2,1)S(1)} %get-tuple-element.113), channel_id=1, source_target_pairs={{0,7},{1,4},{2,5},{3,6},{4,11},{5,8},{6,9},{7,10},{8,15},{9,12},{1... | collective-permute-start | bytes 98312 | tf_op jit(solution)/shard_map/ppermute | solution.py:217
  97.7 13.5 %collective-permute-start.41 = (bf16[32,4096]{1,0:T(8,128)(2,1)S(1)}, bf16[32,4096]{1,0:T(8,128)(2,1)S(1)}, u32[]{:S(2)}, u32[]{:S(2)}) collective-permute-start(bf16[32,4096]{1,0:T(8,128)(2,1)S(1)} %get-tuple-element.117.refs_7_), channel_id=1, source_target_pairs={{0,4},{1,5},{2,6},{3,7},{4,8},{5,9},{6,10},{7,11},{8,12},{9,13},{1... | collective-permute-start | bytes 786440 | tf_op jit(solution)/shard_map/ppermute | solution.py:217
  97.7 12.5 %collective-permute-start.42 = (bf16[32,512]{1,0:T(8,128)(2,1)S(1)}, bf16[32,512]{1,0:T(8,128)(2,1)S(1)}, u32[]{:S(2)}, u32[]{:S(2)}) collective-permute-start(bf16[32,512]{1,0:T(8,128)(2,1)S(1)} %get-tuple-element.122), channel_id=1, source_target_pairs={{0,5},{1,6},{2,7},{3,4},{4,9},{5,10},{6,11},{7,8},{8,13},{9,14},{1... | collective-permute-start | bytes 98312 | tf_op jit(solution)/shard_map/ppermute | solution.py:217
  103.0 8.1 %collective-permute-start.43 = (bf16[32,512]{1,0:T(8,128)(2,1)S(1)}, bf16[32,512]{1,0:T(8,128)(2,1)S(1)}, u32[]{:S(2)}, u32[]{:S(2)}) collective-permute-start(bf16[32,512]{1,0:T(8,128)(2,1)S(1)} %get-tuple-element.123), channel_id=1, source_target_pairs={{0,7},{1,4},{2,5},{3,6},{4,11},{5,8},{6,9},{7,10},{8,15},{9,12},{1... | collective-permute-start | bytes 98312 | tf_op jit(solution)/shard_map/ppermute | solution.py:217
  104.7 13.6 %collective-permute-start.38 = (bf16[32,4096]{1,0:T(8,128)(2,1)S(1)}, bf16[32,4096]{1,0:T(8,128)(2,1)S(1)}, u32[]{:S(2)}, u32[]{:S(2)}) collective-permute-start(bf16[32,4096]{1,0:T(8,128)(2,1)S(1)} %get-tuple-element.119.refs_7_), channel_id=1, source_target_pairs={{0,4},{1,5},{2,6},{3,7},{4,8},{5,9},{6,10},{7,11},{8,12},{9,13},{1... | collective-permute-start | bytes 786440 | tf_op jit(solution)/shard_map/ppermute | solution.py:217
  104.7 13.1 %collective-permute-start.39 = (bf16[32,512]{1,0:T(8,128)(2,1)S(1)}, bf16[32,512]{1,0:T(8,128)(2,1)S(1)}, u32[]{:S(2)}, u32[]{:S(2)}) collective-permute-start(bf16[32,512]{1,0:T(8,128)(2,1)S(1)} %get-tuple-element.120), channel_id=1, source_target_pairs={{0,5},{1,6},{2,7},{3,4},{4,9},{5,10},{6,11},{7,8},{8,13},{9,14},{1... | collective-permute-start | bytes 98312 | tf_op jit(solution)/shard_map/ppermute | solution.py:217
  110.2 8.1 %collective-permute-start.40 = (bf16[32,512]{1,0:T(8,128)(2,1)S(1)}, bf16[32,512]{1,0:T(8,128)(2,1)S(1)}, u32[]{:S(2)}, u32[]{:S(2)}) collective-permute-start(bf16[32,512]{1,0:T(8,128)(2,1)S(1)} %get-tuple-element.121), channel_id=1, source_target_pairs={{0,7},{1,4},{2,5},{3,6},{4,11},{5,8},{6,9},{7,10},{8,15},{9,12},{1... | collective-permute-start | bytes 98312 | tf_op jit(solution)/shard_map/ppermute | solution.py:217

commit v9 on v6

--- a/solution.py
+++ b/solution.py
@@ -60,17 +60,20 @@
 
 def layer_kernel(tick, src_row, rows, brs, nzb, own_slot, prev_slot, aliased, *refs):
     refs = list(refs)
-    meta, main, across, inside, w, bias = refs[:6]
-    del refs[:6]
+    meta, main, across = refs[:3]
+    del refs[:3]
+    inside = refs.pop(0) if tick == 0 else None
+    w, bias = refs[:2]
+    del refs[:2]
     prev = None
     if prev_slot is not None:
         prev = refs.pop(0)
     if aliased:
         refs.pop(0)
     emitted = refs.pop(0) if prev_slot is not None or own_slot is not None else None
-    outer = None
+    outer = inner = None
     if own_slot is None:
-        out, outer, xbuf, sems = refs
+        out, outer, inner, xbuf, sems = refs
     else:
         out, xbuf, sems = refs
     edge = HALO * BLK
@@ -96,9 +99,11 @@
     @pl.when(live)
     def _():
         src = pl.ds(src_row, rows)
-        xbuf[:, edge : edge + width] = main[src, :]
+        xbuf[:, edge : edge + width] = main[src, 0:width]
         xbuf[:, pl.ds(pl.multiple_of(odd * (edge + width), BLK), edge)] = across[src, :]
-        xbuf[:, pl.ds(pl.multiple_of((1 - odd) * (edge + width), BLK), edge)] = inside[src, :]
+        xbuf[:, pl.ds(pl.multiple_of((1 - odd) * (edge + width), BLK), edge)] = (
+            main[src, width : width + edge] if inside is None else inside[src, :]
+        )
         for i in range(brs):
             picked = jnp.concatenate(
                 [xbuf[:, pl.ds(pl.multiple_of(meta[i * nzb + k], BLK), BLK)] for k in range(nzb)], axis=1
@@ -111,12 +116,14 @@
                 own[i // (brs // pieces)].start()
         if outer is not None:
             outer[...] = out[:, pl.ds(pl.multiple_of(odd * (width - edge), BLK), edge)]
+            inner[...] = out[:, pl.ds(pl.multiple_of((1 - odd) * (width - edge), BLK), edge)]
 
     @pl.when(jnp.logical_not(live))
     def _():
         out[...] = jnp.zeros_like(out)
         if outer is not None:
             outer[...] = jnp.zeros_like(outer)
+            inner[...] = jnp.zeros_like(inner)
         for copy in own:
             copy.start()
 
@@ -127,16 +134,17 @@
 
 
 def apply_layer(tick, src_row, row, rows, last, operands, prev, prev_slot, emitted, emitted_aval):
-    meta, main, across, inside, w, bias = operands
+    meta, *local = operands
+    w = local[-2]
     brs, depth = w.shape[:2]
     nzb = depth // BLK
     width = brs * BLK
     edge = HALO * BLK
     args = [
         pltpu.with_memory_space_constraint(meta, pltpu.SMEM),
-        *(pltpu.with_memory_space_constraint(a, pltpu.VMEM) for a in (main, across, inside, w, bias)),
+        *(pltpu.with_memory_space_constraint(a, pltpu.VMEM) for a in local),
     ]
-    specs = [SMEM] + [VMEM] * 5
+    specs = [SMEM] + [VMEM] * len(local)
     out_shape = []
     out_specs = []
     scratch = [
@@ -157,8 +165,8 @@
     if last:
         scratch.insert(0, pltpu.VMEM((rows, width), jnp.bfloat16))
     else:
-        out_shape += [pltpu.VMEM((rows, cols), jnp.bfloat16) for cols in (width, edge)]
-        out_specs += [VMEM] * 2
+        out_shape += [pltpu.VMEM((rows, cols), jnp.bfloat16) for cols in (width + edge, edge, edge)]
+        out_specs += [VMEM] * 3
     body = functools.partial(
         layer_kernel, tick, src_row, rows, brs, nzb, (tick, row) if last else None, prev_slot, emitted is not None
     )
@@ -171,33 +179,28 @@
         input_output_aliases=aliases,
         compiler_params=pltpu.CompilerParams(vmem_limit_bytes=8 * 1024 * 1024),
         cost_estimate=pl.CostEstimate(
-            flops=18 * rows * brs * nzb * BLK * BLK, bytes_accessed=18 * w.size, transcendentals=0
+            flops=40 * rows * brs * nzb * BLK * BLK, bytes_accessed=40 * w.size, transcendentals=0
         ),
         name=f"layer_t{tick}_r{row}",
     )(*args)
 
 
-def edge_kernel(meta, main, far, after, edge):
-    del far, after
-    odd = meta[meta.shape[0] - 1]
-    width = main.shape[1]
-    edge[...] = main[:, pl.ds(pl.multiple_of((1 - odd) * (width - HALO * BLK), BLK), HALO * BLK)]
-
-
-def inner_edge(meta, main, far, after):
+def merge_kernel(near, made, merged):
+    del made
+    edge = near.shape[1]
+    merged[:, merged.shape[1] - edge :] = near[...]
+
+
+def merge(near, made):
     return pl.pallas_call(
-        edge_kernel,
-        out_shape=pltpu.VMEM((main.shape[0], HALO * BLK), main.dtype),
-        in_specs=[SMEM, VMEM, ANY, ANY],
+        merge_kernel,
+        out_shape=pltpu.VMEM(made.shape, made.dtype),
+        in_specs=[VMEM, VMEM],
         out_specs=VMEM,
+        input_output_aliases={1: 0},
         compiler_params=pltpu.CompilerParams(vmem_limit_bytes=1024 * 1024),
-        name="edge",
-    )(
-        pltpu.with_memory_space_constraint(meta, pltpu.SMEM),
-        pltpu.with_memory_space_constraint(main, pltpu.VMEM),
-        far,
-        after,
-    )
+        name="merge",
+    )(*(pltpu.with_memory_space_constraint(a, pltpu.VMEM) for a in (near, made)))
 
 
 def shards(sections, blks, pending_groups, coefficient_tiles, source_block_indices, additive_offsets):
@@ -232,27 +235,22 @@
         additive_offsets,
         source_block_indices[0].T,
     )
-    parts = [(state, far)] * CHUNKS
-    emitted = prev = prev_slot = made = None
+    parts = [(state, far, near)] * CHUNKS
+    emitted = prev = prev_slot = None
     for tick in range(TICKS):
         last = tick + 1 == TICKS
         for c in range(CHUNKS):
-            main, far = parts[c]
-            src_row = c * rows
-            if tick > 0:
-                near = hop(inner_edge(meta, main, far, made), 0, inside)
-                src_row = 0
+            src_row = c * rows if tick == 0 else 0
+            operands = (meta, *parts[c], w, bias)
             outs = list(
-                apply_layer(
-                    tick, src_row, c * rows, rows, last, (meta, main, far, near, w, bias), prev, prev_slot, emitted, emitted_aval
-                )
+                apply_layer(tick, src_row, c * rows, rows, last, operands, prev, prev_slot, emitted, emitted_aval)
             )
             if prev is not None or last:
                 emitted = outs.pop(0)
             prev = prev_slot = None
             if not last:
-                prev, outer = outs
-                made = prev
+                made, outer, inner = outs
+                prev = merge(hop(inner, 0, inside), made)
                 prev_slot = (tick, c * rows)
                 parts[c] = (hop(prev, 1, lambda i: i), hop(outer, 1, across))
     return emitted

time: 124 us -> 138 us (1.11)
  waiting for transfers between devices: 91.2 us -> 103 us
    ppermute x44, waiting for transfers between devices: 91.2 us -> 103 us  [hop(): return lax.ppermute(values, ('section', 'blk'), pairs)]
  transfers between devices with their start and end apart: 44 -> 44, of which waited for: 27 -> 27; matrix products, arithmetic and copies ran while one was open for 0% -> 0% of each run, Pallas kernels for 12% -> 11%
where the time goes in v9:
time: 138 us; the launch traced here: 137 us
  waiting for transfers between devices  103 us (75%)
  Pallas kernels  17.2 us (12%)
  starting transfers between devices  15.2 us (11%)
    ppermute x44, waiting for transfers between devices, hop(): return lax.ppermute(values, ('section', 'blk'), pairs)  103 us
    ppermute x44, starting transfers between devices, hop(): return lax.ppermute(values, ('section', 'blk'), pairs)  15.2 us
    pallas_call x16, Pallas kernels, apply_layer(): pl.pallas_call(body, out_shape=tuple(out_shape), in_specs=specs, out_spec...  13.5 us
    pallas_call x1, Pallas kernels, load(): pl.pallas_call(functools.partial(load_kernel, blks), out_shape=(*(pltpu.V...  3.62 us
  transfers between devices with their start and end apart: 44, of which 27 were waited for; matrix products, arithmetic and copies ran while one was open for 0% of the time, Pallas kernels for 11%

profile of v9, /device:TPU:1, one launch (start us, length us, event | category | flops | bytes accessed | tf_op | source)
XLA Modules:
  0.0 136.9 jit_solution(4742735870851040242)
XLA Ops:
  0.0 0.9 constant_dynamic-slice_fusion
  0.9 2.7 %collective-permute-start = (bf16[64,512]{1,0:T(8,128)(2,1)S(1)}, bf16[64,512]{1,0:T(8,128)(2,1)S(1)}, u32[]{:S(2)}, u32[]{:S(2)}) collective-permute-start(bf16[64,512]{1,0:T(8,128)(2,1)S(1)} %get-tuple-element.124), channel_id=1, source_target_pairs={{0,3},{1,2},{2,1},{3,0},{4,7},{5,6},{6,5},{7,4},{8,11},{9,10},{10,... | collective-permute-start | bytes 196616 | tf_op jit(solution)/shard_map/ppermute | solution.py:219
  3.6 3.6 %load.1 = (bf16[64,4096]{1,0:T(8,128)(2,1)S(1)}, bf16[32,1024,128]{2,1,0:T(8,128)(2,1)S(1)}, f32[1,4096]{1,0:T(1,128)S(1)}, s32[258]{0:T(512)S(4)}) custom-call(bf16[64,4096]{1,0:T(8,128)(2,1)} %state.1, bf16[32,1024,128]{2,1,0:T(8,128)(2,1)} %bitcast.4, f32[1,4096]{1,0:T(1,128)} %bias.1, s32[8,32]{1,0:T(8,128)} %bitcast.5), custom_call_target="tpu_custom_call" | custom-call | bytes 8388608 | tf_op jit(solution)/shard_map/load/pallas_call | solution.py:46
  7.2 1.5 %layer_t0_r0.1 = (bf16[32,4608]{1,0:T(8,128)(2,1)S(1)}, bf16[32,512]{1,0:T(8,128)(2,1)S(1)}, bf16[32,512]{1,0:T(8,128)(2,1)S(1)}) custom-call(s32[258]{0:T(512)S(4)} %get-tuple-element.64.refs_0_, bf16[64,4096]{1,0:T(8,128)(2,1)S(1)} %get-tuple-element.65.refs_1_, bf16[64,512]{1,0:T(8,128)(2,1)S(1)} %collective-permute-done.refs_2_, ...), custom_call_target="tpu_custom_call" | custom-call | flops 5368709120 | bytes 167772160 | tf_op jit(solution)/shard_map/layer_t0_r0/pallas_call | solution.py:173
  8.7 0.6 collective-permute-start.2
  9.3 0.9 collective-permute-done.2.near
  10.1 1.2 collective-permute-start.6
  11.4 1.5 %layer_t0_r32.1 = (bf16[8,64,4096]{2,1,0:T(8,128)(2,1)}, bf16[32,4608]{1,0:T(8,128)(2,1)S(1)}, bf16[32,512]{1,0:T(8,128)(2,1)S(1)}, bf16[32,512]{1,0:T(8,128)(2,1)S(1)}) custom-call(s32[258]{0:T(512)S(4)} %get-tuple-element.64.refs_0_, bf16[64,4096]{1,0:T(8,128)(2,1)S(1)} %get-tuple-element.65.refs_1_, bf16[64,512]{1,0:T(8,128)(2,1)S(1)} %collective-permute-done.refs_2_, ...), custom_call_target="tpu_custom_call" | custom-call | flops 5368709120 | bytes 167772160 | tf_op jit(solution)/shard_map/layer_t0_r32/pallas_call | solution.py:173
  12.8 0.7 collective-permute-start.3
  13.5 1.2 collective-permute-start.7
  14.8 1.2 collective-permute-start.4
  16.0 7.1 %collective-permute-done.7.refs_2_ = bf16[32,512]{1,0:T(8,128)(2,1)S(1)} collective-permute-done((bf16[32,512]{1,0:T(8,128)(2,1)S(1)}, bf16[32,512]{1,0:T(8,128)(2,1)S(1)}, u32[]{:S(2)}, u32[]{:S(2)}) %collective-permute-start.7) | collective-permute-done | bytes 32800 | tf_op jit(solution)/shard_map/ppermute | solution.py:219
  23.1 0.7 layer_t1_r0.1
  24.0 1.1 collective-permute-done.8.near
  25.1 1.8 %collective-permute-start.12 = (bf16[32,4608]{1,0:T(8,128)(2,1)S(1)}, bf16[32,4608]{1,0:T(8,128)(2,1)S(1)}, u32[]{:S(2)}, u32[]{:S(2)}) collective-permute-start(bf16[32,4608]{1,0:T(8,128)(2,1)S(1)} %merge.16.refs_5_), channel_id=1, source_target_pairs={{0,4},{1,5},{2,6},{3,7},{4,8},{5,9},{6,10},{7,11},{8,12},{9,13},{1... | collective-permute-start | bytes 884744 | tf_op jit(solution)/shard_map/ppermute | solution.py:219
  26.9 4.2 %collective-permute-done.5.refs_2_ = bf16[32,512]{1,0:T(8,128)(2,1)S(1)} collective-permute-done((bf16[32,512]{1,0:T(8,128)(2,1)S(1)}, bf16[32,512]{1,0:T(8,128)(2,1)S(1)}, u32[]{:S(2)}, u32[]{:S(2)}) %collective-permute-start.5) | collective-permute-done | bytes 32800 | tf_op jit(solution)/shard_map/ppermute | solution.py:219
  31.1 0.7 layer_t1_r32.1
  31.8 0.5 collective-permute-start.9
  32.3 0.9 collective-permute-done.9.near
  33.2 1.6 %collective-permute-start.10 = (bf16[32,4608]{1,0:T(8,128)(2,1)S(1)}, bf16[32,4608]{1,0:T(8,128)(2,1)S(1)}, u32[]{:S(2)}, u32[]{:S(2)}) collective-permute-start(bf16[32,4608]{1,0:T(8,128)(2,1)S(1)} %merge.17.refs_5_), channel_id=1, source_target_pairs={{0,4},{1,5},{2,6},{3,7},{4,8},{5,9},{6,10},{7,11},{8,12},{9,13},{1... | collective-permute-start | bytes 884744 | tf_op jit(solution)/shard_map/ppermute | solution.py:219
  34.7 4.5 %collective-permute-done.13.refs_2_ = bf16[32,512]{1,0:T(8,128)(2,1)S(1)} collective-permute-done((bf16[32,512]{1,0:T(8,128)(2,1)S(1)}, bf16[32,512]{1,0:T(8,128)(2,1)S(1)}, u32[]{:S(2)}, u32[]{:S(2)}) %collective-permute-start.13) | collective-permute-done | bytes 32800 | tf_op jit(solution)/shard_map/ppermute | solution.py:219
  39.2 0.7 layer_t2_r0.1
  40.0 0.2 collective-permute-start.14
  40.2 1.0 collective-permute-done.14.near
  41.3 1.3 collective-permute-start.18
  42.5 5.4 %collective-permute-done.11.refs_2_ = bf16[32,512]{1,0:T(8,128)(2,1)S(1)} collective-permute-done((bf16[32,512]{1,0:T(8,128)(2,1)S(1)}, bf16[32,512]{1,0:T(8,128)(2,1)S(1)}, u32[]{:S(2)}, u32[]{:S(2)}) %collective-permute-start.11) | collective-permute-done | bytes 32800 | tf_op jit(solution)/shard_map/ppermute | solution.py:219
  48.0 0.7 layer_t2_r32.1
  48.7 0.2 collective-permute-start.15
  48.9 1.1 collective-permute-done.15.near
  50.0 0.4 collective-permute-start.16
  50.4 6.5 %collective-permute-done.19.refs_2_ = bf16[32,512]{1,0:T(8,128)(2,1)S(1)} collective-permute-done((bf16[32,512]{1,0:T(8,128)(2,1)S(1)}, bf16[32,512]{1,0:T(8,128)(2,1)S(1)}, u32[]{:S(2)}, u32[]{:S(2)}) %collective-permute-start.19) | collective-permute-done | bytes 32800 | tf_op jit(solution)/shard_map/ppermute | solution.py:219
  56.8 0.7 layer_t3_r0.1
  57.6 0.2 collective-permute-start.20
  57.8 1.1 collective-permute-done.20.near
  58.9 6.8 %collective-permute-done.17.refs_2_ = bf16[32,512]{1,0:T(8,128)(2,1)S(1)} collective-permute-done((bf16[32,512]{1,0:T(8,128)(2,1)S(1)}, bf16[32,512]{1,0:T(8,128)(2,1)S(1)}, u32[]{:S(2)}, u32[]{:S(2)}) %collective-permute-start.17) | collective-permute-done | bytes 32800 | tf_op jit(solution)/shard_map/ppermute | solution.py:219
  65.7 0.7 layer_t3_r32.1
  66.5 0.2 collective-permute-start.21
  66.7 1.1 collective-permute-done.21.near
  67.7 6.8 %collective-permute-done.25.refs_2_ = bf16[32,512]{1,0:T(8,128)(2,1)S(1)} collective-permute-done((bf16[32,512]{1,0:T(8,128)(2,1)S(1)}, bf16[32,512]{1,0:T(8,128)(2,1)S(1)}, u32[]{:S(2)}, u32[]{:S(2)}) %collective-permute-start.25) | collective-permute-done | bytes 32800 | tf_op jit(solution)/shard_map/ppermute | solution.py:219
  74.6 0.7 layer_t4_r0.1
  75.3 0.2 collective-permute-start.26
  75.5 1.1 collective-permute-done.26.near
  76.6 6.8 %collective-permute-done.23.refs_2_ = bf16[32,512]{1,0:T(8,128)(2,1)S(1)} collective-permute-done((bf16[32,512]{1,0:T(8,128)(2,1)S(1)}, bf16[32,512]{1,0:T(8,128)(2,1)S(1)}, u32[]{:S(2)}, u32[]{:S(2)}) %collective-permute-start.23) | collective-permute-done | bytes 32800 | tf_op jit(solution)/shard_map/ppermute | solution.py:219
  83.5 0.7 layer_t4_r32.1
  84.2 0.2 collective-permute-start.27
  84.4 1.1 collective-permute-done.27.near
  85.5 6.8 %collective-permute-done.31.refs_2_ = bf16[32,512]{1,0:T(8,128)(2,1)S(1)} collective-permute-done((bf16[32,512]{1,0:T(8,128)(2,1)S(1)}, bf16[32,512]{1,0:T(8,128)(2,1)S(1)}, u32[]{:S(2)}, u32[]{:S(2)}) %collective-permute-start.31) | collective-permute-done | bytes 32800 | tf_op jit(solution)/shard_map/ppermute | solution.py:219
  92.3 0.7 layer_t5_r0.1
  93.1 0.2 collective-permute-start.32
  93.3 1.1 collective-permute-done.32.near
  94.4 6.8 %collective-permute-done.29.refs_2_ = bf16[32,512]{1,0:T(8,128)(2,1)S(1)} collective-permute-done((bf16[32,512]{1,0:T(8,128)(2,1)S(1)}, bf16[32,512]{1,0:T(8,128)(2,1)S(1)}, u32[]{:S(2)}, u32[]{:S(2)}) %collective-permute-start.29) | collective-permute-done | bytes 32800 | tf_op jit(solution)/shard_map/ppermute | solution.py:219
  101.2 0.7 layer_t5_r32.1
  102.0 0.2 collective-permute-start.33
  102.2 1.1 collective-permute-done.33.near
  103.2 6.8 %collective-permute-done.37.refs_2_ = bf16[32,512]{1,0:T(8,128)(2,1)S(1)} collective-permute-done((bf16[32,512]{1,0:T(8,128)(2,1)S(1)}, bf16[32,512]{1,0:T(8,128)(2,1)S(1)}, u32[]{:S(2)}, u32[]{:S(2)}) %collective-permute-start.37) | collective-permute-done | bytes 32800 | tf_op jit(solution)/shard_map/ppermute | solution.py:219
  110.1 0.7 layer_t6_r0.1
  111.0 1.1 collective-permute-done.38.near
  112.1 6.8 %collective-permute-done.35.refs_2_ = bf16[32,512]{1,0:T(8,128)(2,1)S(1)} collective-permute-done((bf16[32,512]{1,0:T(8,128)(2,1)S(1)}, bf16[32,512]{1,0:T(8,128)(2,1)S(1)}, u32[]{:S(2)}, u32[]{:S(2)}) %collective-permute-start.35) | collective-permute-done | bytes 32800 | tf_op jit(solution)/shard_map/ppermute | solution.py:219
  119.0 0.7 layer_t6_r32.1
  119.9 1.1 collective-permute-done.39.near
  121.0 7.2 %collective-permute-done.43.refs_2_ = bf16[32,512]{1,0:T(8,128)(2,1)S(1)} collective-permute-done((bf16[32,512]{1,0:T(8,128)(2,1)S(1)}, bf16[32,512]{1,0:T(8,128)(2,1)S(1)}, u32[]{:S(2)}, u32[]{:S(2)}) %collective-permute-start.43) | collective-permute-done | bytes 32800 | tf_op jit(solution)/shard_map/ppermute | solution.py:219
  128.2 0.8 layer_t7_r0.1.refs_5_
  129.0 7.0 %collective-permute-done.40.refs_1_ = bf16[32,4608]{1,0:T(8,128)(2,1)S(1)} collective-permute-done((bf16[32,4608]{1,0:T(8,128)(2,1)S(1)}, bf16[32,4608]{1,0:T(8,128)(2,1)S(1)}, u32[]{:S(2)}, u32[]{:S(2)}) %collective-permute-start.40) | collective-permute-done | bytes 294944 | tf_op jit(solution)/shard_map/ppermute | solution.py:219
  136.0 0.8 layer_t7_r32.1
  (56 shorter events, 0.7 us)
Async XLA Ops:
  0.9 6.3 %collective-permute-start = (bf16[64,512]{1,0:T(8,128)(2,1)S(1)}, bf16[64,512]{1,0:T(8,128)(2,1)S(1)}, u32[]{:S(2)}, u32[]{:S(2)}) collective-permute-start(bf16[64,512]{1,0:T(8,128)(2,1)S(1)} %get-tuple-element.124), channel_id=1, source_target_pairs={{0,3},{1,2},{2,1},{3,0},{4,7},{5,6},{6,5},{7,4},{8,11},{9,10},{10,... | collective-permute-start | bytes 196616 | tf_op jit(solution)/shard_map/ppermute | solution.py:219
  3.6 3.6 %collective-permute-start.1 = (bf16[64,512]{1,0:T(8,128)(2,1)S(1)}, bf16[64,512]{1,0:T(8,128)(2,1)S(1)}, u32[]{:S(2)}, u32[]{:S(2)}) collective-permute-start(bf16[64,512]{1,0:T(8,128)(2,1)S(1)} %get-tuple-element.123), channel_id=1, source_target_pairs={{0,1},{1,0},{2,3},{3,2},{4,5},{5,4},{6,7},{7,6},{8,9},{9,8},{10,11... | collective-permute-start | bytes 196616 | tf_op jit(solution)/shard_map/ppermute | solution.py:219
  8.7 1.4 %collective-permute-start.2 = (bf16[32,512]{1,0:T(8,128)(2,1)S(1)}, bf16[32,512]{1,0:T(8,128)(2,1)S(1)}, u32[]{:S(2)}, u32[]{:S(2)}) collective-permute-start(bf16[32,512]{1,0:T(8,128)(2,1)S(1)} %get-tuple-element.68), channel_id=1, source_target_pairs={{0,1},{1,0},{2,3},{3,2},{4,5},{5,4},{6,7},{7,6},{8,9},{9,8},{10,11... | collective-permute-start | bytes 98312 | tf_op jit(solution)/shard_map/ppermute | solution.py:219
  10.1 13.0 %collective-permute-start.6 = (bf16[32,4608]{1,0:T(8,128)(2,1)S(1)}, bf16[32,4608]{1,0:T(8,128)(2,1)S(1)}, u32[]{:S(2)}, u32[]{:S(2)}) collective-permute-start(bf16[32,4608]{1,0:T(8,128)(2,1)S(1)} %merge.14.refs_6_), channel_id=1, source_target_pairs={{0,4},{1,5},{2,6},{3,7},{4,8},{5,9},{6,10},{7,11},{8,12},{9,13},{1... | collective-permute-start | bytes 884744 | tf_op jit(solution)/shard_map/ppermute | solution.py:219
  12.8 1.9 %collective-permute-start.3 = (bf16[32,512]{1,0:T(8,128)(2,1)S(1)}, bf16[32,512]{1,0:T(8,128)(2,1)S(1)}, u32[]{:S(2)}, u32[]{:S(2)}) collective-permute-start(bf16[32,512]{1,0:T(8,128)(2,1)S(1)} %get-tuple-element.70), channel_id=1, source_target_pairs={{0,1},{1,0},{2,3},{3,2},{4,5},{5,4},{6,7},{7,6},{8,9},{9,8},{10,11... | collective-permute-start | bytes 98312 | tf_op jit(solution)/shard_map/ppermute | solution.py:219
  13.5 9.6 %collective-permute-start.7 = (bf16[32,512]{1,0:T(8,128)(2,1)S(1)}, bf16[32,512]{1,0:T(8,128)(2,1)S(1)}, u32[]{:S(2)}, u32[]{:S(2)}) collective-permute-start(bf16[32,512]{1,0:T(8,128)(2,1)S(1)} %get-tuple-element.73), channel_id=1, source_target_pairs={{0,7},{1,6},{2,5},{3,4},{4,11},{5,10},{6,9},{7,8},{8,15},{9,14},{1... | collective-permute-start | bytes 98312 | tf_op jit(solution)/shard_map/ppermute | solution.py:219
  14.8 16.3 %collective-permute-start.4 = (bf16[32,4608]{1,0:T(8,128)(2,1)S(1)}, bf16[32,4608]{1,0:T(8,128)(2,1)S(1)}, u32[]{:S(2)}, u32[]{:S(2)}) collective-permute-start(bf16[32,4608]{1,0:T(8,128)(2,1)S(1)} %merge.15.refs_5_), channel_id=1, source_target_pairs={{0,4},{1,5},{2,6},{3,7},{4,8},{5,9},{6,10},{7,11},{8,12},{9,13},{1... | collective-permute-start | bytes 884744 | tf_op jit(solution)/shard_map/ppermute | solution.py:219
  23.9 1.3 collective-permute-start.8
  23.9 7.1 %collective-permute-start.5 = (bf16[32,512]{1,0:T(8,128)(2,1)S(1)}, bf16[32,512]{1,0:T(8,128)(2,1)S(1)}, u32[]{:S(2)}, u32[]{:S(2)}) collective-permute-start(bf16[32,512]{1,0:T(8,128)(2,1)S(1)} %get-tuple-element.72), channel_id=1, source_target_pairs={{0,7},{1,6},{2,5},{3,4},{4,11},{5,10},{6,9},{7,8},{8,15},{9,14},{1... | collective-permute-start | bytes 98312 | tf_op jit(solution)/shard_map/ppermute | solution.py:219
  25.1 14.1 %collective-permute-start.12 = (bf16[32,4608]{1,0:T(8,128)(2,1)S(1)}, bf16[32,4608]{1,0:T(8,128)(2,1)S(1)}, u32[]{:S(2)}, u32[]{:S(2)}) collective-permute-start(bf16[32,4608]{1,0:T(8,128)(2,1)S(1)} %merge.16.refs_5_), channel_id=1, source_target_pairs={{0,4},{1,5},{2,6},{3,7},{4,8},{5,9},{6,10},{7,11},{8,12},{9,13},{1... | collective-permute-start | bytes 884744 | tf_op jit(solution)/shard_map/ppermute | solution.py:219
  31.8 1.3 collective-permute-start.9
  32.3 6.9 %collective-permute-start.13 = (bf16[32,512]{1,0:T(8,128)(2,1)S(1)}, bf16[32,512]{1,0:T(8,128)(2,1)S(1)}, u32[]{:S(2)}, u32[]{:S(2)}) collective-permute-start(bf16[32,512]{1,0:T(8,128)(2,1)S(1)} %get-tuple-element.81), channel_id=1, source_target_pairs={{0,7},{1,6},{2,5},{3,4},{4,11},{5,10},{6,9},{7,8},{8,15},{9,14},{1... | collective-permute-start | bytes 98312 | tf_op jit(solution)/shard_map/ppermute | solution.py:219
  33.2 14.8 %collective-permute-start.10 = (bf16[32,4608]{1,0:T(8,128)(2,1)S(1)}, bf16[32,4608]{1,0:T(8,128)(2,1)S(1)}, u32[]{:S(2)}, u32[]{:S(2)}) collective-permute-start(bf16[32,4608]{1,0:T(8,128)(2,1)S(1)} %merge.17.refs_5_), channel_id=1, source_target_pairs={{0,4},{1,5},{2,6},{3,7},{4,8},{5,9},{6,10},{7,11},{8,12},{9,13},{1... | collective-permute-start | bytes 884744 | tf_op jit(solution)/shard_map/ppermute | solution.py:219
  40.0 1.3 collective-permute-start.14
  40.2 7.7 %collective-permute-start.11 = (bf16[32,512]{1,0:T(8,128)(2,1)S(1)}, bf16[32,512]{1,0:T(8,128)(2,1)S(1)}, u32[]{:S(2)}, u32[]{:S(2)}) collective-permute-start(bf16[32,512]{1,0:T(8,128)(2,1)S(1)} %get-tuple-element.80), channel_id=1, source_target_pairs={{0,7},{1,6},{2,5},{3,4},{4,11},{5,10},{6,9},{7,8},{8,15},{9,14},{1... | collective-permute-start | bytes 98312 | tf_op jit(solution)/shard_map/ppermute | solution.py:219
  41.3 15.6 %collective-permute-start.18 = (bf16[32,4608]{1,0:T(8,128)(2,1)S(1)}, bf16[32,4608]{1,0:T(8,128)(2,1)S(1)}, u32[]{:S(2)}, u32[]{:S(2)}) collective-permute-start(bf16[32,4608]{1,0:T(8,128)(2,1)S(1)} %merge.18.refs_5_), channel_id=1, source_target_pairs={{0,4},{1,5},{2,6},{3,7},{4,8},{5,9},{6,10},{7,11},{8,12},{9,13},{1... | collective-permute-start | bytes 884744 | tf_op jit(solution)/shard_map/ppermute | solution.py:219
  48.7 1.3 collective-permute-start.15
  48.9 7.9 %collective-permute-start.19 = (bf16[32,512]{1,0:T(8,128)(2,1)S(1)}, bf16[32,512]{1,0:T(8,128)(2,1)S(1)}, u32[]{:S(2)}, u32[]{:S(2)}) collective-permute-start(bf16[32,512]{1,0:T(8,128)(2,1)S(1)} %get-tuple-element.89), channel_id=1, source_target_pairs={{0,7},{1,6},{2,5},{3,4},{4,11},{5,10},{6,9},{7,8},{8,15},{9,14},{1... | collective-permute-start | bytes 98312 | tf_op jit(solution)/shard_map/ppermute | solution.py:219
  50.0 15.7 %collective-permute-start.16 = (bf16[32,4608]{1,0:T(8,128)(2,1)S(1)}, bf16[32,4608]{1,0:T(8,128)(2,1)S(1)}, u32[]{:S(2)}, u32[]{:S(2)}) collective-permute-start(bf16[32,4608]{1,0:T(8,128)(2,1)S(1)} %merge.19.refs_5_), channel_id=1, source_target_pairs={{0,4},{1,5},{2,6},{3,7},{4,8},{5,9},{6,10},{7,11},{8,12},{9,13},{1... | collective-permute-start | bytes 884744 | tf_op jit(solution)/shard_map/ppermute | solution.py:219
  57.6 1.3 collective-permute-start.20
  57.8 7.9 %collective-permute-start.17 = (bf16[32,512]{1,0:T(8,128)(2,1)S(1)}, bf16[32,512]{1,0:T(8,128)(2,1)S(1)}, u32[]{:S(2)}, u32[]{:S(2)}) collective-permute-start(bf16[32,512]{1,0:T(8,128)(2,1)S(1)} %get-tuple-element.88), channel_id=1, source_target_pairs={{0,7},{1,6},{2,5},{3,4},{4,11},{5,10},{6,9},{7,8},{8,15},{9,14},{1... | collective-permute-start | bytes 98312 | tf_op jit(solution)/shard_map/ppermute | solution.py:219
  58.9 15.7 %collective-permute-start.24 = (bf16[32,4608]{1,0:T(8,128)(2,1)S(1)}, bf16[32,4608]{1,0:T(8,128)(2,1)S(1)}, u32[]{:S(2)}, u32[]{:S(2)}) collective-permute-start(bf16[32,4608]{1,0:T(8,128)(2,1)S(1)} %merge.20.refs_5_), channel_id=1, source_target_pairs={{0,4},{1,5},{2,6},{3,7},{4,8},{5,9},{6,10},{7,11},{8,12},{9,13},{1... | collective-permute-start | bytes 884744 | tf_op jit(solution)/shard_map/ppermute | solution.py:219
  66.5 1.3 collective-permute-start.21
  66.6 7.9 %collective-permute-start.25 = (bf16[32,512]{1,0:T(8,128)(2,1)S(1)}, bf16[32,512]{1,0:T(8,128)(2,1)S(1)}, u32[]{:S(2)}, u32[]{:S(2)}) collective-permute-start(bf16[32,512]{1,0:T(8,128)(2,1)S(1)} %get-tuple-element.97), channel_id=1, source_target_pairs={{0,7},{1,6},{2,5},{3,4},{4,11},{5,10},{6,9},{7,8},{8,15},{9,14},{1... | collective-permute-start | bytes 98312 | tf_op jit(solution)/shard_map/ppermute | solution.py:219
  67.7 15.7 %collective-permute-start.22 = (bf16[32,4608]{1,0:T(8,128)(2,1)S(1)}, bf16[32,4608]{1,0:T(8,128)(2,1)S(1)}, u32[]{:S(2)}, u32[]{:S(2)}) collective-permute-start(bf16[32,4608]{1,0:T(8,128)(2,1)S(1)} %merge.21.refs_5_), channel_id=1, source_target_pairs={{0,4},{1,5},{2,6},{3,7},{4,8},{5,9},{6,10},{7,11},{8,12},{9,13},{1... | collective-permute-start | bytes 884744 | tf_op jit(solution)/shard_map/ppermute | solution.py:219
  75.3 1.3 collective-permute-start.26
  75.5 7.9 %collective-permute-start.23 = (bf16[32,512]{1,0:T(8,128)(2,1)S(1)}, bf16[32,512]{1,0:T(8,128)(2,1)S(1)}, u32[]{:S(2)}, u32[]{:S(2)}) collective-permute-start(bf16[32,512]{1,0:T(8,128)(2,1)S(1)} %get-tuple-element.96), channel_id=1, source_target_pairs={{0,7},{1,6},{2,5},{3,4},{4,11},{5,10},{6,9},{7,8},{8,15},{9,14},{1... | collective-permute-start | bytes 98312 | tf_op jit(solution)/shard_map/ppermute | solution.py:219
  76.6 15.7 %collective-permute-start.30 = (bf16[32,4608]{1,0:T(8,128)(2,1)S(1)}, bf16[32,4608]{1,0:T(8,128)(2,1)S(1)}, u32[]{:S(2)}, u32[]{:S(2)}) collective-permute-start(bf16[32,4608]{1,0:T(8,128)(2,1)S(1)} %merge.22.refs_5_), channel_id=1, source_target_pairs={{0,4},{1,5},{2,6},{3,7},{4,8},{5,9},{6,10},{7,11},{8,12},{9,13},{1... | collective-permute-start | bytes 884744 | tf_op jit(solution)/shard_map/ppermute | solution.py:219
  84.2 1.3 collective-permute-start.27
  84.4 7.9 %collective-permute-start.31 = (bf16[32,512]{1,0:T(8,128)(2,1)S(1)}, bf16[32,512]{1,0:T(8,128)(2,1)S(1)}, u32[]{:S(2)}, u32[]{:S(2)}) collective-permute-start(bf16[32,512]{1,0:T(8,128)(2,1)S(1)} %get-tuple-element.105), channel_id=1, source_target_pairs={{0,7},{1,6},{2,5},{3,4},{4,11},{5,10},{6,9},{7,8},{8,15},{9,14},{1... | collective-permute-start | bytes 98312 | tf_op jit(solution)/shard_map/ppermute | solution.py:219
  85.5 15.7 %collective-permute-start.28 = (bf16[32,4608]{1,0:T(8,128)(2,1)S(1)}, bf16[32,4608]{1,0:T(8,128)(2,1)S(1)}, u32[]{:S(2)}, u32[]{:S(2)}) collective-permute-start(bf16[32,4608]{1,0:T(8,128)(2,1)S(1)} %merge.23.refs_5_), channel_id=1, source_target_pairs={{0,4},{1,5},{2,6},{3,7},{4,8},{5,9},{6,10},{7,11},{8,12},{9,13},{1... | collective-permute-start | bytes 884744 | tf_op jit(solution)/shard_map/ppermute | solution.py:219
  93.1 1.3 collective-permute-start.32
  93.3 7.9 %collective-permute-start.29 = (bf16[32,512]{1,0:T(8,128)(2,1)S(1)}, bf16[32,512]{1,0:T(8,128)(2,1)S(1)}, u32[]{:S(2)}, u32[]{:S(2)}) collective-permute-start(bf16[32,512]{1,0:T(8,128)(2,1)S(1)} %get-tuple-element.104), channel_id=1, source_target_pairs={{0,7},{1,6},{2,5},{3,4},{4,11},{5,10},{6,9},{7,8},{8,15},{9,14},{1... | collective-permute-start | bytes 98312 | tf_op jit(solution)/shard_map/ppermute | solution.py:219
  94.4 15.7 %collective-permute-start.36 = (bf16[32,4608]{1,0:T(8,128)(2,1)S(1)}, bf16[32,4608]{1,0:T(8,128)(2,1)S(1)}, u32[]{:S(2)}, u32[]{:S(2)}) collective-permute-start(bf16[32,4608]{1,0:T(8,128)(2,1)S(1)} %merge.24.refs_5_), channel_id=1, source_target_pairs={{0,4},{1,5},{2,6},{3,7},{4,8},{5,9},{6,10},{7,11},{8,12},{9,13},{1... | collective-permute-start | bytes 884744 | tf_op jit(solution)/shard_map/ppermute | solution.py:219
  102.0 1.3 collective-permute-start.33
  102.1 7.9 %collective-permute-start.37 = (bf16[32,512]{1,0:T(8,128)(2,1)S(1)}, bf16[32,512]{1,0:T(8,128)(2,1)S(1)}, u32[]{:S(2)}, u32[]{:S(2)}) collective-permute-start(bf16[32,512]{1,0:T(8,128)(2,1)S(1)} %get-tuple-element.113), channel_id=1, source_target_pairs={{0,7},{1,6},{2,5},{3,4},{4,11},{5,10},{6,9},{7,8},{8,15},{9,14},{1... | collective-permute-start | bytes 98312 | tf_op jit(solution)/shard_map/ppermute | solution.py:219
  103.2 15.7 %collective-permute-start.34 = (bf16[32,4608]{1,0:T(8,128)(2,1)S(1)}, bf16[32,4608]{1,0:T(8,128)(2,1)S(1)}, u32[]{:S(2)}, u32[]{:S(2)}) collective-permute-start(bf16[32,4608]{1,0:T(8,128)(2,1)S(1)} %merge.25.refs_5_), channel_id=1, source_target_pairs={{0,4},{1,5},{2,6},{3,7},{4,8},{5,9},{6,10},{7,11},{8,12},{9,13},{1... | collective-permute-start | bytes 884744 | tf_op jit(solution)/shard_map/ppermute | solution.py:219
  110.8 1.3 collective-permute-start.38
  111.0 7.9 %collective-permute-start.35 = (bf16[32,512]{1,0:T(8,128)(2,1)S(1)}, bf16[32,512]{1,0:T(8,128)(2,1)S(1)}, u32[]{:S(2)}, u32[]{:S(2)}) collective-permute-start(bf16[32,512]{1,0:T(8,128)(2,1)S(1)} %get-tuple-element.112), channel_id=1, source_target_pairs={{0,7},{1,6},{2,5},{3,4},{4,11},{5,10},{6,9},{7,8},{8,15},{9,14},{1... | collective-permute-start | bytes 98312 | tf_op jit(solution)/shard_map/ppermute | solution.py:219
  112.1 16.1 %collective-permute-start.42 = (bf16[32,4608]{1,0:T(8,128)(2,1)S(1)}, bf16[32,4608]{1,0:T(8,128)(2,1)S(1)}, u32[]{:S(2)}, u32[]{:S(2)}) collective-permute-start(bf16[32,4608]{1,0:T(8,128)(2,1)S(1)} %merge.26.refs_5_), channel_id=1, source_target_pairs={{0,4},{1,5},{2,6},{3,7},{4,8},{5,9},{6,10},{7,11},{8,12},{9,13},{1... | collective-permute-start | bytes 884744 | tf_op jit(solution)/shard_map/ppermute | solution.py:219
  119.7 1.3 collective-permute-start.39
  119.9 8.3 %collective-permute-start.43 = (bf16[32,512]{1,0:T(8,128)(2,1)S(1)}, bf16[32,512]{1,0:T(8,128)(2,1)S(1)}, u32[]{:S(2)}, u32[]{:S(2)}) collective-permute-start(bf16[32,512]{1,0:T(8,128)(2,1)S(1)} %get-tuple-element.121), channel_id=1, source_target_pairs={{0,7},{1,6},{2,5},{3,4},{4,11},{5,10},{6,9},{7,8},{8,15},{9,14},{1... | collective-permute-start | bytes 98312 | tf_op jit(solution)/shard_map/ppermute | solution.py:219
  119.9 9.1 %collective-permute-start.41 = (bf16[32,512]{1,0:T(8,128)(2,1)S(1)}, bf16[32,512]{1,0:T(8,128)(2,1)S(1)}, u32[]{:S(2)}, u32[]{:S(2)}) collective-permute-start(bf16[32,512]{1,0:T(8,128)(2,1)S(1)} %get-tuple-element.120), channel_id=1, source_target_pairs={{0,7},{1,6},{2,5},{3,4},{4,11},{5,10},{6,9},{7,8},{8,15},{9,14},{1... | collective-permute-start | bytes 98312 | tf_op jit(solution)/shard_map/ppermute | solution.py:219
  121.0 15.0 %collective-permute-start.40 = (bf16[32,4608]{1,0:T(8,128)(2,1)S(1)}, bf16[32,4608]{1,0:T(8,128)(2,1)S(1)}, u32[]{:S(2)}, u32[]{:S(2)}) collective-permute-start(bf16[32,4608]{1,0:T(8,128)(2,1)S(1)} %merge.27.refs_5_), channel_id=1, source_target_pairs={{0,4},{1,5},{2,6},{3,7},{4,8},{5,9},{6,10},{7,11},{8,12},{9,13},{1... | collective-permute-start | bytes 884744 | tf_op jit(solution)/shard_map/ppermute | solution.py:219

commit v10 on v6

--- a/solution.py
+++ b/solution.py
@@ -207,10 +207,10 @@
     edge = HALO * BLK
     emitted_aval = jax.ShapeDtypeStruct((TICKS, height, width), jnp.bfloat16)
 
-    def hop(values, step, place):
+    def hop(values, step, place, closed=True):
         pairs = [
             (s * blks + i, (s + step) % sections * blks + place(i) % blks)
-            for s in range(sections)
+            for s in range(sections if closed else sections - step)
             for i in range(blks)
         ]
         return lax.ppermute(values, ("section", "blk"), pairs)
@@ -254,7 +254,7 @@
                 prev, outer = outs
                 made = prev
                 prev_slot = (tick, c * rows)
-                parts[c] = (hop(prev, 1, lambda i: i), hop(outer, 1, across))
+                parts[c] = (hop(prev, 1, lambda i: i), hop(outer, 1, across, closed=False))
     return emitted
 
 

time: 124 us -> 122 us (0.984)
  waiting for transfers between devices: 91.2 us -> 9.18 us
  starting transfers between devices: 14.1 us -> 93.2 us
    ppermute x44, waiting for transfers between devices: 91.2 us -> 9.18 us  [hop(): return lax.ppermute(values, ('section', 'blk'), pairs)]
    ppermute x44, starting transfers between devices: 14.1 us -> 93.2 us  [hop(): return lax.ppermute(values, ('section', 'blk'), pairs)]
  transfers between devices with their start and end apart: 44 -> 44, of which waited for: 27 -> 8; matrix products, arithmetic and copies ran while one was open for 0% -> 0% of each run, Pallas kernels for 12% -> 12%
where the time goes in v10:
time: 122 us; the launch traced here: 121 us
  starting transfers between devices  93.2 us (76%)
  Pallas kernels  17.2 us (14%)
  waiting for transfers between devices  9.18 us (8%)
    ppermute x44, starting transfers between devices, hop(): return lax.ppermute(values, ('section', 'blk'), pairs)  93.2 us
    pallas_call x16, Pallas kernels, apply_layer(): pl.pallas_call(body, out_shape=tuple(out_shape), in_specs=specs, out_spec...  13.6 us
    ppermute x44, waiting for transfers between devices, hop(): return lax.ppermute(values, ('section', 'blk'), pairs)  9.18 us
    pallas_call x1, Pallas kernels, load(): pl.pallas_call(functools.partial(load_kernel, blks), out_shape=(*(pltpu.V...  3.62 us
  transfers between devices with their start and end apart: 44, of which 8 were waited for; matrix products, arithmetic and copies ran while one was open for 0% of the time, Pallas kernels for 12%

profile of v10, /device:TPU:1, one launch (start us, length us, event | category | flops | bytes accessed | tf_op | source)
XLA Modules:
  0.0 121.1 jit_solution(15053633110477134362)
XLA Ops:
  0.0 0.9 constant_dynamic-slice_fusion
  0.9 2.7 %collective-permute-start = (bf16[64,512]{1,0:T(8,128)(2,1)S(1)}, bf16[64,512]{1,0:T(8,128)(2,1)S(1)}, u32[]{:S(2)}, u32[]{:S(2)}) collective-permute-start(bf16[64,512]{1,0:T(8,128)(2,1)S(1)} %get-tuple-element.96), channel_id=1, source_target_pairs={{0,3},{1,2},{2,1},{3,0},{4,7},{5,6},{6,5},{7,4},{8,11},{9,10},{10,... | collective-permute-start | bytes 196616 | tf_op jit(solution)/shard_map/ppermute | solution.py:216
  3.6 3.6 %load.1 = (bf16[64,4096]{1,0:T(8,128)(2,1)S(1)}, bf16[32,1024,128]{2,1,0:T(8,128)(2,1)S(1)}, f32[1,4096]{1,0:T(1,128)S(1)}, s32[258]{0:T(512)S(4)}) custom-call(bf16[64,4096]{1,0:T(8,128)(2,1)} %state.1, bf16[32,1024,128]{2,1,0:T(8,128)(2,1)} %bitcast.4, f32[1,4096]{1,0:T(1,128)} %bias.1, s32[8,32]{1,0:T(8,128)} %bitcast.5), custom_call_target="tpu_custom_call" | custom-call | bytes 8388608 | tf_op jit(solution)/shard_map/load/pallas_call | solution.py:46
  7.2 1.5 %layer_t0_r0.1 = (bf16[32,4096]{1,0:T(8,128)(2,1)S(1)}, bf16[32,512]{1,0:T(8,128)(2,1)S(1)}) custom-call(s32[258]{0:T(512)S(4)} %get-tuple-element.50.refs_0_.meta, bf16[64,4096]{1,0:T(8,128)(2,1)S(1)} %get-tuple-element.51.refs_1_, bf16[64,512]{1,0:T(8,128)(2,1)S(1)} %collective-permute-done.refs_2_, bf16[64,512]{1,0:T(8,128)(2,1)S(1)} %collective-permute-done.1.refs_3_, ...), custom_call_target="tpu_custom_call" | custom-call | flops 2415919104 | bytes 75497472 | tf_op jit(solution)/shard_map/layer_t0_r0/pallas_call | solution.py:165
  8.7 1.3 %collective-permute-start.4 = (bf16[32,4096]{1,0:T(8,128)(2,1)S(1)}, bf16[32,4096]{1,0:T(8,128)(2,1)S(1)}, u32[]{:S(2)}, u32[]{:S(2)}) collective-permute-start(bf16[32,4096]{1,0:T(8,128)(2,1)S(1)} %get-tuple-element.54.refs_6_), channel_id=1, source_target_pairs={{0,4},{1,5},{2,6},{3,7},{4,8},{5,9},{6,10},{7,11},{8,12},{9,13},{1... | collective-permute-start | bytes 786440 | tf_op jit(solution)/shard_map/ppermute | solution.py:216
  10.0 3.8 %collective-permute-start.5 = (bf16[32,512]{1,0:T(8,128)(2,1)S(1)}, bf16[32,512]{1,0:T(8,128)(2,1)S(1)}, u32[]{:S(2)}, u32[]{:S(2)}) collective-permute-start(bf16[32,512]{1,0:T(8,128)(2,1)S(1)} %get-tuple-element.57), channel_id=1, source_target_pairs={{0,7},{1,6},{2,5},{3,4},{4,11},{5,10},{6,9},{7,8},{8,15},{9,14},{1... | collective-permute-start | bytes 98312 | tf_op jit(solution)/shard_map/ppermute | solution.py:216
  13.8 1.5 %layer_t0_r32.1 = (bf16[8,64,4096]{2,1,0:T(8,128)(2,1)}, bf16[32,4096]{1,0:T(8,128)(2,1)S(1)}, bf16[32,512]{1,0:T(8,128)(2,1)S(1)}) custom-call(s32[258]{0:T(512)S(4)} %get-tuple-element.50.refs_0_.meta, bf16[64,4096]{1,0:T(8,128)(2,1)S(1)} %get-tuple-element.51.refs_1_, bf16[64,512]{1,0:T(8,128)(2,1)S(1)} %collective-permute-done.refs_2_, ...), custom_call_target="tpu_custom_call" | custom-call | flops 2415919104 | bytes 75497472 | tf_op jit(solution)/shard_map/layer_t0_r32/pallas_call | solution.py:165
  15.3 1.3 %collective-permute-start.2 = (bf16[32,4096]{1,0:T(8,128)(2,1)S(1)}, bf16[32,4096]{1,0:T(8,128)(2,1)S(1)}, u32[]{:S(2)}, u32[]{:S(2)}) collective-permute-start(bf16[32,4096]{1,0:T(8,128)(2,1)S(1)} %get-tuple-element.55.after.refs_6_), channel_id=1, source_target_pairs={{0,4},{1,5},{2,6},{3,7},{4,8},{5,9},{6,10},{7,11},{8,12},{9,13},{1... | collective-permute-start | bytes 786440 | tf_op jit(solution)/shard_map/ppermute | solution.py:216
  16.6 2.4 %collective-permute-done.4.main.refs_1_ = bf16[32,4096]{1,0:T(8,128)(2,1)S(1)} collective-permute-done((bf16[32,4096]{1,0:T(8,128)(2,1)S(1)}, bf16[32,4096]{1,0:T(8,128)(2,1)S(1)}, u32[]{:S(2)}, u32[]{:S(2)}) %collective-permute-start.4) | collective-permute-done | bytes 262176 | tf_op jit(solution)/shard_map/ppermute | solution.py:216
  19.1 1.2 %collective-permute-start.6 = (bf16[32,512]{1,0:T(8,128)(2,1)S(1)}, bf16[32,512]{1,0:T(8,128)(2,1)S(1)}, u32[]{:S(2)}, u32[]{:S(2)}) collective-permute-start(bf16[32,512]{1,0:T(8,128)(2,1)S(1)} %edge.14), channel_id=1, source_target_pairs={{0,1},{1,0},{2,3},{3,2},{4,5},{5,4},{6,7},{7,6},{8,9},{9,8},{10,11... | collective-permute-start | bytes 98312 | tf_op jit(solution)/shard_map/ppermute | solution.py:216
  20.3 1.3 %collective-permute-start.3 = (bf16[32,512]{1,0:T(8,128)(2,1)S(1)}, bf16[32,512]{1,0:T(8,128)(2,1)S(1)}, u32[]{:S(2)}, u32[]{:S(2)}) collective-permute-start(bf16[32,512]{1,0:T(8,128)(2,1)S(1)} %get-tuple-element.56), channel_id=1, source_target_pairs={{0,7},{1,6},{2,5},{3,4},{4,11},{5,10},{6,9},{7,8},{8,15},{9,14},{1... | collective-permute-start | bytes 98312 | tf_op jit(solution)/shard_map/ppermute | solution.py:216
  21.6 0.8 layer_t1_r0.1
  22.3 3.3 %collective-permute-start.10 = (bf16[32,4096]{1,0:T(8,128)(2,1)S(1)}, bf16[32,4096]{1,0:T(8,128)(2,1)S(1)}, u32[]{:S(2)}, u32[]{:S(2)}) collective-permute-start(bf16[32,4096]{1,0:T(8,128)(2,1)S(1)} %get-tuple-element.59.after.refs_6_), channel_id=1, source_target_pairs={{0,4},{1,5},{2,6},{3,7},{4,8},{5,9},{6,10},{7,11},{8,12},{9,13},{1... | collective-permute-start | bytes 786440 | tf_op jit(solution)/shard_map/ppermute | solution.py:216
  25.6 0.5 collective-permute-done.2.main.refs_1_
  26.1 0.7 collective-permute-start.7
  26.8 2.0 %collective-permute-start.11 = (bf16[32,512]{1,0:T(8,128)(2,1)S(1)}, bf16[32,512]{1,0:T(8,128)(2,1)S(1)}, u32[]{:S(2)}, u32[]{:S(2)}) collective-permute-start(bf16[32,512]{1,0:T(8,128)(2,1)S(1)} %get-tuple-element.63), channel_id=1, source_target_pairs={{0,7},{1,6},{2,5},{3,4},{4,11},{5,10},{6,9},{7,8},{8,15},{9,14},{1... | collective-permute-start | bytes 98312 | tf_op jit(solution)/shard_map/ppermute | solution.py:216
  28.8 0.8 layer_t1_r32.1
  29.6 3.4 %collective-permute-start.8 = (bf16[32,4096]{1,0:T(8,128)(2,1)S(1)}, bf16[32,4096]{1,0:T(8,128)(2,1)S(1)}, u32[]{:S(2)}, u32[]{:S(2)}) collective-permute-start(bf16[32,4096]{1,0:T(8,128)(2,1)S(1)} %get-tuple-element.61.after.refs_6_), channel_id=1, source_target_pairs={{0,4},{1,5},{2,6},{3,7},{4,8},{5,9},{6,10},{7,11},{8,12},{9,13},{1... | collective-permute-start | bytes 786440 | tf_op jit(solution)/shard_map/ppermute | solution.py:216
  33.0 0.9 collective-permute-start.12
  33.8 3.2 %collective-permute-start.9 = (bf16[32,512]{1,0:T(8,128)(2,1)S(1)}, bf16[32,512]{1,0:T(8,128)(2,1)S(1)}, u32[]{:S(2)}, u32[]{:S(2)}) collective-permute-start(bf16[32,512]{1,0:T(8,128)(2,1)S(1)} %get-tuple-element.62), channel_id=1, source_target_pairs={{0,7},{1,6},{2,5},{3,4},{4,11},{5,10},{6,9},{7,8},{8,15},{9,14},{1... | collective-permute-start | bytes 98312 | tf_op jit(solution)/shard_map/ppermute | solution.py:216
  37.0 0.8 layer_t2_r0.1
  37.8 2.2 %collective-permute-start.16 = (bf16[32,4096]{1,0:T(8,128)(2,1)S(1)}, bf16[32,4096]{1,0:T(8,128)(2,1)S(1)}, u32[]{:S(2)}, u32[]{:S(2)}) collective-permute-start(bf16[32,4096]{1,0:T(8,128)(2,1)S(1)} %get-tuple-element.65.after.refs_6_), channel_id=1, source_target_pairs={{0,4},{1,5},{2,6},{3,7},{4,8},{5,9},{6,10},{7,11},{8,12},{9,13},{1... | collective-permute-start | bytes 786440 | tf_op jit(solution)/shard_map/ppermute | solution.py:216
  39.9 1.1 collective-permute-start.13
  41.0 3.4 %collective-permute-start.17 = (bf16[32,512]{1,0:T(8,128)(2,1)S(1)}, bf16[32,512]{1,0:T(8,128)(2,1)S(1)}, u32[]{:S(2)}, u32[]{:S(2)}) collective-permute-start(bf16[32,512]{1,0:T(8,128)(2,1)S(1)} %get-tuple-element.69), channel_id=1, source_target_pairs={{0,7},{1,6},{2,5},{3,4},{4,11},{5,10},{6,9},{7,8},{8,15},{9,14},{1... | collective-permute-start | bytes 98312 | tf_op jit(solution)/shard_map/ppermute | solution.py:216
  44.5 0.8 layer_t2_r32.1
  45.2 2.4 %collective-permute-start.14 = (bf16[32,4096]{1,0:T(8,128)(2,1)S(1)}, bf16[32,4096]{1,0:T(8,128)(2,1)S(1)}, u32[]{:S(2)}, u32[]{:S(2)}) collective-permute-start(bf16[32,4096]{1,0:T(8,128)(2,1)S(1)} %get-tuple-element.67.after.refs_6_), channel_id=1, source_target_pairs={{0,4},{1,5},{2,6},{3,7},{4,8},{5,9},{6,10},{7,11},{8,12},{9,13},{1... | collective-permute-start | bytes 786440 | tf_op jit(solution)/shard_map/ppermute | solution.py:216
  47.9 1.4 %collective-permute-start.18 = (bf16[32,512]{1,0:T(8,128)(2,1)S(1)}, bf16[32,512]{1,0:T(8,128)(2,1)S(1)}, u32[]{:S(2)}, u32[]{:S(2)}) collective-permute-start(bf16[32,512]{1,0:T(8,128)(2,1)S(1)} %edge.18), channel_id=1, source_target_pairs={{0,1},{1,0},{2,3},{3,2},{4,5},{5,4},{6,7},{7,6},{8,9},{9,8},{10,11... | collective-permute-start | bytes 98312 | tf_op jit(solution)/shard_map/ppermute | solution.py:216
  49.2 2.6 %collective-permute-start.15 = (bf16[32,512]{1,0:T(8,128)(2,1)S(1)}, bf16[32,512]{1,0:T(8,128)(2,1)S(1)}, u32[]{:S(2)}, u32[]{:S(2)}) collective-permute-start(bf16[32,512]{1,0:T(8,128)(2,1)S(1)} %get-tuple-element.68), channel_id=1, source_target_pairs={{0,7},{1,6},{2,5},{3,4},{4,11},{5,10},{6,9},{7,8},{8,15},{9,14},{1... | collective-permute-start | bytes 98312 | tf_op jit(solution)/shard_map/ppermute | solution.py:216
  51.9 0.8 layer_t3_r0.1
  52.7 2.4 %collective-permute-start.22 = (bf16[32,4096]{1,0:T(8,128)(2,1)S(1)}, bf16[32,4096]{1,0:T(8,128)(2,1)S(1)}, u32[]{:S(2)}, u32[]{:S(2)}) collective-permute-start(bf16[32,4096]{1,0:T(8,128)(2,1)S(1)} %get-tuple-element.71.after.refs_6_), channel_id=1, source_target_pairs={{0,4},{1,5},{2,6},{3,7},{4,8},{5,9},{6,10},{7,11},{8,12},{9,13},{1... | collective-permute-start | bytes 786440 | tf_op jit(solution)/shard_map/ppermute | solution.py:216
  55.4 1.3 %collective-permute-start.19 = (bf16[32,512]{1,0:T(8,128)(2,1)S(1)}, bf16[32,512]{1,0:T(8,128)(2,1)S(1)}, u32[]{:S(2)}, u32[]{:S(2)}) collective-permute-start(bf16[32,512]{1,0:T(8,128)(2,1)S(1)} %edge.19), channel_id=1, source_target_pairs={{0,1},{1,0},{2,3},{3,2},{4,5},{5,4},{6,7},{7,6},{8,9},{9,8},{10,11... | collective-permute-start | bytes 98312 | tf_op jit(solution)/shard_map/ppermute | solution.py:216
  56.7 2.0 %collective-permute-start.23 = (bf16[32,512]{1,0:T(8,128)(2,1)S(1)}, bf16[32,512]{1,0:T(8,128)(2,1)S(1)}, u32[]{:S(2)}, u32[]{:S(2)}) collective-permute-start(bf16[32,512]{1,0:T(8,128)(2,1)S(1)} %get-tuple-element.75), channel_id=1, source_target_pairs={{0,7},{1,6},{2,5},{3,4},{4,11},{5,10},{6,9},{7,8},{8,15},{9,14},{1... | collective-permute-start | bytes 98312 | tf_op jit(solution)/shard_map/ppermute | solution.py:216
  58.7 0.8 layer_t3_r32.1
  59.5 4.2 %collective-permute-start.20 = (bf16[32,4096]{1,0:T(8,128)(2,1)S(1)}, bf16[32,4096]{1,0:T(8,128)(2,1)S(1)}, u32[]{:S(2)}, u32[]{:S(2)}) collective-permute-start(bf16[32,4096]{1,0:T(8,128)(2,1)S(1)} %get-tuple-element.73.after.refs_6_), channel_id=1, source_target_pairs={{0,4},{1,5},{2,6},{3,7},{4,8},{5,9},{6,10},{7,11},{8,12},{9,13},{1... | collective-permute-start | bytes 786440 | tf_op jit(solution)/shard_map/ppermute | solution.py:216
  63.7 0.4 collective-permute-start.24
  64.1 2.6 %collective-permute-start.21 = (bf16[32,512]{1,0:T(8,128)(2,1)S(1)}, bf16[32,512]{1,0:T(8,128)(2,1)S(1)}, u32[]{:S(2)}, u32[]{:S(2)}) collective-permute-start(bf16[32,512]{1,0:T(8,128)(2,1)S(1)} %get-tuple-element.74), channel_id=1, source_target_pairs={{0,7},{1,6},{2,5},{3,4},{4,11},{5,10},{6,9},{7,8},{8,15},{9,14},{1... | collective-permute-start | bytes 98312 | tf_op jit(solution)/shard_map/ppermute | solution.py:216
  66.8 0.8 layer_t4_r0.1
  67.5 3.9 %collective-permute-start.28 = (bf16[32,4096]{1,0:T(8,128)(2,1)S(1)}, bf16[32,4096]{1,0:T(8,128)(2,1)S(1)}, u32[]{:S(2)}, u32[]{:S(2)}) collective-permute-start(bf16[32,4096]{1,0:T(8,128)(2,1)S(1)} %get-tuple-element.77.after.refs_6_), channel_id=1, source_target_pairs={{0,4},{1,5},{2,6},{3,7},{4,8},{5,9},{6,10},{7,11},{8,12},{9,13},{1... | collective-permute-start | bytes 786440 | tf_op jit(solution)/shard_map/ppermute | solution.py:216
  71.5 0.6 collective-permute-start.25
  72.1 2.8 %collective-permute-start.29 = (bf16[32,512]{1,0:T(8,128)(2,1)S(1)}, bf16[32,512]{1,0:T(8,128)(2,1)S(1)}, u32[]{:S(2)}, u32[]{:S(2)}) collective-permute-start(bf16[32,512]{1,0:T(8,128)(2,1)S(1)} %get-tuple-element.81), channel_id=1, source_target_pairs={{0,7},{1,6},{2,5},{3,4},{4,11},{5,10},{6,9},{7,8},{8,15},{9,14},{1... | collective-permute-start | bytes 98312 | tf_op jit(solution)/shard_map/ppermute | solution.py:216
  74.9 0.8 layer_t4_r32.1
  75.7 3.4 %collective-permute-start.26 = (bf16[32,4096]{1,0:T(8,128)(2,1)S(1)}, bf16[32,4096]{1,0:T(8,128)(2,1)S(1)}, u32[]{:S(2)}, u32[]{:S(2)}) collective-permute-start(bf16[32,4096]{1,0:T(8,128)(2,1)S(1)} %get-tuple-element.79.after.refs_6_), channel_id=1, source_target_pairs={{0,4},{1,5},{2,6},{3,7},{4,8},{5,9},{6,10},{7,11},{8,12},{9,13},{1... | collective-permute-start | bytes 786440 | tf_op jit(solution)/shard_map/ppermute | solution.py:216
  79.4 3.3 %collective-permute-start.27 = (bf16[32,512]{1,0:T(8,128)(2,1)S(1)}, bf16[32,512]{1,0:T(8,128)(2,1)S(1)}, u32[]{:S(2)}, u32[]{:S(2)}) collective-permute-start(bf16[32,512]{1,0:T(8,128)(2,1)S(1)} %get-tuple-element.80), channel_id=1, source_target_pairs={{0,7},{1,6},{2,5},{3,4},{4,11},{5,10},{6,9},{7,8},{8,15},{9,14},{1... | collective-permute-start | bytes 98312 | tf_op jit(solution)/shard_map/ppermute | solution.py:216
  82.7 0.8 layer_t5_r0.1
  83.4 2.9 %collective-permute-start.34 = (bf16[32,4096]{1,0:T(8,128)(2,1)S(1)}, bf16[32,4096]{1,0:T(8,128)(2,1)S(1)}, u32[]{:S(2)}, u32[]{:S(2)}) collective-permute-start(bf16[32,4096]{1,0:T(8,128)(2,1)S(1)} %get-tuple-element.83.after.refs_6_), channel_id=1, source_target_pairs={{0,4},{1,5},{2,6},{3,7},{4,8},{5,9},{6,10},{7,11},{8,12},{9,13},{1... | collective-permute-start | bytes 786440 | tf_op jit(solution)/shard_map/ppermute | solution.py:216
  86.3 0.8 collective-permute-start.31
  87.1 2.9 %collective-permute-start.35 = (bf16[32,512]{1,0:T(8,128)(2,1)S(1)}, bf16[32,512]{1,0:T(8,128)(2,1)S(1)}, u32[]{:S(2)}, u32[]{:S(2)}) collective-permute-start(bf16[32,512]{1,0:T(8,128)(2,1)S(1)} %get-tuple-element.87), channel_id=1, source_target_pairs={{0,7},{1,6},{2,5},{3,4},{4,11},{5,10},{6,9},{7,8},{8,15},{9,14},{1... | collective-permute-start | bytes 98312 | tf_op jit(solution)/shard_map/ppermute | solution.py:216
  90.0 0.8 layer_t5_r32.1
  90.8 3.6 %collective-permute-start.32 = (bf16[32,4096]{1,0:T(8,128)(2,1)S(1)}, bf16[32,4096]{1,0:T(8,128)(2,1)S(1)}, u32[]{:S(2)}, u32[]{:S(2)}) collective-permute-start(bf16[32,4096]{1,0:T(8,128)(2,1)S(1)} %get-tuple-element.85.after.refs_6_), channel_id=1, source_target_pairs={{0,4},{1,5},{2,6},{3,7},{4,8},{5,9},{6,10},{7,11},{8,12},{9,13},{1... | collective-permute-start | bytes 786440 | tf_op jit(solution)/shard_map/ppermute | solution.py:216
  94.4 0.5 collective-permute-start.36
  94.9 2.5 %collective-permute-start.33 = (bf16[32,512]{1,0:T(8,128)(2,1)S(1)}, bf16[32,512]{1,0:T(8,128)(2,1)S(1)}, u32[]{:S(2)}, u32[]{:S(2)}) collective-permute-start(bf16[32,512]{1,0:T(8,128)(2,1)S(1)} %get-tuple-element.86), channel_id=1, source_target_pairs={{0,7},{1,6},{2,5},{3,4},{4,11},{5,10},{6,9},{7,8},{8,15},{9,14},{1... | collective-permute-start | bytes 98312 | tf_op jit(solution)/shard_map/ppermute | solution.py:216
  97.4 0.8 layer_t6_r0.1
  98.4 2.5 %collective-permute-done.32.main.refs_1_ = bf16[32,4096]{1,0:T(8,128)(2,1)S(1)} collective-permute-done((bf16[32,4096]{1,0:T(8,128)(2,1)S(1)}, bf16[32,4096]{1,0:T(8,128)(2,1)S(1)}, u32[]{:S(2)}, u32[]{:S(2)}) %collective-permute-start.32) | collective-permute-done | bytes 262176 | tf_op jit(solution)/shard_map/ppermute | solution.py:216
  100.9 1.4 %collective-permute-start.37 = (bf16[32,512]{1,0:T(8,128)(2,1)S(1)}, bf16[32,512]{1,0:T(8,128)(2,1)S(1)}, u32[]{:S(2)}, u32[]{:S(2)}) collective-permute-start(bf16[32,512]{1,0:T(8,128)(2,1)S(1)} %edge.25), channel_id=1, source_target_pairs={{0,1},{1,0},{2,3},{3,2},{4,5},{5,4},{6,7},{7,6},{8,9},{9,8},{10,11... | collective-permute-start | bytes 98312 | tf_op jit(solution)/shard_map/ppermute | solution.py:216
  102.2 1.6 %collective-permute-start.41 = (bf16[32,4096]{1,0:T(8,128)(2,1)S(1)}, bf16[32,4096]{1,0:T(8,128)(2,1)S(1)}, u32[]{:S(2)}, u32[]{:S(2)}) collective-permute-start(bf16[32,4096]{1,0:T(8,128)(2,1)S(1)} %get-tuple-element.89.after.refs_6_), channel_id=1, source_target_pairs={{0,4},{1,5},{2,6},{3,7},{4,8},{5,9},{6,10},{7,11},{8,12},{9,13},{1... | collective-permute-start | bytes 786440 | tf_op jit(solution)/shard_map/ppermute | solution.py:216
  103.8 0.7 layer_t6_r32.1
  104.6 1.1 collective-permute-start.38
  105.6 5.1 %collective-permute-start.42 = (bf16[32,512]{1,0:T(8,128)(2,1)S(1)}, bf16[32,512]{1,0:T(8,128)(2,1)S(1)}, u32[]{:S(2)}, u32[]{:S(2)}) collective-permute-start(bf16[32,512]{1,0:T(8,128)(2,1)S(1)} %get-tuple-element.93), channel_id=1, source_target_pairs={{0,7},{1,6},{2,5},{3,4},{4,11},{5,10},{6,9},{7,8},{8,15},{9,14},{1... | collective-permute-start | bytes 98312 | tf_op jit(solution)/shard_map/ppermute | solution.py:216
  110.8 3.9 %collective-permute-start.39 = (bf16[32,512]{1,0:T(8,128)(2,1)S(1)}, bf16[32,512]{1,0:T(8,128)(2,1)S(1)}, u32[]{:S(2)}, u32[]{:S(2)}) collective-permute-start(bf16[32,512]{1,0:T(8,128)(2,1)S(1)} %get-tuple-element.92), channel_id=1, source_target_pairs={{0,7},{1,6},{2,5},{3,4},{4,11},{5,10},{6,9},{7,8},{8,15},{9,14},{1... | collective-permute-start | bytes 98312 | tf_op jit(solution)/shard_map/ppermute | solution.py:216
  114.7 0.9 collective-permute-start.43
  115.7 2.8 %collective-permute-done.38.main.refs_1_ = bf16[32,4096]{1,0:T(8,128)(2,1)S(1)} collective-permute-done((bf16[32,4096]{1,0:T(8,128)(2,1)S(1)}, bf16[32,4096]{1,0:T(8,128)(2,1)S(1)}, u32[]{:S(2)}, u32[]{:S(2)}) %collective-permute-start.38) | collective-permute-done | bytes 262176 | tf_op jit(solution)/shard_map/ppermute | solution.py:216
  118.5 0.8 collective-permute-start.40
  119.3 0.8 layer_t7_r0.1.refs_6_
  120.2 0.8 layer_t7_r32.1
  (56 shorter events, 1.4 us)
Async XLA Ops:
  0.9 6.3 %collective-permute-start = (bf16[64,512]{1,0:T(8,128)(2,1)S(1)}, bf16[64,512]{1,0:T(8,128)(2,1)S(1)}, u32[]{:S(2)}, u32[]{:S(2)}) collective-permute-start(bf16[64,512]{1,0:T(8,128)(2,1)S(1)} %get-tuple-element.96), channel_id=1, source_target_pairs={{0,3},{1,2},{2,1},{3,0},{4,7},{5,6},{6,5},{7,4},{8,11},{9,10},{10,... | collective-permute-start | bytes 196616 | tf_op jit(solution)/shard_map/ppermute | solution.py:216
  3.6 3.6 %collective-permute-start.1 = (bf16[64,512]{1,0:T(8,128)(2,1)S(1)}, bf16[64,512]{1,0:T(8,128)(2,1)S(1)}, u32[]{:S(2)}, u32[]{:S(2)}) collective-permute-start(bf16[64,512]{1,0:T(8,128)(2,1)S(1)} %get-tuple-element.95), channel_id=1, source_target_pairs={{0,1},{1,0},{2,3},{3,2},{4,5},{5,4},{6,7},{7,6},{8,9},{9,8},{10,11... | collective-permute-start | bytes 196616 | tf_op jit(solution)/shard_map/ppermute | solution.py:216
  8.7 10.4 %collective-permute-start.4 = (bf16[32,4096]{1,0:T(8,128)(2,1)S(1)}, bf16[32,4096]{1,0:T(8,128)(2,1)S(1)}, u32[]{:S(2)}, u32[]{:S(2)}) collective-permute-start(bf16[32,4096]{1,0:T(8,128)(2,1)S(1)} %get-tuple-element.54.refs_6_), channel_id=1, source_target_pairs={{0,4},{1,5},{2,6},{3,7},{4,8},{5,9},{6,10},{7,11},{8,12},{9,13},{1... | collective-permute-start | bytes 786440 | tf_op jit(solution)/shard_map/ppermute | solution.py:216
  10.0 6.6 %collective-permute-start.5 = (bf16[32,512]{1,0:T(8,128)(2,1)S(1)}, bf16[32,512]{1,0:T(8,128)(2,1)S(1)}, u32[]{:S(2)}, u32[]{:S(2)}) collective-permute-start(bf16[32,512]{1,0:T(8,128)(2,1)S(1)} %get-tuple-element.57), channel_id=1, source_target_pairs={{0,7},{1,6},{2,5},{3,4},{4,11},{5,10},{6,9},{7,8},{8,15},{9,14},{1... | collective-permute-start | bytes 98312 | tf_op jit(solution)/shard_map/ppermute | solution.py:216
  15.3 10.8 %collective-permute-start.2 = (bf16[32,4096]{1,0:T(8,128)(2,1)S(1)}, bf16[32,4096]{1,0:T(8,128)(2,1)S(1)}, u32[]{:S(2)}, u32[]{:S(2)}) collective-permute-start(bf16[32,4096]{1,0:T(8,128)(2,1)S(1)} %get-tuple-element.55.after.refs_6_), channel_id=1, source_target_pairs={{0,4},{1,5},{2,6},{3,7},{4,8},{5,9},{6,10},{7,11},{8,12},{9,13},{1... | collective-permute-start | bytes 786440 | tf_op jit(solution)/shard_map/ppermute | solution.py:216
  19.1 2.5 %collective-permute-start.6 = (bf16[32,512]{1,0:T(8,128)(2,1)S(1)}, bf16[32,512]{1,0:T(8,128)(2,1)S(1)}, u32[]{:S(2)}, u32[]{:S(2)}) collective-permute-start(bf16[32,512]{1,0:T(8,128)(2,1)S(1)} %edge.14), channel_id=1, source_target_pairs={{0,1},{1,0},{2,3},{3,2},{4,5},{5,4},{6,7},{7,6},{8,9},{9,8},{10,11... | collective-permute-start | bytes 98312 | tf_op jit(solution)/shard_map/ppermute | solution.py:216
  20.3 5.3 %collective-permute-start.3 = (bf16[32,512]{1,0:T(8,128)(2,1)S(1)}, bf16[32,512]{1,0:T(8,128)(2,1)S(1)}, u32[]{:S(2)}, u32[]{:S(2)}) collective-permute-start(bf16[32,512]{1,0:T(8,128)(2,1)S(1)} %get-tuple-element.56), channel_id=1, source_target_pairs={{0,7},{1,6},{2,5},{3,4},{4,11},{5,10},{6,9},{7,8},{8,15},{9,14},{1... | collective-permute-start | bytes 98312 | tf_op jit(solution)/shard_map/ppermute | solution.py:216
  22.3 10.6 %collective-permute-start.10 = (bf16[32,4096]{1,0:T(8,128)(2,1)S(1)}, bf16[32,4096]{1,0:T(8,128)(2,1)S(1)}, u32[]{:S(2)}, u32[]{:S(2)}) collective-permute-start(bf16[32,4096]{1,0:T(8,128)(2,1)S(1)} %get-tuple-element.59.after.refs_6_), channel_id=1, source_target_pairs={{0,4},{1,5},{2,6},{3,7},{4,8},{5,9},{6,10},{7,11},{8,12},{9,13},{1... | collective-permute-start | bytes 786440 | tf_op jit(solution)/shard_map/ppermute | solution.py:216
  26.1 2.7 %collective-permute-start.7 = (bf16[32,512]{1,0:T(8,128)(2,1)S(1)}, bf16[32,512]{1,0:T(8,128)(2,1)S(1)}, u32[]{:S(2)}, u32[]{:S(2)}) collective-permute-start(bf16[32,512]{1,0:T(8,128)(2,1)S(1)} %edge.15), channel_id=1, source_target_pairs={{0,1},{1,0},{2,3},{3,2},{4,5},{5,4},{6,7},{7,6},{8,9},{9,8},{10,11... | collective-permute-start | bytes 98312 | tf_op jit(solution)/shard_map/ppermute | solution.py:216
  26.8 6.1 %collective-permute-start.11 = (bf16[32,512]{1,0:T(8,128)(2,1)S(1)}, bf16[32,512]{1,0:T(8,128)(2,1)S(1)}, u32[]{:S(2)}, u32[]{:S(2)}) collective-permute-start(bf16[32,512]{1,0:T(8,128)(2,1)S(1)} %get-tuple-element.63), channel_id=1, source_target_pairs={{0,7},{1,6},{2,5},{3,4},{4,11},{5,10},{6,9},{7,8},{8,15},{9,14},{1... | collective-permute-start | bytes 98312 | tf_op jit(solution)/shard_map/ppermute | solution.py:216
  29.6 10.3 %collective-permute-start.8 = (bf16[32,4096]{1,0:T(8,128)(2,1)S(1)}, bf16[32,4096]{1,0:T(8,128)(2,1)S(1)}, u32[]{:S(2)}, u32[]{:S(2)}) collective-permute-start(bf16[32,4096]{1,0:T(8,128)(2,1)S(1)} %get-tuple-element.61.after.refs_6_), channel_id=1, source_target_pairs={{0,4},{1,5},{2,6},{3,7},{4,8},{5,9},{6,10},{7,11},{8,12},{9,13},{1... | collective-permute-start | bytes 786440 | tf_op jit(solution)/shard_map/ppermute | solution.py:216
  33.0 4.0 %collective-permute-start.12 = (bf16[32,512]{1,0:T(8,128)(2,1)S(1)}, bf16[32,512]{1,0:T(8,128)(2,1)S(1)}, u32[]{:S(2)}, u32[]{:S(2)}) collective-permute-start(bf16[32,512]{1,0:T(8,128)(2,1)S(1)} %edge.16), channel_id=1, source_target_pairs={{0,1},{1,0},{2,3},{3,2},{4,5},{5,4},{6,7},{7,6},{8,9},{9,8},{10,11... | collective-permute-start | bytes 98312 | tf_op jit(solution)/shard_map/ppermute | solution.py:216
  33.8 6.1 %collective-permute-start.9 = (bf16[32,512]{1,0:T(8,128)(2,1)S(1)}, bf16[32,512]{1,0:T(8,128)(2,1)S(1)}, u32[]{:S(2)}, u32[]{:S(2)}) collective-permute-start(bf16[32,512]{1,0:T(8,128)(2,1)S(1)} %get-tuple-element.62), channel_id=1, source_target_pairs={{0,7},{1,6},{2,5},{3,4},{4,11},{5,10},{6,9},{7,8},{8,15},{9,14},{1... | collective-permute-start | bytes 98312 | tf_op jit(solution)/shard_map/ppermute | solution.py:216
  37.8 10.1 %collective-permute-start.16 = (bf16[32,4096]{1,0:T(8,128)(2,1)S(1)}, bf16[32,4096]{1,0:T(8,128)(2,1)S(1)}, u32[]{:S(2)}, u32[]{:S(2)}) collective-permute-start(bf16[32,4096]{1,0:T(8,128)(2,1)S(1)} %get-tuple-element.65.after.refs_6_), channel_id=1, source_target_pairs={{0,4},{1,5},{2,6},{3,7},{4,8},{5,9},{6,10},{7,11},{8,12},{9,13},{1... | collective-permute-start | bytes 786440 | tf_op jit(solution)/shard_map/ppermute | solution.py:216
  39.9 4.5 %collective-permute-start.13 = (bf16[32,512]{1,0:T(8,128)(2,1)S(1)}, bf16[32,512]{1,0:T(8,128)(2,1)S(1)}, u32[]{:S(2)}, u32[]{:S(2)}) collective-permute-start(bf16[32,512]{1,0:T(8,128)(2,1)S(1)} %edge.17), channel_id=1, source_target_pairs={{0,1},{1,0},{2,3},{3,2},{4,5},{5,4},{6,7},{7,6},{8,9},{9,8},{10,11... | collective-permute-start | bytes 98312 | tf_op jit(solution)/shard_map/ppermute | solution.py:216
  41.0 6.5 %collective-permute-start.17 = (bf16[32,512]{1,0:T(8,128)(2,1)S(1)}, bf16[32,512]{1,0:T(8,128)(2,1)S(1)}, u32[]{:S(2)}, u32[]{:S(2)}) collective-permute-start(bf16[32,512]{1,0:T(8,128)(2,1)S(1)} %get-tuple-element.69), channel_id=1, source_target_pairs={{0,7},{1,6},{2,5},{3,4},{4,11},{5,10},{6,9},{7,8},{8,15},{9,14},{1... | collective-permute-start | bytes 98312 | tf_op jit(solution)/shard_map/ppermute | solution.py:216
  45.2 10.1 %collective-permute-start.14 = (bf16[32,4096]{1,0:T(8,128)(2,1)S(1)}, bf16[32,4096]{1,0:T(8,128)(2,1)S(1)}, u32[]{:S(2)}, u32[]{:S(2)}) collective-permute-start(bf16[32,4096]{1,0:T(8,128)(2,1)S(1)} %get-tuple-element.67.after.refs_6_), channel_id=1, source_target_pairs={{0,4},{1,5},{2,6},{3,7},{4,8},{5,9},{6,10},{7,11},{8,12},{9,13},{1... | collective-permute-start | bytes 786440 | tf_op jit(solution)/shard_map/ppermute | solution.py:216
  47.9 4.0 %collective-permute-start.18 = (bf16[32,512]{1,0:T(8,128)(2,1)S(1)}, bf16[32,512]{1,0:T(8,128)(2,1)S(1)}, u32[]{:S(2)}, u32[]{:S(2)}) collective-permute-start(bf16[32,512]{1,0:T(8,128)(2,1)S(1)} %edge.18), channel_id=1, source_target_pairs={{0,1},{1,0},{2,3},{3,2},{4,5},{5,4},{6,7},{7,6},{8,9},{9,8},{10,11... | collective-permute-start | bytes 98312 | tf_op jit(solution)/shard_map/ppermute | solution.py:216
  49.2 5.9 %collective-permute-start.15 = (bf16[32,512]{1,0:T(8,128)(2,1)S(1)}, bf16[32,512]{1,0:T(8,128)(2,1)S(1)}, u32[]{:S(2)}, u32[]{:S(2)}) collective-permute-start(bf16[32,512]{1,0:T(8,128)(2,1)S(1)} %get-tuple-element.68), channel_id=1, source_target_pairs={{0,7},{1,6},{2,5},{3,4},{4,11},{5,10},{6,9},{7,8},{8,15},{9,14},{1... | collective-permute-start | bytes 98312 | tf_op jit(solution)/shard_map/ppermute | solution.py:216
  52.7 11.0 %collective-permute-start.22 = (bf16[32,4096]{1,0:T(8,128)(2,1)S(1)}, bf16[32,4096]{1,0:T(8,128)(2,1)S(1)}, u32[]{:S(2)}, u32[]{:S(2)}) collective-permute-start(bf16[32,4096]{1,0:T(8,128)(2,1)S(1)} %get-tuple-element.71.after.refs_6_), channel_id=1, source_target_pairs={{0,4},{1,5},{2,6},{3,7},{4,8},{5,9},{6,10},{7,11},{8,12},{9,13},{1... | collective-permute-start | bytes 786440 | tf_op jit(solution)/shard_map/ppermute | solution.py:216
  55.4 3.3 %collective-permute-start.19 = (bf16[32,512]{1,0:T(8,128)(2,1)S(1)}, bf16[32,512]{1,0:T(8,128)(2,1)S(1)}, u32[]{:S(2)}, u32[]{:S(2)}) collective-permute-start(bf16[32,512]{1,0:T(8,128)(2,1)S(1)} %edge.19), channel_id=1, source_target_pairs={{0,1},{1,0},{2,3},{3,2},{4,5},{5,4},{6,7},{7,6},{8,9},{9,8},{10,11... | collective-permute-start | bytes 98312 | tf_op jit(solution)/shard_map/ppermute | solution.py:216
  56.7 7.0 %collective-permute-start.23 = (bf16[32,512]{1,0:T(8,128)(2,1)S(1)}, bf16[32,512]{1,0:T(8,128)(2,1)S(1)}, u32[]{:S(2)}, u32[]{:S(2)}) collective-permute-start(bf16[32,512]{1,0:T(8,128)(2,1)S(1)} %get-tuple-element.75), channel_id=1, source_target_pairs={{0,7},{1,6},{2,5},{3,4},{4,11},{5,10},{6,9},{7,8},{8,15},{9,14},{1... | collective-permute-start | bytes 98312 | tf_op jit(solution)/shard_map/ppermute | solution.py:216
  59.5 12.0 %collective-permute-start.20 = (bf16[32,4096]{1,0:T(8,128)(2,1)S(1)}, bf16[32,4096]{1,0:T(8,128)(2,1)S(1)}, u32[]{:S(2)}, u32[]{:S(2)}) collective-permute-start(bf16[32,4096]{1,0:T(8,128)(2,1)S(1)} %get-tuple-element.73.after.refs_6_), channel_id=1, source_target_pairs={{0,4},{1,5},{2,6},{3,7},{4,8},{5,9},{6,10},{7,11},{8,12},{9,13},{1... | collective-permute-start | bytes 786440 | tf_op jit(solution)/shard_map/ppermute | solution.py:216
  63.7 3.0 %collective-permute-start.24 = (bf16[32,512]{1,0:T(8,128)(2,1)S(1)}, bf16[32,512]{1,0:T(8,128)(2,1)S(1)}, u32[]{:S(2)}, u32[]{:S(2)}) collective-permute-start(bf16[32,512]{1,0:T(8,128)(2,1)S(1)} %edge.20), channel_id=1, source_target_pairs={{0,1},{1,0},{2,3},{3,2},{4,5},{5,4},{6,7},{7,6},{8,9},{9,8},{10,11... | collective-permute-start | bytes 98312 | tf_op jit(solution)/shard_map/ppermute | solution.py:216
  64.1 7.3 %collective-permute-start.21 = (bf16[32,512]{1,0:T(8,128)(2,1)S(1)}, bf16[32,512]{1,0:T(8,128)(2,1)S(1)}, u32[]{:S(2)}, u32[]{:S(2)}) collective-permute-start(bf16[32,512]{1,0:T(8,128)(2,1)S(1)} %get-tuple-element.74), channel_id=1, source_target_pairs={{0,7},{1,6},{2,5},{3,4},{4,11},{5,10},{6,9},{7,8},{8,15},{9,14},{1... | collective-permute-start | bytes 98312 | tf_op jit(solution)/shard_map/ppermute | solution.py:216
  67.5 11.5 %collective-permute-start.28 = (bf16[32,4096]{1,0:T(8,128)(2,1)S(1)}, bf16[32,4096]{1,0:T(8,128)(2,1)S(1)}, u32[]{:S(2)}, u32[]{:S(2)}) collective-permute-start(bf16[32,4096]{1,0:T(8,128)(2,1)S(1)} %get-tuple-element.77.after.refs_6_), channel_id=1, source_target_pairs={{0,4},{1,5},{2,6},{3,7},{4,8},{5,9},{6,10},{7,11},{8,12},{9,13},{1... | collective-permute-start | bytes 786440 | tf_op jit(solution)/shard_map/ppermute | solution.py:216
  71.5 3.4 %collective-permute-start.25 = (bf16[32,512]{1,0:T(8,128)(2,1)S(1)}, bf16[32,512]{1,0:T(8,128)(2,1)S(1)}, u32[]{:S(2)}, u32[]{:S(2)}) collective-permute-start(bf16[32,512]{1,0:T(8,128)(2,1)S(1)} %edge.21), channel_id=1, source_target_pairs={{0,1},{1,0},{2,3},{3,2},{4,5},{5,4},{6,7},{7,6},{8,9},{9,8},{10,11... | collective-permute-start | bytes 98312 | tf_op jit(solution)/shard_map/ppermute | solution.py:216
  72.1 6.9 %collective-permute-start.29 = (bf16[32,512]{1,0:T(8,128)(2,1)S(1)}, bf16[32,512]{1,0:T(8,128)(2,1)S(1)}, u32[]{:S(2)}, u32[]{:S(2)}) collective-permute-start(bf16[32,512]{1,0:T(8,128)(2,1)S(1)} %get-tuple-element.81), channel_id=1, source_target_pairs={{0,7},{1,6},{2,5},{3,4},{4,11},{5,10},{6,9},{7,8},{8,15},{9,14},{1... | collective-permute-start | bytes 98312 | tf_op jit(solution)/shard_map/ppermute | solution.py:216
  75.7 10.7 %collective-permute-start.26 = (bf16[32,4096]{1,0:T(8,128)(2,1)S(1)}, bf16[32,4096]{1,0:T(8,128)(2,1)S(1)}, u32[]{:S(2)}, u32[]{:S(2)}) collective-permute-start(bf16[32,4096]{1,0:T(8,128)(2,1)S(1)} %get-tuple-element.79.after.refs_6_), channel_id=1, source_target_pairs={{0,4},{1,5},{2,6},{3,7},{4,8},{5,9},{6,10},{7,11},{8,12},{9,13},{1... | collective-permute-start | bytes 786440 | tf_op jit(solution)/shard_map/ppermute | solution.py:216
  79.0 3.7 %collective-permute-start.30 = (bf16[32,512]{1,0:T(8,128)(2,1)S(1)}, bf16[32,512]{1,0:T(8,128)(2,1)S(1)}, u32[]{:S(2)}, u32[]{:S(2)}) collective-permute-start(bf16[32,512]{1,0:T(8,128)(2,1)S(1)} %edge.22), channel_id=1, source_target_pairs={{0,1},{1,0},{2,3},{3,2},{4,5},{5,4},{6,7},{7,6},{8,9},{9,8},{10,11... | collective-permute-start | bytes 98312 | tf_op jit(solution)/shard_map/ppermute | solution.py:216
  79.4 6.9 %collective-permute-start.27 = (bf16[32,512]{1,0:T(8,128)(2,1)S(1)}, bf16[32,512]{1,0:T(8,128)(2,1)S(1)}, u32[]{:S(2)}, u32[]{:S(2)}) collective-permute-start(bf16[32,512]{1,0:T(8,128)(2,1)S(1)} %get-tuple-element.80), channel_id=1, source_target_pairs={{0,7},{1,6},{2,5},{3,4},{4,11},{5,10},{6,9},{7,8},{8,15},{9,14},{1... | collective-permute-start | bytes 98312 | tf_op jit(solution)/shard_map/ppermute | solution.py:216
  83.4 10.9 %collective-permute-start.34 = (bf16[32,4096]{1,0:T(8,128)(2,1)S(1)}, bf16[32,4096]{1,0:T(8,128)(2,1)S(1)}, u32[]{:S(2)}, u32[]{:S(2)}) collective-permute-start(bf16[32,4096]{1,0:T(8,128)(2,1)S(1)} %get-tuple-element.83.after.refs_6_), channel_id=1, source_target_pairs={{0,4},{1,5},{2,6},{3,7},{4,8},{5,9},{6,10},{7,11},{8,12},{9,13},{1... | collective-permute-start | bytes 786440 | tf_op jit(solution)/shard_map/ppermute | solution.py:216
  86.3 3.7 %collective-permute-start.31 = (bf16[32,512]{1,0:T(8,128)(2,1)S(1)}, bf16[32,512]{1,0:T(8,128)(2,1)S(1)}, u32[]{:S(2)}, u32[]{:S(2)}) collective-permute-start(bf16[32,512]{1,0:T(8,128)(2,1)S(1)} %edge.23), channel_id=1, source_target_pairs={{0,1},{1,0},{2,3},{3,2},{4,5},{5,4},{6,7},{7,6},{8,9},{9,8},{10,11... | collective-permute-start | bytes 98312 | tf_op jit(solution)/shard_map/ppermute | solution.py:216
  87.1 7.3 %collective-permute-start.35 = (bf16[32,512]{1,0:T(8,128)(2,1)S(1)}, bf16[32,512]{1,0:T(8,128)(2,1)S(1)}, u32[]{:S(2)}, u32[]{:S(2)}) collective-permute-start(bf16[32,512]{1,0:T(8,128)(2,1)S(1)} %get-tuple-element.87), channel_id=1, source_target_pairs={{0,7},{1,6},{2,5},{3,4},{4,11},{5,10},{6,9},{7,8},{8,15},{9,14},{1... | collective-permute-start | bytes 98312 | tf_op jit(solution)/shard_map/ppermute | solution.py:216
  90.8 10.1 %collective-permute-start.32 = (bf16[32,4096]{1,0:T(8,128)(2,1)S(1)}, bf16[32,4096]{1,0:T(8,128)(2,1)S(1)}, u32[]{:S(2)}, u32[]{:S(2)}) collective-permute-start(bf16[32,4096]{1,0:T(8,128)(2,1)S(1)} %get-tuple-element.85.after.refs_6_), channel_id=1, source_target_pairs={{0,4},{1,5},{2,6},{3,7},{4,8},{5,9},{6,10},{7,11},{8,12},{9,13},{1... | collective-permute-start | bytes 786440 | tf_op jit(solution)/shard_map/ppermute | solution.py:216
  94.4 3.0 %collective-permute-start.36 = (bf16[32,512]{1,0:T(8,128)(2,1)S(1)}, bf16[32,512]{1,0:T(8,128)(2,1)S(1)}, u32[]{:S(2)}, u32[]{:S(2)}) collective-permute-start(bf16[32,512]{1,0:T(8,128)(2,1)S(1)} %edge.24), channel_id=1, source_target_pairs={{0,1},{1,0},{2,3},{3,2},{4,5},{5,4},{6,7},{7,6},{8,9},{9,8},{10,11... | collective-permute-start | bytes 98312 | tf_op jit(solution)/shard_map/ppermute | solution.py:216
  94.9 3.5 %collective-permute-start.33 = (bf16[32,512]{1,0:T(8,128)(2,1)S(1)}, bf16[32,512]{1,0:T(8,128)(2,1)S(1)}, u32[]{:S(2)}, u32[]{:S(2)}) collective-permute-start(bf16[32,512]{1,0:T(8,128)(2,1)S(1)} %get-tuple-element.86), channel_id=1, source_target_pairs={{0,7},{1,6},{2,5},{3,4},{4,11},{5,10},{6,9},{7,8},{8,15},{9,14},{1... | collective-permute-start | bytes 98312 | tf_op jit(solution)/shard_map/ppermute | solution.py:216
  100.9 2.9 %collective-permute-start.37 = (bf16[32,512]{1,0:T(8,128)(2,1)S(1)}, bf16[32,512]{1,0:T(8,128)(2,1)S(1)}, u32[]{:S(2)}, u32[]{:S(2)}) collective-permute-start(bf16[32,512]{1,0:T(8,128)(2,1)S(1)} %edge.25), channel_id=1, source_target_pairs={{0,1},{1,0},{2,3},{3,2},{4,5},{5,4},{6,7},{7,6},{8,9},{9,8},{10,11... | collective-permute-start | bytes 98312 | tf_op jit(solution)/shard_map/ppermute | solution.py:216
  102.2 12.5 %collective-permute-start.41 = (bf16[32,4096]{1,0:T(8,128)(2,1)S(1)}, bf16[32,4096]{1,0:T(8,128)(2,1)S(1)}, u32[]{:S(2)}, u32[]{:S(2)}) collective-permute-start(bf16[32,4096]{1,0:T(8,128)(2,1)S(1)} %get-tuple-element.89.after.refs_6_), channel_id=1, source_target_pairs={{0,4},{1,5},{2,6},{3,7},{4,8},{5,9},{6,10},{7,11},{8,12},{9,13},{1... | collective-permute-start | bytes 786440 | tf_op jit(solution)/shard_map/ppermute | solution.py:216
  104.6 13.9 %collective-permute-start.38 = (bf16[32,4096]{1,0:T(8,128)(2,1)S(1)}, bf16[32,4096]{1,0:T(8,128)(2,1)S(1)}, u32[]{:S(2)}, u32[]{:S(2)}) collective-permute-start(bf16[32,4096]{1,0:T(8,128)(2,1)S(1)} %get-tuple-element.91.after.refs_6_), channel_id=1, source_target_pairs={{0,4},{1,5},{2,6},{3,7},{4,8},{5,9},{6,10},{7,11},{8,12},{9,13},{1... | collective-permute-start | bytes 786440 | tf_op jit(solution)/shard_map/ppermute | solution.py:216
  105.6 9.1 %collective-permute-start.42 = (bf16[32,512]{1,0:T(8,128)(2,1)S(1)}, bf16[32,512]{1,0:T(8,128)(2,1)S(1)}, u32[]{:S(2)}, u32[]{:S(2)}) collective-permute-start(bf16[32,512]{1,0:T(8,128)(2,1)S(1)} %get-tuple-element.93), channel_id=1, source_target_pairs={{0,7},{1,6},{2,5},{3,4},{4,11},{5,10},{6,9},{7,8},{8,15},{9,14},{1... | collective-permute-start | bytes 98312 | tf_op jit(solution)/shard_map/ppermute | solution.py:216
  110.8 4.9 %collective-permute-start.39 = (bf16[32,512]{1,0:T(8,128)(2,1)S(1)}, bf16[32,512]{1,0:T(8,128)(2,1)S(1)}, u32[]{:S(2)}, u32[]{:S(2)}) collective-permute-start(bf16[32,512]{1,0:T(8,128)(2,1)S(1)} %get-tuple-element.92), channel_id=1, source_target_pairs={{0,7},{1,6},{2,5},{3,4},{4,11},{5,10},{6,9},{7,8},{8,15},{9,14},{1... | collective-permute-start | bytes 98312 | tf_op jit(solution)/shard_map/ppermute | solution.py:216
  114.7 4.6 %collective-permute-start.43 = (bf16[32,512]{1,0:T(8,128)(2,1)S(1)}, bf16[32,512]{1,0:T(8,128)(2,1)S(1)}, u32[]{:S(2)}, u32[]{:S(2)}) collective-permute-start(bf16[32,512]{1,0:T(8,128)(2,1)S(1)} %edge.27), channel_id=1, source_target_pairs={{0,1},{1,0},{2,3},{3,2},{4,5},{5,4},{6,7},{7,6},{8,9},{9,8},{10,11... | collective-permute-start | bytes 98312 | tf_op jit(solution)/shard_map/ppermute | solution.py:216
  118.5 1.6 %collective-permute-start.40 = (bf16[32,512]{1,0:T(8,128)(2,1)S(1)}, bf16[32,512]{1,0:T(8,128)(2,1)S(1)}, u32[]{:S(2)}, u32[]{:S(2)}) collective-permute-start(bf16[32,512]{1,0:T(8,128)(2,1)S(1)} %edge.26), channel_id=1, source_target_pairs={{0,1},{1,0},{2,3},{3,2},{4,5},{5,4},{6,7},{7,6},{8,9},{9,8},{10,11... | collective-permute-start | bytes 98312 | tf_op jit(solution)/shard_map/ppermute | solution.py:216

commit v11 on v4

--- a/solution.py
+++ b/solution.py
@@ -23,7 +23,7 @@
     ]
     for copy in copies:
         copy.start()
-    brs, nzb = indices.shape
+    nzb, brs = indices.shape
     columns = brs * blks
     start = lax.axis_index("blk") * brs - HALO
     meta[brs * nzb] = lax.axis_index("section")
@@ -32,7 +32,7 @@
     @pl.loop(0, brs)
     def _(i):
         for k in range(nzb):
-            col = raw[i, k] - start
+            col = raw[k, i] - start
             col = jnp.where(col < 0, col + columns, col)
             meta[i * nzb + k] = jnp.where(col >= columns, col - columns, col) * BLK
 
@@ -198,7 +198,7 @@
         pending_groups,
         coefficient_tiles.reshape(block_rows, nzb * BLK, BLK),
         additive_offsets,
-        source_block_indices[0],
+        source_block_indices[0].T,
     )
     parts = [(state, low, high, c * rows) for c in range(CHUNKS)]
     emitted = prev = prev_slot = None

time: 119 us -> 117 us (0.983)
  local copies, waits for them, and re-layouts: 2.25 us -> 0.88 us
    unnamed x1 -> x0, local copies, waits for them, and re-layouts: 1.37 us -> none
  transfers between devices with their start and end apart: 44 -> 44, of which waited for: 27 -> 28; matrix products, arithmetic and copies ran while one was open for 1% -> 0% of each run, Pallas kernels for 13% -> 13%
where the time goes in v11:
time: 117 us
  waiting for transfers between devices  63.7 us (54%)
  starting transfers between devices  35.2 us (30%)
  Pallas kernels  17.1 us (15%)
    ppermute x44, waiting for transfers between devices, hop(): return lax.ppermute(values, ('section', 'blk'), pairs)  63.7 us
    ppermute x44, starting transfers between devices, hop(): return lax.ppermute(values, ('section', 'blk'), pairs)  35.2 us
    pallas_call x16, Pallas kernels, apply_layer(): pl.pallas_call(body, out_shape=tuple(out_shape), in_specs=specs, out_spec...  13.5 us
    pallas_call x1, Pallas kernels, load(): pl.pallas_call(functools.partial(load_kernel, blks), out_shape=(*(pltpu.V...  3.62 us
  transfers between devices with their start and end apart: 44, of which 28 were waited for; matrix products, arithmetic and copies ran while one was open for 0% of the time, Pallas kernels for 13%

profile of v11, /device:TPU:1, one launch (start us, length us, event | category | flops | bytes accessed | tf_op | source)
XLA Modules:
  0.0 117.3 jit_solution(11883523996725738367)
XLA Ops:
  0.0 0.9 fusion
  0.9 2.7 %collective-permute-start = (bf16[64,512]{1,0:T(8,128)(2,1)S(1)}, bf16[64,512]{1,0:T(8,128)(2,1)S(1)}, u32[]{:S(2)}, u32[]{:S(2)}) collective-permute-start(bf16[64,512]{1,0:T(8,128)(2,1)S(1)} %get-tuple-element.124), channel_id=1, source_target_pairs={{0,1},{1,2},{2,3},{3,0},{4,5},{5,6},{6,7},{7,4},{8,9},{9,10},{10,1... | collective-permute-start | bytes 196616 | tf_op jit(solution)/shard_map/ppermute | solution.py:192
  3.5 3.6 %load.1 = (bf16[64,4096]{1,0:T(8,128)(2,1)S(1)}, bf16[32,1024,128]{2,1,0:T(8,128)(2,1)S(1)}, f32[1,4096]{1,0:T(1,128)S(1)}, s32[257]{0:T(512)S(4)}) custom-call(bf16[64,4096]{1,0:T(8,128)(2,1)} %state.1, bf16[32,1024,128]{2,1,0:T(8,128)(2,1)} %bitcast.4, f32[1,4096]{1,0:T(1,128)} %bias.1, s32[8,32]{1,0:T(8,128)} %bitcast.5), custom_call_target="tpu_custom_call" | custom-call | bytes 8388608 | tf_op jit(solution)/shard_map/load/pallas_call | solution.py:45
  7.2 1.5 %layer_t0_r0.1 = (bf16[32,4096]{1,0:T(8,128)(2,1)S(1)}, bf16[32,512]{1,0:T(8,128)(2,1)S(1)}, bf16[32,512]{1,0:T(8,128)(2,1)S(1)}) custom-call(s32[257]{0:T(512)S(4)} %get-tuple-element.64.refs_0_, bf16[64,4096]{1,0:T(8,128)(2,1)S(1)} %get-tuple-element.65.refs_1_, bf16[64,512]{1,0:T(8,128)(2,1)S(1)} %collective-permute-done.refs_2_, ...), custom_call_target="tpu_custom_call" | custom-call | flops 2684354560 | bytes 83886080 | tf_op jit(solution)/shard_map/layer_t0_r0/pallas_call | solution.py:164
  8.7 1.3 %collective-permute-start.5 = (bf16[32,4096]{1,0:T(8,128)(2,1)S(1)}, bf16[32,4096]{1,0:T(8,128)(2,1)S(1)}, u32[]{:S(2)}, u32[]{:S(2)}) collective-permute-start(bf16[32,4096]{1,0:T(8,128)(2,1)S(1)} %get-tuple-element.68.refs_6_), channel_id=1, source_target_pairs={{0,4},{1,5},{2,6},{3,7},{4,8},{5,9},{6,10},{7,11},{8,12},{9,13},{1... | collective-permute-start | bytes 786440 | tf_op jit(solution)/shard_map/ppermute | solution.py:192
  10.0 2.9 %collective-permute-start.6 = (bf16[32,512]{1,0:T(8,128)(2,1)S(1)}, bf16[32,512]{1,0:T(8,128)(2,1)S(1)}, u32[]{:S(2)}, u32[]{:S(2)}) collective-permute-start(bf16[32,512]{1,0:T(8,128)(2,1)S(1)} %get-tuple-element.72), channel_id=1, source_target_pairs={{0,5},{1,6},{2,7},{3,4},{4,9},{5,10},{6,11},{7,8},{8,13},{9,14},{1... | collective-permute-start | bytes 98312 | tf_op jit(solution)/shard_map/ppermute | solution.py:192
  12.9 1.5 %layer_t0_r32.1 = (bf16[8,64,4096]{2,1,0:T(8,128)(2,1)}, bf16[32,4096]{1,0:T(8,128)(2,1)S(1)}, bf16[32,512]{1,0:T(8,128)(2,1)S(1)}, bf16[32,512]{1,0:T(8,128)(2,1)S(1)}) custom-call(s32[257]{0:T(512)S(4)} %get-tuple-element.64.refs_0_, bf16[64,4096]{1,0:T(8,128)(2,1)S(1)} %get-tuple-element.65.refs_1_, bf16[64,512]{1,0:T(8,128)(2,1)S(1)} %collective-permute-done.refs_2_, ...), custom_call_target="tpu_custom_call" | custom-call | flops 2684354560 | bytes 83886080 | tf_op jit(solution)/shard_map/layer_t0_r32/pallas_call | solution.py:164
  14.4 1.3 %collective-permute-start.2 = (bf16[32,4096]{1,0:T(8,128)(2,1)S(1)}, bf16[32,4096]{1,0:T(8,128)(2,1)S(1)}, u32[]{:S(2)}, u32[]{:S(2)}) collective-permute-start(bf16[32,4096]{1,0:T(8,128)(2,1)S(1)} %get-tuple-element.69.refs_6_), channel_id=1, source_target_pairs={{0,4},{1,5},{2,6},{3,7},{4,8},{5,9},{6,10},{7,11},{8,12},{9,13},{1... | collective-permute-start | bytes 786440 | tf_op jit(solution)/shard_map/ppermute | solution.py:192
  15.7 3.9 %collective-permute-start.3 = (bf16[32,512]{1,0:T(8,128)(2,1)S(1)}, bf16[32,512]{1,0:T(8,128)(2,1)S(1)}, u32[]{:S(2)}, u32[]{:S(2)}) collective-permute-start(bf16[32,512]{1,0:T(8,128)(2,1)S(1)} %get-tuple-element.70), channel_id=1, source_target_pairs={{0,5},{1,6},{2,7},{3,4},{4,9},{5,10},{6,11},{7,8},{8,13},{9,14},{1... | collective-permute-start | bytes 98312 | tf_op jit(solution)/shard_map/ppermute | solution.py:192
  19.6 1.5 %collective-permute-done.6.refs_2_ = bf16[32,512]{1,0:T(8,128)(2,1)S(1)} collective-permute-done((bf16[32,512]{1,0:T(8,128)(2,1)S(1)}, bf16[32,512]{1,0:T(8,128)(2,1)S(1)}, u32[]{:S(2)}, u32[]{:S(2)}) %collective-permute-start.6) | collective-permute-done | bytes 32800 | tf_op jit(solution)/shard_map/ppermute | solution.py:192
  21.1 1.7 %collective-permute-done.7.refs_3_ = bf16[32,512]{1,0:T(8,128)(2,1)S(1)} collective-permute-done((bf16[32,512]{1,0:T(8,128)(2,1)S(1)}, bf16[32,512]{1,0:T(8,128)(2,1)S(1)}, u32[]{:S(2)}, u32[]{:S(2)}) %collective-permute-start.7) | collective-permute-done | bytes 32800 | tf_op jit(solution)/shard_map/ppermute | solution.py:192
  22.9 0.7 layer_t1_r0.1
  23.6 0.1 collective-permute-start.11
  23.7 2.1 %collective-permute-start.12 = (bf16[32,512]{1,0:T(8,128)(2,1)S(1)}, bf16[32,512]{1,0:T(8,128)(2,1)S(1)}, u32[]{:S(2)}, u32[]{:S(2)}) collective-permute-start(bf16[32,512]{1,0:T(8,128)(2,1)S(1)} %get-tuple-element.80), channel_id=1, source_target_pairs={{0,5},{1,6},{2,7},{3,4},{4,9},{5,10},{6,11},{7,8},{8,13},{9,14},{1... | collective-permute-start | bytes 98312 | tf_op jit(solution)/shard_map/ppermute | solution.py:192
  25.8 2.4 %collective-permute-done.3.refs_2_ = bf16[32,512]{1,0:T(8,128)(2,1)S(1)} collective-permute-done((bf16[32,512]{1,0:T(8,128)(2,1)S(1)}, bf16[32,512]{1,0:T(8,128)(2,1)S(1)}, u32[]{:S(2)}, u32[]{:S(2)}) %collective-permute-start.3) | collective-permute-done | bytes 32800 | tf_op jit(solution)/shard_map/ppermute | solution.py:192
  28.2 0.3 collective-permute-done.4.refs_3_
  28.4 0.7 layer_t1_r32.1
  29.2 0.5 collective-permute-start.8
  29.7 3.8 %collective-permute-start.10 = (bf16[32,512]{1,0:T(8,128)(2,1)S(1)}, bf16[32,512]{1,0:T(8,128)(2,1)S(1)}, u32[]{:S(2)}, u32[]{:S(2)}) collective-permute-start(bf16[32,512]{1,0:T(8,128)(2,1)S(1)} %get-tuple-element.79), channel_id=1, source_target_pairs={{0,7},{1,4},{2,5},{3,6},{4,11},{5,8},{6,9},{7,10},{8,15},{9,12},{1... | collective-permute-start | bytes 98312 | tf_op jit(solution)/shard_map/ppermute | solution.py:192
  33.5 2.2 %collective-permute-done.12.refs_2_ = bf16[32,512]{1,0:T(8,128)(2,1)S(1)} collective-permute-done((bf16[32,512]{1,0:T(8,128)(2,1)S(1)}, bf16[32,512]{1,0:T(8,128)(2,1)S(1)}, u32[]{:S(2)}, u32[]{:S(2)}) %collective-permute-start.12) | collective-permute-done | bytes 32800 | tf_op jit(solution)/shard_map/ppermute | solution.py:192
  35.7 0.9 collective-permute-done.13.refs_3_
  36.6 0.7 layer_t2_r0.1
  37.5 1.2 %collective-permute-start.18 = (bf16[32,512]{1,0:T(8,128)(2,1)S(1)}, bf16[32,512]{1,0:T(8,128)(2,1)S(1)}, u32[]{:S(2)}, u32[]{:S(2)}) collective-permute-start(bf16[32,512]{1,0:T(8,128)(2,1)S(1)} %get-tuple-element.88), channel_id=1, source_target_pairs={{0,5},{1,6},{2,7},{3,4},{4,9},{5,10},{6,11},{7,8},{8,13},{9,14},{1... | collective-permute-start | bytes 98312 | tf_op jit(solution)/shard_map/ppermute | solution.py:192
  38.7 4.7 %collective-permute-done.10.refs_3_ = bf16[32,512]{1,0:T(8,128)(2,1)S(1)} collective-permute-done((bf16[32,512]{1,0:T(8,128)(2,1)S(1)}, bf16[32,512]{1,0:T(8,128)(2,1)S(1)}, u32[]{:S(2)}, u32[]{:S(2)}) %collective-permute-start.10) | collective-permute-done | bytes 32800 | tf_op jit(solution)/shard_map/ppermute | solution.py:192
  43.4 0.8 layer_t2_r32.1
  44.2 2.4 %collective-permute-start.15 = (bf16[32,512]{1,0:T(8,128)(2,1)S(1)}, bf16[32,512]{1,0:T(8,128)(2,1)S(1)}, u32[]{:S(2)}, u32[]{:S(2)}) collective-permute-start(bf16[32,512]{1,0:T(8,128)(2,1)S(1)} %get-tuple-element.86), channel_id=1, source_target_pairs={{0,5},{1,6},{2,7},{3,4},{4,9},{5,10},{6,11},{7,8},{8,13},{9,14},{1... | collective-permute-start | bytes 98312 | tf_op jit(solution)/shard_map/ppermute | solution.py:192
  46.6 2.9 %collective-permute-done.18.refs_2_ = bf16[32,512]{1,0:T(8,128)(2,1)S(1)} collective-permute-done((bf16[32,512]{1,0:T(8,128)(2,1)S(1)}, bf16[32,512]{1,0:T(8,128)(2,1)S(1)}, u32[]{:S(2)}, u32[]{:S(2)}) %collective-permute-start.18) | collective-permute-done | bytes 32800 | tf_op jit(solution)/shard_map/ppermute | solution.py:192
  49.5 1.7 %collective-permute-done.19.refs_3_ = bf16[32,512]{1,0:T(8,128)(2,1)S(1)} collective-permute-done((bf16[32,512]{1,0:T(8,128)(2,1)S(1)}, bf16[32,512]{1,0:T(8,128)(2,1)S(1)}, u32[]{:S(2)}, u32[]{:S(2)}) %collective-permute-start.19) | collective-permute-done | bytes 32800 | tf_op jit(solution)/shard_map/ppermute | solution.py:192
  51.2 0.7 layer_t3_r0.1
  52.0 2.0 %collective-permute-start.24 = (bf16[32,512]{1,0:T(8,128)(2,1)S(1)}, bf16[32,512]{1,0:T(8,128)(2,1)S(1)}, u32[]{:S(2)}, u32[]{:S(2)}) collective-permute-start(bf16[32,512]{1,0:T(8,128)(2,1)S(1)} %get-tuple-element.96), channel_id=1, source_target_pairs={{0,5},{1,6},{2,7},{3,4},{4,9},{5,10},{6,11},{7,8},{8,13},{9,14},{1... | collective-permute-start | bytes 98312 | tf_op jit(solution)/shard_map/ppermute | solution.py:192
  54.0 3.6 %collective-permute-done.15.refs_2_ = bf16[32,512]{1,0:T(8,128)(2,1)S(1)} collective-permute-done((bf16[32,512]{1,0:T(8,128)(2,1)S(1)}, bf16[32,512]{1,0:T(8,128)(2,1)S(1)}, u32[]{:S(2)}, u32[]{:S(2)}) %collective-permute-start.15) | collective-permute-done | bytes 32800 | tf_op jit(solution)/shard_map/ppermute | solution.py:192
  57.6 1.0 collective-permute-done.16.refs_3_
  58.6 0.7 layer_t3_r32.1
  59.4 1.3 %collective-permute-start.21 = (bf16[32,512]{1,0:T(8,128)(2,1)S(1)}, bf16[32,512]{1,0:T(8,128)(2,1)S(1)}, u32[]{:S(2)}, u32[]{:S(2)}) collective-permute-start(bf16[32,512]{1,0:T(8,128)(2,1)S(1)} %get-tuple-element.94), channel_id=1, source_target_pairs={{0,5},{1,6},{2,7},{3,4},{4,9},{5,10},{6,11},{7,8},{8,13},{9,14},{1... | collective-permute-start | bytes 98312 | tf_op jit(solution)/shard_map/ppermute | solution.py:192
  60.7 3.8 %collective-permute-done.24.refs_2_ = bf16[32,512]{1,0:T(8,128)(2,1)S(1)} collective-permute-done((bf16[32,512]{1,0:T(8,128)(2,1)S(1)}, bf16[32,512]{1,0:T(8,128)(2,1)S(1)}, u32[]{:S(2)}, u32[]{:S(2)}) %collective-permute-start.24) | collective-permute-done | bytes 32800 | tf_op jit(solution)/shard_map/ppermute | solution.py:192
  64.6 1.2 collective-permute-done.25.refs_3_
  65.7 0.7 layer_t4_r0.1
  66.6 1.5 %collective-permute-start.30 = (bf16[32,512]{1,0:T(8,128)(2,1)S(1)}, bf16[32,512]{1,0:T(8,128)(2,1)S(1)}, u32[]{:S(2)}, u32[]{:S(2)}) collective-permute-start(bf16[32,512]{1,0:T(8,128)(2,1)S(1)} %get-tuple-element.104), channel_id=1, source_target_pairs={{0,5},{1,6},{2,7},{3,4},{4,9},{5,10},{6,11},{7,8},{8,13},{9,14},{1... | collective-permute-start | bytes 98312 | tf_op jit(solution)/shard_map/ppermute | solution.py:192
  68.0 4.0 %collective-permute-done.21.refs_2_ = bf16[32,512]{1,0:T(8,128)(2,1)S(1)} collective-permute-done((bf16[32,512]{1,0:T(8,128)(2,1)S(1)}, bf16[32,512]{1,0:T(8,128)(2,1)S(1)}, u32[]{:S(2)}, u32[]{:S(2)}) %collective-permute-start.21) | collective-permute-done | bytes 32800 | tf_op jit(solution)/shard_map/ppermute | solution.py:192
  72.0 1.1 collective-permute-done.22.refs_3_
  73.1 0.7 layer_t4_r32.1
  73.9 1.4 %collective-permute-start.27 = (bf16[32,512]{1,0:T(8,128)(2,1)S(1)}, bf16[32,512]{1,0:T(8,128)(2,1)S(1)}, u32[]{:S(2)}, u32[]{:S(2)}) collective-permute-start(bf16[32,512]{1,0:T(8,128)(2,1)S(1)} %get-tuple-element.102), channel_id=1, source_target_pairs={{0,5},{1,6},{2,7},{3,4},{4,9},{5,10},{6,11},{7,8},{8,13},{9,14},{1... | collective-permute-start | bytes 98312 | tf_op jit(solution)/shard_map/ppermute | solution.py:192
  75.4 3.8 %collective-permute-done.30.refs_2_ = bf16[32,512]{1,0:T(8,128)(2,1)S(1)} collective-permute-done((bf16[32,512]{1,0:T(8,128)(2,1)S(1)}, bf16[32,512]{1,0:T(8,128)(2,1)S(1)}, u32[]{:S(2)}, u32[]{:S(2)}) %collective-permute-start.30) | collective-permute-done | bytes 32800 | tf_op jit(solution)/shard_map/ppermute | solution.py:192
  79.2 1.1 collective-permute-done.31.refs_3_
  80.3 0.7 layer_t5_r0.1
  81.2 1.5 %collective-permute-start.36 = (bf16[32,512]{1,0:T(8,128)(2,1)S(1)}, bf16[32,512]{1,0:T(8,128)(2,1)S(1)}, u32[]{:S(2)}, u32[]{:S(2)}) collective-permute-start(bf16[32,512]{1,0:T(8,128)(2,1)S(1)} %get-tuple-element.112), channel_id=1, source_target_pairs={{0,5},{1,6},{2,7},{3,4},{4,9},{5,10},{6,11},{7,8},{8,13},{9,14},{1... | collective-permute-start | bytes 98312 | tf_op jit(solution)/shard_map/ppermute | solution.py:192
  82.7 4.2 %collective-permute-done.27.refs_2_ = bf16[32,512]{1,0:T(8,128)(2,1)S(1)} collective-permute-done((bf16[32,512]{1,0:T(8,128)(2,1)S(1)}, bf16[32,512]{1,0:T(8,128)(2,1)S(1)}, u32[]{:S(2)}, u32[]{:S(2)}) %collective-permute-start.27) | collective-permute-done | bytes 32800 | tf_op jit(solution)/shard_map/ppermute | solution.py:192
  86.8 0.9 collective-permute-done.28.refs_3_
  87.8 0.7 layer_t5_r32.1
  88.6 1.4 %collective-permute-start.33 = (bf16[32,512]{1,0:T(8,128)(2,1)S(1)}, bf16[32,512]{1,0:T(8,128)(2,1)S(1)}, u32[]{:S(2)}, u32[]{:S(2)}) collective-permute-start(bf16[32,512]{1,0:T(8,128)(2,1)S(1)} %get-tuple-element.110), channel_id=1, source_target_pairs={{0,5},{1,6},{2,7},{3,4},{4,9},{5,10},{6,11},{7,8},{8,13},{9,14},{1... | collective-permute-start | bytes 98312 | tf_op jit(solution)/shard_map/ppermute | solution.py:192
  90.0 3.7 %collective-permute-done.36.refs_2_ = bf16[32,512]{1,0:T(8,128)(2,1)S(1)} collective-permute-done((bf16[32,512]{1,0:T(8,128)(2,1)S(1)}, bf16[32,512]{1,0:T(8,128)(2,1)S(1)}, u32[]{:S(2)}, u32[]{:S(2)}) %collective-permute-start.36) | collective-permute-done | bytes 32800 | tf_op jit(solution)/shard_map/ppermute | solution.py:192
  93.7 1.2 %collective-permute-done.37.refs_3_ = bf16[32,512]{1,0:T(8,128)(2,1)S(1)} collective-permute-done((bf16[32,512]{1,0:T(8,128)(2,1)S(1)}, bf16[32,512]{1,0:T(8,128)(2,1)S(1)}, u32[]{:S(2)}, u32[]{:S(2)}) %collective-permute-start.37) | collective-permute-done | bytes 32800 | tf_op jit(solution)/shard_map/ppermute | solution.py:192
  95.0 0.7 layer_t6_r0.1
  95.8 1.5 %collective-permute-start.42 = (bf16[32,512]{1,0:T(8,128)(2,1)S(1)}, bf16[32,512]{1,0:T(8,128)(2,1)S(1)}, u32[]{:S(2)}, u32[]{:S(2)}) collective-permute-start(bf16[32,512]{1,0:T(8,128)(2,1)S(1)} %get-tuple-element.120), channel_id=1, source_target_pairs={{0,5},{1,6},{2,7},{3,4},{4,9},{5,10},{6,11},{7,8},{8,13},{9,14},{1... | collective-permute-start | bytes 98312 | tf_op jit(solution)/shard_map/ppermute | solution.py:192
  97.3 3.8 %collective-permute-done.33.refs_2_ = bf16[32,512]{1,0:T(8,128)(2,1)S(1)} collective-permute-done((bf16[32,512]{1,0:T(8,128)(2,1)S(1)}, bf16[32,512]{1,0:T(8,128)(2,1)S(1)}, u32[]{:S(2)}, u32[]{:S(2)}) %collective-permute-start.33) | collective-permute-done | bytes 32800 | tf_op jit(solution)/shard_map/ppermute | solution.py:192
  101.1 1.0 collective-permute-done.34.refs_3_
  102.1 0.7 layer_t6_r32.1
  103.0 1.7 %collective-permute-start.39 = (bf16[32,512]{1,0:T(8,128)(2,1)S(1)}, bf16[32,512]{1,0:T(8,128)(2,1)S(1)}, u32[]{:S(2)}, u32[]{:S(2)}) collective-permute-start(bf16[32,512]{1,0:T(8,128)(2,1)S(1)} %get-tuple-element.118), channel_id=1, source_target_pairs={{0,5},{1,6},{2,7},{3,4},{4,9},{5,10},{6,11},{7,8},{8,13},{9,14},{1... | collective-permute-start | bytes 98312 | tf_op jit(solution)/shard_map/ppermute | solution.py:192
  104.6 3.7 %collective-permute-done.42.refs_2_ = bf16[32,512]{1,0:T(8,128)(2,1)S(1)} collective-permute-done((bf16[32,512]{1,0:T(8,128)(2,1)S(1)}, bf16[32,512]{1,0:T(8,128)(2,1)S(1)}, u32[]{:S(2)}, u32[]{:S(2)}) %collective-permute-start.42) | collective-permute-done | bytes 32800 | tf_op jit(solution)/shard_map/ppermute | solution.py:192
  108.3 1.2 %collective-permute-done.43.refs_3_ = bf16[32,512]{1,0:T(8,128)(2,1)S(1)} collective-permute-done((bf16[32,512]{1,0:T(8,128)(2,1)S(1)}, bf16[32,512]{1,0:T(8,128)(2,1)S(1)}, u32[]{:S(2)}, u32[]{:S(2)}) %collective-permute-start.43) | collective-permute-done | bytes 32800 | tf_op jit(solution)/shard_map/ppermute | solution.py:192
  109.5 0.8 layer_t7_r0.1.refs_6_
  110.4 5.5 %collective-permute-done.39.refs_2_ = bf16[32,512]{1,0:T(8,128)(2,1)S(1)} collective-permute-done((bf16[32,512]{1,0:T(8,128)(2,1)S(1)}, bf16[32,512]{1,0:T(8,128)(2,1)S(1)}, u32[]{:S(2)}, u32[]{:S(2)}) %collective-permute-start.39) | collective-permute-done | bytes 32800 | tf_op jit(solution)/shard_map/ppermute | solution.py:192
  115.9 0.4 collective-permute-done.40.refs_3_
  116.3 0.8 layer_t7_r32.1
  (42 shorter events, 0.7 us)
Async XLA Ops:
  0.9 6.3 %collective-permute-start = (bf16[64,512]{1,0:T(8,128)(2,1)S(1)}, bf16[64,512]{1,0:T(8,128)(2,1)S(1)}, u32[]{:S(2)}, u32[]{:S(2)}) collective-permute-start(bf16[64,512]{1,0:T(8,128)(2,1)S(1)} %get-tuple-element.124), channel_id=1, source_target_pairs={{0,1},{1,2},{2,3},{3,0},{4,5},{5,6},{6,7},{7,4},{8,9},{9,10},{10,1... | collective-permute-start | bytes 196616 | tf_op jit(solution)/shard_map/ppermute | solution.py:192
  3.5 3.7 %collective-permute-start.1 = (bf16[64,512]{1,0:T(8,128)(2,1)S(1)}, bf16[64,512]{1,0:T(8,128)(2,1)S(1)}, u32[]{:S(2)}, u32[]{:S(2)}) collective-permute-start(bf16[64,512]{1,0:T(8,128)(2,1)S(1)} %get-tuple-element.123), channel_id=1, source_target_pairs={{0,3},{1,0},{2,1},{3,2},{4,7},{5,4},{6,5},{7,6},{8,11},{9,8},{10,9... | collective-permute-start | bytes 196616 | tf_op jit(solution)/shard_map/ppermute | solution.py:192
  8.7 14.2 %collective-permute-start.5 = (bf16[32,4096]{1,0:T(8,128)(2,1)S(1)}, bf16[32,4096]{1,0:T(8,128)(2,1)S(1)}, u32[]{:S(2)}, u32[]{:S(2)}) collective-permute-start(bf16[32,4096]{1,0:T(8,128)(2,1)S(1)} %get-tuple-element.68.refs_6_), channel_id=1, source_target_pairs={{0,4},{1,5},{2,6},{3,7},{4,8},{5,9},{6,10},{7,11},{8,12},{9,13},{1... | collective-permute-start | bytes 786440 | tf_op jit(solution)/shard_map/ppermute | solution.py:192
  10.0 11.1 %collective-permute-start.6 = (bf16[32,512]{1,0:T(8,128)(2,1)S(1)}, bf16[32,512]{1,0:T(8,128)(2,1)S(1)}, u32[]{:S(2)}, u32[]{:S(2)}) collective-permute-start(bf16[32,512]{1,0:T(8,128)(2,1)S(1)} %get-tuple-element.72), channel_id=1, source_target_pairs={{0,5},{1,6},{2,7},{3,4},{4,9},{5,10},{6,11},{7,8},{8,13},{9,14},{1... | collective-permute-start | bytes 98312 | tf_op jit(solution)/shard_map/ppermute | solution.py:192
  12.9 9.9 %collective-permute-start.7 = (bf16[32,512]{1,0:T(8,128)(2,1)S(1)}, bf16[32,512]{1,0:T(8,128)(2,1)S(1)}, u32[]{:S(2)}, u32[]{:S(2)}) collective-permute-start(bf16[32,512]{1,0:T(8,128)(2,1)S(1)} %get-tuple-element.73), channel_id=1, source_target_pairs={{0,7},{1,4},{2,5},{3,6},{4,11},{5,8},{6,9},{7,10},{8,15},{9,12},{1... | collective-permute-start | bytes 98312 | tf_op jit(solution)/shard_map/ppermute | solution.py:192
  14.4 14.0 %collective-permute-start.2 = (bf16[32,4096]{1,0:T(8,128)(2,1)S(1)}, bf16[32,4096]{1,0:T(8,128)(2,1)S(1)}, u32[]{:S(2)}, u32[]{:S(2)}) collective-permute-start(bf16[32,4096]{1,0:T(8,128)(2,1)S(1)} %get-tuple-element.69.refs_6_), channel_id=1, source_target_pairs={{0,4},{1,5},{2,6},{3,7},{4,8},{5,9},{6,10},{7,11},{8,12},{9,13},{1... | collective-permute-start | bytes 786440 | tf_op jit(solution)/shard_map/ppermute | solution.py:192
  15.7 12.4 %collective-permute-start.3 = (bf16[32,512]{1,0:T(8,128)(2,1)S(1)}, bf16[32,512]{1,0:T(8,128)(2,1)S(1)}, u32[]{:S(2)}, u32[]{:S(2)}) collective-permute-start(bf16[32,512]{1,0:T(8,128)(2,1)S(1)} %get-tuple-element.70), channel_id=1, source_target_pairs={{0,5},{1,6},{2,7},{3,4},{4,9},{5,10},{6,11},{7,8},{8,13},{9,14},{1... | collective-permute-start | bytes 98312 | tf_op jit(solution)/shard_map/ppermute | solution.py:192
  21.1 7.3 %collective-permute-start.4 = (bf16[32,512]{1,0:T(8,128)(2,1)S(1)}, bf16[32,512]{1,0:T(8,128)(2,1)S(1)}, u32[]{:S(2)}, u32[]{:S(2)}) collective-permute-start(bf16[32,512]{1,0:T(8,128)(2,1)S(1)} %get-tuple-element.71), channel_id=1, source_target_pairs={{0,7},{1,4},{2,5},{3,6},{4,11},{5,8},{6,9},{7,10},{8,15},{9,12},{1... | collective-permute-start | bytes 98312 | tf_op jit(solution)/shard_map/ppermute | solution.py:192
  23.6 13.0 %collective-permute-start.11 = (bf16[32,4096]{1,0:T(8,128)(2,1)S(1)}, bf16[32,4096]{1,0:T(8,128)(2,1)S(1)}, u32[]{:S(2)}, u32[]{:S(2)}) collective-permute-start(bf16[32,4096]{1,0:T(8,128)(2,1)S(1)} %get-tuple-element.75.refs_6_), channel_id=1, source_target_pairs={{0,4},{1,5},{2,6},{3,7},{4,8},{5,9},{6,10},{7,11},{8,12},{9,13},{1... | collective-permute-start | bytes 786440 | tf_op jit(solution)/shard_map/ppermute | solution.py:192
  23.7 12.1 %collective-permute-start.12 = (bf16[32,512]{1,0:T(8,128)(2,1)S(1)}, bf16[32,512]{1,0:T(8,128)(2,1)S(1)}, u32[]{:S(2)}, u32[]{:S(2)}) collective-permute-start(bf16[32,512]{1,0:T(8,128)(2,1)S(1)} %get-tuple-element.80), channel_id=1, source_target_pairs={{0,5},{1,6},{2,7},{3,4},{4,9},{5,10},{6,11},{7,8},{8,13},{9,14},{1... | collective-permute-start | bytes 98312 | tf_op jit(solution)/shard_map/ppermute | solution.py:192
  28.2 8.5 %collective-permute-start.13 = (bf16[32,512]{1,0:T(8,128)(2,1)S(1)}, bf16[32,512]{1,0:T(8,128)(2,1)S(1)}, u32[]{:S(2)}, u32[]{:S(2)}) collective-permute-start(bf16[32,512]{1,0:T(8,128)(2,1)S(1)} %get-tuple-element.81), channel_id=1, source_target_pairs={{0,7},{1,4},{2,5},{3,6},{4,11},{5,8},{6,9},{7,10},{8,15},{9,12},{1... | collective-permute-start | bytes 98312 | tf_op jit(solution)/shard_map/ppermute | solution.py:192
  29.2 14.2 %collective-permute-start.8 = (bf16[32,4096]{1,0:T(8,128)(2,1)S(1)}, bf16[32,4096]{1,0:T(8,128)(2,1)S(1)}, u32[]{:S(2)}, u32[]{:S(2)}) collective-permute-start(bf16[32,4096]{1,0:T(8,128)(2,1)S(1)} %get-tuple-element.77.refs_6_), channel_id=1, source_target_pairs={{0,4},{1,5},{2,6},{3,7},{4,8},{5,9},{6,10},{7,11},{8,12},{9,13},{1... | collective-permute-start | bytes 786440 | tf_op jit(solution)/shard_map/ppermute | solution.py:192
  29.7 13.6 %collective-permute-start.10 = (bf16[32,512]{1,0:T(8,128)(2,1)S(1)}, bf16[32,512]{1,0:T(8,128)(2,1)S(1)}, u32[]{:S(2)}, u32[]{:S(2)}) collective-permute-start(bf16[32,512]{1,0:T(8,128)(2,1)S(1)} %get-tuple-element.79), channel_id=1, source_target_pairs={{0,7},{1,4},{2,5},{3,6},{4,11},{5,8},{6,9},{7,10},{8,15},{9,12},{1... | collective-permute-start | bytes 98312 | tf_op jit(solution)/shard_map/ppermute | solution.py:192
  35.7 7.7 %collective-permute-start.9 = (bf16[32,512]{1,0:T(8,128)(2,1)S(1)}, bf16[32,512]{1,0:T(8,128)(2,1)S(1)}, u32[]{:S(2)}, u32[]{:S(2)}) collective-permute-start(bf16[32,512]{1,0:T(8,128)(2,1)S(1)} %get-tuple-element.78), channel_id=1, source_target_pairs={{0,5},{1,6},{2,7},{3,4},{4,9},{5,10},{6,11},{7,8},{8,13},{9,14},{1... | collective-permute-start | bytes 98312 | tf_op jit(solution)/shard_map/ppermute | solution.py:192
  37.4 13.8 %collective-permute-start.17 = (bf16[32,4096]{1,0:T(8,128)(2,1)S(1)}, bf16[32,4096]{1,0:T(8,128)(2,1)S(1)}, u32[]{:S(2)}, u32[]{:S(2)}) collective-permute-start(bf16[32,4096]{1,0:T(8,128)(2,1)S(1)} %get-tuple-element.83.refs_6_), channel_id=1, source_target_pairs={{0,4},{1,5},{2,6},{3,7},{4,8},{5,9},{6,10},{7,11},{8,12},{9,13},{1... | collective-permute-start | bytes 786440 | tf_op jit(solution)/shard_map/ppermute | solution.py:192
  37.5 12.0 %collective-permute-start.18 = (bf16[32,512]{1,0:T(8,128)(2,1)S(1)}, bf16[32,512]{1,0:T(8,128)(2,1)S(1)}, u32[]{:S(2)}, u32[]{:S(2)}) collective-permute-start(bf16[32,512]{1,0:T(8,128)(2,1)S(1)} %get-tuple-element.88), channel_id=1, source_target_pairs={{0,5},{1,6},{2,7},{3,4},{4,9},{5,10},{6,11},{7,8},{8,13},{9,14},{1... | collective-permute-start | bytes 98312 | tf_op jit(solution)/shard_map/ppermute | solution.py:192
  43.4 7.8 %collective-permute-start.19 = (bf16[32,512]{1,0:T(8,128)(2,1)S(1)}, bf16[32,512]{1,0:T(8,128)(2,1)S(1)}, u32[]{:S(2)}, u32[]{:S(2)}) collective-permute-start(bf16[32,512]{1,0:T(8,128)(2,1)S(1)} %get-tuple-element.89), channel_id=1, source_target_pairs={{0,7},{1,4},{2,5},{3,6},{4,11},{5,8},{6,9},{7,10},{8,15},{9,12},{1... | collective-permute-start | bytes 98312 | tf_op jit(solution)/shard_map/ppermute | solution.py:192
  44.2 14.4 %collective-permute-start.14 = (bf16[32,4096]{1,0:T(8,128)(2,1)S(1)}, bf16[32,4096]{1,0:T(8,128)(2,1)S(1)}, u32[]{:S(2)}, u32[]{:S(2)}) collective-permute-start(bf16[32,4096]{1,0:T(8,128)(2,1)S(1)} %get-tuple-element.85.refs_6_), channel_id=1, source_target_pairs={{0,4},{1,5},{2,6},{3,7},{4,8},{5,9},{6,10},{7,11},{8,12},{9,13},{1... | collective-permute-start | bytes 786440 | tf_op jit(solution)/shard_map/ppermute | solution.py:192
  44.2 13.4 %collective-permute-start.15 = (bf16[32,512]{1,0:T(8,128)(2,1)S(1)}, bf16[32,512]{1,0:T(8,128)(2,1)S(1)}, u32[]{:S(2)}, u32[]{:S(2)}) collective-permute-start(bf16[32,512]{1,0:T(8,128)(2,1)S(1)} %get-tuple-element.86), channel_id=1, source_target_pairs={{0,5},{1,6},{2,7},{3,4},{4,9},{5,10},{6,11},{7,8},{8,13},{9,14},{1... | collective-permute-start | bytes 98312 | tf_op jit(solution)/shard_map/ppermute | solution.py:192
  49.5 9.1 %collective-permute-start.16 = (bf16[32,512]{1,0:T(8,128)(2,1)S(1)}, bf16[32,512]{1,0:T(8,128)(2,1)S(1)}, u32[]{:S(2)}, u32[]{:S(2)}) collective-permute-start(bf16[32,512]{1,0:T(8,128)(2,1)S(1)} %get-tuple-element.87), channel_id=1, source_target_pairs={{0,7},{1,4},{2,5},{3,6},{4,11},{5,8},{6,9},{7,10},{8,15},{9,12},{1... | collective-permute-start | bytes 98312 | tf_op jit(solution)/shard_map/ppermute | solution.py:192
  51.9 13.8 %collective-permute-start.23 = (bf16[32,4096]{1,0:T(8,128)(2,1)S(1)}, bf16[32,4096]{1,0:T(8,128)(2,1)S(1)}, u32[]{:S(2)}, u32[]{:S(2)}) collective-permute-start(bf16[32,4096]{1,0:T(8,128)(2,1)S(1)} %get-tuple-element.91.refs_6_), channel_id=1, source_target_pairs={{0,4},{1,5},{2,6},{3,7},{4,8},{5,9},{6,10},{7,11},{8,12},{9,13},{1... | collective-permute-start | bytes 786440 | tf_op jit(solution)/shard_map/ppermute | solution.py:192
  52.0 12.6 %collective-permute-start.24 = (bf16[32,512]{1,0:T(8,128)(2,1)S(1)}, bf16[32,512]{1,0:T(8,128)(2,1)S(1)}, u32[]{:S(2)}, u32[]{:S(2)}) collective-permute-start(bf16[32,512]{1,0:T(8,128)(2,1)S(1)} %get-tuple-element.96), channel_id=1, source_target_pairs={{0,5},{1,6},{2,7},{3,4},{4,9},{5,10},{6,11},{7,8},{8,13},{9,14},{1... | collective-permute-start | bytes 98312 | tf_op jit(solution)/shard_map/ppermute | solution.py:192
  57.6 8.1 %collective-permute-start.25 = (bf16[32,512]{1,0:T(8,128)(2,1)S(1)}, bf16[32,512]{1,0:T(8,128)(2,1)S(1)}, u32[]{:S(2)}, u32[]{:S(2)}) collective-permute-start(bf16[32,512]{1,0:T(8,128)(2,1)S(1)} %get-tuple-element.97), channel_id=1, source_target_pairs={{0,7},{1,4},{2,5},{3,6},{4,11},{5,8},{6,9},{7,10},{8,15},{9,12},{1... | collective-permute-start | bytes 98312 | tf_op jit(solution)/shard_map/ppermute | solution.py:192
  59.3 13.7 %collective-permute-start.20 = (bf16[32,4096]{1,0:T(8,128)(2,1)S(1)}, bf16[32,4096]{1,0:T(8,128)(2,1)S(1)}, u32[]{:S(2)}, u32[]{:S(2)}) collective-permute-start(bf16[32,4096]{1,0:T(8,128)(2,1)S(1)} %get-tuple-element.93.refs_6_), channel_id=1, source_target_pairs={{0,4},{1,5},{2,6},{3,7},{4,8},{5,9},{6,10},{7,11},{8,12},{9,13},{1... | collective-permute-start | bytes 786440 | tf_op jit(solution)/shard_map/ppermute | solution.py:192
  59.4 12.6 %collective-permute-start.21 = (bf16[32,512]{1,0:T(8,128)(2,1)S(1)}, bf16[32,512]{1,0:T(8,128)(2,1)S(1)}, u32[]{:S(2)}, u32[]{:S(2)}) collective-permute-start(bf16[32,512]{1,0:T(8,128)(2,1)S(1)} %get-tuple-element.94), channel_id=1, source_target_pairs={{0,5},{1,6},{2,7},{3,4},{4,9},{5,10},{6,11},{7,8},{8,13},{9,14},{1... | collective-permute-start | bytes 98312 | tf_op jit(solution)/shard_map/ppermute | solution.py:192
  64.6 8.5 %collective-permute-start.22 = (bf16[32,512]{1,0:T(8,128)(2,1)S(1)}, bf16[32,512]{1,0:T(8,128)(2,1)S(1)}, u32[]{:S(2)}, u32[]{:S(2)}) collective-permute-start(bf16[32,512]{1,0:T(8,128)(2,1)S(1)} %get-tuple-element.95), channel_id=1, source_target_pairs={{0,7},{1,4},{2,5},{3,6},{4,11},{5,8},{6,9},{7,10},{8,15},{9,12},{1... | collective-permute-start | bytes 98312 | tf_op jit(solution)/shard_map/ppermute | solution.py:192
  66.5 13.9 %collective-permute-start.29 = (bf16[32,4096]{1,0:T(8,128)(2,1)S(1)}, bf16[32,4096]{1,0:T(8,128)(2,1)S(1)}, u32[]{:S(2)}, u32[]{:S(2)}) collective-permute-start(bf16[32,4096]{1,0:T(8,128)(2,1)S(1)} %get-tuple-element.99.refs_6_), channel_id=1, source_target_pairs={{0,4},{1,5},{2,6},{3,7},{4,8},{5,9},{6,10},{7,11},{8,12},{9,13},{1... | collective-permute-start | bytes 786440 | tf_op jit(solution)/shard_map/ppermute | solution.py:192
  66.6 12.6 %collective-permute-start.30 = (bf16[32,512]{1,0:T(8,128)(2,1)S(1)}, bf16[32,512]{1,0:T(8,128)(2,1)S(1)}, u32[]{:S(2)}, u32[]{:S(2)}) collective-permute-start(bf16[32,512]{1,0:T(8,128)(2,1)S(1)} %get-tuple-element.104), channel_id=1, source_target_pairs={{0,5},{1,6},{2,7},{3,4},{4,9},{5,10},{6,11},{7,8},{8,13},{9,14},{1... | collective-permute-start | bytes 98312 | tf_op jit(solution)/shard_map/ppermute | solution.py:192
  72.0 8.4 %collective-permute-start.31 = (bf16[32,512]{1,0:T(8,128)(2,1)S(1)}, bf16[32,512]{1,0:T(8,128)(2,1)S(1)}, u32[]{:S(2)}, u32[]{:S(2)}) collective-permute-start(bf16[32,512]{1,0:T(8,128)(2,1)S(1)} %get-tuple-element.105), channel_id=1, source_target_pairs={{0,7},{1,4},{2,5},{3,6},{4,11},{5,8},{6,9},{7,10},{8,15},{9,12},{1... | collective-permute-start | bytes 98312 | tf_op jit(solution)/shard_map/ppermute | solution.py:192
  73.8 13.9 %collective-permute-start.26 = (bf16[32,4096]{1,0:T(8,128)(2,1)S(1)}, bf16[32,4096]{1,0:T(8,128)(2,1)S(1)}, u32[]{:S(2)}, u32[]{:S(2)}) collective-permute-start(bf16[32,4096]{1,0:T(8,128)(2,1)S(1)} %get-tuple-element.101.refs_6_), channel_id=1, source_target_pairs={{0,4},{1,5},{2,6},{3,7},{4,8},{5,9},{6,10},{7,11},{8,12},{9,13},{1... | collective-permute-start | bytes 786440 | tf_op jit(solution)/shard_map/ppermute | solution.py:192
  73.9 12.9 %collective-permute-start.27 = (bf16[32,512]{1,0:T(8,128)(2,1)S(1)}, bf16[32,512]{1,0:T(8,128)(2,1)S(1)}, u32[]{:S(2)}, u32[]{:S(2)}) collective-permute-start(bf16[32,512]{1,0:T(8,128)(2,1)S(1)} %get-tuple-element.102), channel_id=1, source_target_pairs={{0,5},{1,6},{2,7},{3,4},{4,9},{5,10},{6,11},{7,8},{8,13},{9,14},{1... | collective-permute-start | bytes 98312 | tf_op jit(solution)/shard_map/ppermute | solution.py:192
  79.2 8.6 %collective-permute-start.28 = (bf16[32,512]{1,0:T(8,128)(2,1)S(1)}, bf16[32,512]{1,0:T(8,128)(2,1)S(1)}, u32[]{:S(2)}, u32[]{:S(2)}) collective-permute-start(bf16[32,512]{1,0:T(8,128)(2,1)S(1)} %get-tuple-element.103), channel_id=1, source_target_pairs={{0,7},{1,4},{2,5},{3,6},{4,11},{5,8},{6,9},{7,10},{8,15},{9,12},{1... | collective-permute-start | bytes 98312 | tf_op jit(solution)/shard_map/ppermute | solution.py:192
  81.1 13.9 %collective-permute-start.35 = (bf16[32,4096]{1,0:T(8,128)(2,1)S(1)}, bf16[32,4096]{1,0:T(8,128)(2,1)S(1)}, u32[]{:S(2)}, u32[]{:S(2)}) collective-permute-start(bf16[32,4096]{1,0:T(8,128)(2,1)S(1)} %get-tuple-element.107.refs_6_), channel_id=1, source_target_pairs={{0,4},{1,5},{2,6},{3,7},{4,8},{5,9},{6,10},{7,11},{8,12},{9,13},{1... | collective-permute-start | bytes 786440 | tf_op jit(solution)/shard_map/ppermute | solution.py:192
  81.2 12.5 %collective-permute-start.36 = (bf16[32,512]{1,0:T(8,128)(2,1)S(1)}, bf16[32,512]{1,0:T(8,128)(2,1)S(1)}, u32[]{:S(2)}, u32[]{:S(2)}) collective-permute-start(bf16[32,512]{1,0:T(8,128)(2,1)S(1)} %get-tuple-element.112), channel_id=1, source_target_pairs={{0,5},{1,6},{2,7},{3,4},{4,9},{5,10},{6,11},{7,8},{8,13},{9,14},{1... | collective-permute-start | bytes 98312 | tf_op jit(solution)/shard_map/ppermute | solution.py:192
  86.8 8.1 %collective-permute-start.37 = (bf16[32,512]{1,0:T(8,128)(2,1)S(1)}, bf16[32,512]{1,0:T(8,128)(2,1)S(1)}, u32[]{:S(2)}, u32[]{:S(2)}) collective-permute-start(bf16[32,512]{1,0:T(8,128)(2,1)S(1)} %get-tuple-element.113), channel_id=1, source_target_pairs={{0,7},{1,4},{2,5},{3,6},{4,11},{5,8},{6,9},{7,10},{8,15},{9,12},{1... | collective-permute-start | bytes 98312 | tf_op jit(solution)/shard_map/ppermute | solution.py:192
  88.5 13.6 %collective-permute-start.32 = (bf16[32,4096]{1,0:T(8,128)(2,1)S(1)}, bf16[32,4096]{1,0:T(8,128)(2,1)S(1)}, u32[]{:S(2)}, u32[]{:S(2)}) collective-permute-start(bf16[32,4096]{1,0:T(8,128)(2,1)S(1)} %get-tuple-element.109.refs_6_), channel_id=1, source_target_pairs={{0,4},{1,5},{2,6},{3,7},{4,8},{5,9},{6,10},{7,11},{8,12},{9,13},{1... | collective-permute-start | bytes 786440 | tf_op jit(solution)/shard_map/ppermute | solution.py:192
  88.6 12.5 %collective-permute-start.33 = (bf16[32,512]{1,0:T(8,128)(2,1)S(1)}, bf16[32,512]{1,0:T(8,128)(2,1)S(1)}, u32[]{:S(2)}, u32[]{:S(2)}) collective-permute-start(bf16[32,512]{1,0:T(8,128)(2,1)S(1)} %get-tuple-element.110), channel_id=1, source_target_pairs={{0,5},{1,6},{2,7},{3,4},{4,9},{5,10},{6,11},{7,8},{8,13},{9,14},{1... | collective-permute-start | bytes 98312 | tf_op jit(solution)/shard_map/ppermute | solution.py:192
  93.7 8.4 %collective-permute-start.34 = (bf16[32,512]{1,0:T(8,128)(2,1)S(1)}, bf16[32,512]{1,0:T(8,128)(2,1)S(1)}, u32[]{:S(2)}, u32[]{:S(2)}) collective-permute-start(bf16[32,512]{1,0:T(8,128)(2,1)S(1)} %get-tuple-element.111), channel_id=1, source_target_pairs={{0,7},{1,4},{2,5},{3,6},{4,11},{5,8},{6,9},{7,10},{8,15},{9,12},{1... | collective-permute-start | bytes 98312 | tf_op jit(solution)/shard_map/ppermute | solution.py:192
  95.7 13.8 %collective-permute-start.41 = (bf16[32,4096]{1,0:T(8,128)(2,1)S(1)}, bf16[32,4096]{1,0:T(8,128)(2,1)S(1)}, u32[]{:S(2)}, u32[]{:S(2)}) collective-permute-start(bf16[32,4096]{1,0:T(8,128)(2,1)S(1)} %get-tuple-element.115.refs_6_), channel_id=1, source_target_pairs={{0,4},{1,5},{2,6},{3,7},{4,8},{5,9},{6,10},{7,11},{8,12},{9,13},{1... | collective-permute-start | bytes 786440 | tf_op jit(solution)/shard_map/ppermute | solution.py:192
  95.8 12.5 %collective-permute-start.42 = (bf16[32,512]{1,0:T(8,128)(2,1)S(1)}, bf16[32,512]{1,0:T(8,128)(2,1)S(1)}, u32[]{:S(2)}, u32[]{:S(2)}) collective-permute-start(bf16[32,512]{1,0:T(8,128)(2,1)S(1)} %get-tuple-element.120), channel_id=1, source_target_pairs={{0,5},{1,6},{2,7},{3,4},{4,9},{5,10},{6,11},{7,8},{8,13},{9,14},{1... | collective-permute-start | bytes 98312 | tf_op jit(solution)/shard_map/ppermute | solution.py:192
  101.1 8.4 %collective-permute-start.43 = (bf16[32,512]{1,0:T(8,128)(2,1)S(1)}, bf16[32,512]{1,0:T(8,128)(2,1)S(1)}, u32[]{:S(2)}, u32[]{:S(2)}) collective-permute-start(bf16[32,512]{1,0:T(8,128)(2,1)S(1)} %get-tuple-element.121), channel_id=1, source_target_pairs={{0,7},{1,4},{2,5},{3,6},{4,11},{5,8},{6,9},{7,10},{8,15},{9,12},{1... | collective-permute-start | bytes 98312 | tf_op jit(solution)/shard_map/ppermute | solution.py:192
  102.9 13.4 %collective-permute-start.38 = (bf16[32,4096]{1,0:T(8,128)(2,1)S(1)}, bf16[32,4096]{1,0:T(8,128)(2,1)S(1)}, u32[]{:S(2)}, u32[]{:S(2)}) collective-permute-start(bf16[32,4096]{1,0:T(8,128)(2,1)S(1)} %get-tuple-element.117.refs_6_), channel_id=1, source_target_pairs={{0,4},{1,5},{2,6},{3,7},{4,8},{5,9},{6,10},{7,11},{8,12},{9,13},{1... | collective-permute-start | bytes 786440 | tf_op jit(solution)/shard_map/ppermute | solution.py:192
  103.0 12.9 %collective-permute-start.39 = (bf16[32,512]{1,0:T(8,128)(2,1)S(1)}, bf16[32,512]{1,0:T(8,128)(2,1)S(1)}, u32[]{:S(2)}, u32[]{:S(2)}) collective-permute-start(bf16[32,512]{1,0:T(8,128)(2,1)S(1)} %get-tuple-element.118), channel_id=1, source_target_pairs={{0,5},{1,6},{2,7},{3,4},{4,9},{5,10},{6,11},{7,8},{8,13},{9,14},{1... | collective-permute-start | bytes 98312 | tf_op jit(solution)/shard_map/ppermute | solution.py:192
  108.3 8.0 %collective-permute-start.40 = (bf16[32,512]{1,0:T(8,128)(2,1)S(1)}, bf16[32,512]{1,0:T(8,128)(2,1)S(1)}, u32[]{:S(2)}, u32[]{:S(2)}) collective-permute-start(bf16[32,512]{1,0:T(8,128)(2,1)S(1)} %get-tuple-element.119), channel_id=1, source_target_pairs={{0,7},{1,4},{2,5},{3,6},{4,11},{5,8},{6,9},{7,10},{8,15},{9,12},{1... | collective-permute-start | bytes 98312 | tf_op jit(solution)/shard_map/ppermute | solution.py:192

commit v12 on v11

--- a/solution.py
+++ b/solution.py
@@ -183,10 +183,10 @@
     edge = HALO * BLK
     emitted_aval = jax.ShapeDtypeStruct((TICKS, height, width), jnp.bfloat16)
 
-    def hop(values, step, shift):
+    def hop(values, step, shift, closed=True):
         pairs = [
             (s * blks + i, (s + step) % sections * blks + (i + shift) % blks)
-            for s in range(sections)
+            for s in range(sections if closed else sections - step)
             for i in range(blks)
         ]
         return lax.ppermute(values, ("section", "blk"), pairs)
@@ -217,7 +217,7 @@
             if not last:
                 prev, left, right = outs
                 prev_slot = (tick, c * rows)
-                parts[c] = (hop(prev, 1, 0), hop(right, 1, 1), hop(left, 1, -1), 0)
+                parts[c] = (hop(prev, 1, 0), hop(right, 1, 1), hop(left, 1, -1, closed=False), 0)
     return emitted
 
 

time: 117 us -> 121 us (1.034)
  starting transfers between devices: 35.2 us -> 97.1 us
  waiting for transfers between devices: 63.7 us -> 4.4 us
    ppermute x44, starting transfers between devices: 35.2 us -> 97.1 us  [hop(): return lax.ppermute(values, ('section', 'blk'), pairs)]
    ppermute x44, waiting for transfers between devices: 63.7 us -> 4.4 us  [hop(): return lax.ppermute(values, ('section', 'blk'), pairs)]
  transfers between devices with their start and end apart: 44 -> 44, of which waited for: 28 -> 3; matrix products, arithmetic and copies ran while one was open for 0% -> 0% of each run, Pallas kernels for 13% -> 13%
where the time goes in v12:
time: 121 us; the launch traced here: 120 us
  starting transfers between devices  97.1 us (80%)
  Pallas kernels  17.3 us (14%)
  waiting for transfers between devices  4.4 us (4%)
    ppermute x44, starting transfers between devices, hop(): return lax.ppermute(values, ('section', 'blk'), pairs)  97.1 us
    pallas_call x16, Pallas kernels, apply_layer(): pl.pallas_call(body, out_shape=tuple(out_shape), in_specs=specs, out_spec...  13.7 us
    ppermute x44, waiting for transfers between devices, hop(): return lax.ppermute(values, ('section', 'blk'), pairs)  4.4 us
    pallas_call x1, Pallas kernels, load(): pl.pallas_call(functools.partial(load_kernel, blks), out_shape=(*(pltpu.V...  3.62 us
  transfers between devices with their start and end apart: 44, of which 3 were waited for; matrix products, arithmetic and copies ran while one was open for 0% of the time, Pallas kernels for 13%

profile of v12, /device:TPU:1, one launch (start us, length us, event | category | flops | bytes accessed | tf_op | source)
XLA Modules:
  0.0 120.4 jit_solution(1851856123518168264)
XLA Ops:
  0.0 0.9 fusion
  0.9 2.7 %collective-permute-start = (bf16[64,512]{1,0:T(8,128)(2,1)S(1)}, bf16[64,512]{1,0:T(8,128)(2,1)S(1)}, u32[]{:S(2)}, u32[]{:S(2)}) collective-permute-start(bf16[64,512]{1,0:T(8,128)(2,1)S(1)} %get-tuple-element.124), channel_id=1, source_target_pairs={{0,1},{1,2},{2,3},{3,0},{4,5},{5,6},{6,7},{7,4},{8,9},{9,10},{10,1... | collective-permute-start | bytes 196616 | tf_op jit(solution)/shard_map/ppermute | solution.py:192
  3.5 3.6 %load.1 = (bf16[64,4096]{1,0:T(8,128)(2,1)S(1)}, bf16[32,1024,128]{2,1,0:T(8,128)(2,1)S(1)}, f32[1,4096]{1,0:T(1,128)S(1)}, s32[257]{0:T(512)S(4)}) custom-call(bf16[64,4096]{1,0:T(8,128)(2,1)} %state.1, bf16[32,1024,128]{2,1,0:T(8,128)(2,1)} %bitcast.4, f32[1,4096]{1,0:T(1,128)} %bias.1, s32[8,32]{1,0:T(8,128)} %bitcast.5), custom_call_target="tpu_custom_call" | custom-call | bytes 8388608 | tf_op jit(solution)/shard_map/load/pallas_call | solution.py:45
  7.2 0.1 collective-permute-done.1.refs_3_
  7.2 1.5 %layer_t0_r0.1 = (bf16[32,4096]{1,0:T(8,128)(2,1)S(1)}, bf16[32,512]{1,0:T(8,128)(2,1)S(1)}, bf16[32,512]{1,0:T(8,128)(2,1)S(1)}) custom-call(s32[257]{0:T(512)S(4)} %get-tuple-element.64.refs_0_, bf16[64,4096]{1,0:T(8,128)(2,1)S(1)} %get-tuple-element.65.refs_1_, bf16[64,512]{1,0:T(8,128)(2,1)S(1)} %collective-permute-done.refs_2_, ...), custom_call_target="tpu_custom_call" | custom-call | flops 2684354560 | bytes 83886080 | tf_op jit(solution)/shard_map/layer_t0_r0/pallas_call | solution.py:164
  8.7 1.3 %collective-permute-start.5 = (bf16[32,4096]{1,0:T(8,128)(2,1)S(1)}, bf16[32,4096]{1,0:T(8,128)(2,1)S(1)}, u32[]{:S(2)}, u32[]{:S(2)}) collective-permute-start(bf16[32,4096]{1,0:T(8,128)(2,1)S(1)} %get-tuple-element.68.refs_6_), channel_id=1, source_target_pairs={{0,4},{1,5},{2,6},{3,7},{4,8},{5,9},{6,10},{7,11},{8,12},{9,13},{1... | collective-permute-start | bytes 786440 | tf_op jit(solution)/shard_map/ppermute | solution.py:192
  10.0 2.9 %collective-permute-start.6 = (bf16[32,512]{1,0:T(8,128)(2,1)S(1)}, bf16[32,512]{1,0:T(8,128)(2,1)S(1)}, u32[]{:S(2)}, u32[]{:S(2)}) collective-permute-start(bf16[32,512]{1,0:T(8,128)(2,1)S(1)} %get-tuple-element.72), channel_id=1, source_target_pairs={{0,5},{1,6},{2,7},{3,4},{4,9},{5,10},{6,11},{7,8},{8,13},{9,14},{1... | collective-permute-start | bytes 98312 | tf_op jit(solution)/shard_map/ppermute | solution.py:192
  12.9 1.7 %collective-permute-start.7 = (bf16[32,512]{1,0:T(8,128)(2,1)S(1)}, bf16[32,512]{1,0:T(8,128)(2,1)S(1)}, u32[]{:S(2)}, u32[]{:S(2)}) collective-permute-start(bf16[32,512]{1,0:T(8,128)(2,1)S(1)} %get-tuple-element.73), channel_id=1, source_target_pairs={{0,7},{1,4},{2,5},{3,6},{4,11},{5,8},{6,9},{7,10},{8,15},{9,12},{1... | collective-permute-start | bytes 98312 | tf_op jit(solution)/shard_map/ppermute | solution.py:192
  14.7 1.5 %layer_t0_r32.1 = (bf16[8,64,4096]{2,1,0:T(8,128)(2,1)}, bf16[32,4096]{1,0:T(8,128)(2,1)S(1)}, bf16[32,512]{1,0:T(8,128)(2,1)S(1)}, bf16[32,512]{1,0:T(8,128)(2,1)S(1)}) custom-call(s32[257]{0:T(512)S(4)} %get-tuple-element.64.refs_0_, bf16[64,4096]{1,0:T(8,128)(2,1)S(1)} %get-tuple-element.65.refs_1_, bf16[64,512]{1,0:T(8,128)(2,1)S(1)} %collective-permute-done.refs_2_, ...), custom_call_target="tpu_custom_call" | custom-call | flops 2684354560 | bytes 83886080 | tf_op jit(solution)/shard_map/layer_t0_r32/pallas_call | solution.py:164
  16.1 1.5 %collective-permute-start.2 = (bf16[32,4096]{1,0:T(8,128)(2,1)S(1)}, bf16[32,4096]{1,0:T(8,128)(2,1)S(1)}, u32[]{:S(2)}, u32[]{:S(2)}) collective-permute-start(bf16[32,4096]{1,0:T(8,128)(2,1)S(1)} %get-tuple-element.69.refs_6_), channel_id=1, source_target_pairs={{0,4},{1,5},{2,6},{3,7},{4,8},{5,9},{6,10},{7,11},{8,12},{9,13},{1... | collective-permute-start | bytes 786440 | tf_op jit(solution)/shard_map/ppermute | solution.py:192
  17.7 3.9 %collective-permute-start.3 = (bf16[32,512]{1,0:T(8,128)(2,1)S(1)}, bf16[32,512]{1,0:T(8,128)(2,1)S(1)}, u32[]{:S(2)}, u32[]{:S(2)}) collective-permute-start(bf16[32,512]{1,0:T(8,128)(2,1)S(1)} %get-tuple-element.70), channel_id=1, source_target_pairs={{0,5},{1,6},{2,7},{3,4},{4,9},{5,10},{6,11},{7,8},{8,13},{9,14},{1... | collective-permute-start | bytes 98312 | tf_op jit(solution)/shard_map/ppermute | solution.py:192
  21.6 1.3 %collective-permute-start.4 = (bf16[32,512]{1,0:T(8,128)(2,1)S(1)}, bf16[32,512]{1,0:T(8,128)(2,1)S(1)}, u32[]{:S(2)}, u32[]{:S(2)}) collective-permute-start(bf16[32,512]{1,0:T(8,128)(2,1)S(1)} %get-tuple-element.71), channel_id=1, source_target_pairs={{0,7},{1,4},{2,5},{3,6},{4,11},{5,8},{6,9},{7,10},{8,15},{9,12},{1... | collective-permute-start | bytes 98312 | tf_op jit(solution)/shard_map/ppermute | solution.py:192
  22.9 0.8 layer_t1_r0.1
  23.7 2.6 %collective-permute-start.11 = (bf16[32,4096]{1,0:T(8,128)(2,1)S(1)}, bf16[32,4096]{1,0:T(8,128)(2,1)S(1)}, u32[]{:S(2)}, u32[]{:S(2)}) collective-permute-start(bf16[32,4096]{1,0:T(8,128)(2,1)S(1)} %get-tuple-element.75.refs_6_), channel_id=1, source_target_pairs={{0,4},{1,5},{2,6},{3,7},{4,8},{5,9},{6,10},{7,11},{8,12},{9,13},{1... | collective-permute-start | bytes 786440 | tf_op jit(solution)/shard_map/ppermute | solution.py:192
  26.3 2.6 %collective-permute-start.12 = (bf16[32,512]{1,0:T(8,128)(2,1)S(1)}, bf16[32,512]{1,0:T(8,128)(2,1)S(1)}, u32[]{:S(2)}, u32[]{:S(2)}) collective-permute-start(bf16[32,512]{1,0:T(8,128)(2,1)S(1)} %get-tuple-element.80), channel_id=1, source_target_pairs={{0,5},{1,6},{2,7},{3,4},{4,9},{5,10},{6,11},{7,8},{8,13},{9,14},{1... | collective-permute-start | bytes 98312 | tf_op jit(solution)/shard_map/ppermute | solution.py:192
  28.9 1.3 %collective-permute-start.13 = (bf16[32,512]{1,0:T(8,128)(2,1)S(1)}, bf16[32,512]{1,0:T(8,128)(2,1)S(1)}, u32[]{:S(2)}, u32[]{:S(2)}) collective-permute-start(bf16[32,512]{1,0:T(8,128)(2,1)S(1)} %get-tuple-element.81), channel_id=1, source_target_pairs={{0,7},{1,4},{2,5},{3,6},{4,11},{5,8},{6,9},{7,10},{8,15},{9,12},{1... | collective-permute-start | bytes 98312 | tf_op jit(solution)/shard_map/ppermute | solution.py:192
  30.2 0.8 layer_t1_r32.1
  31.0 2.7 %collective-permute-start.8 = (bf16[32,4096]{1,0:T(8,128)(2,1)S(1)}, bf16[32,4096]{1,0:T(8,128)(2,1)S(1)}, u32[]{:S(2)}, u32[]{:S(2)}) collective-permute-start(bf16[32,4096]{1,0:T(8,128)(2,1)S(1)} %get-tuple-element.77.refs_6_), channel_id=1, source_target_pairs={{0,4},{1,5},{2,6},{3,7},{4,8},{5,9},{6,10},{7,11},{8,12},{9,13},{1... | collective-permute-start | bytes 786440 | tf_op jit(solution)/shard_map/ppermute | solution.py:192
  33.6 4.9 %collective-permute-start.10 = (bf16[32,512]{1,0:T(8,128)(2,1)S(1)}, bf16[32,512]{1,0:T(8,128)(2,1)S(1)}, u32[]{:S(2)}, u32[]{:S(2)}) collective-permute-start(bf16[32,512]{1,0:T(8,128)(2,1)S(1)} %get-tuple-element.79), channel_id=1, source_target_pairs={{0,7},{1,4},{2,5},{3,6},{4,11},{5,8},{6,9},{7,10},{8,15},{9,12},{1... | collective-permute-start | bytes 98312 | tf_op jit(solution)/shard_map/ppermute | solution.py:192
  38.5 1.0 collective-permute-start.9
  39.5 0.7 layer_t2_r0.1
  40.3 1.3 %collective-permute-start.17 = (bf16[32,4096]{1,0:T(8,128)(2,1)S(1)}, bf16[32,4096]{1,0:T(8,128)(2,1)S(1)}, u32[]{:S(2)}, u32[]{:S(2)}) collective-permute-start(bf16[32,4096]{1,0:T(8,128)(2,1)S(1)} %get-tuple-element.83.refs_6_), channel_id=1, source_target_pairs={{0,4},{1,5},{2,6},{3,7},{4,8},{5,9},{6,10},{7,11},{8,12},{9,13},{1... | collective-permute-start | bytes 786440 | tf_op jit(solution)/shard_map/ppermute | solution.py:192
  41.6 3.0 %collective-permute-start.18 = (bf16[32,512]{1,0:T(8,128)(2,1)S(1)}, bf16[32,512]{1,0:T(8,128)(2,1)S(1)}, u32[]{:S(2)}, u32[]{:S(2)}) collective-permute-start(bf16[32,512]{1,0:T(8,128)(2,1)S(1)} %get-tuple-element.88), channel_id=1, source_target_pairs={{0,5},{1,6},{2,7},{3,4},{4,9},{5,10},{6,11},{7,8},{8,13},{9,14},{1... | collective-permute-start | bytes 98312 | tf_op jit(solution)/shard_map/ppermute | solution.py:192
  44.6 1.6 %collective-permute-start.19 = (bf16[32,512]{1,0:T(8,128)(2,1)S(1)}, bf16[32,512]{1,0:T(8,128)(2,1)S(1)}, u32[]{:S(2)}, u32[]{:S(2)}) collective-permute-start(bf16[32,512]{1,0:T(8,128)(2,1)S(1)} %get-tuple-element.89), channel_id=1, source_target_pairs={{0,7},{1,4},{2,5},{3,6},{4,11},{5,8},{6,9},{7,10},{8,15},{9,12},{1... | collective-permute-start | bytes 98312 | tf_op jit(solution)/shard_map/ppermute | solution.py:192
  46.3 0.8 layer_t2_r32.1
  47.0 2.3 %collective-permute-start.14 = (bf16[32,4096]{1,0:T(8,128)(2,1)S(1)}, bf16[32,4096]{1,0:T(8,128)(2,1)S(1)}, u32[]{:S(2)}, u32[]{:S(2)}) collective-permute-start(bf16[32,4096]{1,0:T(8,128)(2,1)S(1)} %get-tuple-element.85.refs_6_), channel_id=1, source_target_pairs={{0,4},{1,5},{2,6},{3,7},{4,8},{5,9},{6,10},{7,11},{8,12},{9,13},{1... | collective-permute-start | bytes 786440 | tf_op jit(solution)/shard_map/ppermute | solution.py:192
  49.3 2.6 %collective-permute-start.15 = (bf16[32,512]{1,0:T(8,128)(2,1)S(1)}, bf16[32,512]{1,0:T(8,128)(2,1)S(1)}, u32[]{:S(2)}, u32[]{:S(2)}) collective-permute-start(bf16[32,512]{1,0:T(8,128)(2,1)S(1)} %get-tuple-element.86), channel_id=1, source_target_pairs={{0,5},{1,6},{2,7},{3,4},{4,9},{5,10},{6,11},{7,8},{8,13},{9,14},{1... | collective-permute-start | bytes 98312 | tf_op jit(solution)/shard_map/ppermute | solution.py:192
  51.9 1.3 %collective-permute-start.16 = (bf16[32,512]{1,0:T(8,128)(2,1)S(1)}, bf16[32,512]{1,0:T(8,128)(2,1)S(1)}, u32[]{:S(2)}, u32[]{:S(2)}) collective-permute-start(bf16[32,512]{1,0:T(8,128)(2,1)S(1)} %get-tuple-element.87), channel_id=1, source_target_pairs={{0,7},{1,4},{2,5},{3,6},{4,11},{5,8},{6,9},{7,10},{8,15},{9,12},{1... | collective-permute-start | bytes 98312 | tf_op jit(solution)/shard_map/ppermute | solution.py:192
  53.2 0.8 layer_t3_r0.1
  54.0 1.3 %collective-permute-start.23 = (bf16[32,4096]{1,0:T(8,128)(2,1)S(1)}, bf16[32,4096]{1,0:T(8,128)(2,1)S(1)}, u32[]{:S(2)}, u32[]{:S(2)}) collective-permute-start(bf16[32,4096]{1,0:T(8,128)(2,1)S(1)} %get-tuple-element.91.refs_6_), channel_id=1, source_target_pairs={{0,4},{1,5},{2,6},{3,7},{4,8},{5,9},{6,10},{7,11},{8,12},{9,13},{1... | collective-permute-start | bytes 786440 | tf_op jit(solution)/shard_map/ppermute | solution.py:192
  55.3 4.6 %collective-permute-start.24 = (bf16[32,512]{1,0:T(8,128)(2,1)S(1)}, bf16[32,512]{1,0:T(8,128)(2,1)S(1)}, u32[]{:S(2)}, u32[]{:S(2)}) collective-permute-start(bf16[32,512]{1,0:T(8,128)(2,1)S(1)} %get-tuple-element.96), channel_id=1, source_target_pairs={{0,5},{1,6},{2,7},{3,4},{4,9},{5,10},{6,11},{7,8},{8,13},{9,14},{1... | collective-permute-start | bytes 98312 | tf_op jit(solution)/shard_map/ppermute | solution.py:192
  59.8 1.7 %collective-permute-start.25 = (bf16[32,512]{1,0:T(8,128)(2,1)S(1)}, bf16[32,512]{1,0:T(8,128)(2,1)S(1)}, u32[]{:S(2)}, u32[]{:S(2)}) collective-permute-start(bf16[32,512]{1,0:T(8,128)(2,1)S(1)} %get-tuple-element.97), channel_id=1, source_target_pairs={{0,7},{1,4},{2,5},{3,6},{4,11},{5,8},{6,9},{7,10},{8,15},{9,12},{1... | collective-permute-start | bytes 98312 | tf_op jit(solution)/shard_map/ppermute | solution.py:192
  61.5 0.8 layer_t3_r32.1
  62.3 1.0 collective-permute-start.20
  63.3 5.2 %collective-permute-start.21 = (bf16[32,512]{1,0:T(8,128)(2,1)S(1)}, bf16[32,512]{1,0:T(8,128)(2,1)S(1)}, u32[]{:S(2)}, u32[]{:S(2)}) collective-permute-start(bf16[32,512]{1,0:T(8,128)(2,1)S(1)} %get-tuple-element.94), channel_id=1, source_target_pairs={{0,5},{1,6},{2,7},{3,4},{4,9},{5,10},{6,11},{7,8},{8,13},{9,14},{1... | collective-permute-start | bytes 98312 | tf_op jit(solution)/shard_map/ppermute | solution.py:192
  68.5 1.6 %collective-permute-start.22 = (bf16[32,512]{1,0:T(8,128)(2,1)S(1)}, bf16[32,512]{1,0:T(8,128)(2,1)S(1)}, u32[]{:S(2)}, u32[]{:S(2)}) collective-permute-start(bf16[32,512]{1,0:T(8,128)(2,1)S(1)} %get-tuple-element.95), channel_id=1, source_target_pairs={{0,7},{1,4},{2,5},{3,6},{4,11},{5,8},{6,9},{7,10},{8,15},{9,12},{1... | collective-permute-start | bytes 98312 | tf_op jit(solution)/shard_map/ppermute | solution.py:192
  70.2 0.8 layer_t4_r0.1
  70.9 1.0 collective-permute-start.29
  71.9 2.7 %collective-permute-start.30 = (bf16[32,512]{1,0:T(8,128)(2,1)S(1)}, bf16[32,512]{1,0:T(8,128)(2,1)S(1)}, u32[]{:S(2)}, u32[]{:S(2)}) collective-permute-start(bf16[32,512]{1,0:T(8,128)(2,1)S(1)} %get-tuple-element.104), channel_id=1, source_target_pairs={{0,5},{1,6},{2,7},{3,4},{4,9},{5,10},{6,11},{7,8},{8,13},{9,14},{1... | collective-permute-start | bytes 98312 | tf_op jit(solution)/shard_map/ppermute | solution.py:192
  74.6 1.9 %collective-permute-start.31 = (bf16[32,512]{1,0:T(8,128)(2,1)S(1)}, bf16[32,512]{1,0:T(8,128)(2,1)S(1)}, u32[]{:S(2)}, u32[]{:S(2)}) collective-permute-start(bf16[32,512]{1,0:T(8,128)(2,1)S(1)} %get-tuple-element.105), channel_id=1, source_target_pairs={{0,7},{1,4},{2,5},{3,6},{4,11},{5,8},{6,9},{7,10},{8,15},{9,12},{1... | collective-permute-start | bytes 98312 | tf_op jit(solution)/shard_map/ppermute | solution.py:192
  76.5 0.8 layer_t4_r32.1
  77.3 2.7 %collective-permute-start.26 = (bf16[32,4096]{1,0:T(8,128)(2,1)S(1)}, bf16[32,4096]{1,0:T(8,128)(2,1)S(1)}, u32[]{:S(2)}, u32[]{:S(2)}) collective-permute-start(bf16[32,4096]{1,0:T(8,128)(2,1)S(1)} %get-tuple-element.101.refs_6_), channel_id=1, source_target_pairs={{0,4},{1,5},{2,6},{3,7},{4,8},{5,9},{6,10},{7,11},{8,12},{9,13},{1... | collective-permute-start | bytes 786440 | tf_op jit(solution)/shard_map/ppermute | solution.py:192
  79.9 2.7 %collective-permute-start.27 = (bf16[32,512]{1,0:T(8,128)(2,1)S(1)}, bf16[32,512]{1,0:T(8,128)(2,1)S(1)}, u32[]{:S(2)}, u32[]{:S(2)}) collective-permute-start(bf16[32,512]{1,0:T(8,128)(2,1)S(1)} %get-tuple-element.102), channel_id=1, source_target_pairs={{0,5},{1,6},{2,7},{3,4},{4,9},{5,10},{6,11},{7,8},{8,13},{9,14},{1... | collective-permute-start | bytes 98312 | tf_op jit(solution)/shard_map/ppermute | solution.py:192
  82.6 1.7 %collective-permute-start.28 = (bf16[32,512]{1,0:T(8,128)(2,1)S(1)}, bf16[32,512]{1,0:T(8,128)(2,1)S(1)}, u32[]{:S(2)}, u32[]{:S(2)}) collective-permute-start(bf16[32,512]{1,0:T(8,128)(2,1)S(1)} %get-tuple-element.103), channel_id=1, source_target_pairs={{0,7},{1,4},{2,5},{3,6},{4,11},{5,8},{6,9},{7,10},{8,15},{9,12},{1... | collective-permute-start | bytes 98312 | tf_op jit(solution)/shard_map/ppermute | solution.py:192
  84.3 0.8 layer_t5_r0.1
  85.1 0.8 collective-permute-start.35
  85.9 5.2 %collective-permute-start.36 = (bf16[32,512]{1,0:T(8,128)(2,1)S(1)}, bf16[32,512]{1,0:T(8,128)(2,1)S(1)}, u32[]{:S(2)}, u32[]{:S(2)}) collective-permute-start(bf16[32,512]{1,0:T(8,128)(2,1)S(1)} %get-tuple-element.112), channel_id=1, source_target_pairs={{0,5},{1,6},{2,7},{3,4},{4,9},{5,10},{6,11},{7,8},{8,13},{9,14},{1... | collective-permute-start | bytes 98312 | tf_op jit(solution)/shard_map/ppermute | solution.py:192
  91.1 1.3 %collective-permute-start.37 = (bf16[32,512]{1,0:T(8,128)(2,1)S(1)}, bf16[32,512]{1,0:T(8,128)(2,1)S(1)}, u32[]{:S(2)}, u32[]{:S(2)}) collective-permute-start(bf16[32,512]{1,0:T(8,128)(2,1)S(1)} %get-tuple-element.113), channel_id=1, source_target_pairs={{0,7},{1,4},{2,5},{3,6},{4,11},{5,8},{6,9},{7,10},{8,15},{9,12},{1... | collective-permute-start | bytes 98312 | tf_op jit(solution)/shard_map/ppermute | solution.py:192
  92.4 0.8 layer_t5_r32.1
  93.2 0.8 collective-permute-start.32
  94.0 5.1 %collective-permute-start.33 = (bf16[32,512]{1,0:T(8,128)(2,1)S(1)}, bf16[32,512]{1,0:T(8,128)(2,1)S(1)}, u32[]{:S(2)}, u32[]{:S(2)}) collective-permute-start(bf16[32,512]{1,0:T(8,128)(2,1)S(1)} %get-tuple-element.110), channel_id=1, source_target_pairs={{0,5},{1,6},{2,7},{3,4},{4,9},{5,10},{6,11},{7,8},{8,13},{9,14},{1... | collective-permute-start | bytes 98312 | tf_op jit(solution)/shard_map/ppermute | solution.py:192
  99.1 1.3 %collective-permute-start.34 = (bf16[32,512]{1,0:T(8,128)(2,1)S(1)}, bf16[32,512]{1,0:T(8,128)(2,1)S(1)}, u32[]{:S(2)}, u32[]{:S(2)}) collective-permute-start(bf16[32,512]{1,0:T(8,128)(2,1)S(1)} %get-tuple-element.111), channel_id=1, source_target_pairs={{0,7},{1,4},{2,5},{3,6},{4,11},{5,8},{6,9},{7,10},{8,15},{9,12},{1... | collective-permute-start | bytes 98312 | tf_op jit(solution)/shard_map/ppermute | solution.py:192
  100.4 0.8 layer_t6_r0.1
  101.2 1.2 collective-permute-start.41
  102.4 2.7 %collective-permute-start.42 = (bf16[32,512]{1,0:T(8,128)(2,1)S(1)}, bf16[32,512]{1,0:T(8,128)(2,1)S(1)}, u32[]{:S(2)}, u32[]{:S(2)}) collective-permute-start(bf16[32,512]{1,0:T(8,128)(2,1)S(1)} %get-tuple-element.120), channel_id=1, source_target_pairs={{0,5},{1,6},{2,7},{3,4},{4,9},{5,10},{6,11},{7,8},{8,13},{9,14},{1... | collective-permute-start | bytes 98312 | tf_op jit(solution)/shard_map/ppermute | solution.py:192
  105.1 1.3 %collective-permute-start.43 = (bf16[32,512]{1,0:T(8,128)(2,1)S(1)}, bf16[32,512]{1,0:T(8,128)(2,1)S(1)}, u32[]{:S(2)}, u32[]{:S(2)}) collective-permute-start(bf16[32,512]{1,0:T(8,128)(2,1)S(1)} %get-tuple-element.121), channel_id=1, source_target_pairs={{0,7},{1,4},{2,5},{3,6},{4,11},{5,8},{6,9},{7,10},{8,15},{9,12},{1... | collective-permute-start | bytes 98312 | tf_op jit(solution)/shard_map/ppermute | solution.py:192
  106.4 0.8 layer_t6_r32.1
  107.2 1.6 %collective-permute-start.38 = (bf16[32,4096]{1,0:T(8,128)(2,1)S(1)}, bf16[32,4096]{1,0:T(8,128)(2,1)S(1)}, u32[]{:S(2)}, u32[]{:S(2)}) collective-permute-start(bf16[32,4096]{1,0:T(8,128)(2,1)S(1)} %get-tuple-element.117.refs_6_), channel_id=1, source_target_pairs={{0,4},{1,5},{2,6},{3,7},{4,8},{5,9},{6,10},{7,11},{8,12},{9,13},{1... | collective-permute-start | bytes 786440 | tf_op jit(solution)/shard_map/ppermute | solution.py:192
  108.8 4.1 %collective-permute-start.39 = (bf16[32,512]{1,0:T(8,128)(2,1)S(1)}, bf16[32,512]{1,0:T(8,128)(2,1)S(1)}, u32[]{:S(2)}, u32[]{:S(2)}) collective-permute-start(bf16[32,512]{1,0:T(8,128)(2,1)S(1)} %get-tuple-element.118), channel_id=1, source_target_pairs={{0,5},{1,6},{2,7},{3,4},{4,9},{5,10},{6,11},{7,8},{8,13},{9,14},{1... | collective-permute-start | bytes 98312 | tf_op jit(solution)/shard_map/ppermute | solution.py:192
  112.8 0.2 collective-permute-done.42.refs_2_
  113.0 1.3 %collective-permute-start.40 = (bf16[32,512]{1,0:T(8,128)(2,1)S(1)}, bf16[32,512]{1,0:T(8,128)(2,1)S(1)}, u32[]{:S(2)}, u32[]{:S(2)}) collective-permute-start(bf16[32,512]{1,0:T(8,128)(2,1)S(1)} %get-tuple-element.119), channel_id=1, source_target_pairs={{0,7},{1,4},{2,5},{3,6},{4,11},{5,8},{6,9},{7,10},{8,15},{9,12},{1... | collective-permute-start | bytes 98312 | tf_op jit(solution)/shard_map/ppermute | solution.py:192
  114.4 1.0 layer_t7_r0.1.refs_6_
  115.4 4.1 %collective-permute-done.39.refs_2_ = bf16[32,512]{1,0:T(8,128)(2,1)S(1)} collective-permute-done((bf16[32,512]{1,0:T(8,128)(2,1)S(1)}, bf16[32,512]{1,0:T(8,128)(2,1)S(1)}, u32[]{:S(2)}, u32[]{:S(2)}) %collective-permute-start.39) | collective-permute-done | bytes 32800 | tf_op jit(solution)/shard_map/ppermute | solution.py:192
  119.4 0.8 layer_t7_r32.1
  (42 shorter events, 0.1 us)
Async XLA Ops:
  0.9 6.3 %collective-permute-start = (bf16[64,512]{1,0:T(8,128)(2,1)S(1)}, bf16[64,512]{1,0:T(8,128)(2,1)S(1)}, u32[]{:S(2)}, u32[]{:S(2)}) collective-permute-start(bf16[64,512]{1,0:T(8,128)(2,1)S(1)} %get-tuple-element.124), channel_id=1, source_target_pairs={{0,1},{1,2},{2,3},{3,0},{4,5},{5,6},{6,7},{7,4},{8,9},{9,10},{10,1... | collective-permute-start | bytes 196616 | tf_op jit(solution)/shard_map/ppermute | solution.py:192
  3.5 3.7 %collective-permute-start.1 = (bf16[64,512]{1,0:T(8,128)(2,1)S(1)}, bf16[64,512]{1,0:T(8,128)(2,1)S(1)}, u32[]{:S(2)}, u32[]{:S(2)}) collective-permute-start(bf16[64,512]{1,0:T(8,128)(2,1)S(1)} %get-tuple-element.123), channel_id=1, source_target_pairs={{0,3},{1,0},{2,1},{3,2},{4,7},{5,4},{6,5},{7,6},{8,11},{9,8},{10,9... | collective-permute-start | bytes 196616 | tf_op jit(solution)/shard_map/ppermute | solution.py:192
  8.7 14.2 %collective-permute-start.5 = (bf16[32,4096]{1,0:T(8,128)(2,1)S(1)}, bf16[32,4096]{1,0:T(8,128)(2,1)S(1)}, u32[]{:S(2)}, u32[]{:S(2)}) collective-permute-start(bf16[32,4096]{1,0:T(8,128)(2,1)S(1)} %get-tuple-element.68.refs_6_), channel_id=1, source_target_pairs={{0,4},{1,5},{2,6},{3,7},{4,8},{5,9},{6,10},{7,11},{8,12},{9,13},{1... | collective-permute-start | bytes 786440 | tf_op jit(solution)/shard_map/ppermute | solution.py:192
  10.0 11.6 %collective-permute-start.6 = (bf16[32,512]{1,0:T(8,128)(2,1)S(1)}, bf16[32,512]{1,0:T(8,128)(2,1)S(1)}, u32[]{:S(2)}, u32[]{:S(2)}) collective-permute-start(bf16[32,512]{1,0:T(8,128)(2,1)S(1)} %get-tuple-element.72), channel_id=1, source_target_pairs={{0,5},{1,6},{2,7},{3,4},{4,9},{5,10},{6,11},{7,8},{8,13},{9,14},{1... | collective-permute-start | bytes 98312 | tf_op jit(solution)/shard_map/ppermute | solution.py:192
  12.9 9.9 %collective-permute-start.7 = (bf16[32,512]{1,0:T(8,128)(2,1)S(1)}, bf16[32,512]{1,0:T(8,128)(2,1)S(1)}, u32[]{:S(2)}, u32[]{:S(2)}) collective-permute-start(bf16[32,512]{1,0:T(8,128)(2,1)S(1)} %get-tuple-element.73), channel_id=1, source_target_pairs={{0,7},{1,4},{2,5},{3,6},{4,11},{5,8},{6,9},{7,10},{8,15},{9,12},{1... | collective-permute-start | bytes 98312 | tf_op jit(solution)/shard_map/ppermute | solution.py:192
  16.1 14.0 %collective-permute-start.2 = (bf16[32,4096]{1,0:T(8,128)(2,1)S(1)}, bf16[32,4096]{1,0:T(8,128)(2,1)S(1)}, u32[]{:S(2)}, u32[]{:S(2)}) collective-permute-start(bf16[32,4096]{1,0:T(8,128)(2,1)S(1)} %get-tuple-element.69.refs_6_), channel_id=1, source_target_pairs={{0,4},{1,5},{2,6},{3,7},{4,8},{5,9},{6,10},{7,11},{8,12},{9,13},{1... | collective-permute-start | bytes 786440 | tf_op jit(solution)/shard_map/ppermute | solution.py:192
  17.7 11.2 %collective-permute-start.3 = (bf16[32,512]{1,0:T(8,128)(2,1)S(1)}, bf16[32,512]{1,0:T(8,128)(2,1)S(1)}, u32[]{:S(2)}, u32[]{:S(2)}) collective-permute-start(bf16[32,512]{1,0:T(8,128)(2,1)S(1)} %get-tuple-element.70), channel_id=1, source_target_pairs={{0,5},{1,6},{2,7},{3,4},{4,9},{5,10},{6,11},{7,8},{8,13},{9,14},{1... | collective-permute-start | bytes 98312 | tf_op jit(solution)/shard_map/ppermute | solution.py:192
  21.6 8.6 %collective-permute-start.4 = (bf16[32,512]{1,0:T(8,128)(2,1)S(1)}, bf16[32,512]{1,0:T(8,128)(2,1)S(1)}, u32[]{:S(2)}, u32[]{:S(2)}) collective-permute-start(bf16[32,512]{1,0:T(8,128)(2,1)S(1)} %get-tuple-element.71), channel_id=1, source_target_pairs={{0,7},{1,4},{2,5},{3,6},{4,11},{5,8},{6,9},{7,10},{8,15},{9,12},{1... | collective-permute-start | bytes 98312 | tf_op jit(solution)/shard_map/ppermute | solution.py:192
  23.7 15.9 %collective-permute-start.11 = (bf16[32,4096]{1,0:T(8,128)(2,1)S(1)}, bf16[32,4096]{1,0:T(8,128)(2,1)S(1)}, u32[]{:S(2)}, u32[]{:S(2)}) collective-permute-start(bf16[32,4096]{1,0:T(8,128)(2,1)S(1)} %get-tuple-element.75.refs_6_), channel_id=1, source_target_pairs={{0,4},{1,5},{2,6},{3,7},{4,8},{5,9},{6,10},{7,11},{8,12},{9,13},{1... | collective-permute-start | bytes 786440 | tf_op jit(solution)/shard_map/ppermute | solution.py:192
  26.3 12.2 %collective-permute-start.12 = (bf16[32,512]{1,0:T(8,128)(2,1)S(1)}, bf16[32,512]{1,0:T(8,128)(2,1)S(1)}, u32[]{:S(2)}, u32[]{:S(2)}) collective-permute-start(bf16[32,512]{1,0:T(8,128)(2,1)S(1)} %get-tuple-element.80), channel_id=1, source_target_pairs={{0,5},{1,6},{2,7},{3,4},{4,9},{5,10},{6,11},{7,8},{8,13},{9,14},{1... | collective-permute-start | bytes 98312 | tf_op jit(solution)/shard_map/ppermute | solution.py:192
  28.9 10.6 %collective-permute-start.13 = (bf16[32,512]{1,0:T(8,128)(2,1)S(1)}, bf16[32,512]{1,0:T(8,128)(2,1)S(1)}, u32[]{:S(2)}, u32[]{:S(2)}) collective-permute-start(bf16[32,512]{1,0:T(8,128)(2,1)S(1)} %get-tuple-element.81), channel_id=1, source_target_pairs={{0,7},{1,4},{2,5},{3,6},{4,11},{5,8},{6,9},{7,10},{8,15},{9,12},{1... | collective-permute-start | bytes 98312 | tf_op jit(solution)/shard_map/ppermute | solution.py:192
  31.0 15.3 %collective-permute-start.8 = (bf16[32,4096]{1,0:T(8,128)(2,1)S(1)}, bf16[32,4096]{1,0:T(8,128)(2,1)S(1)}, u32[]{:S(2)}, u32[]{:S(2)}) collective-permute-start(bf16[32,4096]{1,0:T(8,128)(2,1)S(1)} %get-tuple-element.77.refs_6_), channel_id=1, source_target_pairs={{0,4},{1,5},{2,6},{3,7},{4,8},{5,9},{6,10},{7,11},{8,12},{9,13},{1... | collective-permute-start | bytes 786440 | tf_op jit(solution)/shard_map/ppermute | solution.py:192
  33.6 11.0 %collective-permute-start.10 = (bf16[32,512]{1,0:T(8,128)(2,1)S(1)}, bf16[32,512]{1,0:T(8,128)(2,1)S(1)}, u32[]{:S(2)}, u32[]{:S(2)}) collective-permute-start(bf16[32,512]{1,0:T(8,128)(2,1)S(1)} %get-tuple-element.79), channel_id=1, source_target_pairs={{0,7},{1,4},{2,5},{3,6},{4,11},{5,8},{6,9},{7,10},{8,15},{9,12},{1... | collective-permute-start | bytes 98312 | tf_op jit(solution)/shard_map/ppermute | solution.py:192
  38.5 7.7 %collective-permute-start.9 = (bf16[32,512]{1,0:T(8,128)(2,1)S(1)}, bf16[32,512]{1,0:T(8,128)(2,1)S(1)}, u32[]{:S(2)}, u32[]{:S(2)}) collective-permute-start(bf16[32,512]{1,0:T(8,128)(2,1)S(1)} %get-tuple-element.78), channel_id=1, source_target_pairs={{0,5},{1,6},{2,7},{3,4},{4,9},{5,10},{6,11},{7,8},{8,13},{9,14},{1... | collective-permute-start | bytes 98312 | tf_op jit(solution)/shard_map/ppermute | solution.py:192
  40.3 12.9 %collective-permute-start.17 = (bf16[32,4096]{1,0:T(8,128)(2,1)S(1)}, bf16[32,4096]{1,0:T(8,128)(2,1)S(1)}, u32[]{:S(2)}, u32[]{:S(2)}) collective-permute-start(bf16[32,4096]{1,0:T(8,128)(2,1)S(1)} %get-tuple-element.83.refs_6_), channel_id=1, source_target_pairs={{0,4},{1,5},{2,6},{3,7},{4,8},{5,9},{6,10},{7,11},{8,12},{9,13},{1... | collective-permute-start | bytes 786440 | tf_op jit(solution)/shard_map/ppermute | solution.py:192
  41.6 10.3 %collective-permute-start.18 = (bf16[32,512]{1,0:T(8,128)(2,1)S(1)}, bf16[32,512]{1,0:T(8,128)(2,1)S(1)}, u32[]{:S(2)}, u32[]{:S(2)}) collective-permute-start(bf16[32,512]{1,0:T(8,128)(2,1)S(1)} %get-tuple-element.88), channel_id=1, source_target_pairs={{0,5},{1,6},{2,7},{3,4},{4,9},{5,10},{6,11},{7,8},{8,13},{9,14},{1... | collective-permute-start | bytes 98312 | tf_op jit(solution)/shard_map/ppermute | solution.py:192
  44.6 8.6 %collective-permute-start.19 = (bf16[32,512]{1,0:T(8,128)(2,1)S(1)}, bf16[32,512]{1,0:T(8,128)(2,1)S(1)}, u32[]{:S(2)}, u32[]{:S(2)}) collective-permute-start(bf16[32,512]{1,0:T(8,128)(2,1)S(1)} %get-tuple-element.89), channel_id=1, source_target_pairs={{0,7},{1,4},{2,5},{3,6},{4,11},{5,8},{6,9},{7,10},{8,15},{9,12},{1... | collective-permute-start | bytes 98312 | tf_op jit(solution)/shard_map/ppermute | solution.py:192
  47.0 14.5 %collective-permute-start.14 = (bf16[32,4096]{1,0:T(8,128)(2,1)S(1)}, bf16[32,4096]{1,0:T(8,128)(2,1)S(1)}, u32[]{:S(2)}, u32[]{:S(2)}) collective-permute-start(bf16[32,4096]{1,0:T(8,128)(2,1)S(1)} %get-tuple-element.85.refs_6_), channel_id=1, source_target_pairs={{0,4},{1,5},{2,6},{3,7},{4,8},{5,9},{6,10},{7,11},{8,12},{9,13},{1... | collective-permute-start | bytes 786440 | tf_op jit(solution)/shard_map/ppermute | solution.py:192
  49.3 10.5 %collective-permute-start.15 = (bf16[32,512]{1,0:T(8,128)(2,1)S(1)}, bf16[32,512]{1,0:T(8,128)(2,1)S(1)}, u32[]{:S(2)}, u32[]{:S(2)}) collective-permute-start(bf16[32,512]{1,0:T(8,128)(2,1)S(1)} %get-tuple-element.86), channel_id=1, source_target_pairs={{0,5},{1,6},{2,7},{3,4},{4,9},{5,10},{6,11},{7,8},{8,13},{9,14},{1... | collective-permute-start | bytes 98312 | tf_op jit(solution)/shard_map/ppermute | solution.py:192
  51.9 9.6 %collective-permute-start.16 = (bf16[32,512]{1,0:T(8,128)(2,1)S(1)}, bf16[32,512]{1,0:T(8,128)(2,1)S(1)}, u32[]{:S(2)}, u32[]{:S(2)}) collective-permute-start(bf16[32,512]{1,0:T(8,128)(2,1)S(1)} %get-tuple-element.87), channel_id=1, source_target_pairs={{0,7},{1,4},{2,5},{3,6},{4,11},{5,8},{6,9},{7,10},{8,15},{9,12},{1... | collective-permute-start | bytes 98312 | tf_op jit(solution)/shard_map/ppermute | solution.py:192
  54.0 16.2 %collective-permute-start.23 = (bf16[32,4096]{1,0:T(8,128)(2,1)S(1)}, bf16[32,4096]{1,0:T(8,128)(2,1)S(1)}, u32[]{:S(2)}, u32[]{:S(2)}) collective-permute-start(bf16[32,4096]{1,0:T(8,128)(2,1)S(1)} %get-tuple-element.91.refs_6_), channel_id=1, source_target_pairs={{0,4},{1,5},{2,6},{3,7},{4,8},{5,9},{6,10},{7,11},{8,12},{9,13},{1... | collective-permute-start | bytes 786440 | tf_op jit(solution)/shard_map/ppermute | solution.py:192
  55.3 13.2 %collective-permute-start.24 = (bf16[32,512]{1,0:T(8,128)(2,1)S(1)}, bf16[32,512]{1,0:T(8,128)(2,1)S(1)}, u32[]{:S(2)}, u32[]{:S(2)}) collective-permute-start(bf16[32,512]{1,0:T(8,128)(2,1)S(1)} %get-tuple-element.96), channel_id=1, source_target_pairs={{0,5},{1,6},{2,7},{3,4},{4,9},{5,10},{6,11},{7,8},{8,13},{9,14},{1... | collective-permute-start | bytes 98312 | tf_op jit(solution)/shard_map/ppermute | solution.py:192
  59.8 10.3 %collective-permute-start.25 = (bf16[32,512]{1,0:T(8,128)(2,1)S(1)}, bf16[32,512]{1,0:T(8,128)(2,1)S(1)}, u32[]{:S(2)}, u32[]{:S(2)}) collective-permute-start(bf16[32,512]{1,0:T(8,128)(2,1)S(1)} %get-tuple-element.97), channel_id=1, source_target_pairs={{0,7},{1,4},{2,5},{3,6},{4,11},{5,8},{6,9},{7,10},{8,15},{9,12},{1... | collective-permute-start | bytes 98312 | tf_op jit(solution)/shard_map/ppermute | solution.py:192
  62.3 14.2 %collective-permute-start.20 = (bf16[32,4096]{1,0:T(8,128)(2,1)S(1)}, bf16[32,4096]{1,0:T(8,128)(2,1)S(1)}, u32[]{:S(2)}, u32[]{:S(2)}) collective-permute-start(bf16[32,4096]{1,0:T(8,128)(2,1)S(1)} %get-tuple-element.93.refs_6_), channel_id=1, source_target_pairs={{0,4},{1,5},{2,6},{3,7},{4,8},{5,9},{6,10},{7,11},{8,12},{9,13},{1... | collective-permute-start | bytes 786440 | tf_op jit(solution)/shard_map/ppermute | solution.py:192
  63.3 11.4 %collective-permute-start.21 = (bf16[32,512]{1,0:T(8,128)(2,1)S(1)}, bf16[32,512]{1,0:T(8,128)(2,1)S(1)}, u32[]{:S(2)}, u32[]{:S(2)}) collective-permute-start(bf16[32,512]{1,0:T(8,128)(2,1)S(1)} %get-tuple-element.94), channel_id=1, source_target_pairs={{0,5},{1,6},{2,7},{3,4},{4,9},{5,10},{6,11},{7,8},{8,13},{9,14},{1... | collective-permute-start | bytes 98312 | tf_op jit(solution)/shard_map/ppermute | solution.py:192
  68.5 8.0 %collective-permute-start.22 = (bf16[32,512]{1,0:T(8,128)(2,1)S(1)}, bf16[32,512]{1,0:T(8,128)(2,1)S(1)}, u32[]{:S(2)}, u32[]{:S(2)}) collective-permute-start(bf16[32,512]{1,0:T(8,128)(2,1)S(1)} %get-tuple-element.95), channel_id=1, source_target_pairs={{0,7},{1,4},{2,5},{3,6},{4,11},{5,8},{6,9},{7,10},{8,15},{9,12},{1... | collective-permute-start | bytes 98312 | tf_op jit(solution)/shard_map/ppermute | solution.py:192
  70.9 13.4 %collective-permute-start.29 = (bf16[32,4096]{1,0:T(8,128)(2,1)S(1)}, bf16[32,4096]{1,0:T(8,128)(2,1)S(1)}, u32[]{:S(2)}, u32[]{:S(2)}) collective-permute-start(bf16[32,4096]{1,0:T(8,128)(2,1)S(1)} %get-tuple-element.99.refs_6_), channel_id=1, source_target_pairs={{0,4},{1,5},{2,6},{3,7},{4,8},{5,9},{6,10},{7,11},{8,12},{9,13},{1... | collective-permute-start | bytes 786440 | tf_op jit(solution)/shard_map/ppermute | solution.py:192
  71.9 10.7 %collective-permute-start.30 = (bf16[32,512]{1,0:T(8,128)(2,1)S(1)}, bf16[32,512]{1,0:T(8,128)(2,1)S(1)}, u32[]{:S(2)}, u32[]{:S(2)}) collective-permute-start(bf16[32,512]{1,0:T(8,128)(2,1)S(1)} %get-tuple-element.104), channel_id=1, source_target_pairs={{0,5},{1,6},{2,7},{3,4},{4,9},{5,10},{6,11},{7,8},{8,13},{9,14},{1... | collective-permute-start | bytes 98312 | tf_op jit(solution)/shard_map/ppermute | solution.py:192
  74.6 9.7 %collective-permute-start.31 = (bf16[32,512]{1,0:T(8,128)(2,1)S(1)}, bf16[32,512]{1,0:T(8,128)(2,1)S(1)}, u32[]{:S(2)}, u32[]{:S(2)}) collective-permute-start(bf16[32,512]{1,0:T(8,128)(2,1)S(1)} %get-tuple-element.105), channel_id=1, source_target_pairs={{0,7},{1,4},{2,5},{3,6},{4,11},{5,8},{6,9},{7,10},{8,15},{9,12},{1... | collective-permute-start | bytes 98312 | tf_op jit(solution)/shard_map/ppermute | solution.py:192
  77.3 15.1 %collective-permute-start.26 = (bf16[32,4096]{1,0:T(8,128)(2,1)S(1)}, bf16[32,4096]{1,0:T(8,128)(2,1)S(1)}, u32[]{:S(2)}, u32[]{:S(2)}) collective-permute-start(bf16[32,4096]{1,0:T(8,128)(2,1)S(1)} %get-tuple-element.101.refs_6_), channel_id=1, source_target_pairs={{0,4},{1,5},{2,6},{3,7},{4,8},{5,9},{6,10},{7,11},{8,12},{9,13},{1... | collective-permute-start | bytes 786440 | tf_op jit(solution)/shard_map/ppermute | solution.py:192
  79.9 11.2 %collective-permute-start.27 = (bf16[32,512]{1,0:T(8,128)(2,1)S(1)}, bf16[32,512]{1,0:T(8,128)(2,1)S(1)}, u32[]{:S(2)}, u32[]{:S(2)}) collective-permute-start(bf16[32,512]{1,0:T(8,128)(2,1)S(1)} %get-tuple-element.102), channel_id=1, source_target_pairs={{0,5},{1,6},{2,7},{3,4},{4,9},{5,10},{6,11},{7,8},{8,13},{9,14},{1... | collective-permute-start | bytes 98312 | tf_op jit(solution)/shard_map/ppermute | solution.py:192
  82.6 9.8 %collective-permute-start.28 = (bf16[32,512]{1,0:T(8,128)(2,1)S(1)}, bf16[32,512]{1,0:T(8,128)(2,1)S(1)}, u32[]{:S(2)}, u32[]{:S(2)}) collective-permute-start(bf16[32,512]{1,0:T(8,128)(2,1)S(1)} %get-tuple-element.103), channel_id=1, source_target_pairs={{0,7},{1,4},{2,5},{3,6},{4,11},{5,8},{6,9},{7,10},{8,15},{9,12},{1... | collective-permute-start | bytes 98312 | tf_op jit(solution)/shard_map/ppermute | solution.py:192
  85.1 15.3 %collective-permute-start.35 = (bf16[32,4096]{1,0:T(8,128)(2,1)S(1)}, bf16[32,4096]{1,0:T(8,128)(2,1)S(1)}, u32[]{:S(2)}, u32[]{:S(2)}) collective-permute-start(bf16[32,4096]{1,0:T(8,128)(2,1)S(1)} %get-tuple-element.107.refs_6_), channel_id=1, source_target_pairs={{0,4},{1,5},{2,6},{3,7},{4,8},{5,9},{6,10},{7,11},{8,12},{9,13},{1... | collective-permute-start | bytes 786440 | tf_op jit(solution)/shard_map/ppermute | solution.py:192
  85.9 13.2 %collective-permute-start.36 = (bf16[32,512]{1,0:T(8,128)(2,1)S(1)}, bf16[32,512]{1,0:T(8,128)(2,1)S(1)}, u32[]{:S(2)}, u32[]{:S(2)}) collective-permute-start(bf16[32,512]{1,0:T(8,128)(2,1)S(1)} %get-tuple-element.112), channel_id=1, source_target_pairs={{0,5},{1,6},{2,7},{3,4},{4,9},{5,10},{6,11},{7,8},{8,13},{9,14},{1... | collective-permute-start | bytes 98312 | tf_op jit(solution)/shard_map/ppermute | solution.py:192
  91.1 9.3 %collective-permute-start.37 = (bf16[32,512]{1,0:T(8,128)(2,1)S(1)}, bf16[32,512]{1,0:T(8,128)(2,1)S(1)}, u32[]{:S(2)}, u32[]{:S(2)}) collective-permute-start(bf16[32,512]{1,0:T(8,128)(2,1)S(1)} %get-tuple-element.113), channel_id=1, source_target_pairs={{0,7},{1,4},{2,5},{3,6},{4,11},{5,8},{6,9},{7,10},{8,15},{9,12},{1... | collective-permute-start | bytes 98312 | tf_op jit(solution)/shard_map/ppermute | solution.py:192
  93.2 13.3 %collective-permute-start.32 = (bf16[32,4096]{1,0:T(8,128)(2,1)S(1)}, bf16[32,4096]{1,0:T(8,128)(2,1)S(1)}, u32[]{:S(2)}, u32[]{:S(2)}) collective-permute-start(bf16[32,4096]{1,0:T(8,128)(2,1)S(1)} %get-tuple-element.109.refs_6_), channel_id=1, source_target_pairs={{0,4},{1,5},{2,6},{3,7},{4,8},{5,9},{6,10},{7,11},{8,12},{9,13},{1... | collective-permute-start | bytes 786440 | tf_op jit(solution)/shard_map/ppermute | solution.py:192
  94.0 11.1 %collective-permute-start.33 = (bf16[32,512]{1,0:T(8,128)(2,1)S(1)}, bf16[32,512]{1,0:T(8,128)(2,1)S(1)}, u32[]{:S(2)}, u32[]{:S(2)}) collective-permute-start(bf16[32,512]{1,0:T(8,128)(2,1)S(1)} %get-tuple-element.110), channel_id=1, source_target_pairs={{0,5},{1,6},{2,7},{3,4},{4,9},{5,10},{6,11},{7,8},{8,13},{9,14},{1... | collective-permute-start | bytes 98312 | tf_op jit(solution)/shard_map/ppermute | solution.py:192
  99.1 7.3 %collective-permute-start.34 = (bf16[32,512]{1,0:T(8,128)(2,1)S(1)}, bf16[32,512]{1,0:T(8,128)(2,1)S(1)}, u32[]{:S(2)}, u32[]{:S(2)}) collective-permute-start(bf16[32,512]{1,0:T(8,128)(2,1)S(1)} %get-tuple-element.111), channel_id=1, source_target_pairs={{0,7},{1,4},{2,5},{3,6},{4,11},{5,8},{6,9},{7,10},{8,15},{9,12},{1... | collective-permute-start | bytes 98312 | tf_op jit(solution)/shard_map/ppermute | solution.py:192
  101.2 13.2 %collective-permute-start.41 = (bf16[32,4096]{1,0:T(8,128)(2,1)S(1)}, bf16[32,4096]{1,0:T(8,128)(2,1)S(1)}, u32[]{:S(2)}, u32[]{:S(2)}) collective-permute-start(bf16[32,4096]{1,0:T(8,128)(2,1)S(1)} %get-tuple-element.115.refs_6_), channel_id=1, source_target_pairs={{0,4},{1,5},{2,6},{3,7},{4,8},{5,9},{6,10},{7,11},{8,12},{9,13},{1... | collective-permute-start | bytes 786440 | tf_op jit(solution)/shard_map/ppermute | solution.py:192
  102.4 10.7 %collective-permute-start.42 = (bf16[32,512]{1,0:T(8,128)(2,1)S(1)}, bf16[32,512]{1,0:T(8,128)(2,1)S(1)}, u32[]{:S(2)}, u32[]{:S(2)}) collective-permute-start(bf16[32,512]{1,0:T(8,128)(2,1)S(1)} %get-tuple-element.120), channel_id=1, source_target_pairs={{0,5},{1,6},{2,7},{3,4},{4,9},{5,10},{6,11},{7,8},{8,13},{9,14},{1... | collective-permute-start | bytes 98312 | tf_op jit(solution)/shard_map/ppermute | solution.py:192
  105.1 9.3 %collective-permute-start.43 = (bf16[32,512]{1,0:T(8,128)(2,1)S(1)}, bf16[32,512]{1,0:T(8,128)(2,1)S(1)}, u32[]{:S(2)}, u32[]{:S(2)}) collective-permute-start(bf16[32,512]{1,0:T(8,128)(2,1)S(1)} %get-tuple-element.121), channel_id=1, source_target_pairs={{0,7},{1,4},{2,5},{3,6},{4,11},{5,8},{6,9},{7,10},{8,15},{9,12},{1... | collective-permute-start | bytes 98312 | tf_op jit(solution)/shard_map/ppermute | solution.py:192
  107.2 12.2 %collective-permute-start.38 = (bf16[32,4096]{1,0:T(8,128)(2,1)S(1)}, bf16[32,4096]{1,0:T(8,128)(2,1)S(1)}, u32[]{:S(2)}, u32[]{:S(2)}) collective-permute-start(bf16[32,4096]{1,0:T(8,128)(2,1)S(1)} %get-tuple-element.117.refs_6_), channel_id=1, source_target_pairs={{0,4},{1,5},{2,6},{3,7},{4,8},{5,9},{6,10},{7,11},{8,12},{9,13},{1... | collective-permute-start | bytes 786440 | tf_op jit(solution)/shard_map/ppermute | solution.py:192
  108.8 10.6 %collective-permute-start.39 = (bf16[32,512]{1,0:T(8,128)(2,1)S(1)}, bf16[32,512]{1,0:T(8,128)(2,1)S(1)}, u32[]{:S(2)}, u32[]{:S(2)}) collective-permute-start(bf16[32,512]{1,0:T(8,128)(2,1)S(1)} %get-tuple-element.118), channel_id=1, source_target_pairs={{0,5},{1,6},{2,7},{3,4},{4,9},{5,10},{6,11},{7,8},{8,13},{9,14},{1... | collective-permute-start | bytes 98312 | tf_op jit(solution)/shard_map/ppermute | solution.py:192
  113.0 6.4 %collective-permute-start.40 = (bf16[32,512]{1,0:T(8,128)(2,1)S(1)}, bf16[32,512]{1,0:T(8,128)(2,1)S(1)}, u32[]{:S(2)}, u32[]{:S(2)}) collective-permute-start(bf16[32,512]{1,0:T(8,128)(2,1)S(1)} %get-tuple-element.119), channel_id=1, source_target_pairs={{0,7},{1,4},{2,5},{3,6},{4,11},{5,8},{6,9},{7,10},{8,15},{9,12},{1... | collective-permute-start | bytes 98312 | tf_op jit(solution)/shard_map/ppermute | solution.py:192

commit v13 on v11

--- a/solution.py
+++ b/solution.py
@@ -11,15 +11,20 @@
 HALO = 4
 TICKS = 8
 CHUNKS = 2
+PIECES = 8
 VMEM = pl.BlockSpec(memory_space=pltpu.VMEM)
 SMEM = pl.BlockSpec(memory_space=pltpu.SMEM)
 ANY = pl.BlockSpec(memory_space=pl.ANY)
 
 
 def load_kernel(blks, state, w, bias, indices, state_out, w_out, bias_out, meta, raw, sems):
+    part = w.shape[0] // PIECES
     copies = [
         pltpu.make_async_copy(src, dst, sems.at[i])
-        for i, (src, dst) in enumerate(((indices, raw), (state, state_out), (bias, bias_out), (w, w_out)))
+        for i, (src, dst) in enumerate(
+            [(indices, raw), (state, state_out), (bias, bias_out)]
+            + [(w.at[pl.ds(n * part, part)], w_out.at[pl.ds(n * part, part)]) for n in range(PIECES)]
+        )
     ]
     for copy in copies:
         copy.start()
@@ -50,7 +55,7 @@
         ),
         in_specs=[ANY] * 4,
         out_specs=(VMEM,) * 3 + (SMEM,),
-        scratch_shapes=[pltpu.SMEM(indices.shape, jnp.int32), pltpu.SemaphoreType.DMA((4,))],
+        scratch_shapes=[pltpu.SMEM(indices.shape, jnp.int32), pltpu.SemaphoreType.DMA((3 + PIECES,))],
         compiler_params=pltpu.CompilerParams(vmem_limit_bytes=16 * 1024 * 1024),
         cost_estimate=pl.CostEstimate(flops=0, bytes_accessed=w.size * 2, transcendentals=0),
         name="load",

time: 117 us -> 118 us (level)
  transfers between devices with their start and end apart: 44 -> 44, of which waited for: 28 -> 27; matrix products, arithmetic and copies ran while one was open for 0% -> 0% of each run, Pallas kernels for 13% -> 13%
where the time goes in v13:
time: 118 us; the launch traced here: 117 us
  waiting for transfers between devices  64 us (54%)
  starting transfers between devices  34.8 us (29%)
  Pallas kernels  17.2 us (15%)
    ppermute x44, waiting for transfers between devices, hop(): return lax.ppermute(values, ('section', 'blk'), pairs)  64 us
    ppermute x44, starting transfers between devices, hop(): return lax.ppermute(values, ('section', 'blk'), pairs)  34.8 us
    pallas_call x16, Pallas kernels, apply_layer(): pl.pallas_call(body, out_shape=tuple(out_shape), in_specs=specs, out_spec...  13.5 us
    pallas_call x1, Pallas kernels, load(): pl.pallas_call(functools.partial(load_kernel, blks), out_shape=(*(pltpu.V...  3.67 us
  transfers between devices with their start and end apart: 44, of which 27 were waited for; matrix products, arithmetic and copies ran while one was open for 0% of the time, Pallas kernels for 13%

profile of v13, /device:TPU:1, one launch (start us, length us, event | category | flops | bytes accessed | tf_op | source)
XLA Modules:
  0.0 117.3 jit_solution(5816521319111133203)
XLA Ops:
  0.0 0.9 fusion
  0.9 2.7 %collective-permute-start = (bf16[64,512]{1,0:T(8,128)(2,1)S(1)}, bf16[64,512]{1,0:T(8,128)(2,1)S(1)}, u32[]{:S(2)}, u32[]{:S(2)}) collective-permute-start(bf16[64,512]{1,0:T(8,128)(2,1)S(1)} %get-tuple-element.124), channel_id=1, source_target_pairs={{0,1},{1,2},{2,3},{3,0},{4,5},{5,6},{6,7},{7,4},{8,9},{9,10},{10,1... | collective-permute-start | bytes 196616 | tf_op jit(solution)/shard_map/ppermute | solution.py:197
  3.5 3.7 %load.1 = (bf16[64,4096]{1,0:T(8,128)(2,1)S(1)}, bf16[32,1024,128]{2,1,0:T(8,128)(2,1)S(1)}, f32[1,4096]{1,0:T(1,128)S(1)}, s32[257]{0:T(512)S(4)}) custom-call(bf16[64,4096]{1,0:T(8,128)(2,1)} %state.1, bf16[32,1024,128]{2,1,0:T(8,128)(2,1)} %bitcast.4, f32[1,4096]{1,0:T(1,128)} %bias.1, s32[8,32]{1,0:T(8,128)} %bitcast.5), custom_call_target="tpu_custom_call" | custom-call | bytes 8388608 | tf_op jit(solution)/shard_map/load/pallas_call | solution.py:50
  7.2 1.5 %layer_t0_r0.1 = (bf16[32,4096]{1,0:T(8,128)(2,1)S(1)}, bf16[32,512]{1,0:T(8,128)(2,1)S(1)}, bf16[32,512]{1,0:T(8,128)(2,1)S(1)}) custom-call(s32[257]{0:T(512)S(4)} %get-tuple-element.64.refs_0_, bf16[64,4096]{1,0:T(8,128)(2,1)S(1)} %get-tuple-element.65.refs_1_, bf16[64,512]{1,0:T(8,128)(2,1)S(1)} %collective-permute-done.refs_2_, ...), custom_call_target="tpu_custom_call" | custom-call | flops 2684354560 | bytes 83886080 | tf_op jit(solution)/shard_map/layer_t0_r0/pallas_call | solution.py:169
  8.7 1.3 %collective-permute-start.5 = (bf16[32,4096]{1,0:T(8,128)(2,1)S(1)}, bf16[32,4096]{1,0:T(8,128)(2,1)S(1)}, u32[]{:S(2)}, u32[]{:S(2)}) collective-permute-start(bf16[32,4096]{1,0:T(8,128)(2,1)S(1)} %get-tuple-element.68.refs_6_), channel_id=1, source_target_pairs={{0,4},{1,5},{2,6},{3,7},{4,8},{5,9},{6,10},{7,11},{8,12},{9,13},{1... | collective-permute-start | bytes 786440 | tf_op jit(solution)/shard_map/ppermute | solution.py:197
  10.0 3.0 %collective-permute-start.6 = (bf16[32,512]{1,0:T(8,128)(2,1)S(1)}, bf16[32,512]{1,0:T(8,128)(2,1)S(1)}, u32[]{:S(2)}, u32[]{:S(2)}) collective-permute-start(bf16[32,512]{1,0:T(8,128)(2,1)S(1)} %get-tuple-element.72), channel_id=1, source_target_pairs={{0,5},{1,6},{2,7},{3,4},{4,9},{5,10},{6,11},{7,8},{8,13},{9,14},{1... | collective-permute-start | bytes 98312 | tf_op jit(solution)/shard_map/ppermute | solution.py:197
  13.0 1.5 %layer_t0_r32.1 = (bf16[8,64,4096]{2,1,0:T(8,128)(2,1)}, bf16[32,4096]{1,0:T(8,128)(2,1)S(1)}, bf16[32,512]{1,0:T(8,128)(2,1)S(1)}, bf16[32,512]{1,0:T(8,128)(2,1)S(1)}) custom-call(s32[257]{0:T(512)S(4)} %get-tuple-element.64.refs_0_, bf16[64,4096]{1,0:T(8,128)(2,1)S(1)} %get-tuple-element.65.refs_1_, bf16[64,512]{1,0:T(8,128)(2,1)S(1)} %collective-permute-done.refs_2_, ...), custom_call_target="tpu_custom_call" | custom-call | flops 2684354560 | bytes 83886080 | tf_op jit(solution)/shard_map/layer_t0_r32/pallas_call | solution.py:169
  14.5 1.3 %collective-permute-start.2 = (bf16[32,4096]{1,0:T(8,128)(2,1)S(1)}, bf16[32,4096]{1,0:T(8,128)(2,1)S(1)}, u32[]{:S(2)}, u32[]{:S(2)}) collective-permute-start(bf16[32,4096]{1,0:T(8,128)(2,1)S(1)} %get-tuple-element.69.refs_6_), channel_id=1, source_target_pairs={{0,4},{1,5},{2,6},{3,7},{4,8},{5,9},{6,10},{7,11},{8,12},{9,13},{1... | collective-permute-start | bytes 786440 | tf_op jit(solution)/shard_map/ppermute | solution.py:197
  15.8 3.9 %collective-permute-start.3 = (bf16[32,512]{1,0:T(8,128)(2,1)S(1)}, bf16[32,512]{1,0:T(8,128)(2,1)S(1)}, u32[]{:S(2)}, u32[]{:S(2)}) collective-permute-start(bf16[32,512]{1,0:T(8,128)(2,1)S(1)} %get-tuple-element.70), channel_id=1, source_target_pairs={{0,5},{1,6},{2,7},{3,4},{4,9},{5,10},{6,11},{7,8},{8,13},{9,14},{1... | collective-permute-start | bytes 98312 | tf_op jit(solution)/shard_map/ppermute | solution.py:197
  19.7 1.5 %collective-permute-done.6.refs_2_ = bf16[32,512]{1,0:T(8,128)(2,1)S(1)} collective-permute-done((bf16[32,512]{1,0:T(8,128)(2,1)S(1)}, bf16[32,512]{1,0:T(8,128)(2,1)S(1)}, u32[]{:S(2)}, u32[]{:S(2)}) %collective-permute-start.6) | collective-permute-done | bytes 32800 | tf_op jit(solution)/shard_map/ppermute | solution.py:197
  21.2 1.6 %collective-permute-done.7.refs_3_ = bf16[32,512]{1,0:T(8,128)(2,1)S(1)} collective-permute-done((bf16[32,512]{1,0:T(8,128)(2,1)S(1)}, bf16[32,512]{1,0:T(8,128)(2,1)S(1)}, u32[]{:S(2)}, u32[]{:S(2)}) %collective-permute-start.7) | collective-permute-done | bytes 32800 | tf_op jit(solution)/shard_map/ppermute | solution.py:197
  22.8 0.7 layer_t1_r0.1
  23.6 0.1 collective-permute-start.11
  23.7 2.1 %collective-permute-start.12 = (bf16[32,512]{1,0:T(8,128)(2,1)S(1)}, bf16[32,512]{1,0:T(8,128)(2,1)S(1)}, u32[]{:S(2)}, u32[]{:S(2)}) collective-permute-start(bf16[32,512]{1,0:T(8,128)(2,1)S(1)} %get-tuple-element.80), channel_id=1, source_target_pairs={{0,5},{1,6},{2,7},{3,4},{4,9},{5,10},{6,11},{7,8},{8,13},{9,14},{1... | collective-permute-start | bytes 98312 | tf_op jit(solution)/shard_map/ppermute | solution.py:197
  25.8 2.4 %collective-permute-done.3.refs_2_ = bf16[32,512]{1,0:T(8,128)(2,1)S(1)} collective-permute-done((bf16[32,512]{1,0:T(8,128)(2,1)S(1)}, bf16[32,512]{1,0:T(8,128)(2,1)S(1)}, u32[]{:S(2)}, u32[]{:S(2)}) %collective-permute-start.3) | collective-permute-done | bytes 32800 | tf_op jit(solution)/shard_map/ppermute | solution.py:197
  28.2 0.3 collective-permute-done.4.refs_3_
  28.5 0.7 layer_t1_r32.1
  29.2 0.5 collective-permute-start.8
  29.7 3.9 %collective-permute-start.10 = (bf16[32,512]{1,0:T(8,128)(2,1)S(1)}, bf16[32,512]{1,0:T(8,128)(2,1)S(1)}, u32[]{:S(2)}, u32[]{:S(2)}) collective-permute-start(bf16[32,512]{1,0:T(8,128)(2,1)S(1)} %get-tuple-element.79), channel_id=1, source_target_pairs={{0,7},{1,4},{2,5},{3,6},{4,11},{5,8},{6,9},{7,10},{8,15},{9,12},{1... | collective-permute-start | bytes 98312 | tf_op jit(solution)/shard_map/ppermute | solution.py:197
  33.6 2.1 %collective-permute-done.12.refs_2_ = bf16[32,512]{1,0:T(8,128)(2,1)S(1)} collective-permute-done((bf16[32,512]{1,0:T(8,128)(2,1)S(1)}, bf16[32,512]{1,0:T(8,128)(2,1)S(1)}, u32[]{:S(2)}, u32[]{:S(2)}) %collective-permute-start.12) | collective-permute-done | bytes 32800 | tf_op jit(solution)/shard_map/ppermute | solution.py:197
  35.7 1.1 collective-permute-done.13.refs_3_
  36.8 0.7 layer_t2_r0.1
  37.6 1.1 collective-permute-start.18
  38.7 4.8 %collective-permute-done.10.refs_3_ = bf16[32,512]{1,0:T(8,128)(2,1)S(1)} collective-permute-done((bf16[32,512]{1,0:T(8,128)(2,1)S(1)}, bf16[32,512]{1,0:T(8,128)(2,1)S(1)}, u32[]{:S(2)}, u32[]{:S(2)}) %collective-permute-start.10) | collective-permute-done | bytes 32800 | tf_op jit(solution)/shard_map/ppermute | solution.py:197
  43.5 0.8 layer_t2_r32.1
  44.3 2.4 %collective-permute-start.15 = (bf16[32,512]{1,0:T(8,128)(2,1)S(1)}, bf16[32,512]{1,0:T(8,128)(2,1)S(1)}, u32[]{:S(2)}, u32[]{:S(2)}) collective-permute-start(bf16[32,512]{1,0:T(8,128)(2,1)S(1)} %get-tuple-element.86), channel_id=1, source_target_pairs={{0,5},{1,6},{2,7},{3,4},{4,9},{5,10},{6,11},{7,8},{8,13},{9,14},{1... | collective-permute-start | bytes 98312 | tf_op jit(solution)/shard_map/ppermute | solution.py:197
  46.7 2.9 %collective-permute-done.18.refs_2_ = bf16[32,512]{1,0:T(8,128)(2,1)S(1)} collective-permute-done((bf16[32,512]{1,0:T(8,128)(2,1)S(1)}, bf16[32,512]{1,0:T(8,128)(2,1)S(1)}, u32[]{:S(2)}, u32[]{:S(2)}) %collective-permute-start.18) | collective-permute-done | bytes 32800 | tf_op jit(solution)/shard_map/ppermute | solution.py:197
  49.6 1.7 %collective-permute-done.19.refs_3_ = bf16[32,512]{1,0:T(8,128)(2,1)S(1)} collective-permute-done((bf16[32,512]{1,0:T(8,128)(2,1)S(1)}, bf16[32,512]{1,0:T(8,128)(2,1)S(1)}, u32[]{:S(2)}, u32[]{:S(2)}) %collective-permute-start.19) | collective-permute-done | bytes 32800 | tf_op jit(solution)/shard_map/ppermute | solution.py:197
  51.3 0.7 layer_t3_r0.1
  52.1 2.0 %collective-permute-start.24 = (bf16[32,512]{1,0:T(8,128)(2,1)S(1)}, bf16[32,512]{1,0:T(8,128)(2,1)S(1)}, u32[]{:S(2)}, u32[]{:S(2)}) collective-permute-start(bf16[32,512]{1,0:T(8,128)(2,1)S(1)} %get-tuple-element.96), channel_id=1, source_target_pairs={{0,5},{1,6},{2,7},{3,4},{4,9},{5,10},{6,11},{7,8},{8,13},{9,14},{1... | collective-permute-start | bytes 98312 | tf_op jit(solution)/shard_map/ppermute | solution.py:197
  54.1 3.6 %collective-permute-done.15.refs_2_ = bf16[32,512]{1,0:T(8,128)(2,1)S(1)} collective-permute-done((bf16[32,512]{1,0:T(8,128)(2,1)S(1)}, bf16[32,512]{1,0:T(8,128)(2,1)S(1)}, u32[]{:S(2)}, u32[]{:S(2)}) %collective-permute-start.15) | collective-permute-done | bytes 32800 | tf_op jit(solution)/shard_map/ppermute | solution.py:197
  57.7 0.9 collective-permute-done.16.refs_3_
  58.6 0.7 layer_t3_r32.1
  59.4 1.3 %collective-permute-start.21 = (bf16[32,512]{1,0:T(8,128)(2,1)S(1)}, bf16[32,512]{1,0:T(8,128)(2,1)S(1)}, u32[]{:S(2)}, u32[]{:S(2)}) collective-permute-start(bf16[32,512]{1,0:T(8,128)(2,1)S(1)} %get-tuple-element.94), channel_id=1, source_target_pairs={{0,5},{1,6},{2,7},{3,4},{4,9},{5,10},{6,11},{7,8},{8,13},{9,14},{1... | collective-permute-start | bytes 98312 | tf_op jit(solution)/shard_map/ppermute | solution.py:197
  60.7 3.9 %collective-permute-done.24.refs_2_ = bf16[32,512]{1,0:T(8,128)(2,1)S(1)} collective-permute-done((bf16[32,512]{1,0:T(8,128)(2,1)S(1)}, bf16[32,512]{1,0:T(8,128)(2,1)S(1)}, u32[]{:S(2)}, u32[]{:S(2)}) %collective-permute-start.24) | collective-permute-done | bytes 32800 | tf_op jit(solution)/shard_map/ppermute | solution.py:197
  64.6 1.1 collective-permute-done.25.refs_3_
  65.7 0.7 layer_t4_r0.1
  66.6 1.5 %collective-permute-start.30 = (bf16[32,512]{1,0:T(8,128)(2,1)S(1)}, bf16[32,512]{1,0:T(8,128)(2,1)S(1)}, u32[]{:S(2)}, u32[]{:S(2)}) collective-permute-start(bf16[32,512]{1,0:T(8,128)(2,1)S(1)} %get-tuple-element.104), channel_id=1, source_target_pairs={{0,5},{1,6},{2,7},{3,4},{4,9},{5,10},{6,11},{7,8},{8,13},{9,14},{1... | collective-permute-start | bytes 98312 | tf_op jit(solution)/shard_map/ppermute | solution.py:197
  68.1 4.0 %collective-permute-done.21.refs_2_ = bf16[32,512]{1,0:T(8,128)(2,1)S(1)} collective-permute-done((bf16[32,512]{1,0:T(8,128)(2,1)S(1)}, bf16[32,512]{1,0:T(8,128)(2,1)S(1)}, u32[]{:S(2)}, u32[]{:S(2)}) %collective-permute-start.21) | collective-permute-done | bytes 32800 | tf_op jit(solution)/shard_map/ppermute | solution.py:197
  72.1 1.1 collective-permute-done.22.refs_3_
  73.1 0.7 layer_t4_r32.1
  74.0 1.4 %collective-permute-start.27 = (bf16[32,512]{1,0:T(8,128)(2,1)S(1)}, bf16[32,512]{1,0:T(8,128)(2,1)S(1)}, u32[]{:S(2)}, u32[]{:S(2)}) collective-permute-start(bf16[32,512]{1,0:T(8,128)(2,1)S(1)} %get-tuple-element.102), channel_id=1, source_target_pairs={{0,5},{1,6},{2,7},{3,4},{4,9},{5,10},{6,11},{7,8},{8,13},{9,14},{1... | collective-permute-start | bytes 98312 | tf_op jit(solution)/shard_map/ppermute | solution.py:197
  75.4 3.9 %collective-permute-done.30.refs_2_ = bf16[32,512]{1,0:T(8,128)(2,1)S(1)} collective-permute-done((bf16[32,512]{1,0:T(8,128)(2,1)S(1)}, bf16[32,512]{1,0:T(8,128)(2,1)S(1)}, u32[]{:S(2)}, u32[]{:S(2)}) %collective-permute-start.30) | collective-permute-done | bytes 32800 | tf_op jit(solution)/shard_map/ppermute | solution.py:197
  79.3 1.1 collective-permute-done.31.refs_3_
  80.4 0.7 layer_t5_r0.1
  81.2 1.5 %collective-permute-start.36 = (bf16[32,512]{1,0:T(8,128)(2,1)S(1)}, bf16[32,512]{1,0:T(8,128)(2,1)S(1)}, u32[]{:S(2)}, u32[]{:S(2)}) collective-permute-start(bf16[32,512]{1,0:T(8,128)(2,1)S(1)} %get-tuple-element.112), channel_id=1, source_target_pairs={{0,5},{1,6},{2,7},{3,4},{4,9},{5,10},{6,11},{7,8},{8,13},{9,14},{1... | collective-permute-start | bytes 98312 | tf_op jit(solution)/shard_map/ppermute | solution.py:197
  82.7 4.2 %collective-permute-done.27.refs_2_ = bf16[32,512]{1,0:T(8,128)(2,1)S(1)} collective-permute-done((bf16[32,512]{1,0:T(8,128)(2,1)S(1)}, bf16[32,512]{1,0:T(8,128)(2,1)S(1)}, u32[]{:S(2)}, u32[]{:S(2)}) %collective-permute-start.27) | collective-permute-done | bytes 32800 | tf_op jit(solution)/shard_map/ppermute | solution.py:197
  86.9 0.9 collective-permute-done.28.refs_3_
  87.8 0.7 layer_t5_r32.1
  88.6 1.4 %collective-permute-start.33 = (bf16[32,512]{1,0:T(8,128)(2,1)S(1)}, bf16[32,512]{1,0:T(8,128)(2,1)S(1)}, u32[]{:S(2)}, u32[]{:S(2)}) collective-permute-start(bf16[32,512]{1,0:T(8,128)(2,1)S(1)} %get-tuple-element.110), channel_id=1, source_target_pairs={{0,5},{1,6},{2,7},{3,4},{4,9},{5,10},{6,11},{7,8},{8,13},{9,14},{1... | collective-permute-start | bytes 98312 | tf_op jit(solution)/shard_map/ppermute | solution.py:197
  90.0 3.8 %collective-permute-done.36.refs_2_ = bf16[32,512]{1,0:T(8,128)(2,1)S(1)} collective-permute-done((bf16[32,512]{1,0:T(8,128)(2,1)S(1)}, bf16[32,512]{1,0:T(8,128)(2,1)S(1)}, u32[]{:S(2)}, u32[]{:S(2)}) %collective-permute-start.36) | collective-permute-done | bytes 32800 | tf_op jit(solution)/shard_map/ppermute | solution.py:197
  93.8 1.3 %collective-permute-done.37.refs_3_ = bf16[32,512]{1,0:T(8,128)(2,1)S(1)} collective-permute-done((bf16[32,512]{1,0:T(8,128)(2,1)S(1)}, bf16[32,512]{1,0:T(8,128)(2,1)S(1)}, u32[]{:S(2)}, u32[]{:S(2)}) %collective-permute-start.37) | collective-permute-done | bytes 32800 | tf_op jit(solution)/shard_map/ppermute | solution.py:197
  95.1 0.7 layer_t6_r0.1
  95.9 1.4 %collective-permute-start.42 = (bf16[32,512]{1,0:T(8,128)(2,1)S(1)}, bf16[32,512]{1,0:T(8,128)(2,1)S(1)}, u32[]{:S(2)}, u32[]{:S(2)}) collective-permute-start(bf16[32,512]{1,0:T(8,128)(2,1)S(1)} %get-tuple-element.120), channel_id=1, source_target_pairs={{0,5},{1,6},{2,7},{3,4},{4,9},{5,10},{6,11},{7,8},{8,13},{9,14},{1... | collective-permute-start | bytes 98312 | tf_op jit(solution)/shard_map/ppermute | solution.py:197
  97.3 3.9 %collective-permute-done.33.refs_2_ = bf16[32,512]{1,0:T(8,128)(2,1)S(1)} collective-permute-done((bf16[32,512]{1,0:T(8,128)(2,1)S(1)}, bf16[32,512]{1,0:T(8,128)(2,1)S(1)}, u32[]{:S(2)}, u32[]{:S(2)}) %collective-permute-start.33) | collective-permute-done | bytes 32800 | tf_op jit(solution)/shard_map/ppermute | solution.py:197
  101.2 1.0 collective-permute-done.34.refs_3_
  102.2 0.7 layer_t6_r32.1
  103.0 1.6 %collective-permute-start.39 = (bf16[32,512]{1,0:T(8,128)(2,1)S(1)}, bf16[32,512]{1,0:T(8,128)(2,1)S(1)}, u32[]{:S(2)}, u32[]{:S(2)}) collective-permute-start(bf16[32,512]{1,0:T(8,128)(2,1)S(1)} %get-tuple-element.118), channel_id=1, source_target_pairs={{0,5},{1,6},{2,7},{3,4},{4,9},{5,10},{6,11},{7,8},{8,13},{9,14},{1... | collective-permute-start | bytes 98312 | tf_op jit(solution)/shard_map/ppermute | solution.py:197
  104.6 3.8 %collective-permute-done.42.refs_2_ = bf16[32,512]{1,0:T(8,128)(2,1)S(1)} collective-permute-done((bf16[32,512]{1,0:T(8,128)(2,1)S(1)}, bf16[32,512]{1,0:T(8,128)(2,1)S(1)}, u32[]{:S(2)}, u32[]{:S(2)}) %collective-permute-start.42) | collective-permute-done | bytes 32800 | tf_op jit(solution)/shard_map/ppermute | solution.py:197
  108.5 1.2 collective-permute-done.43.refs_3_
  109.6 0.8 layer_t7_r0.1.refs_6_
  110.5 5.5 %collective-permute-done.39.refs_2_ = bf16[32,512]{1,0:T(8,128)(2,1)S(1)} collective-permute-done((bf16[32,512]{1,0:T(8,128)(2,1)S(1)}, bf16[32,512]{1,0:T(8,128)(2,1)S(1)}, u32[]{:S(2)}, u32[]{:S(2)}) %collective-permute-start.39) | collective-permute-done | bytes 32800 | tf_op jit(solution)/shard_map/ppermute | solution.py:197
  115.9 0.4 collective-permute-done.40.refs_3_
  116.4 0.8 layer_t7_r32.1
  (42 shorter events, 0.7 us)
Async XLA Ops:
  0.9 6.3 %collective-permute-start = (bf16[64,512]{1,0:T(8,128)(2,1)S(1)}, bf16[64,512]{1,0:T(8,128)(2,1)S(1)}, u32[]{:S(2)}, u32[]{:S(2)}) collective-permute-start(bf16[64,512]{1,0:T(8,128)(2,1)S(1)} %get-tuple-element.124), channel_id=1, source_target_pairs={{0,1},{1,2},{2,3},{3,0},{4,5},{5,6},{6,7},{7,4},{8,9},{9,10},{10,1... | collective-permute-start | bytes 196616 | tf_op jit(solution)/shard_map/ppermute | solution.py:197
  3.5 3.7 %collective-permute-start.1 = (bf16[64,512]{1,0:T(8,128)(2,1)S(1)}, bf16[64,512]{1,0:T(8,128)(2,1)S(1)}, u32[]{:S(2)}, u32[]{:S(2)}) collective-permute-start(bf16[64,512]{1,0:T(8,128)(2,1)S(1)} %get-tuple-element.123), channel_id=1, source_target_pairs={{0,3},{1,0},{2,1},{3,2},{4,7},{5,4},{6,5},{7,6},{8,11},{9,8},{10,9... | collective-permute-start | bytes 196616 | tf_op jit(solution)/shard_map/ppermute | solution.py:197
  8.7 14.1 %collective-permute-start.5 = (bf16[32,4096]{1,0:T(8,128)(2,1)S(1)}, bf16[32,4096]{1,0:T(8,128)(2,1)S(1)}, u32[]{:S(2)}, u32[]{:S(2)}) collective-permute-start(bf16[32,4096]{1,0:T(8,128)(2,1)S(1)} %get-tuple-element.68.refs_6_), channel_id=1, source_target_pairs={{0,4},{1,5},{2,6},{3,7},{4,8},{5,9},{6,10},{7,11},{8,12},{9,13},{1... | collective-permute-start | bytes 786440 | tf_op jit(solution)/shard_map/ppermute | solution.py:197
  10.0 11.2 %collective-permute-start.6 = (bf16[32,512]{1,0:T(8,128)(2,1)S(1)}, bf16[32,512]{1,0:T(8,128)(2,1)S(1)}, u32[]{:S(2)}, u32[]{:S(2)}) collective-permute-start(bf16[32,512]{1,0:T(8,128)(2,1)S(1)} %get-tuple-element.72), channel_id=1, source_target_pairs={{0,5},{1,6},{2,7},{3,4},{4,9},{5,10},{6,11},{7,8},{8,13},{9,14},{1... | collective-permute-start | bytes 98312 | tf_op jit(solution)/shard_map/ppermute | solution.py:197
  13.0 9.8 %collective-permute-start.7 = (bf16[32,512]{1,0:T(8,128)(2,1)S(1)}, bf16[32,512]{1,0:T(8,128)(2,1)S(1)}, u32[]{:S(2)}, u32[]{:S(2)}) collective-permute-start(bf16[32,512]{1,0:T(8,128)(2,1)S(1)} %get-tuple-element.73), channel_id=1, source_target_pairs={{0,7},{1,4},{2,5},{3,6},{4,11},{5,8},{6,9},{7,10},{8,15},{9,12},{1... | collective-permute-start | bytes 98312 | tf_op jit(solution)/shard_map/ppermute | solution.py:197
  14.5 14.0 %collective-permute-start.2 = (bf16[32,4096]{1,0:T(8,128)(2,1)S(1)}, bf16[32,4096]{1,0:T(8,128)(2,1)S(1)}, u32[]{:S(2)}, u32[]{:S(2)}) collective-permute-start(bf16[32,4096]{1,0:T(8,128)(2,1)S(1)} %get-tuple-element.69.refs_6_), channel_id=1, source_target_pairs={{0,4},{1,5},{2,6},{3,7},{4,8},{5,9},{6,10},{7,11},{8,12},{9,13},{1... | collective-permute-start | bytes 786440 | tf_op jit(solution)/shard_map/ppermute | solution.py:197
  15.8 12.4 %collective-permute-start.3 = (bf16[32,512]{1,0:T(8,128)(2,1)S(1)}, bf16[32,512]{1,0:T(8,128)(2,1)S(1)}, u32[]{:S(2)}, u32[]{:S(2)}) collective-permute-start(bf16[32,512]{1,0:T(8,128)(2,1)S(1)} %get-tuple-element.70), channel_id=1, source_target_pairs={{0,5},{1,6},{2,7},{3,4},{4,9},{5,10},{6,11},{7,8},{8,13},{9,14},{1... | collective-permute-start | bytes 98312 | tf_op jit(solution)/shard_map/ppermute | solution.py:197
  21.2 7.3 %collective-permute-start.4 = (bf16[32,512]{1,0:T(8,128)(2,1)S(1)}, bf16[32,512]{1,0:T(8,128)(2,1)S(1)}, u32[]{:S(2)}, u32[]{:S(2)}) collective-permute-start(bf16[32,512]{1,0:T(8,128)(2,1)S(1)} %get-tuple-element.71), channel_id=1, source_target_pairs={{0,7},{1,4},{2,5},{3,6},{4,11},{5,8},{6,9},{7,10},{8,15},{9,12},{1... | collective-permute-start | bytes 98312 | tf_op jit(solution)/shard_map/ppermute | solution.py:197
  23.6 13.2 %collective-permute-start.11 = (bf16[32,4096]{1,0:T(8,128)(2,1)S(1)}, bf16[32,4096]{1,0:T(8,128)(2,1)S(1)}, u32[]{:S(2)}, u32[]{:S(2)}) collective-permute-start(bf16[32,4096]{1,0:T(8,128)(2,1)S(1)} %get-tuple-element.75.refs_6_), channel_id=1, source_target_pairs={{0,4},{1,5},{2,6},{3,7},{4,8},{5,9},{6,10},{7,11},{8,12},{9,13},{1... | collective-permute-start | bytes 786440 | tf_op jit(solution)/shard_map/ppermute | solution.py:197
  23.7 12.1 %collective-permute-start.12 = (bf16[32,512]{1,0:T(8,128)(2,1)S(1)}, bf16[32,512]{1,0:T(8,128)(2,1)S(1)}, u32[]{:S(2)}, u32[]{:S(2)}) collective-permute-start(bf16[32,512]{1,0:T(8,128)(2,1)S(1)} %get-tuple-element.80), channel_id=1, source_target_pairs={{0,5},{1,6},{2,7},{3,4},{4,9},{5,10},{6,11},{7,8},{8,13},{9,14},{1... | collective-permute-start | bytes 98312 | tf_op jit(solution)/shard_map/ppermute | solution.py:197
  28.2 8.6 %collective-permute-start.13 = (bf16[32,512]{1,0:T(8,128)(2,1)S(1)}, bf16[32,512]{1,0:T(8,128)(2,1)S(1)}, u32[]{:S(2)}, u32[]{:S(2)}) collective-permute-start(bf16[32,512]{1,0:T(8,128)(2,1)S(1)} %get-tuple-element.81), channel_id=1, source_target_pairs={{0,7},{1,4},{2,5},{3,6},{4,11},{5,8},{6,9},{7,10},{8,15},{9,12},{1... | collective-permute-start | bytes 98312 | tf_op jit(solution)/shard_map/ppermute | solution.py:197
  29.2 14.2 %collective-permute-start.8 = (bf16[32,4096]{1,0:T(8,128)(2,1)S(1)}, bf16[32,4096]{1,0:T(8,128)(2,1)S(1)}, u32[]{:S(2)}, u32[]{:S(2)}) collective-permute-start(bf16[32,4096]{1,0:T(8,128)(2,1)S(1)} %get-tuple-element.77.refs_6_), channel_id=1, source_target_pairs={{0,4},{1,5},{2,6},{3,7},{4,8},{5,9},{6,10},{7,11},{8,12},{9,13},{1... | collective-permute-start | bytes 786440 | tf_op jit(solution)/shard_map/ppermute | solution.py:197
  29.7 13.7 %collective-permute-start.10 = (bf16[32,512]{1,0:T(8,128)(2,1)S(1)}, bf16[32,512]{1,0:T(8,128)(2,1)S(1)}, u32[]{:S(2)}, u32[]{:S(2)}) collective-permute-start(bf16[32,512]{1,0:T(8,128)(2,1)S(1)} %get-tuple-element.79), channel_id=1, source_target_pairs={{0,7},{1,4},{2,5},{3,6},{4,11},{5,8},{6,9},{7,10},{8,15},{9,12},{1... | collective-permute-start | bytes 98312 | tf_op jit(solution)/shard_map/ppermute | solution.py:197
  35.7 7.8 %collective-permute-start.9 = (bf16[32,512]{1,0:T(8,128)(2,1)S(1)}, bf16[32,512]{1,0:T(8,128)(2,1)S(1)}, u32[]{:S(2)}, u32[]{:S(2)}) collective-permute-start(bf16[32,512]{1,0:T(8,128)(2,1)S(1)} %get-tuple-element.78), channel_id=1, source_target_pairs={{0,5},{1,6},{2,7},{3,4},{4,9},{5,10},{6,11},{7,8},{8,13},{9,14},{1... | collective-permute-start | bytes 98312 | tf_op jit(solution)/shard_map/ppermute | solution.py:197
  37.6 13.7 %collective-permute-start.17 = (bf16[32,4096]{1,0:T(8,128)(2,1)S(1)}, bf16[32,4096]{1,0:T(8,128)(2,1)S(1)}, u32[]{:S(2)}, u32[]{:S(2)}) collective-permute-start(bf16[32,4096]{1,0:T(8,128)(2,1)S(1)} %get-tuple-element.83.refs_6_), channel_id=1, source_target_pairs={{0,4},{1,5},{2,6},{3,7},{4,8},{5,9},{6,10},{7,11},{8,12},{9,13},{1... | collective-permute-start | bytes 786440 | tf_op jit(solution)/shard_map/ppermute | solution.py:197
  37.6 12.0 %collective-permute-start.18 = (bf16[32,512]{1,0:T(8,128)(2,1)S(1)}, bf16[32,512]{1,0:T(8,128)(2,1)S(1)}, u32[]{:S(2)}, u32[]{:S(2)}) collective-permute-start(bf16[32,512]{1,0:T(8,128)(2,1)S(1)} %get-tuple-element.88), channel_id=1, source_target_pairs={{0,5},{1,6},{2,7},{3,4},{4,9},{5,10},{6,11},{7,8},{8,13},{9,14},{1... | collective-permute-start | bytes 98312 | tf_op jit(solution)/shard_map/ppermute | solution.py:197
  43.5 7.8 %collective-permute-start.19 = (bf16[32,512]{1,0:T(8,128)(2,1)S(1)}, bf16[32,512]{1,0:T(8,128)(2,1)S(1)}, u32[]{:S(2)}, u32[]{:S(2)}) collective-permute-start(bf16[32,512]{1,0:T(8,128)(2,1)S(1)} %get-tuple-element.89), channel_id=1, source_target_pairs={{0,7},{1,4},{2,5},{3,6},{4,11},{5,8},{6,9},{7,10},{8,15},{9,12},{1... | collective-permute-start | bytes 98312 | tf_op jit(solution)/shard_map/ppermute | solution.py:197
  44.2 14.4 %collective-permute-start.14 = (bf16[32,4096]{1,0:T(8,128)(2,1)S(1)}, bf16[32,4096]{1,0:T(8,128)(2,1)S(1)}, u32[]{:S(2)}, u32[]{:S(2)}) collective-permute-start(bf16[32,4096]{1,0:T(8,128)(2,1)S(1)} %get-tuple-element.85.refs_6_), channel_id=1, source_target_pairs={{0,4},{1,5},{2,6},{3,7},{4,8},{5,9},{6,10},{7,11},{8,12},{9,13},{1... | collective-permute-start | bytes 786440 | tf_op jit(solution)/shard_map/ppermute | solution.py:197
  44.3 13.4 %collective-permute-start.15 = (bf16[32,512]{1,0:T(8,128)(2,1)S(1)}, bf16[32,512]{1,0:T(8,128)(2,1)S(1)}, u32[]{:S(2)}, u32[]{:S(2)}) collective-permute-start(bf16[32,512]{1,0:T(8,128)(2,1)S(1)} %get-tuple-element.86), channel_id=1, source_target_pairs={{0,5},{1,6},{2,7},{3,4},{4,9},{5,10},{6,11},{7,8},{8,13},{9,14},{1... | collective-permute-start | bytes 98312 | tf_op jit(solution)/shard_map/ppermute | solution.py:197
  49.6 9.0 %collective-permute-start.16 = (bf16[32,512]{1,0:T(8,128)(2,1)S(1)}, bf16[32,512]{1,0:T(8,128)(2,1)S(1)}, u32[]{:S(2)}, u32[]{:S(2)}) collective-permute-start(bf16[32,512]{1,0:T(8,128)(2,1)S(1)} %get-tuple-element.87), channel_id=1, source_target_pairs={{0,7},{1,4},{2,5},{3,6},{4,11},{5,8},{6,9},{7,10},{8,15},{9,12},{1... | collective-permute-start | bytes 98312 | tf_op jit(solution)/shard_map/ppermute | solution.py:197
  52.0 13.7 %collective-permute-start.23 = (bf16[32,4096]{1,0:T(8,128)(2,1)S(1)}, bf16[32,4096]{1,0:T(8,128)(2,1)S(1)}, u32[]{:S(2)}, u32[]{:S(2)}) collective-permute-start(bf16[32,4096]{1,0:T(8,128)(2,1)S(1)} %get-tuple-element.91.refs_6_), channel_id=1, source_target_pairs={{0,4},{1,5},{2,6},{3,7},{4,8},{5,9},{6,10},{7,11},{8,12},{9,13},{1... | collective-permute-start | bytes 786440 | tf_op jit(solution)/shard_map/ppermute | solution.py:197
  52.1 12.5 %collective-permute-start.24 = (bf16[32,512]{1,0:T(8,128)(2,1)S(1)}, bf16[32,512]{1,0:T(8,128)(2,1)S(1)}, u32[]{:S(2)}, u32[]{:S(2)}) collective-permute-start(bf16[32,512]{1,0:T(8,128)(2,1)S(1)} %get-tuple-element.96), channel_id=1, source_target_pairs={{0,5},{1,6},{2,7},{3,4},{4,9},{5,10},{6,11},{7,8},{8,13},{9,14},{1... | collective-permute-start | bytes 98312 | tf_op jit(solution)/shard_map/ppermute | solution.py:197
  57.7 8.1 %collective-permute-start.25 = (bf16[32,512]{1,0:T(8,128)(2,1)S(1)}, bf16[32,512]{1,0:T(8,128)(2,1)S(1)}, u32[]{:S(2)}, u32[]{:S(2)}) collective-permute-start(bf16[32,512]{1,0:T(8,128)(2,1)S(1)} %get-tuple-element.97), channel_id=1, source_target_pairs={{0,7},{1,4},{2,5},{3,6},{4,11},{5,8},{6,9},{7,10},{8,15},{9,12},{1... | collective-permute-start | bytes 98312 | tf_op jit(solution)/shard_map/ppermute | solution.py:197
  59.3 13.8 %collective-permute-start.20 = (bf16[32,4096]{1,0:T(8,128)(2,1)S(1)}, bf16[32,4096]{1,0:T(8,128)(2,1)S(1)}, u32[]{:S(2)}, u32[]{:S(2)}) collective-permute-start(bf16[32,4096]{1,0:T(8,128)(2,1)S(1)} %get-tuple-element.93.refs_6_), channel_id=1, source_target_pairs={{0,4},{1,5},{2,6},{3,7},{4,8},{5,9},{6,10},{7,11},{8,12},{9,13},{1... | collective-permute-start | bytes 786440 | tf_op jit(solution)/shard_map/ppermute | solution.py:197
  59.4 12.7 %collective-permute-start.21 = (bf16[32,512]{1,0:T(8,128)(2,1)S(1)}, bf16[32,512]{1,0:T(8,128)(2,1)S(1)}, u32[]{:S(2)}, u32[]{:S(2)}) collective-permute-start(bf16[32,512]{1,0:T(8,128)(2,1)S(1)} %get-tuple-element.94), channel_id=1, source_target_pairs={{0,5},{1,6},{2,7},{3,4},{4,9},{5,10},{6,11},{7,8},{8,13},{9,14},{1... | collective-permute-start | bytes 98312 | tf_op jit(solution)/shard_map/ppermute | solution.py:197
  64.6 8.5 %collective-permute-start.22 = (bf16[32,512]{1,0:T(8,128)(2,1)S(1)}, bf16[32,512]{1,0:T(8,128)(2,1)S(1)}, u32[]{:S(2)}, u32[]{:S(2)}) collective-permute-start(bf16[32,512]{1,0:T(8,128)(2,1)S(1)} %get-tuple-element.95), channel_id=1, source_target_pairs={{0,7},{1,4},{2,5},{3,6},{4,11},{5,8},{6,9},{7,10},{8,15},{9,12},{1... | collective-permute-start | bytes 98312 | tf_op jit(solution)/shard_map/ppermute | solution.py:197
  66.5 13.9 %collective-permute-start.29 = (bf16[32,4096]{1,0:T(8,128)(2,1)S(1)}, bf16[32,4096]{1,0:T(8,128)(2,1)S(1)}, u32[]{:S(2)}, u32[]{:S(2)}) collective-permute-start(bf16[32,4096]{1,0:T(8,128)(2,1)S(1)} %get-tuple-element.99.refs_6_), channel_id=1, source_target_pairs={{0,4},{1,5},{2,6},{3,7},{4,8},{5,9},{6,10},{7,11},{8,12},{9,13},{1... | collective-permute-start | bytes 786440 | tf_op jit(solution)/shard_map/ppermute | solution.py:197
  66.6 12.7 %collective-permute-start.30 = (bf16[32,512]{1,0:T(8,128)(2,1)S(1)}, bf16[32,512]{1,0:T(8,128)(2,1)S(1)}, u32[]{:S(2)}, u32[]{:S(2)}) collective-permute-start(bf16[32,512]{1,0:T(8,128)(2,1)S(1)} %get-tuple-element.104), channel_id=1, source_target_pairs={{0,5},{1,6},{2,7},{3,4},{4,9},{5,10},{6,11},{7,8},{8,13},{9,14},{1... | collective-permute-start | bytes 98312 | tf_op jit(solution)/shard_map/ppermute | solution.py:197
  72.1 8.4 %collective-permute-start.31 = (bf16[32,512]{1,0:T(8,128)(2,1)S(1)}, bf16[32,512]{1,0:T(8,128)(2,1)S(1)}, u32[]{:S(2)}, u32[]{:S(2)}) collective-permute-start(bf16[32,512]{1,0:T(8,128)(2,1)S(1)} %get-tuple-element.105), channel_id=1, source_target_pairs={{0,7},{1,4},{2,5},{3,6},{4,11},{5,8},{6,9},{7,10},{8,15},{9,12},{1... | collective-permute-start | bytes 98312 | tf_op jit(solution)/shard_map/ppermute | solution.py:197
  73.9 13.9 %collective-permute-start.26 = (bf16[32,4096]{1,0:T(8,128)(2,1)S(1)}, bf16[32,4096]{1,0:T(8,128)(2,1)S(1)}, u32[]{:S(2)}, u32[]{:S(2)}) collective-permute-start(bf16[32,4096]{1,0:T(8,128)(2,1)S(1)} %get-tuple-element.101.refs_6_), channel_id=1, source_target_pairs={{0,4},{1,5},{2,6},{3,7},{4,8},{5,9},{6,10},{7,11},{8,12},{9,13},{1... | collective-permute-start | bytes 786440 | tf_op jit(solution)/shard_map/ppermute | solution.py:197
  74.0 12.9 %collective-permute-start.27 = (bf16[32,512]{1,0:T(8,128)(2,1)S(1)}, bf16[32,512]{1,0:T(8,128)(2,1)S(1)}, u32[]{:S(2)}, u32[]{:S(2)}) collective-permute-start(bf16[32,512]{1,0:T(8,128)(2,1)S(1)} %get-tuple-element.102), channel_id=1, source_target_pairs={{0,5},{1,6},{2,7},{3,4},{4,9},{5,10},{6,11},{7,8},{8,13},{9,14},{1... | collective-permute-start | bytes 98312 | tf_op jit(solution)/shard_map/ppermute | solution.py:197
  79.3 8.5 %collective-permute-start.28 = (bf16[32,512]{1,0:T(8,128)(2,1)S(1)}, bf16[32,512]{1,0:T(8,128)(2,1)S(1)}, u32[]{:S(2)}, u32[]{:S(2)}) collective-permute-start(bf16[32,512]{1,0:T(8,128)(2,1)S(1)} %get-tuple-element.103), channel_id=1, source_target_pairs={{0,7},{1,4},{2,5},{3,6},{4,11},{5,8},{6,9},{7,10},{8,15},{9,12},{1... | collective-permute-start | bytes 98312 | tf_op jit(solution)/shard_map/ppermute | solution.py:197
  81.2 13.9 %collective-permute-start.35 = (bf16[32,4096]{1,0:T(8,128)(2,1)S(1)}, bf16[32,4096]{1,0:T(8,128)(2,1)S(1)}, u32[]{:S(2)}, u32[]{:S(2)}) collective-permute-start(bf16[32,4096]{1,0:T(8,128)(2,1)S(1)} %get-tuple-element.107.refs_6_), channel_id=1, source_target_pairs={{0,4},{1,5},{2,6},{3,7},{4,8},{5,9},{6,10},{7,11},{8,12},{9,13},{1... | collective-permute-start | bytes 786440 | tf_op jit(solution)/shard_map/ppermute | solution.py:197
  81.2 12.6 %collective-permute-start.36 = (bf16[32,512]{1,0:T(8,128)(2,1)S(1)}, bf16[32,512]{1,0:T(8,128)(2,1)S(1)}, u32[]{:S(2)}, u32[]{:S(2)}) collective-permute-start(bf16[32,512]{1,0:T(8,128)(2,1)S(1)} %get-tuple-element.112), channel_id=1, source_target_pairs={{0,5},{1,6},{2,7},{3,4},{4,9},{5,10},{6,11},{7,8},{8,13},{9,14},{1... | collective-permute-start | bytes 98312 | tf_op jit(solution)/shard_map/ppermute | solution.py:197
  86.9 8.2 %collective-permute-start.37 = (bf16[32,512]{1,0:T(8,128)(2,1)S(1)}, bf16[32,512]{1,0:T(8,128)(2,1)S(1)}, u32[]{:S(2)}, u32[]{:S(2)}) collective-permute-start(bf16[32,512]{1,0:T(8,128)(2,1)S(1)} %get-tuple-element.113), channel_id=1, source_target_pairs={{0,7},{1,4},{2,5},{3,6},{4,11},{5,8},{6,9},{7,10},{8,15},{9,12},{1... | collective-permute-start | bytes 98312 | tf_op jit(solution)/shard_map/ppermute | solution.py:197
  88.6 13.6 %collective-permute-start.32 = (bf16[32,4096]{1,0:T(8,128)(2,1)S(1)}, bf16[32,4096]{1,0:T(8,128)(2,1)S(1)}, u32[]{:S(2)}, u32[]{:S(2)}) collective-permute-start(bf16[32,4096]{1,0:T(8,128)(2,1)S(1)} %get-tuple-element.109.refs_6_), channel_id=1, source_target_pairs={{0,4},{1,5},{2,6},{3,7},{4,8},{5,9},{6,10},{7,11},{8,12},{9,13},{1... | collective-permute-start | bytes 786440 | tf_op jit(solution)/shard_map/ppermute | solution.py:197
  88.6 12.6 %collective-permute-start.33 = (bf16[32,512]{1,0:T(8,128)(2,1)S(1)}, bf16[32,512]{1,0:T(8,128)(2,1)S(1)}, u32[]{:S(2)}, u32[]{:S(2)}) collective-permute-start(bf16[32,512]{1,0:T(8,128)(2,1)S(1)} %get-tuple-element.110), channel_id=1, source_target_pairs={{0,5},{1,6},{2,7},{3,4},{4,9},{5,10},{6,11},{7,8},{8,13},{9,14},{1... | collective-permute-start | bytes 98312 | tf_op jit(solution)/shard_map/ppermute | solution.py:197
  93.8 8.4 %collective-permute-start.34 = (bf16[32,512]{1,0:T(8,128)(2,1)S(1)}, bf16[32,512]{1,0:T(8,128)(2,1)S(1)}, u32[]{:S(2)}, u32[]{:S(2)}) collective-permute-start(bf16[32,512]{1,0:T(8,128)(2,1)S(1)} %get-tuple-element.111), channel_id=1, source_target_pairs={{0,7},{1,4},{2,5},{3,6},{4,11},{5,8},{6,9},{7,10},{8,15},{9,12},{1... | collective-permute-start | bytes 98312 | tf_op jit(solution)/shard_map/ppermute | solution.py:197
  95.8 13.8 %collective-permute-start.41 = (bf16[32,4096]{1,0:T(8,128)(2,1)S(1)}, bf16[32,4096]{1,0:T(8,128)(2,1)S(1)}, u32[]{:S(2)}, u32[]{:S(2)}) collective-permute-start(bf16[32,4096]{1,0:T(8,128)(2,1)S(1)} %get-tuple-element.115.refs_6_), channel_id=1, source_target_pairs={{0,4},{1,5},{2,6},{3,7},{4,8},{5,9},{6,10},{7,11},{8,12},{9,13},{1... | collective-permute-start | bytes 786440 | tf_op jit(solution)/shard_map/ppermute | solution.py:197
  95.9 12.6 %collective-permute-start.42 = (bf16[32,512]{1,0:T(8,128)(2,1)S(1)}, bf16[32,512]{1,0:T(8,128)(2,1)S(1)}, u32[]{:S(2)}, u32[]{:S(2)}) collective-permute-start(bf16[32,512]{1,0:T(8,128)(2,1)S(1)} %get-tuple-element.120), channel_id=1, source_target_pairs={{0,5},{1,6},{2,7},{3,4},{4,9},{5,10},{6,11},{7,8},{8,13},{9,14},{1... | collective-permute-start | bytes 98312 | tf_op jit(solution)/shard_map/ppermute | solution.py:197
  101.2 8.4 %collective-permute-start.43 = (bf16[32,512]{1,0:T(8,128)(2,1)S(1)}, bf16[32,512]{1,0:T(8,128)(2,1)S(1)}, u32[]{:S(2)}, u32[]{:S(2)}) collective-permute-start(bf16[32,512]{1,0:T(8,128)(2,1)S(1)} %get-tuple-element.121), channel_id=1, source_target_pairs={{0,7},{1,4},{2,5},{3,6},{4,11},{5,8},{6,9},{7,10},{8,15},{9,12},{1... | collective-permute-start | bytes 98312 | tf_op jit(solution)/shard_map/ppermute | solution.py:197
  102.9 13.5 %collective-permute-start.38 = (bf16[32,4096]{1,0:T(8,128)(2,1)S(1)}, bf16[32,4096]{1,0:T(8,128)(2,1)S(1)}, u32[]{:S(2)}, u32[]{:S(2)}) collective-permute-start(bf16[32,4096]{1,0:T(8,128)(2,1)S(1)} %get-tuple-element.117.refs_6_), channel_id=1, source_target_pairs={{0,4},{1,5},{2,6},{3,7},{4,8},{5,9},{6,10},{7,11},{8,12},{9,13},{1... | collective-permute-start | bytes 786440 | tf_op jit(solution)/shard_map/ppermute | solution.py:197
  103.0 12.9 %collective-permute-start.39 = (bf16[32,512]{1,0:T(8,128)(2,1)S(1)}, bf16[32,512]{1,0:T(8,128)(2,1)S(1)}, u32[]{:S(2)}, u32[]{:S(2)}) collective-permute-start(bf16[32,512]{1,0:T(8,128)(2,1)S(1)} %get-tuple-element.118), channel_id=1, source_target_pairs={{0,5},{1,6},{2,7},{3,4},{4,9},{5,10},{6,11},{7,8},{8,13},{9,14},{1... | collective-permute-start | bytes 98312 | tf_op jit(solution)/shard_map/ppermute | solution.py:197
  108.5 7.9 %collective-permute-start.40 = (bf16[32,512]{1,0:T(8,128)(2,1)S(1)}, bf16[32,512]{1,0:T(8,128)(2,1)S(1)}, u32[]{:S(2)}, u32[]{:S(2)}) collective-permute-start(bf16[32,512]{1,0:T(8,128)(2,1)S(1)} %get-tuple-element.119), channel_id=1, source_target_pairs={{0,7},{1,4},{2,5},{3,6},{4,11},{5,8},{6,9},{7,10},{8,15},{9,12},{1... | collective-permute-start | bytes 98312 | tf_op jit(solution)/shard_map/ppermute | solution.py:197
